TPU v7x, 32 devices: a whole 2x2x4 slice. The times are simulated.
32 devices in a mesh: section: 4 (over y, core), seq: 8 (over z, x).
Axes of the slice: x: 2, y: 2, z: 4, core: 2. Of those that a mesh axis runs over, the one named last changes fastest.
Arguments:
- activations: bfloat16 [4, 1088, 1024], P('section', 'seq'), may hold values from -60 to 60
- incoming: bfloat16 [4, 1088, 1024], P('section', 'seq'), may hold values from -6 to 6
- w_query: bfloat16 [4, 1024, 512], P('section'), may hold values from -0.1875 to 0.1875
- w_key: bfloat16 [4, 1024, 512], P('section'), may hold values from -0.1875 to 0.1875
- w_value: bfloat16 [4, 1024, 512], P('section'), may hold values from -0.1875 to 0.1875
- w_out: bfloat16 [4, 512, 2048], P('section'), may hold values from -0.25 to 0.25
- block_ids: int32 [1088], replicated, may hold values from 0 to 33, never falling along the last dimension, each value on 1 to 256 neighbouring positions
- flip_order: int32 [4, 136], P('section'), may hold values from 0 to 135, each once within a row
Outputs:
- carry_out: bfloat16 [4, 1088, 1024], P('section', 'seq')
- grad_query: float32 [4, 1024, 512], P('section', 'seq')
- grad_key: float32 [4, 1024, 512], P('section', 'seq')
- grad_value: float32 [4, 1024, 512], P('section', 'seq')
- grad_out: float32 [4, 512, 2048], P('section', 'seq')
Inputs may be any that keep to these rules, and one draw needn't show every extreme that they name: `block_ids`: block ids never fall along the sequence; each block holds 1 to 256 tokens, one exactly 256. `flip_order`: each row is a permutation.
All inputs are finite; a program needn't handle non-finite values.
Results may differ from a plain program's by a relative error of at most 0.03.
Values may be sent and summed in bfloat16 or wider, within the bound.
No kernel may reach another device: no remote copies, remote signals or barrier semaphores. Data moves between devices by JAX's collectives and lax.ppermute only.
A program may use at most 128 MiB of HBM per device.

v0:
```python
import jax
import jax.numpy as jnp
from jax import lax
from jax.sharding import PartitionSpec as P

HEADS = 8
HEAD_DIM = 64


EPSILON = 1e-06


def partner(block, axis, stride):
    count = lax.axis_size(axis)
    route = []
    for low in range(count):
        high = low | 1 << stride
        if high != low and high < count:
            route += [(low, high), (high, low)]
    return lax.ppermute(block, axis, route)


def shifted(block, axis, distance):
    devices = range(lax.axis_size(axis))
    route = [(i - distance, i) for i in devices if i - distance in devices]
    return lax.ppermute(block, axis, route)


def split_heads(matrix):
    return matrix.reshape(matrix.shape[0], HEADS, HEAD_DIM)


def head_major(matrix):
    return jnp.transpose(split_heads(matrix), (1, 0, 2))


def unit_heads(projected):
    parts = split_heads(projected)
    factor = lax.rsqrt(jnp.mean(parts * parts, axis=-1, keepdims=True) + EPSILON)
    return (parts * factor, factor)


def unit_back(grad_heads, unit, factor):
    return factor * (grad_heads - unit * jnp.mean(grad_heads * unit, axis=-1, keepdims=True))


def mirror(rows):
    for bit in range(lax.axis_size("seq").bit_length() - 1):
        rows = partner(rows, "seq", bit)
    return rows


def to_previous(rows):
    return shifted(rows, "section", -1)


def shards(activations, incoming, w_query, w_key, w_value, w_out, block_ids, flip_order):
    field = activations[0].astype(jnp.float32)
    upstream = incoming[0].astype(jnp.float32)
    weight_query = w_query[0]
    weight_key = w_key[0]
    weight_value = w_value[0]
    weight_out = w_out[0]
    flip_row = flip_order[0]
    rows = field.shape[0]
    width = field.shape[1]
    inner = weight_query.shape[1]
    scale = HEAD_DIM ** (-0.5)
    first = lax.axis_index("seq") * rows
    my_blocks = lax.dynamic_slice_in_dim(block_ids, first, rows)
    row_scale = lax.rsqrt(jnp.mean(field * field, axis=-1, keepdims=True) + EPSILON)
    unit_rows = field * row_scale
    normed = unit_rows.astype(jnp.bfloat16)
    query_raw = jnp.dot(normed, weight_query, preferred_element_type=jnp.float32)
    key_raw = jnp.dot(normed, weight_key, preferred_element_type=jnp.float32)
    values = jnp.dot(normed, weight_value, preferred_element_type=jnp.float32).astype(jnp.bfloat16)
    query_unit, query_scale = unit_heads(query_raw)
    key_unit, key_scale = unit_heads(key_raw)
    queries = query_unit.astype(jnp.bfloat16).reshape(rows, inner)
    keys = key_unit.astype(jnp.bfloat16).reshape(rows, inner)
    keys_all, values_all = (
        lax.all_gather(keys, "seq", axis=0, tiled=True),
        lax.all_gather(values, "seq", axis=0, tiled=True),
    )
    allowed = block_ids[None, :] <= my_blocks[:, None]
    query_heads = head_major(queries)
    key_heads_all = head_major(keys_all)
    value_heads_all = head_major(values_all)

    def probabilities(query_part, key_part):
        scores = jnp.dot(query_part, key_part.T, preferred_element_type=jnp.float32) * scale
        numerator = jnp.where(allowed, jnp.exp(scores), 0.0)
        denominator = jnp.sum(numerator, axis=-1, keepdims=True)
        return (numerator / denominator, denominator)

    def forward_head(operands):
        query_part, key_part, value_part = operands
        probs, denominator = probabilities(query_part, key_part)
        out_part = jnp.dot(
            probs.astype(jnp.bfloat16), value_part, preferred_element_type=jnp.float32
        ).astype(jnp.bfloat16)
        return (out_part, denominator[:, 0])

    heads_out, denominators = lax.map(forward_head, (query_heads, key_heads_all, value_heads_all))
    attended = jnp.transpose(heads_out, (1, 0, 2)).reshape(rows, inner)
    affine = jnp.dot(attended, weight_out, preferred_element_type=jnp.float32)
    shift_part = affine[:, :width]
    log_scale = affine[:, width:]
    factor = jnp.exp(-log_scale)
    latent = (field - shift_part) * factor
    grad_affine = jnp.concatenate([-upstream * factor, 1.0 - upstream * latent], axis=-1).astype(
        jnp.bfloat16
    )
    out_term = jnp.dot(attended.T, grad_affine, preferred_element_type=jnp.float32)
    grad_attn = jnp.dot(grad_affine, weight_out.T, preferred_element_type=jnp.float32).astype(
        jnp.bfloat16
    )
    correction = jnp.sum(
        split_heads(grad_attn.astype(jnp.float32)) * split_heads(attended.astype(jnp.float32)),
        axis=-1,
    )
    grad_heads = head_major(grad_attn)
    correction_heads = jnp.transpose(correction)[:, :, None]

    def backward_head(operands):
        query_part, key_part, value_part, grad_part, corr_part = operands
        probs, denominator = probabilities(query_part, key_part)
        grad_probs = jnp.dot(grad_part, value_part.T, preferred_element_type=jnp.float32)
        grad_scores = (probs * (grad_probs - corr_part)).astype(jnp.bfloat16)
        grad_qpart = jnp.dot(grad_scores, key_part, preferred_element_type=jnp.float32) * scale
        grad_kpart = jnp.dot(grad_scores.T, query_part, preferred_element_type=jnp.float32) * scale
        grad_vpart = jnp.dot(
            probs.astype(jnp.bfloat16).T, grad_part, preferred_element_type=jnp.float32
        )
        return (grad_qpart, grad_kpart, grad_vpart)

    grad_qheads, grad_kall, grad_vall = lax.map(
        backward_head, (query_heads, key_heads_all, value_heads_all, grad_heads, correction_heads)
    )
    key_terms = jnp.transpose(grad_kall, (1, 0, 2)).reshape(-1, inner)
    value_terms = jnp.transpose(grad_vall, (1, 0, 2)).reshape(-1, inner)
    grad_kunit, grad_vsum = (
        lax.psum_scatter(
            key_terms.astype(jnp.bfloat16), "seq", scatter_dimension=0, tiled=True
        ).astype(jnp.float32),
        lax.psum_scatter(
            value_terms.astype(jnp.bfloat16), "seq", scatter_dimension=0, tiled=True
        ).astype(jnp.float32),
    )
    grad_queries = (
        unit_back(jnp.transpose(grad_qheads, (1, 0, 2)), query_unit, query_scale)
        .reshape(rows, inner)
        .astype(jnp.bfloat16)
    )
    grad_keys = (
        unit_back(split_heads(grad_kunit), key_unit, key_scale)
        .reshape(rows, inner)
        .astype(jnp.bfloat16)
    )
    grad_values = grad_vsum.astype(jnp.bfloat16)
    query_term = jnp.dot(normed.T, grad_queries, preferred_element_type=jnp.float32)
    key_term = jnp.dot(normed.T, grad_keys, preferred_element_type=jnp.float32)
    value_term = jnp.dot(normed.T, grad_values, preferred_element_type=jnp.float32)
    sums = (
        lax.psum_scatter(
            query_term.astype(jnp.bfloat16), "seq", scatter_dimension=0, tiled=True
        ).astype(jnp.float32),
        lax.psum_scatter(
            key_term.astype(jnp.bfloat16), "seq", scatter_dimension=0, tiled=True
        ).astype(jnp.float32),
        lax.psum_scatter(
            value_term.astype(jnp.bfloat16), "seq", scatter_dimension=0, tiled=True
        ).astype(jnp.float32),
        lax.psum_scatter(
            out_term.astype(jnp.bfloat16), "seq", scatter_dimension=0, tiled=True
        ).astype(jnp.float32),
    )
    grad_normed = jnp.dot(grad_queries, weight_query.T, preferred_element_type=jnp.float32)
    grad_normed = grad_normed + jnp.dot(grad_keys, weight_key.T, preferred_element_type=jnp.float32)
    grad_normed = grad_normed + jnp.dot(
        grad_values, weight_value.T, preferred_element_type=jnp.float32
    )
    grad_input = upstream * factor + row_scale * (
        grad_normed - unit_rows * jnp.mean(grad_normed * unit_rows, axis=-1, keepdims=True)
    )
    grad_input = grad_input.astype(jnp.bfloat16)
    moved = mirror(to_previous(grad_input))
    carry = jnp.take(moved, flip_row, axis=0)
    return (carry[None], sums[0][None], sums[1][None], sums[2][None], sums[3][None])


def solution(mesh):
    in_specs = (
        P("section", "seq", None),
        P("section", "seq", None),
        P("section", None, None),
        P("section", None, None),
        P("section", None, None),
        P("section", None, None),
        P(),
        P("section", None),
    )
    out_specs = (
        P("section", "seq", None),
        P("section", "seq", None),
        P("section", "seq", None),
        P("section", "seq", None),
        P("section", "seq", None),
    )
    return jax.shard_map(shards, mesh=mesh, in_specs=in_specs, out_specs=out_specs, check_vma=False)
```

profile of v0, /device:TPU:5, one launch (start us, length us, event | category | flops | bytes accessed | tf_op | source)
XLA Modules:
  0.0 617.0 jit_solution(4793008536332040663)
XLA Ops:
  12.1 1.8 copy.44
  14.0 2.3 convolution_convert_fusion.5
  17.7 1.8 multiply_reduce_fusion.2
  22.5 32.5 %all-gather.3.cloned.1.call-done = bf16[1088,512]{1,0:T(8,128)(2,1)} async-done(((bf16[136,512]{1,0:T(8,128)(2,1)}), bf16[1088,512]{1,0:T(8,128)(2,1)}) %all-gather.3.cloned.1.call-update) | async-done | bytes 1114128 | tf_op jit(solution)/shard_map/all_gather | solution.py:82
  56.6 2.4 copy.48
  59.1 38.2 %all-gather.5.cloned.1.call-done = bf16[1088,512]{1,0:T(8,128)(2,1)} async-done(((bf16[136,512]{1,0:T(8,128)(2,1)}), bf16[1088,512]{1,0:T(8,128)(2,1)}) %all-gather.5.cloned.1.call-update) | async-done | bytes 1114128 | tf_op jit(solution)/shard_map/all_gather | solution.py:83
  98.9 2.4 copy.49
  101.3 26.0 %while.26 = (s32[]{:T(128)}, bf16[8,136,64]{1,2,0:T(8,128)(2,1)}, bf16[8,136,64]{2,1,0:T(8,128)(2,1)}, bf16[8,1088,64]{2,1,0:T(8,128)(2,1)}, bf16[8,1088,64]{2,1...) while((s32[]{:T(128)}, bf16[8,136,64]{1,2,0:T(8,128)(2,1)}, ...), condition=%wide.region_5.6_spmd.clone, body=%wide.region_3.5_spmd.clone.sunk | while | flops 38776184 | bytes 1820821 | solution.py:104
  102.7 1.9 fusion.133
  105.9 1.9 fusion.133
  109.2 1.9 fusion.133
  112.4 1.9 fusion.133
  115.7 1.9 fusion.133
  118.9 1.9 fusion.133
  122.2 1.9 fusion.133
  125.4 1.9 fusion.133
  134.1 1.8 reshape.196
  135.9 1.9 multiply_reduce_fusion
  138.8 1.7 copy.53
  140.5 63.2 %while.27 = (s32[]{:T(128)}, f32[8,136,64]{1,2,0:T(8,128)}, bf16[8,1088,64]{1,2,0:T(8,128)(2,1)}, bf16[8,1088,64]{1,2,0:T(8,128)(2,1)}, bf16[8,136,64]{2,1,0:T(8...) while((s32[]{:T(128)}, f32[8,136,64]{1,2,0:T(8,128)}, ...), condition=%wide.region_9.10_spmd.clone, body=%wide.region_7.9_spmd.clone.sunk | while | flops 96257400 | bytes 4307033 | solution.py:137
  141.9 1.7 fusion.146
  146.5 1.9 fusion.144
  149.8 1.7 fusion.146
  154.5 1.9 fusion.144
  162.3 1.9 fusion.144
  165.6 1.7 fusion.146
  168.6 1.7 fusion.145
  170.3 1.9 fusion.144
  178.1 1.9 fusion.144
  186.0 1.9 fusion.144
  193.9 1.9 fusion.144
  201.8 1.9 fusion.144
  203.7 2.4 copy.56
  206.1 2.4 copy.58
  213.5 3.2 convolution_convert_fusion.1
  216.8 51.6 %reduce-scatter.19.cloned.1.call-done = bf16[136,512]{1,0:T(8,128)(2,1)} async-done(((bf16[1088,512]{1,0:T(8,128)(2,1)}), bf16[136,512]{1,0:T(8,128)(2,1)}) %reduce-scatter.19.cloned.1.call-update) | async-done | bytes 139280
  268.4 1.7 copy.57
  274.9 1.9 fusion.54
  278.1 56.6 %reduce-scatter.21.cloned.1.call-done = bf16[136,512]{1,0:T(8,128)(2,1)} async-done(((bf16[1088,512]{1,0:T(8,128)(2,1)}), bf16[136,512]{1,0:T(8,128)(2,1)}) %reduce-scatter.21.cloned.1.call-update) | async-done | bytes 139280
  334.7 2.1 fusion.64
  337.7 4.3 collective-permute-start
  344.5 7.1 %collective-permute-done.1 = bf16[136,1024]{1,0:T(8,128)(2,1)S(1)} collective-permute-done((bf16[136,1024]{1,0:T(8,128)(2,1)S(1)}, bf16[136,1024]{1,0:T(8,128)(2,1)S(1)}, u32[]{:S(2)}, u32[]{:S(2)}) %collective-permute-start.1) | collective-permute-done | bytes 278560 | tf_op jit(solution)/shard_map/ppermute | solution.py:20
  352.7 8.9 %collective-permute-done.2 = bf16[136,1024]{1,0:T(8,128)(2,1)S(1)} collective-permute-done((bf16[136,1024]{1,0:T(8,128)(2,1)S(1)}, bf16[136,1024]{1,0:T(8,128)(2,1)S(1)}, u32[]{:S(2)}, u32[]{:S(2)}) %collective-permute-start.2) | collective-permute-done | bytes 278560 | tf_op jit(solution)/shard_map/ppermute | solution.py:20
  361.5 44.4 %reduce-scatter.11.cloned.1.call-done = bf16[128,512]{1,0:T(8,128)(2,1)} async-done(((bf16[1024,512]{1,0:T(8,128)(2,1)}), bf16[128,512]{1,0:T(8,128)(2,1)}) %reduce-scatter.11.cloned.1.call-update) | async-done | bytes 131088 | tf_op jit(solution)/shard_map/reduce_scatter | solution.py:165
  409.3 66.8 %reduce-scatter.17.cloned.1.call-done = bf16[64,2048]{1,0:T(8,128)(2,1)} async-done(((bf16[512,2048]{1,0:T(8,128)(2,1)}), bf16[64,2048]{1,0:T(8,128)(2,1)}) %reduce-scatter.17.cloned.1.call-update) | async-done | bytes 262160 | tf_op jit(solution)/shard_map/reduce_scatter | solution.py:174
  476.1 1.8 bitcast_convert_fusion
  477.9 64.9 %reduce-scatter.13.cloned.1.call-done = bf16[128,512]{1,0:T(8,128)(2,1)} async-done(((bf16[1024,512]{1,0:T(8,128)(2,1)}), bf16[128,512]{1,0:T(8,128)(2,1)}) %reduce-scatter.13.cloned.1.call-update) | async-done | bytes 131088 | tf_op jit(solution)/shard_map/reduce_scatter | solution.py:168
  544.4 64.2 %reduce-scatter.15.cloned.1.call-done = bf16[128,512]{1,0:T(8,128)(2,1)} async-done(((bf16[1024,512]{1,0:T(8,128)(2,1)}), bf16[128,512]{1,0:T(8,128)(2,1)}) %reduce-scatter.15.cloned.1.call-update) | async-done | bytes 131088 | tf_op jit(solution)/shard_map/reduce_scatter | solution.py:171
  (158 shorter events, 94.3 us)
Async XLA Ops:
  7.2 122.9 %copy-start = (bf16[1,512,2048]{2,1,0:T(8,128)(2,1)S(1)}, bf16[1,512,2048]{2,1,0:T(8,128)(2,1)}, u32[]{:S(2)}) copy-start(bf16[1,512,2048]{2,1,0:T(8,128)(2,1)} %param.17) | copy-start | bytes 6291460
  7.2 2.8 copy-start.1
  7.2 47.8 %all-gather.3.cloned.1.call-start = ((), (), s32[]{:S(2)}) async-start(), calls=%async_computation.6 | async-start | bytes 1253376 | tf_op jit(solution)/shard_map/all_gather | solution.py:82
  8.5 9.2 %copy-start.20 = (f32[136]{0:T(256)}, f32[136]{0:T(256)S(1)}, u32[]{:S(2)}) copy-start(f32[136]{0:T(256)S(1)} %add_rsqrt_fusion.2) | copy-start | bytes 1636
  10.6 0.8 copy-start.2
  10.6 1.5 copy-start.17
  12.1 4.3 copy-start.6
  13.9 83.3 %all-gather.5.cloned.1.call-start = ((), (), s32[]{:S(2)}) async-start(), calls=%async_computation.7 | async-start | bytes 1253376 | tf_op jit(solution)/shard_map/all_gather | solution.py:83
  16.3 252.1 %reduce-scatter.19.cloned.1.call-start = ((), (), s32[]{:S(2)}) async-start(), calls=%async_computation.12 | async-start | bytes 1253376
  19.5 0.8 copy-start.4
  128.5 0.7 copy-start.8
  130.1 1.4 copy-start.12
  131.8 0.7 copy-start.14
  131.8 0.8 copy-start.15
  134.1 6.4 %copy-start.23 = (s32[136]{0:T(256)S(1)}, s32[136]{0:T(256)}, u32[]{:S(2)}) copy-start(s32[136]{0:T(256)} %get-tuple-element.475) | copy-start | bytes 1636
  134.1 6.4 %copy-start.24 = (s32[1088]{0:T(1024)S(1)}, s32[1088]{0:T(1024)}, u32[]{:S(2)}) copy-start(s32[1088]{0:T(1024)} %get-tuple-element.476) | copy-start | bytes 13060
  206.1 128.6 %reduce-scatter.21.cloned.1.call-start = ((), (), s32[]{:S(2)}) async-start(), calls=%async_computation.13 | async-start | bytes 1253376
  206.1 2.5 copy-start.19
  208.6 197.4 %reduce-scatter.11.cloned.1.call-start = ((), (), s32[]{:S(2)}) async-start(), calls=%async_computation.8 | async-start | bytes 1179648 | tf_op jit(solution)/shard_map/reduce_scatter | solution.py:165
  208.6 1.4 copy-start.5
  208.6 3.2 copy-start.21
  211.1 0.7 copy-start.9
  213.4 262.6 %reduce-scatter.17.cloned.1.call-start = ((), (), s32[]{:S(2)}) async-start(), calls=%async_computation.11 | async-start | bytes 2359296 | tf_op jit(solution)/shard_map/reduce_scatter | solution.py:174
  216.7 53.4 %copy-start.18 = (f32[136,8]{0,1:T(8,128)S(1)}, f32[136,8]{0,1:T(8,128)}, u32[]{:S(2)}) copy-start(f32[136,8]{0,1:T(8,128)} %copy-done.17) | copy-start | bytes 13060
  216.8 326.0 %reduce-scatter.13.cloned.1.call-start = ((), (), s32[]{:S(2)}) async-start(), calls=%async_computation.9 | async-start | bytes 1179648 | tf_op jit(solution)/shard_map/reduce_scatter | solution.py:168
  270.2 1.3 copy-start.3
  272.5 0.7 copy-start.10
  274.8 333.8 %reduce-scatter.15.cloned.1.call-start = ((), (), s32[]{:S(2)}) async-start(), calls=%async_computation.10 | async-start | bytes 1179648 | tf_op jit(solution)/shard_map/reduce_scatter | solution.py:171
  274.8 1.9 copy-start.7
  274.9 1.9 copy-start.11
  334.7 2.1 copy-start.13
  336.7 5.3 copy-start.16
  337.7 15.0 %copy-start.22 = (s32[1,136]{1,0:T(1,128)S(1)}, s32[1,136]{1,0:T(1,128)}, u32[]{:S(2)}) copy-start(s32[1,136]{1,0:T(1,128)} %param.19) | copy-start | bytes 1636
  337.7 5.9 collective-permute-start
  343.6 8.1 %collective-permute-start.1 = (bf16[136,1024]{1,0:T(8,128)(2,1)S(1)}, bf16[136,1024]{1,0:T(8,128)(2,1)S(1)}, u32[]{:S(2)}, u32[]{:S(2)}) collective-permute-start(bf16[136,1024]{1,0:T(8,128)(2,1)S(1)} %collective-permute-done), channel_id=1, source_target_pairs={{0,1},{1,0},{2,3},{3,2},{4,5},{5,4},{6,7},{7,6},{8,9},{9,8},{10,11... | collective-permute-start | bytes 835592 | tf_op jit(solution)/shard_map/ppermute | solution.py:20
  351.6 9.9 %collective-permute-start.2 = (bf16[136,1024]{1,0:T(8,128)(2,1)S(1)}, bf16[136,1024]{1,0:T(8,128)(2,1)S(1)}, u32[]{:S(2)}, u32[]{:S(2)}) collective-permute-start(bf16[136,1024]{1,0:T(8,128)(2,1)S(1)} %collective-permute-done.1), channel_id=1, source_target_pairs={{0,2},{2,0},{1,3},{3,1},{4,6},{6,4},{5,7},{7,5},{8,10},{10,8},{9,1... | collective-permute-start | bytes 835592 | tf_op jit(solution)/shard_map/ppermute | solution.py:20
  361.5 46.0 %collective-permute-start.3 = (bf16[136,1024]{1,0:T(8,128)(2,1)S(1)}, bf16[136,1024]{1,0:T(8,128)(2,1)S(1)}, u32[]{:S(2)}, u32[]{:S(2)}) collective-permute-start(bf16[136,1024]{1,0:T(8,128)(2,1)S(1)} %collective-permute-done.2), channel_id=1, source_target_pairs={{0,4},{4,0},{1,5},{5,1},{2,6},{6,2},{3,7},{7,3},{8,12},{12,8},{9,1... | collective-permute-start | bytes 835592 | tf_op jit(solution)/shard_map/ppermute | solution.py:20
Sparse Core Ops, SparseCore 0:
  14.1 40.8 all-gather.2
  57.7 39.4 all-gather.4
  206.2 62.1 reduce-scatter.18
  271.7 62.9 reduce-scatter.20
  337.9 67.9 reduce-scatter.10
  409.7 66.3 reduce-scatter.16
  479.9 62.8 reduce-scatter.12
  546.1 62.3 reduce-scatter.14
where the time goes:
time: 623 us; the launch traced here: 617 us
  waiting for transfers between devices  435 us (70%)
  matrix products  110 us (18%)
  local copies, waits for them, and re-layouts  32.8 us (5%)
  other arithmetic  18.1 us (3%)
  between operations  14.5 us (2%)
  starting transfers between devices  6.59 us (1%)
    unnamed x10, waiting for transfers between devices  108 us
    reduce_scatter x1, waiting for transfers between devices, shards(): lax.psum_scatter(out_term.astype(jnp.bfloat16), 'seq', scatter_dimension=...  66.8 us
    reduce_scatter x1, waiting for transfers between devices, shards(): lax.psum_scatter(key_term.astype(jnp.bfloat16), 'seq', scatter_dimension=...  64.9 us
    reduce_scatter x1, waiting for transfers between devices, shards(): lax.psum_scatter(value_term.astype(jnp.bfloat16), 'seq', scatter_dimensio...  64.2 us
    reduce_scatter x1, waiting for transfers between devices, shards(): lax.psum_scatter(query_term.astype(jnp.bfloat16), 'seq', scatter_dimensio...  44.4 us
    all_gather x1, waiting for transfers between devices, shards(): lax.all_gather(values, 'seq', axis=0, tiled=True)  38.2 us
    all_gather x1, waiting for transfers between devices, shards(): lax.all_gather(keys, 'seq', axis=0, tiled=True)  32.5 us
    dot_general x16, matrix products, probabilities(): jnp.dot(query_part, key_part.T, preferred_element_type=jnp.float32) * scale  21.6 us
  transfers between devices with their start and end apart: 12, of which 10 were waited for; matrix products, arithmetic and copies ran while one was open for 7% of the time, Pallas kernels for 0%

commit v1 on v0

--- a/solution.py
+++ b/solution.py
@@ -54,7 +54,7 @@
     return shifted(rows, "section", -1)
 
 
-def shards(activations, incoming, w_query, w_key, w_value, w_out, block_ids, flip_order):
+def general_shards(activations, incoming, w_query, w_key, w_value, w_out, block_ids, flip_order):
     field = activations[0].astype(jnp.float32)
     upstream = incoming[0].astype(jnp.float32)
     weight_query = w_query[0]
@@ -189,7 +189,116 @@
     return (carry[None], sums[0][None], sums[1][None], sums[2][None], sums[3][None])
 
 
+def to_heads(matrix, parts):
+    rows = matrix[0].shape[0]
+    slabs = jnp.concatenate([head_major(part) for part in matrix], axis=-1)
+    moved = lax.all_to_all(slabs, "seq", split_axis=0, concat_axis=0, tiled=True)
+    return moved.reshape(parts * rows, -1)
+
+
+def to_tokens(columns, parts):
+    slabs = columns.reshape(parts, -1, columns.shape[-1])
+    return lax.all_to_all(slabs, "seq", split_axis=0, concat_axis=0, tiled=True)
+
+
+def side_by_side(slabs):
+    return jnp.transpose(slabs, (1, 0, 2)).reshape(slabs.shape[1], -1)
+
+
+def head_shards(
+    activations, incoming, w_query, w_key, w_value, w_out, block_ids, flip_order
+):
+    parts = lax.axis_size("seq")
+    sections = lax.axis_size("section")
+    mine = lax.axis_index("seq")
+    field = activations[0].astype(jnp.float32)
+    upstream = incoming[0].astype(jnp.float32)
+    weight_query, weight_key, weight_value, weight_out = w_query[0], w_key[0], w_value[0], w_out[0]
+    rows, width = field.shape
+    inner = weight_query.shape[1]
+    scale = HEAD_DIM ** (-0.5)
+    row_scale = lax.rsqrt(jnp.mean(field * field, axis=-1, keepdims=True) + EPSILON)
+    unit_rows = field * row_scale
+    normed = unit_rows.astype(jnp.bfloat16)
+    query_raw = jnp.dot(normed, weight_query, preferred_element_type=jnp.float32)
+    key_raw = jnp.dot(normed, weight_key, preferred_element_type=jnp.float32)
+    values = jnp.dot(normed, weight_value, preferred_element_type=jnp.float32).astype(jnp.bfloat16)
+    queries = unit_heads(query_raw)[0].astype(jnp.bfloat16).reshape(rows, inner)
+    keys = unit_heads(key_raw)[0].astype(jnp.bfloat16).reshape(rows, inner)
+    own = to_heads((queries, keys, values), parts)
+    normed_all = lax.all_gather(normed, "seq", axis=0, tiled=True)
+    query, key, value = jnp.split(own, 3, axis=-1)
+    allowed = block_ids[None, :] <= block_ids[:, None]
+    scores = jnp.dot(query, key.T, preferred_element_type=jnp.float32) * scale
+    numerator = jnp.where(allowed, jnp.exp(scores), 0.0)
+    probs = numerator / jnp.sum(numerator, axis=-1, keepdims=True)
+    probs_low = probs.astype(jnp.bfloat16)
+    head_out = jnp.dot(probs_low, value, preferred_element_type=jnp.float32).astype(jnp.bfloat16)
+    attended = side_by_side(to_tokens(head_out, parts))
+    affine = jnp.dot(attended, weight_out, preferred_element_type=jnp.float32)
+    factor = jnp.exp(-affine[:, width:])
+    latent = (field - affine[:, :width]) * factor
+    grad_affine = jnp.concatenate([-upstream * factor, 1.0 - upstream * latent], axis=-1).astype(
+        jnp.bfloat16
+    )
+    grad_attn = jnp.dot(grad_affine, weight_out.T, preferred_element_type=jnp.float32).astype(
+        jnp.bfloat16
+    )
+    grad_own = to_heads((grad_attn,), parts)
+    out_term = jnp.dot(attended.T, grad_affine, preferred_element_type=jnp.float32)
+    grad_out = lax.psum_scatter(
+        out_term.astype(jnp.bfloat16), "seq", scatter_dimension=0, tiled=True
+    ).astype(jnp.float32)
+    correction = jnp.sum(
+        grad_own.astype(jnp.float32) * head_out.astype(jnp.float32), axis=-1, keepdims=True
+    )
+    grad_probs = jnp.dot(grad_own, value.T, preferred_element_type=jnp.float32)
+    grad_scores = (probs * (grad_probs - correction)).astype(jnp.bfloat16)
+    grad_q = jnp.dot(grad_scores, key, preferred_element_type=jnp.float32) * scale
+    grad_k = jnp.dot(grad_scores.T, query, preferred_element_type=jnp.float32) * scale
+    grad_v = jnp.dot(probs_low.T, grad_own, preferred_element_type=jnp.float32)
+
+    def own_columns(weight):
+        return lax.dynamic_slice_in_dim(weight, mine * HEAD_DIM, HEAD_DIM, axis=1)
+
+    def own_back(grad, weight):
+        raw = jnp.dot(normed_all, own_columns(weight), preferred_element_type=jnp.float32)
+        back_scale = lax.rsqrt(jnp.mean(raw * raw, axis=-1, keepdims=True) + EPSILON)
+        return unit_back(grad, raw * back_scale, back_scale)
+
+    grads = jnp.concatenate(
+        [own_back(grad_q, weight_query), own_back(grad_k, weight_key), grad_v], axis=-1
+    ).astype(jnp.bfloat16)
+    token_grads = to_tokens(grads, parts)
+    grad_queries, grad_keys, grad_values = [
+        side_by_side(part) for part in jnp.split(token_grads, 3, axis=-1)
+    ]
+    weight_terms = jnp.dot(normed_all.T, grads, preferred_element_type=jnp.float32)
+    weight_terms = to_tokens(weight_terms.astype(jnp.bfloat16), parts)
+    sums = [
+        side_by_side(part).astype(jnp.float32) for part in jnp.split(weight_terms, 3, axis=-1)
+    ]
+    grad_normed = jnp.dot(grad_queries, weight_query.T, preferred_element_type=jnp.float32)
+    grad_normed = grad_normed + jnp.dot(grad_keys, weight_key.T, preferred_element_type=jnp.float32)
+    grad_normed = grad_normed + jnp.dot(
+        grad_values, weight_value.T, preferred_element_type=jnp.float32
+    )
+    grad_input = upstream * factor + row_scale * (
+        grad_normed - unit_rows * jnp.mean(grad_normed * unit_rows, axis=-1, keepdims=True)
+    )
+    grad_input = grad_input.astype(jnp.bfloat16)
+    route = [
+        (s * parts + d, (s - 1) * parts + parts - 1 - d)
+        for s in range(1, sections)
+        for d in range(parts)
+    ]
+    moved = lax.ppermute(grad_input, ("section", "seq"), route)
+    carry = jnp.take(moved, flip_order[0], axis=0)
+    return (carry[None], sums[0][None], sums[1][None], sums[2][None], grad_out[None])
+
+
 def solution(mesh):
+    shards = head_shards if mesh.shape["seq"] == HEADS else general_shards
     in_specs = (
         P("section", "seq", None),
         P("section", "seq", None),

time: 623 us -> 221 us (0.35)
  waiting for transfers between devices: 435 us -> 61.3 us
  matrix products: 110 us -> 38.1 us
  blocking collectives: 0 us -> 31.3 us
  starting transfers between devices: 6.59 us -> 20.7 us
    reduce_scatter x4 -> x1, waiting for transfers between devices: 240 us -> 15.5 us  [head_shards(): lax.psum_scatter(out_term.astype(jnp.bfloat16), 'seq', scatter_dimension=...]
    unnamed x10 -> x2, waiting for transfers between devices: 108 us -> 0.03 us
    dot_general x68 -> x18, matrix products: 110 us -> 38.1 us  [the longest x2 5.2 us: own_back(): jnp.dot(normed_all, own_columns(weight), preferred_element_type=jnp.float32)]
    all_gather x2 -> x1, waiting for transfers between devices: 70.6 us -> 17.2 us  [head_shards(): normed_all = lax.all_gather(normed, 'seq', axis=0, tiled=True)]
    all_to_all x0 -> x2, blocking collectives: none -> 31.3 us  [the longest x1 20.8 us: to_heads(): lax.all_to_all(slabs, 'seq', split_axis=0, concat_axis=0, tiled=True)]
    all_to_all x0 -> x3, waiting for transfers between devices: none -> 28.6 us  [the longest x2 20.3 us: to_tokens(): return lax.all_to_all(slabs, 'seq', split_axis=0, concat_axis=0, tiled=True)]
    ppermute x4 -> x1, waiting for transfers between devices: 16 us -> 0.01 us  [head_shards(): moved = lax.ppermute(grad_input, ('section', 'seq'), route)]
    all_to_all x0 -> x3, starting transfers between devices: none -> 13.3 us  [the longest x2 8.28 us: to_tokens(): return lax.all_to_all(slabs, 'seq', split_axis=0, concat_axis=0, tiled=True)]
  transfers between devices with their start and end apart: 12 -> 6, of which waited for: 10 -> 4; matrix products, arithmetic and copies ran while one was open for 7% -> 30% of each run, Pallas kernels for 0% -> 0%
where the time goes in v1:
time: 221 us; the launch traced here: 219 us
  waiting for transfers between devices  61.3 us (28%)
  local copies, waits for them, and re-layouts  38.7 us (18%)
  matrix products  38.1 us (17%)
  blocking collectives  31.3 us (14%)
  starting transfers between devices  20.7 us (9%)
  other arithmetic  14.4 us (7%)
  between operations  14.4 us (7%)
    all_to_all x1, blocking collectives, to_heads(): lax.all_to_all(slabs, 'seq', split_axis=0, concat_axis=0, tiled=True)  20.8 us
    all_to_all x2, waiting for transfers between devices, to_tokens(): return lax.all_to_all(slabs, 'seq', split_axis=0, concat_axis=0, tiled=True)  20.3 us
    all_gather x1, waiting for transfers between devices, head_shards(): normed_all = lax.all_gather(normed, 'seq', axis=0, tiled=True)  17.2 us
    reduce_scatter x1, waiting for transfers between devices, head_shards(): lax.psum_scatter(out_term.astype(jnp.bfloat16), 'seq', scatter_dimension=...  15.5 us
    all_to_all x1, blocking collectives, to_tokens(): return lax.all_to_all(slabs, 'seq', split_axis=0, concat_axis=0, tiled=True)  10.4 us
    unnamed x45, local copies, waits for them, and re-layouts  10.2 us
    all_to_all x2, starting transfers between devices, to_tokens(): return lax.all_to_all(slabs, 'seq', split_axis=0, concat_axis=0, tiled=True)  8.28 us
    all_to_all x1, waiting for transfers between devices, to_heads(): lax.all_to_all(slabs, 'seq', split_axis=0, concat_axis=0, tiled=True)  8.24 us
  transfers between devices with their start and end apart: 6, of which 4 were waited for; matrix products, arithmetic and copies ran while one was open for 30% of the time, Pallas kernels for 0%

profile of v1, /device:TPU:5, one launch (start us, length us, event | category | flops | bytes accessed | tf_op | source)
XLA Modules:
  0.0 219.0 jit_solution(15514069767167066872)
XLA Ops:
  7.2 1.2 fusion.29
  8.5 2.3 %copy.36 = bf16[1,1024,512]{1,2,0:T(8,128)(2,1)} copy(bf16[1,1024,512]{2,1,0:T(8,128)(2,1)} %param.11) | data formatting | bytes 2097152 | tf_op args[3]
  10.8 2.5 %multiply_reduce_fusion = (f32[136,8]{0,1:T(8,128)S(1)}, f32[136,8,64]{0,2,1:T(8,128)}) fusion(bf16[8,64,1024]{2,1,0:T(8,128)(2,1)} %bitcast.175, f32[136]{0:T(256)S(1)} %add_rsqrt_fusion.2, bf16[1,136,1024]{2,1,0:T(8,128)(2,1)S(1)} %copy-done.4), kind=kOutput, calls=%fused_computation.61 | convolution fusion | flops 143162304 | bytes 1610528 | tf_op jit(solution)/shard_map/dot_general | solution.py:224
  13.3 1.3 copy.35
  14.7 2.6 %multiply_reduce_fusion.1 = (f32[136,8]{0,1:T(8,128)S(1)}, f32[136,8,64]{0,2,1:T(8,128)}) fusion(bf16[8,64,1024]{2,1,0:T(8,128)(2,1)} %bitcast.176, f32[136]{0:T(256)S(1)} %add_rsqrt_fusion.2, bf16[1,136,1024]{2,1,0:T(8,128)(2,1)S(1)} %copy-done.4), kind=kOutput, calls=%fused_computation.62 | convolution fusion | flops 143162304 | bytes 1610528 | tf_op jit(solution)/shard_map/dot_general | solution.py:223
  17.3 1.6 convolution_convert_fusion.4
  19.7 1.2 fusion.37
  22.0 1.1 copy.38
  23.2 20.8 %all_to_all.25 = bf16[8,136,192]{2,1,0:T(8,128)(2,1)S(1)} all-to-all(bf16[8,136,192]{2,1,0:T(8,128)(2,1)} %copy.38), channel_id=1, replica_groups=mesh['section'=4,'seq'=8] {'seq'}, dimensions={0} | all-to-all | bytes 835584 | tf_op jit(solution)/shard_map/all_to_all | solution.py:195
  44.0 1.3 fusion.69
  45.7 1.8 copy-done.7
  47.5 1.5 copy-done.1
  50.0 10.4 %all_to_all.26 = bf16[8,136,64]{1,2,0:T(8,128)(2,1)S(1)} all-to-all(bf16[8,136,64]{1,2,0:T(8,128)(2,1)S(1)} %copy.39), channel_id=1, replica_groups=mesh['section'=4,'seq'=8] {'seq'}, dimensions={0} | all-to-all | bytes 278528 | tf_op jit(solution)/shard_map/all_to_all | solution.py:201
  61.7 1.2 fusion.33
  62.9 2.5 %fusion.10 = bf16[136,512]{1,0:T(8,128)(2,1)} fusion(bf16[1,512,2048]{2,1,0:T(8,128)(2,1)S(1)} %copy-done, bf16[136,1024]{1,0:T(8,128)(2,1)} %get-tuple-element.16, bf16[136,1024]{1,0:T(8,128)(2,1)} %get-tuple-element.15), kind=kOutput, calls=%fused_computation.22 | convolution fusion | flops 286396416 | bytes 2793472 | tf_op jit(solution)/shard_map/dot_general | solution.py:244
  65.4 1.8 reshape.237
  67.3 1.9 copy.41
  69.1 5.0 %all-to-all-start.2 = ((bf16[8,136,64]{1,2,0:T(8,128)(2,1)}), bf16[8,136,64]{1,2,0:T(8,128)(2,1)}, u32[]{:S(2)}, u32[]{:S(2)}) async-start(bf16[8,136,64]{1,2,0:T(8,128)(2,1)} %copy.41), calls=%async_computation.2 | async-start | bytes 524288 | tf_op jit(solution)/shard_map/all_to_all | solution.py:195
  74.3 3.1 %convolution_convert_fusion = bf16[512,2048]{1,0:T(8,128)(2,1)} fusion(bf16[136,512]{0,1:T(8,128)(2,1)} %bitcast.169, bf16[136,1024]{1,0:T(8,128)(2,1)} %get-tuple-element.16, bf16[136,1024]{1,0:T(8,128)(2,1)} %get-tuple-element.15), kind=kOutput, calls=%fused_computation.7 | convolution fusion | flops 287375360 | bytes 2793472 | tf_op jit(solution)/shard_map/dot_general | solution.py:248
  77.5 8.2 %all-to-all-done.2 = bf16[8,136,64]{1,2,0:T(8,128)(2,1)} async-done(((bf16[8,136,64]{1,2,0:T(8,128)(2,1)}), bf16[8,136,64]{1,2,0:T(8,128)(2,1)}, u32[]{:S(2)}, u32[]{:S(2)}) %all-to-all-start.2) | async-done | bytes 139296 | tf_op jit(solution)/shard_map/all_to_all | solution.py:195
  85.7 1.8 copy.42
  87.5 1.9 reshape.238
  90.5 3.3 %convolution_convert_fusion.1 = bf16[1088,64]{0,1:T(8,128)(2,1)} fusion(bf16[1088,1088]{0,1:T(8,128)(2,1)} %copy-done.1, bf16[1088,64]{0,1:T(8,128)(2,1)} %reshape.238), kind=kOutput, calls=%fused_computation.11 | convolution fusion | flops 151588864 | bytes 2646016 | tf_op jit(solution)/shard_map/dot_general | solution.py:259
  93.8 4.9 %fusion.3 = bf16[1088,1088]{0,1:T(8,128)(2,1)} fusion(bf16[1088,64]{0,1:T(8,128)(2,1)S(1)} %copy-done.13, f32[1088]{0:T(1024)S(1)} %multiply_reduce_fusion.5, f32[1088,1088]{0,1:T(8,128)} %copy-done.7, f32[1088]{0:T(1024)S(1)} %get-tuple-element.28, bf16[1088,192]{1,0:T(8,128)(2,1)S(1)} %bitcast.167), kind=kOutput, calls=%fused_computation.6 | convolution fusion | flops 156254208 | bytes 7544832 | tf_op jit(solution)/shard_map/dot_general | solution.py:255
  98.6 1.8 copy.58
  100.4 17.2 %all-gather.2.cloned.1.call-done = bf16[1088,1024]{1,0:T(8,128)(2,1)} async-done(((bf16[136,1024]{1,0:T(8,128)(2,1)}), bf16[1088,1024]{1,0:T(8,128)(2,1)}) %all-gather.2.cloned.1.call-update) | async-done | bytes 2228240 | tf_op jit(solution)/shard_map/all_gather | solution.py:229
  117.6 2.6 %multiply_reduce_fusion.6 = (f32[1088]{0:T(1024)S(1)}, f32[1088,64]{0,1:T(8,128)S(1)}) fusion(bf16[1088,1024]{1,0:T(8,128)(2,1)} %all-gather.2.cloned.1.call-done, bf16[1,1024,512]{2,1,0:T(8,128)(2,1)} %param.10, s32[]{:T(128)S(6)} %select_n.37), kind=kOutput, calls=%fused_computation.75 | convolution fusion | flops 142744512 | bytes 2773252 | tf_op jit(solution)/shard_map/dot_general | solution.py:265
  120.3 1.6 multiply_reduce_fusion.4
  122.6 1.8 copy.56
  124.4 2.6 %multiply_reduce_fusion.3 = (f32[1088]{0:T(1024)S(1)}, f32[1088,64]{0,1:T(8,128)S(1)}) fusion(bf16[1088,1024]{1,0:T(8,128)(2,1)} %all-gather.2.cloned.1.call-done, bf16[1,1024,512]{2,1,0:T(8,128)(2,1)} %param.11, s32[]{:T(128)S(6)} %select_n.37), kind=kOutput, calls=%fused_computation.71 | convolution fusion | flops 142744512 | bytes 2773252 | tf_op jit(solution)/shard_map/dot_general | solution.py:265
  127.0 1.8 multiply_reduce_fusion.2
  129.5 1.8 copy.57
  131.3 2.2 pad_maximum_fusion.2
  133.5 4.2 %all-to-all-start.3 = ((bf16[8,136,192]{2,1,0:T(8,128)(2,1)}), bf16[8,136,192]{2,1,0:T(8,128)(2,1)}, u32[]{:S(2)}, u32[]{:S(2)}) async-start(bf16[8,136,192]{2,1,0:T(8,128)(2,1)} %pad_maximum_fusion.2), calls=%async_computation.3 | async-start | bytes 1114112 | tf_op jit(solution)/shard_map/all_to_all | solution.py:201
  137.8 2.6 %fusion.9 = bf16[24,8,8,128]{3,2,1,0:T(8,128)(2,1)S(1)} fusion(bf16[1088,1024]{1,0:T(8,128)(2,1)} %all-gather.2.cloned.1.call-done, bf16[1088,64]{0,1:T(8,128)(2,1)} %convolution_convert_fusion.1, bf16[1088,64]{0,1:T(8,128)(2,1)} %multiply_convert_fusion, bf16[1088,64]{0,1:T(8,128)(2,1)} %multiply_convert_fusion.1), kind=kOutput, calls=%fused_computation.21 | convolution fusion | flops 429268992 | bytes 3039232 | tf_op jit(solution)/shard_map/dot_general | solution.py:276
  141.2 20.3 %all-to-all-done.3 = bf16[8,136,192]{2,1,0:T(8,128)(2,1)} async-done(((bf16[8,136,192]{2,1,0:T(8,128)(2,1)}), bf16[8,136,192]{2,1,0:T(8,128)(2,1)}, u32[]{:S(2)}, u32[]{:S(2)}) %all-to-all-start.3) | async-done | bytes 417824 | tf_op jit(solution)/shard_map/all_to_all | solution.py:201
  161.5 4.1 %all-to-all-start.4 = ((bf16[8,128,192]{1,2,0:T(8,128)(2,1)}), bf16[8,128,192]{1,2,0:T(8,128)(2,1)}, u32[]{:S(2)}, u32[]{:S(2)}) async-start(bf16[8,128,192]{1,2,0:T(8,128)(2,1)} %bitcast.170), calls=%async_computation.4 | async-start | bytes 786432 | tf_op jit(solution)/shard_map/all_to_all | solution.py:201
  165.6 2.0 slice_bitcast_fusion
  168.4 1.8 reshape.239
  170.3 1.7 copy.48
  172.0 1.8 reshape.240
  173.8 1.7 copy.49
  175.5 1.8 reshape.241
  177.3 1.9 fusion.14
  179.3 1.4 convolution_add_fusion.1
  182.3 7.2 %collective-permute-start = (bf16[136,1024]{1,0:T(8,128)(2,1)}, bf16[136,1024]{1,0:T(8,128)(2,1)S(1)}, u32[]{:S(2)}, u32[]{:S(2)}) collective-permute-start(bf16[136,1024]{1,0:T(8,128)(2,1)} %fusion.28), channel_id=1, source_target_pairs={{8,7},{9,6},{10,5},{11,4},{12,3},{13,2},{14,1},{15,0},{16,15},{17,... | collective-permute-start | bytes 835592 | tf_op jit(solution)/shard_map/ppermute | solution.py:295
  189.6 15.5 %reduce-scatter.2.cloned.1.call-done = bf16[64,2048]{1,0:T(8,128)(2,1)} async-done(((bf16[512,2048]{1,0:T(8,128)(2,1)}), bf16[64,2048]{1,0:T(8,128)(2,1)}) %reduce-scatter.2.cloned.1.call-update) | async-done | bytes 262160 | tf_op jit(solution)/shard_map/reduce_scatter | solution.py:249
  205.0 1.8 bitcast_convert_fusion
  (75 shorter events, 15.8 us)
Async XLA Ops:
  7.2 54.0 %copy-start = (bf16[1,512,2048]{2,1,0:T(8,128)(2,1)S(1)}, bf16[1,512,2048]{2,1,0:T(8,128)(2,1)}, u32[]{:S(2)}) copy-start(bf16[1,512,2048]{2,1,0:T(8,128)(2,1)} %param.13) | copy-start | bytes 6291460
  7.2 3.6 %copy-start.4 = (bf16[1,136,1024]{2,1,0:T(8,128)(2,1)S(1)}, bf16[1,136,1024]{2,1,0:T(8,128)(2,1)}, u32[]{:S(2)}) copy-start(bf16[1,136,1024]{2,1,0:T(8,128)(2,1)} %param.8) | copy-start | bytes 835588
  7.2 6.1 %copy-start.5 = (bf16[1,1024,512]{2,1,0:T(8,128)(2,1)S(1)}, bf16[1,1024,512]{2,1,0:T(8,128)(2,1)}, u32[]{:S(2)}) copy-start(bf16[1,1024,512]{2,1,0:T(8,128)(2,1)} %param.10) | copy-start | bytes 3145732
  7.2 110.4 %all-gather.2.cloned.1.call-start = ((), (), s32[]{:S(2)}) async-start(), calls=%async_computation.6 | async-start | bytes 2506752 | tf_op jit(solution)/shard_map/all_gather | solution.py:229
  14.7 5.1 %copy-start.17 = (f32[136,8,64]{0,2,1:T(8,128)S(1)}, f32[136,8,64]{0,2,1:T(8,128)}, u32[]{:S(2)}) copy-start(f32[136,8,64]{0,2,1:T(8,128)} %get-tuple-element.25) | copy-start | bytes 835588
  20.9 23.1 %copy-start.19 = (s32[1088]{0:T(1024)S(1)}, s32[1088]{0:T(1024)}, u32[]{:S(2)}) copy-start(s32[1088]{0:T(1024)} %param.14) | copy-start | bytes 13060
  44.0 1.7 copy-start.9
  45.3 2.2 %copy-start.7 = (f32[1088,1088]{0,1:T(8,128)}, f32[1088,1088]{0,1:T(8,128)S(1)}, u32[]{:S(2)}) copy-start(f32[1088,1088]{0,1:T(8,128)S(1)} %get-tuple-element.29) | copy-start | bytes 14204932
  47.5 1.5 copy-start.1
  49.6 10.9 %copy-start.12 = (bf16[1088,64]{0,1:T(8,128)(2,1)}, bf16[1088,64]{0,1:T(8,128)(2,1)S(1)}, u32[]{:S(2)}) copy-start(bf16[1088,64]{0,1:T(8,128)(2,1)S(1)} %convolution_convert_fusion.2) | copy-start | bytes 417796
  50.0 11.7 %copy-start.14 = (bf16[1,136,1024]{2,1,0:T(8,128)(2,1)S(1)}, bf16[1,136,1024]{2,1,0:T(8,128)(2,1)}, u32[]{:S(2)}) copy-start(bf16[1,136,1024]{2,1,0:T(8,128)(2,1)} %param.9) | copy-start | bytes 835588
  60.5 0.7 copy-start.11
  69.1 16.6 %all-to-all-start.2 = ((bf16[8,136,64]{1,2,0:T(8,128)(2,1)}), bf16[8,136,64]{1,2,0:T(8,128)(2,1)}, u32[]{:S(2)}, u32[]{:S(2)}) async-start(bf16[8,136,64]{1,2,0:T(8,128)(2,1)} %copy.41), calls=%async_computation.2 | async-start | bytes 524288 | tf_op jit(solution)/shard_map/all_to_all | solution.py:195
  74.1 130.9 %reduce-scatter.2.cloned.1.call-start = ((), (), s32[]{:S(2)}) async-start(), calls=%async_computation.7 | async-start | bytes 2359296 | tf_op jit(solution)/shard_map/reduce_scatter | solution.py:249
  90.4 3.3 %copy-start.10 = (bf16[8,136,192]{2,1,0:T(8,128)(2,1)S(1)}, bf16[8,136,192]{2,1,0:T(8,128)(2,1)}, u32[]{:S(2)}) copy-start(bf16[8,136,192]{2,1,0:T(8,128)(2,1)} %copy-done.9) | copy-start | bytes 1253380
  90.5 3.3 %copy-start.13 = (bf16[1088,64]{0,1:T(8,128)(2,1)S(1)}, bf16[1088,64]{0,1:T(8,128)(2,1)}, u32[]{:S(2)}) copy-start(bf16[1088,64]{0,1:T(8,128)(2,1)} %reshape.238) | copy-start | bytes 417796
  117.6 2.6 %copy-start.2 = (bf16[1088,1088]{0,1:T(8,128)(2,1)S(1)}, bf16[1088,1088]{0,1:T(8,128)(2,1)}, u32[]{:S(2)}) copy-start(bf16[1088,1088]{0,1:T(8,128)(2,1)} %fusion.3) | copy-start | bytes 7102468
  124.4 2.6 %copy-start.3 = (bf16[1088,1088]{0,1:T(8,128)(2,1)S(1)}, bf16[1088,1088]{0,1:T(8,128)(2,1)}, u32[]{:S(2)}) copy-start(bf16[1088,1088]{0,1:T(8,128)(2,1)} %fusion.3) | copy-start | bytes 7102468
  128.8 8.9 %copy-start.18 = (s32[1,136]{1,0:T(1,128)S(1)}, s32[1,136]{1,0:T(1,128)}, u32[]{:S(2)}) copy-start(s32[1,136]{1,0:T(1,128)} %param.15) | copy-start | bytes 1636
  133.5 28.0 %all-to-all-start.3 = ((bf16[8,136,192]{2,1,0:T(8,128)(2,1)}), bf16[8,136,192]{2,1,0:T(8,128)(2,1)}, u32[]{:S(2)}, u32[]{:S(2)}) async-start(bf16[8,136,192]{2,1,0:T(8,128)(2,1)} %pad_maximum_fusion.2), calls=%async_computation.3 | async-start | bytes 1114112 | tf_op jit(solution)/shard_map/all_to_all | solution.py:201
  161.5 45.3 %all-to-all-start.4 = ((bf16[8,128,192]{1,2,0:T(8,128)(2,1)}), bf16[8,128,192]{1,2,0:T(8,128)(2,1)}, u32[]{:S(2)}, u32[]{:S(2)}) async-start(bf16[8,128,192]{1,2,0:T(8,128)(2,1)} %bitcast.170), calls=%async_computation.4 | async-start | bytes 786432 | tf_op jit(solution)/shard_map/all_to_all | solution.py:201
  177.3 1.9 copy-start.6
  177.3 3.4 %copy-start.8 = (bf16[1,1024,512]{2,1,0:T(8,128)(2,1)S(1)}, bf16[1,1024,512]{2,1,0:T(8,128)(2,1)}, u32[]{:S(2)}) copy-start(bf16[1,1024,512]{2,1,0:T(8,128)(2,1)} %param.12) | copy-start | bytes 3145732
  177.3 3.4 %copy-start.16 = (bf16[136,512]{1,0:T(8,128)(2,1)S(1)}, bf16[136,512]{1,0:T(8,128)(2,1)}, u32[]{:S(2)}) copy-start(bf16[136,512]{1,0:T(8,128)(2,1)} %reshape.241) | copy-start | bytes 417796
  179.3 2.1 copy-start.15
  182.3 28.1 %collective-permute-start = (bf16[136,1024]{1,0:T(8,128)(2,1)}, bf16[136,1024]{1,0:T(8,128)(2,1)S(1)}, u32[]{:S(2)}, u32[]{:S(2)}) collective-permute-start(bf16[136,1024]{1,0:T(8,128)(2,1)} %fusion.28), channel_id=1, source_target_pairs={{8,7},{9,6},{10,5},{11,4},{12,3},{13,2},{14,1},{15,0},{16,15},{17,... | collective-permute-start | bytes 835592 | tf_op jit(solution)/shard_map/ppermute | solution.py:295
Sparse Core Ops, SparseCore 0:
  63.0 54.5 all-gather.1
  121.2 83.8 reduce-scatter.1

commit v2 on v0

--- a/solution.py
+++ b/solution.py
@@ -1,6 +1,8 @@
 import jax
 import jax.numpy as jnp
 from jax import lax
+from jax.experimental import pallas as pl
+from jax.experimental.pallas import tpu as pltpu
 from jax.sharding import PartitionSpec as P
 
 HEADS = 8
@@ -54,7 +56,7 @@
     return shifted(rows, "section", -1)
 
 
-def shards(activations, incoming, w_query, w_key, w_value, w_out, block_ids, flip_order):
+def general_shards(activations, incoming, w_query, w_key, w_value, w_out, block_ids, flip_order):
     field = activations[0].astype(jnp.float32)
     upstream = incoming[0].astype(jnp.float32)
     weight_query = w_query[0]
@@ -189,7 +191,389 @@
     return (carry[None], sums[0][None], sums[1][None], sums[2][None], sums[3][None])
 
 
+PACKED = 80
+
+
+def call(kernel, outs, operands, flops=0, specs=None, scratch=()):
+    moved = sum(x.size * x.dtype.itemsize for x in operands) + sum(
+        x.size * x.dtype.itemsize for x in outs
+    )
+    single = pl.BlockSpec(memory_space=pltpu.VMEM)
+    return pl.pallas_call(
+        kernel,
+        out_shape=tuple(outs),
+        in_specs=specs or [single] * len(operands),
+        out_specs=tuple([single] * len(outs)),
+        scratch_shapes=list(scratch),
+        compiler_params=pltpu.CompilerParams(vmem_limit_bytes=40 * 2**20),
+        cost_estimate=pl.CostEstimate(flops=flops, bytes_accessed=moved, transcendentals=0),
+    )(*operands)
+
+
+def shape(*dims, dtype=jnp.bfloat16):
+    return jax.ShapeDtypeStruct(dims, dtype)
+
+
+def dot(left, right, contract=((1,), (0,))):
+    return lax.dot_general(left, right, (contract, ((), ())), preferred_element_type=jnp.float32)
+
+
+def low_lanes(block):
+    return lax.broadcasted_iota(jnp.int32, block.shape, len(block.shape) - 1) < HEAD_DIM
+
+
+def swap(block):
+    return pltpu.roll(block, HEAD_DIM, 1)
+
+
+def half_sums(block):
+    low = low_lanes(block)
+    first = jnp.sum(jnp.where(low, block, 0.0), axis=-1, keepdims=True)
+    second = jnp.sum(jnp.where(low, 0.0, block), axis=-1, keepdims=True)
+    return jnp.where(low, first, second)
+
+
+def pack(block):
+    rows = block.shape[0]
+    return jnp.concatenate([block[:PACKED], block[rows - PACKED :]], axis=1)
+
+
+def unpack(slab, rows):
+    right = swap(slab)[2 * PACKED - rows :, :HEAD_DIM]
+    return jnp.concatenate([slab[:, :HEAD_DIM], right], axis=0)
+
+
+def normalize(block):
+    field = block.astype(jnp.float32)
+    row_scale = lax.rsqrt(jnp.mean(field * field, axis=-1, keepdims=True) + EPSILON)
+    return field * row_scale, row_scale
+
+
+def project_kernel(act_ref, wq_ref, wk_ref, wv_ref, out_ref):
+    normed = normalize(act_ref[...])[0].astype(jnp.bfloat16)
+    rows = normed.shape[0]
+    query, key = dot(normed, wq_ref[...]), dot(normed, wk_ref[...])
+    value = dot(normed, wv_ref[...])
+    for pair in range(HEADS // 2):
+        lanes = slice(pair * 2 * HEAD_DIM, (pair + 1) * 2 * HEAD_DIM)
+        q, k, v = query[:, lanes], key[:, lanes], value[:, lanes]
+        q = q * lax.rsqrt(half_sums(q * q) / HEAD_DIM + EPSILON)
+        k = k * lax.rsqrt(half_sums(k * k) / HEAD_DIM + EPSILON)
+        first, last = v[:PACKED], v[rows - PACKED :]
+        low, low_v = low_lanes(q), low_lanes(first)
+        even = (jnp.where(low_v, first, swap(last)), jnp.where(low, q, swap(k)))
+        odd = (jnp.where(low_v, swap(first), last), jnp.where(low, swap(q), k))
+        for head, (upper, lower) in enumerate((even, odd)):
+            out_ref[2 * pair + head, :PACKED, :] = upper.astype(jnp.bfloat16)
+            out_ref[2 * pair + head, PACKED:, :] = lower.astype(jnp.bfloat16)
+
+
+def tiles(tokens):
+    size = 256
+    return [
+        (start, min(tokens, start + size), min(tokens, start + 2 * size))
+        for start in range(0, tokens, size)
+    ]
+
+
+def attend_kernel(slab_ref, row_ids, column_ids, prob_ref, qk_ref, v_ref, out_t_ref, out_ref):
+    parts, length, _ = slab_ref.shape
+    rows = length - PACKED
+    tokens = parts * rows
+    slabs = [slab_ref[g].astype(jnp.float32) for g in range(parts)]
+    qk = jnp.concatenate([slab[PACKED:] for slab in slabs], axis=0).astype(jnp.bfloat16)
+    value = jnp.concatenate([unpack(slab[:PACKED], rows) for slab in slabs], axis=0)
+    value = value.astype(jnp.bfloat16)
+    qk_ref[...] = qk
+    v_ref[...] = value
+    query, key = qk[:, :HEAD_DIM] * HEAD_DIM ** (-0.5), qk[:, HEAD_DIM:]
+    for start, stop, seen in tiles(tokens):
+        scores = dot(key[:seen], query[start:stop], ((1,), (1,)))
+        allowed = column_ids[:seen, :] <= row_ids[:, start:stop]
+        numerator = jnp.where(allowed, jnp.exp(scores), 0.0)
+        probs = numerator * (1.0 / jnp.sum(numerator, axis=0, keepdims=True))
+        probs = probs.astype(jnp.bfloat16)
+        prob_ref[:seen, start:stop] = probs
+        out_t = dot(value[:seen], probs, ((0,), (0,)))
+        out_t_ref[:, start:stop] = out_t.astype(jnp.bfloat16).astype(jnp.float32)
+    out = jnp.transpose(out_t_ref[...])
+    for g in range(parts):
+        out_ref[g] = pack(out[g * rows : (g + 1) * rows]).astype(jnp.bfloat16)
+
+
+def affine_kernel(slab_ref, act_ref, inc_ref, w_ref, att_ref, aff_ref, up_ref, out_ref):
+    heads = slab_ref.shape[0]
+    rows, width = act_ref.shape
+    attended = jnp.concatenate(
+        [unpack(slab_ref[h].astype(jnp.float32), rows) for h in range(heads)], axis=1
+    ).astype(jnp.bfloat16)
+    att_ref[...] = attended
+    factor = jnp.exp(-dot(attended, w_ref[:, width:]))
+    scaled = inc_ref[...].astype(jnp.float32) * factor
+    up_ref[...] = scaled
+    shift_part = dot(attended, w_ref[:, :width])
+    aff_ref[:, :width] = (-scaled).astype(jnp.bfloat16)
+    latent_part = scaled * (act_ref[...].astype(jnp.float32) - shift_part)
+    aff_ref[:, width:] = (1.0 - latent_part).astype(jnp.bfloat16)
+    grad = dot(aff_ref[...], w_ref[...], ((1,), (1,)))
+    for h in range(heads):
+        block = grad[:, h * HEAD_DIM : (h + 1) * HEAD_DIM]
+        out_ref[h] = pack(block).astype(jnp.bfloat16)
+
+
+def out_term_kernel(me_ref, slab_ref, aff_ref, *out_refs):
+    heads = slab_ref.shape[0]
+    rows, width = aff_ref.shape[0], aff_ref.shape[1] // 2
+    columns = [
+        unpack(slab_ref[me_ref[0] ^ m].astype(jnp.float32), rows) for m in range(heads)
+    ]
+    for half, order in enumerate(ORDERS):
+        for out_ref, group in zip(out_refs[4 * half : 4 * half + 4], order):
+            left = jnp.concatenate([columns[m] for m in group], axis=1).astype(jnp.bfloat16)
+            right = aff_ref[:, half * width : (half + 1) * width]
+            out_ref[...] = dot(left, right, ((0,), (0,))).astype(jnp.bfloat16)
+
+
+ORDERS = (((1, 3, 5, 7), (2, 6), (4,), (0,)), ((2, 3, 6, 7), (1, 5), (4,), (0,)))
+
+
+def gathered_kernel(me_ref, *refs):
+    blocks, (wq_ref, wk_ref, normed_ref, back_ref) = refs[:HEADS], refs[HEADS:]
+    me = me_ref[0]
+    odd = lax.rem(me, 2) == 1
+    pair = lax.div(me, 2)
+    weights = [None, None]
+    for i, ref in enumerate((wq_ref, wk_ref)):
+        weights[i] = ref[:, pl.ds(pl.multiple_of(pair * 2 * HEAD_DIM, 2 * HEAD_DIM), 2 * HEAD_DIM)]
+    for m, block in enumerate(blocks):
+        normed = normalize(block[...])[0].astype(jnp.bfloat16)
+        q, k = dot(normed, weights[0]), dot(normed, weights[1])
+        low = low_lanes(q)
+        raw = jnp.where(low, jnp.where(odd, swap(q), q), jnp.where(odd, k, swap(k)))
+        scale = lax.rsqrt(half_sums(raw * raw) / HEAD_DIM + EPSILON)
+        group = me ^ m
+        normed_ref[group] = normed
+        back_ref[group, :, : 2 * HEAD_DIM] = raw * scale
+        back_ref[group, :, 2 * HEAD_DIM :] = scale
+
+
+def backward_kernel(
+    slab_ref, prob_ref, qk_ref, v_ref, out_t_ref, back_ref, out_ref, gk_ref, gv_ref, gq_ref
+):
+    parts, rows = back_ref.shape[:2]
+    tokens = parts * rows
+    grad_f = jnp.concatenate(
+        [unpack(slab_ref[g].astype(jnp.float32), rows) for g in range(parts)], axis=0
+    )
+    grad = grad_f.astype(jnp.bfloat16)
+    grad_t = jnp.transpose(grad_f)
+    correction = jnp.sum(grad_t * out_t_ref[...], axis=0, keepdims=True)
+    grad_t = grad_t.astype(jnp.bfloat16)
+    qk, value = qk_ref[...], v_ref[...]
+    query, key = qk[:, :HEAD_DIM], qk[:, HEAD_DIM:]
+    gk_ref[...] = jnp.zeros_like(gk_ref)
+    gv_ref[...] = jnp.zeros_like(gv_ref)
+    for start, stop, seen in tiles(tokens):
+        probs = prob_ref[:seen, start:stop]
+        grad_probs = dot(value[:seen], grad_t[:, start:stop])
+        scores = probs.astype(jnp.float32) * (grad_probs - correction[:, start:stop])
+        scores = scores.astype(jnp.bfloat16)
+        gv_ref[:seen, :] += dot(probs, grad[start:stop])
+        gk_ref[:seen, :] += dot(scores, query[start:stop])
+        gq_ref[:, start:stop] = dot(key[:seen], scores, ((0,), (0,)))
+    grad_q = jnp.transpose(gq_ref[...])
+    for g in range(parts):
+        own = slice(g * rows, (g + 1) * rows)
+        raw = jnp.concatenate([grad_q[own], gk_ref[own, :]], axis=1) * HEAD_DIM ** (-0.5)
+        unit, scale = back_ref[g, :, : 2 * HEAD_DIM], back_ref[g, :, 2 * HEAD_DIM :]
+        back = scale * (raw - unit * (half_sums(raw * unit) / HEAD_DIM))
+        out_ref[g, :PACKED, :] = pack(gv_ref[own, :]).astype(jnp.bfloat16)
+        out_ref[g, PACKED:, :] = back.astype(jnp.bfloat16)
+
+
+def weights_kernel(slab_ref, normed_ref, out_ref):
+    parts, rows, width = normed_ref.shape
+    qk_sum = v_sum = 0.0
+    for g in range(parts):
+        slab = slab_ref[g].astype(jnp.float32)
+        normed = normed_ref[g]
+        qk, v = slab[PACKED:].astype(jnp.bfloat16), unpack(slab[:PACKED], rows)
+        qk_sum = qk_sum + dot(qk, normed, ((0,), (0,)))
+        v_sum = v_sum + dot(v.astype(jnp.bfloat16), normed, ((0,), (0,)))
+    step = width // parts
+    for g in range(parts):
+        own = slice(g * step, (g + 1) * step)
+        out_ref[g, : 2 * HEAD_DIM, :] = qk_sum[:, own].astype(jnp.bfloat16)
+        out_ref[g, 2 * HEAD_DIM :, :] = v_sum[:, own].astype(jnp.bfloat16)
+
+
+def turn_kernel(slab_ref, *out_refs):
+    for i, out_ref in enumerate(out_refs):
+        own = slice(i * HEAD_DIM, (i + 1) * HEAD_DIM)
+        heads = [slab_ref[h, own, :].astype(jnp.float32) for h in range(slab_ref.shape[0])]
+        out_ref[0] = jnp.transpose(jnp.concatenate(heads, axis=0))
+
+
+def input_kernel(slab_ref, wq_ref, wk_ref, wv_ref, act_ref, up_ref, out_ref):
+    rows = act_ref.shape[0]
+    unit, row_scale = normalize(act_ref[...])
+    queries, keys, values = [], [], []
+    for pair in range(HEADS // 2):
+        even = slab_ref[2 * pair].astype(jnp.float32)
+        odd = slab_ref[2 * pair + 1].astype(jnp.float32)
+        low = low_lanes(even[PACKED:])
+        queries.append(jnp.where(low, even[PACKED:], swap(odd[PACKED:])))
+        keys.append(jnp.where(low, swap(even[PACKED:]), odd[PACKED:]))
+        values += [unpack(even[:PACKED], rows), unpack(odd[:PACKED], rows)]
+    total = 0.0
+    for parts, ref in ((queries, wq_ref), (keys, wk_ref), (values, wv_ref)):
+        left = jnp.concatenate(parts, axis=1).astype(jnp.bfloat16)
+        total = total + dot(left, ref[...], ((1,), (1,)))
+    total = total - unit * jnp.mean(total * unit, axis=-1, keepdims=True)
+    out_ref[...] = (up_ref[...] + row_scale * total).astype(jnp.bfloat16)
+
+
+def reorder_kernel(order_ref, rows_ref, out_ref):
+    rows = rows_ref.shape[0]
+    chosen = lax.broadcasted_iota(jnp.int32, (rows, rows), 1) == order_ref[...]
+    chosen = jnp.where(chosen, 1.0, 0.0).astype(jnp.bfloat16)
+    out_ref[0] = dot(chosen, rows_ref[...]).astype(jnp.bfloat16)
+
+
+def exchange(slabs):
+    return lax.all_to_all(slabs, "seq", split_axis=0, concat_axis=0, tiled=True)
+
+
+def spread(block):
+    side, near, far = [partner(block, "seq", bit) for bit in range(3)]
+    side_far = partner(far, "seq", 0)
+    near_far = partner(far, "seq", 1)
+    side_near = partner(near, "seq", 0)
+    last = partner(side_far, "seq", 1)
+    return block, side, near, side_near, far, side_far, near_far, last
+
+
+def wide(matrix):
+    return matrix.astype(jnp.float32)
+
+
+def sum_to_owner(terms, bits):
+    first, second, third, keep = terms
+    size = keep.shape[0]
+    got = wide(partner(first, "seq", bits[0]))
+    at = {0: got[:size], 1: got[size : 2 * size], 2: got[2 * size : 3 * size], 3: got[3 * size :]}
+    second = (wide(second) + jnp.concatenate([at[1], at[3]], axis=0)).astype(jnp.bfloat16)
+    third, keep = wide(third) + at[2], wide(keep) + at[0]
+    got = wide(partner(second, "seq", bits[1]))
+    third, keep = (third + got[size:]).astype(jnp.bfloat16), keep + got[:size]
+    return keep + wide(partner(third, "seq", bits[2]))
+
+
+def head_shards(
+    activations, incoming, w_query, w_key, w_value, w_out, block_ids, flip_order
+):
+    parts = lax.axis_size("seq")
+    sections = lax.axis_size("section")
+    me = lax.axis_index("seq").astype(jnp.int32).reshape(1)
+    field, upstream = activations[0], incoming[0]
+    wq, wk, wv, wo = w_query[0], w_key[0], w_value[0], w_out[0]
+    rows, width = field.shape
+    inner = wq.shape[1]
+    tokens = parts * rows
+    length = PACKED + rows
+    smem = pl.BlockSpec(memory_space=pltpu.SMEM)
+    vmem = pl.BlockSpec(memory_space=pltpu.VMEM)
+    f32 = jnp.float32
+
+    (slabs,) = call(
+        project_kernel, [shape(HEADS, length, 128)], [field, wq, wk, wv], 6 * rows * width * inner
+    )
+    slabs = exchange(slabs)
+    blocks = spread(field)
+    probs, qk, value, out_t, packed = call(
+        attend_kernel,
+        [
+            shape(tokens, tokens),
+            shape(tokens, 128),
+            shape(tokens, HEAD_DIM),
+            shape(HEAD_DIM, tokens, dtype=f32),
+            shape(parts, PACKED, 128),
+        ],
+        [slabs, block_ids[None, :], block_ids[:, None]],
+        4 * tokens * tokens * 256,
+    )
+    packed = exchange(packed)
+    attended, grad_affine, scaled, grad_slabs = call(
+        affine_kernel,
+        [
+            shape(rows, inner),
+            shape(rows, 2 * width),
+            shape(rows, width, dtype=f32),
+            shape(HEADS, PACKED, 128),
+        ],
+        [packed, field, upstream, wo],
+        8 * rows * width * inner,
+    )
+    grad_slabs = exchange(grad_slabs)
+    terms = call(
+        out_term_kernel,
+        [shape(len(group) * HEAD_DIM, width) for order in ORDERS for group in order],
+        [me, packed, grad_affine],
+        4 * rows * width * inner,
+        specs=[smem, vmem, vmem],
+    )
+    normed, back = call(
+        gathered_kernel,
+        [shape(parts, rows, width), shape(parts, rows, 256, dtype=f32)],
+        [me, *blocks, wq, wk],
+        4 * tokens * width * 128,
+        specs=[smem] + [vmem] * (HEADS + 2),
+    )
+    (grads,) = call(
+        backward_kernel,
+        [shape(parts, length, 128)],
+        [grad_slabs, probs, qk, value, out_t, back],
+        8 * tokens * tokens * 256,
+        scratch=[
+            pltpu.VMEM((tokens, HEAD_DIM), f32),
+            pltpu.VMEM((tokens, HEAD_DIM), f32),
+            pltpu.VMEM((HEAD_DIM, tokens), f32),
+        ],
+    )
+    token_grads = exchange(grads)
+    (weight_terms,) = call(
+        weights_kernel,
+        [shape(parts, 3 * HEAD_DIM, width // parts)],
+        [grads, normed],
+        2 * tokens * width * 256,
+    )
+    weight_terms = exchange(weight_terms)
+    (grad_input,) = call(
+        input_kernel,
+        [shape(rows, width)],
+        [token_grads, wq, wk, wv, field, scaled],
+        6 * rows * width * inner,
+    )
+    route = [
+        (s * parts + d, (s - 1) * parts + parts - 1 - d)
+        for s in range(1, sections)
+        for d in range(parts)
+    ]
+    moved = lax.ppermute(grad_input, ("section", "seq"), route)
+    grad_out = jnp.concatenate(
+        [sum_to_owner(terms[:4], (0, 1, 2)), sum_to_owner(terms[4:], (1, 0, 2))], axis=1
+    )
+    grad_q, grad_k, grad_v = call(
+        turn_kernel, [shape(1, width // parts, inner, dtype=f32)] * 3, [weight_terms]
+    )
+    (carry,) = call(
+        reorder_kernel, [shape(1, rows, width)], [flip_order[0][:, None], moved], 2 * rows * rows * width
+    )
+    return (carry, grad_q, grad_k, grad_v, grad_out[None])
+
+
 def solution(mesh):
+    shards = head_shards if mesh.shape["seq"] == HEADS else general_shards
     in_specs = (
         P("section", "seq", None),
         P("section", "seq", None),

time: 623 us -> 148 us (0.24)
  the two profiles are of different devices: /device:TPU:5 before, /device:TPU:9 now
where the time goes in v2:
time: 148 us; the launch traced here: 147 us
  starting transfers between devices  56.9 us (38%)
  waiting for transfers between devices  28.2 us (19%)
  local copies, waits for them, and re-layouts  27.4 us (19%)
  Pallas kernels  25.9 us (18%)
  other arithmetic  7.55 us (5%)
    all_to_all x5, starting transfers between devices, exchange(): return lax.all_to_all(slabs, 'seq', split_axis=0, concat_axis=0, tiled=True)  28.9 us
    pallas_call x10, Pallas kernels, call(): pl.pallas_call(kernel, out_shape=tuple(outs), in_specs=specs or [single]...  25.9 us
    unnamed x86, local copies, waits for them, and re-layouts  24.9 us
    ppermute x1, starting transfers between devices, head_shards(): moved = lax.ppermute(grad_input, ('section', 'seq'), route)  15.6 us
    all_to_all x5, waiting for transfers between devices, exchange(): return lax.all_to_all(slabs, 'seq', split_axis=0, concat_axis=0, tiled=True)  13 us
    ppermute x13, starting transfers between devices, partner(): return lax.ppermute(block, axis, route)  12.4 us
    ppermute x1, waiting for transfers between devices, head_shards(): moved = lax.ppermute(grad_input, ('section', 'seq'), route)  10.4 us
    ppermute x13, waiting for transfers between devices, partner(): return lax.ppermute(block, axis, route)  4.81 us
  transfers between devices with their start and end apart: 19, of which 3 were waited for; matrix products, arithmetic and copies ran while one was open for 7% of the time, Pallas kernels for 16%

profile of v2, /device:TPU:9, one launch (start us, length us, event | category | flops | bytes accessed | tf_op | source)
XLA Modules:
  0.0 146.9 jit_solution(11503601821569051350)
XLA Ops:
  0.6 1.2 copy-done
  1.9 1.2 copy-done.2
  3.1 1.0 copy-done.4
  4.0 1.2 copy-done.6
  5.3 1.8 %shard_map.119 = bf16[8,216,128]{2,1,0:T(8,128)(2,1)} custom-call(bf16[136,1024]{1,0:T(8,128)(2,1)S(1)} %bitcast.16, bf16[1024,512]{1,0:T(8,128)(2,1)S(1)} %bitcast.10, bf16[1024,512]{1,0:T(8,128)(2,1)S(1)} %bitcast.13, bf16[1024,512]{1,0:T(8,128)(2,1)S(1)} %bitcast.23), custom_call_target="tpu_custom_call" | custom-call | flops 427819008 | bytes 3866624 | tf_op jit(solution)/shard_map/pallas_call | solution.py:202
  7.0 5.7 %all-to-all-start = ((bf16[8,216,128]{2,1,0:T(8,128)(2,1)}), bf16[8,216,128]{2,1,0:T(8,128)(2,1)S(1)}, u32[]{:S(2)}, u32[]{:S(2)}) async-start(bf16[8,216,128]{2,1,0:T(8,128)(2,1)} %shard_map.119), calls=%async_computation | async-start | bytes 884736 | tf_op jit(solution)/shard_map/all_to_all | solution.py:444
  12.7 2.1 %collective-permute-start.3 = (bf16[136,1024]{1,0:T(8,128)(2,1)S(1)}, bf16[136,1024]{1,0:T(8,128)(2,1)S(1)}, u32[]{:S(2)}, u32[]{:S(2)}) collective-permute-start(bf16[136,1024]{1,0:T(8,128)(2,1)S(1)} %bitcast.17), channel_id=1, source_target_pairs={{0,4},{4,0},{1,5},{5,1},{2,6},{6,2},{3,7},{7,3},{8,12},{12,8},{9,1... | collective-permute-start | bytes 835592 | tf_op jit(solution)/shard_map/ppermute | solution.py:22
  15.0 12.9 %all-to-all-done.slab_ref = bf16[8,216,128]{2,1,0:T(8,128)(2,1)S(1)} async-done(((bf16[8,216,128]{2,1,0:T(8,128)(2,1)}), bf16[8,216,128]{2,1,0:T(8,128)(2,1)S(1)}, u32[]{:S(2)}, u32[]{:S(2)}) %all-to-all-start) | async-done | bytes 442400 | tf_op jit(solution)/shard_map/all_to_all | solution.py:444
  28.0 3.5 %shard_map.120 = (bf16[1088,1088]{1,0:T(8,128)(2,1)S(1)}, bf16[1088,128]{1,0:T(8,128)(2,1)S(1)}, bf16[1088,64]{1,0:T(8,128)(2,1)S(1)}, f32[64,1088]{1,0:T(8,128)S(1)}, bf16[8,80,128]{2,1,0:T(8,128)(2,1)}) custom-call(bf16[8,216,128]{2,1,0:T(8,128)(2,1)S(1)} %all-to-all-done.slab_ref, s32[1,1088]{1,0:T(1,128)S(1)} %broadcast_in_dim.9.row_ids, ...), custom_call_target="tpu_custom_call" | custom-call | flops 1212153856 | bytes 3678720 | tf_op jit(solution)/shard_map/pallas_call | solution.py:202
  31.5 1.4 copy-done.28
  35.1 7.3 %all-to-all-start.1 = ((bf16[8,80,128]{2,1,0:T(8,128)(2,1)}), bf16[8,80,128]{2,1,0:T(8,128)(2,1)S(1)}, u32[]{:S(2)}, u32[]{:S(2)}) async-start(bf16[8,80,128]{2,1,0:T(8,128)(2,1)} %get-tuple-element.26), calls=%async_computation.1 | async-start | bytes 327680 | tf_op jit(solution)/shard_map/all_to_all | solution.py:444
  42.4 1.4 collective-permute-start.4
  43.9 1.4 collective-permute-start.5
  45.3 4.8 %collective-permute-done.1.refs_2_ = bf16[136,1024]{1,0:T(8,128)(2,1)S(1)} collective-permute-done((bf16[136,1024]{1,0:T(8,128)(2,1)S(1)}, bf16[136,1024]{1,0:T(8,128)(2,1)S(1)}, u32[]{:S(2)}, u32[]{:S(2)}) %collective-permute-start.1) | collective-permute-done | bytes 278560 | tf_op jit(solution)/shard_map/ppermute | solution.py:22
  50.1 1.2 collective-permute-start.2
  51.3 1.8 %collective-permute-start.6 = (bf16[136,1024]{1,0:T(8,128)(2,1)S(1)}, bf16[136,1024]{1,0:T(8,128)(2,1)}, u32[]{:S(2)}, u32[]{:S(2)}) collective-permute-start(bf16[136,1024]{1,0:T(8,128)(2,1)S(1)} %collective-permute-done.4.refs_5_), channel_id=1, source_target_pairs={{0,2},{2,0},{1,3},{3,1},{4,6},{6,4},{5,7},{7,5},{8,10},{10,8},{9,1... | collective-permute-start | bytes 835592 | tf_op jit(solution)/shard_map/ppermute | solution.py:22
  53.1 1.6 %copy-done.10 = bf16[1,512,2048]{2,1,0:T(8,128)(2,1)S(1)} copy-done((bf16[1,512,2048]{2,1,0:T(8,128)(2,1)S(1)}, bf16[1,512,2048]{2,1,0:T(8,128)(2,1)}, u32[]{:S(2)}) %copy-start.10) | copy-done | bytes 2097176
  54.7 1.0 copy-done.14
  55.7 2.1 %shard_map.121 = (bf16[136,512]{1,0:T(8,128)(2,1)}, bf16[136,2048]{1,0:T(8,128)(2,1)S(1)}, f32[136,1024]{1,0:T(8,128)S(1)}, bf16[8,80,128]{2,1,0:T(8,128)(2,1)}) custom-call(bf16[8,80,128]{2,1,0:T(8,128)(2,1)S(1)} %all-to-all-done.1.slab_ref, bf16[136,1024]{1,0:T(8,128)(2,1)S(1)} %bitcast.20, bf16[136,1024]{1,0:T(8,128)(2,1)S(1)} %bitcast.26, ...), custom_call_target="tpu_custom_call" | custom-call | flops 570425344 | bytes 4235264 | tf_op jit(solution)/shard_map/pallas_call | solution.py:202
  58.6 1.8 %shard_map.128 = (bf16[256,1024]{1,0:T(8,128)(2,1)}, bf16[128,1024]{1,0:T(8,128)(2,1)S(1)}, bf16[64,1024]{1,0:T(8,128)(2,1)S(1)}, bf16[64,1024]{1,0:T(8,128)(2,1...) custom-call(s32[1]{0:T(128)} %bitcast.7.me_ref, ...), custom_call_target="tpu_custom_call" | custom-call | flops 285212672 | bytes 2818052 | tf_op jit(solution)/shard_map/pallas_call | solution.py:202
  64.7 4.7 %all-to-all-start.2 = ((bf16[8,80,128]{2,1,0:T(8,128)(2,1)}), bf16[8,80,128]{2,1,0:T(8,128)(2,1)S(1)}, u32[]{:S(2)}, u32[]{:S(2)}) async-start(bf16[8,80,128]{2,1,0:T(8,128)(2,1)} %get-tuple-element.27), calls=%async_computation.2 | async-start | bytes 327680 | tf_op jit(solution)/shard_map/all_to_all | solution.py:444
  69.6 4.3 %shard_map.122 = (bf16[8,136,1024]{2,1,0:T(8,128)(2,1)S(1)}, f32[8,136,256]{2,1,0:T(8,128)S(1)}) custom-call(s32[1]{0:T(128)} %bitcast.7.me_ref, bf16[136,1024]{1,0:T(8,128)(2,1)S(1)} %bitcast.21, bf16[136,1024]{1,0:T(8,128)(2,1)} %collective-permute-done.refs_1_, bf16[136,1024]{1,0:T(8,128)(2,1)S(1)} %collective-permute-done.1.refs_2_, ...), custom_call_target="tpu_custom_call" | custom-call | flops 570425344 | bytes 7667716 | tf_op jit(solution)/shard_map/pallas_call | solution.py:202
  73.9 1.4 copy-done.8
  75.3 1.0 copy-done.26
  76.3 1.2 copy-done.27
  77.5 1.7 %copy-done.29 = bf16[1088,1088]{1,0:T(8,128)(2,1)S(1)} copy-done((bf16[1088,1088]{1,0:T(8,128)(2,1)S(1)}, bf16[1088,1088]{1,0:T(8,128)(2,1)}, u32[]{:S(2)}) %copy-start.29) | copy-done | bytes 2367512
  79.2 1.0 copy-done.31
  80.2 1.0 copy-done.33
  81.2 1.0 copy-done.35
  82.1 4.2 %shard_map.123.slab_ref = bf16[8,216,128]{2,1,0:T(8,128)(2,1)} custom-call(bf16[8,80,128]{2,1,0:T(8,128)(2,1)S(1)} %all-to-all-done.2.slab_ref, bf16[1088,1088]{1,0:T(8,128)(2,1)S(1)} %copy-done.29, bf16[1088,128]{1,0:T(8,128)(2,1)S(1)} %copy-done.33, bf16[1088,64]{1,0:T(8,128)(2,1)S(1)} %copy-done.35, f32[64,1088]{1,0:T(8,128)S(1)} %copy-done.31, ...), custom_call_target="tpu_custom_call" | custom-call | flops 2424307712 | bytes 4784128 | tf_op jit(solution)/shard_map/pallas_call | solution.py:202
  86.3 6.0 %all-to-all-start.3 = ((bf16[8,216,128]{2,1,0:T(8,128)(2,1)}), bf16[8,216,128]{2,1,0:T(8,128)(2,1)}, u32[]{:S(2)}, u32[]{:S(2)}) async-start(bf16[8,216,128]{2,1,0:T(8,128)(2,1)} %shard_map.123.slab_ref), calls=%async_computation.3 | async-start | bytes 884736 | tf_op jit(solution)/shard_map/all_to_all | solution.py:444
  92.4 1.2 fusion.6
  93.7 1.0 fusion.7
  94.8 1.5 %collective-permute-start.12 = (bf16[128,1024]{1,0:T(8,128)(2,1)S(1)}, bf16[128,1024]{1,0:T(8,128)(2,1)S(1)}, u32[]{:S(2)}, u32[]{:S(2)}) collective-permute-start(bf16[128,1024]{1,0:T(8,128)(2,1)S(1)} %fusion.1), channel_id=1, source_target_pairs={{0,1},{1,0},{2,3},{3,2},{4,5},{5,4},{6,7},{7,6},{8,9},{9,8},{10,11... | collective-permute-start | bytes 786440 | tf_op jit(solution)/shard_map/ppermute | solution.py:22
  96.3 2.1 %shard_map.126 = bf16[8,192,128]{2,1,0:T(8,128)(2,1)S(1)} custom-call(bf16[8,216,128]{2,1,0:T(8,128)(2,1)} %shard_map.123.slab_ref, bf16[8,136,1024]{2,1,0:T(8,128)(2,1)S(1)} %copy-done.9), custom_call_target="tpu_custom_call" | custom-call | flops 570425344 | bytes 3063808 | tf_op jit(solution)/shard_map/pallas_call | solution.py:202
  98.4 1.3 convert_element_type.49
  99.8 1.5 %convert_element_type.57 = f32[256,1024]{1,0:T(8,128)S(1)} convert(bf16[256,1024]{1,0:T(8,128)(2,1)} %collective-permute-done.11) | non-fusion elementwise | flops 262144 | bytes 1572864 | tf_op jit(solution)/shard_map/convert_element_type | solution.py:457
  102.1 2.1 %collective-permute-start.10 = (bf16[64,1024]{1,0:T(8,128)(2,1)}, bf16[64,1024]{1,0:T(8,128)(2,1)}, u32[]{:S(2)}, u32[]{:S(2)}) collective-permute-start(bf16[64,1024]{1,0:T(8,128)(2,1)} %fusion.4), channel_id=1, source_target_pairs={{0,4},{4,0},{1,5},{5,1},{2,6},{6,2},{3,7},{7,3},{8,12},{12,8},{9,1... | collective-permute-start | bytes 393224 | tf_op jit(solution)/shard_map/ppermute | solution.py:22
  105.4 5.2 %all-to-all-start.4 = ((bf16[8,192,128]{2,1,0:T(8,128)(2,1)}), bf16[8,192,128]{2,1,0:T(8,128)(2,1)}, u32[]{:S(2)}, u32[]{:S(2)}) async-start(bf16[8,192,128]{2,1,0:T(8,128)(2,1)} %copy-done.11), calls=%async_computation.4 | async-start | bytes 786432 | tf_op jit(solution)/shard_map/all_to_all | solution.py:444
  110.6 1.2 fusion.5
  111.8 1.0 copy-done.13
  112.8 3.1 %shard_map.124 = bf16[136,1024]{1,0:T(8,128)(2,1)} custom-call(bf16[8,216,128]{2,1,0:T(8,128)(2,1)} %all-to-all-done.3.slab_ref, bf16[1024,512]{1,0:T(8,128)(2,1)S(1)} %bitcast.12, bf16[1024,512]{1,0:T(8,128)(2,1)S(1)} %bitcast.15, bf16[1024,512]{1,0:T(8,128)(2,1)S(1)} %bitcast.24, bf16[136,1024]{1,0:T(8,128)(2,1)S(1)} %bitcast.22, f32[136,1024]{1,0:T(8,128)S(1)} %copy-done.13), custom_call_target="tpu_custom_call" | custom-call | flops 427819008 | bytes 4702208 | tf_op jit(solution)/shard_map/pallas_call | solution.py:202
  115.9 15.6 %collective-permute-start.7 = (bf16[136,1024]{1,0:T(8,128)(2,1)}, bf16[136,1024]{1,0:T(8,128)(2,1)S(1)}, u32[]{:S(2)}, u32[]{:S(2)}) collective-permute-start(bf16[136,1024]{1,0:T(8,128)(2,1)} %shard_map.124), channel_id=1, source_target_pairs={{8,7},{9,6},{10,5},{11,4},{12,3},{13,2},{14,1},{15,0},{16,15},{17,... | collective-permute-start | bytes 835592 | tf_op jit(solution)/shard_map/ppermute | solution.py:562
  131.6 1.1 fusion.3
  132.7 0.8 maximum_bitcast_fusion
  133.5 2.0 %shard_map.127 = (f32[1,128,512]{2,1,0:T(8,128)}, f32[1,128,512]{2,1,0:T(8,128)}, f32[1,128,512]{2,1,0:T(8,128)}) custom-call(bf16[8,192,128]{2,1,0:T(8,128)(2,1)} %all-to-all-done.4.slab_ref), custom_call_target="tpu_custom_call" | custom-call | bytes 1179648 | tf_op jit(solution)/shard_map/pallas_call | solution.py:202
  135.5 10.4 %collective-permute-done.7.rows_ref = bf16[136,1024]{1,0:T(8,128)(2,1)S(1)} collective-permute-done((bf16[136,1024]{1,0:T(8,128)(2,1)}, bf16[136,1024]{1,0:T(8,128)(2,1)S(1)}, u32[]{:S(2)}, u32[]{:S(2)}) %collective-permute-start.7) | collective-permute-done | bytes 278560 | tf_op jit(solution)/shard_map/ppermute | solution.py:562
  145.9 1.0 shard_map.125
  (102 shorter events, 9.9 us)
Async XLA Ops:
  0.6 1.2 copy-start
  1.9 1.2 copy-start.2
  4.0 1.2 copy-start.6
  5.3 7.5 %copy-start.5 = (bf16[1,136,1024]{2,1,0:T(8,128)(2,1)S(1)}, bf16[1,136,1024]{2,1,0:T(8,128)(2,1)}, u32[]{:S(2)}) copy-start(bf16[1,136,1024]{2,1,0:T(8,128)(2,1)} %param.8) | copy-start | bytes 835588
  5.3 9.6 %copy-start.41 = (s32[1088]{0:T(1024)S(1)}, s32[1088]{0:T(1024)}, u32[]{:S(2)}) copy-start(s32[1088]{0:T(1024)} %param.14) | copy-start | bytes 13060
  7.0 20.9 %all-to-all-start = ((bf16[8,216,128]{2,1,0:T(8,128)(2,1)}), bf16[8,216,128]{2,1,0:T(8,128)(2,1)S(1)}, u32[]{:S(2)}, u32[]{:S(2)}) async-start(bf16[8,216,128]{2,1,0:T(8,128)(2,1)} %shard_map.119), calls=%async_computation | async-start | bytes 884736 | tf_op jit(solution)/shard_map/all_to_all | solution.py:444
  12.7 29.6 %collective-permute-start.3 = (bf16[136,1024]{1,0:T(8,128)(2,1)S(1)}, bf16[136,1024]{1,0:T(8,128)(2,1)S(1)}, u32[]{:S(2)}, u32[]{:S(2)}) collective-permute-start(bf16[136,1024]{1,0:T(8,128)(2,1)S(1)} %bitcast.17), channel_id=1, source_target_pairs={{0,4},{4,0},{1,5},{5,1},{2,6},{6,2},{3,7},{7,3},{8,12},{12,8},{9,1... | collective-permute-start | bytes 835592 | tf_op jit(solution)/shard_map/ppermute | solution.py:22
  31.5 1.4 copy-start.28
  35.1 34.4 %copy-start.42 = (s32[1,136]{1,0:T(1,128)S(1)}, s32[1,136]{1,0:T(1,128)}, u32[]{:S(2)}) copy-start(s32[1,136]{1,0:T(1,128)} %param.15) | copy-start | bytes 1636
  35.1 34.5 %copy-start.1 = (bf16[1,1024,512]{2,1,0:T(8,128)(2,1)S(1)}, bf16[1,1024,512]{2,1,0:T(8,128)(2,1)}, u32[]{:S(2)}) copy-start(bf16[1,1024,512]{2,1,0:T(8,128)(2,1)} %param.10) | copy-start | bytes 3145732
  35.1 34.5 %copy-start.3 = (bf16[1,1024,512]{2,1,0:T(8,128)(2,1)S(1)}, bf16[1,1024,512]{2,1,0:T(8,128)(2,1)}, u32[]{:S(2)}) copy-start(bf16[1,1024,512]{2,1,0:T(8,128)(2,1)} %param.11) | copy-start | bytes 3145732
  35.1 18.1 %all-to-all-start.1 = ((bf16[8,80,128]{2,1,0:T(8,128)(2,1)}), bf16[8,80,128]{2,1,0:T(8,128)(2,1)S(1)}, u32[]{:S(2)}, u32[]{:S(2)}) async-start(bf16[8,80,128]{2,1,0:T(8,128)(2,1)} %get-tuple-element.26), calls=%async_computation.1 | async-start | bytes 327680 | tf_op jit(solution)/shard_map/all_to_all | solution.py:444
  42.3 7.7 %collective-permute-start.1 = (bf16[136,1024]{1,0:T(8,128)(2,1)S(1)}, bf16[136,1024]{1,0:T(8,128)(2,1)S(1)}, u32[]{:S(2)}, u32[]{:S(2)}) collective-permute-start(bf16[136,1024]{1,0:T(8,128)(2,1)S(1)} %bitcast.18), channel_id=1, source_target_pairs={{0,2},{2,0},{1,3},{3,1},{4,6},{6,4},{5,7},{7,5},{8,10},{10,8},{9,1... | collective-permute-start | bytes 835592 | tf_op jit(solution)/shard_map/ppermute | solution.py:22
  42.4 8.9 %collective-permute-start.4 = (bf16[136,1024]{1,0:T(8,128)(2,1)S(1)}, bf16[136,1024]{1,0:T(8,128)(2,1)S(1)}, u32[]{:S(2)}, u32[]{:S(2)}) collective-permute-start(bf16[136,1024]{1,0:T(8,128)(2,1)S(1)} %collective-permute-done.3.refs_4_), channel_id=1, source_target_pairs={{0,1},{1,0},{2,3},{3,2},{4,5},{5,4},{6,7},{7,6},{8,9},{9,8},{10,11... | collective-permute-start | bytes 835592 | tf_op jit(solution)/shard_map/ppermute | solution.py:22
  43.8 25.7 %collective-permute-start = (bf16[136,1024]{1,0:T(8,128)(2,1)S(1)}, bf16[136,1024]{1,0:T(8,128)(2,1)}, u32[]{:S(2)}, u32[]{:S(2)}) collective-permute-start(bf16[136,1024]{1,0:T(8,128)(2,1)S(1)} %bitcast.19), channel_id=1, source_target_pairs={{0,1},{1,0},{2,3},{3,2},{4,5},{5,4},{6,7},{7,6},{8,9},{9,8},{10,11... | collective-permute-start | bytes 835592 | tf_op jit(solution)/shard_map/ppermute | solution.py:22
  43.9 25.7 %collective-permute-start.5 = (bf16[136,1024]{1,0:T(8,128)(2,1)S(1)}, bf16[136,1024]{1,0:T(8,128)(2,1)}, u32[]{:S(2)}, u32[]{:S(2)}) collective-permute-start(bf16[136,1024]{1,0:T(8,128)(2,1)S(1)} %collective-permute-done.3.refs_4_), channel_id=1, source_target_pairs={{0,2},{2,0},{1,3},{3,1},{4,6},{6,4},{5,7},{7,5},{8,10},{10,8},{9,1... | collective-permute-start | bytes 835592 | tf_op jit(solution)/shard_map/ppermute | solution.py:22
  50.1 19.5 %collective-permute-start.2 = (bf16[136,1024]{1,0:T(8,128)(2,1)S(1)}, bf16[136,1024]{1,0:T(8,128)(2,1)}, u32[]{:S(2)}, u32[]{:S(2)}) collective-permute-start(bf16[136,1024]{1,0:T(8,128)(2,1)S(1)} %collective-permute-done.1.refs_2_), channel_id=1, source_target_pairs={{0,1},{1,0},{2,3},{3,2},{4,5},{5,4},{6,7},{7,6},{8,9},{9,8},{10,11... | collective-permute-start | bytes 835592 | tf_op jit(solution)/shard_map/ppermute | solution.py:22
  51.3 18.3 %collective-permute-start.6 = (bf16[136,1024]{1,0:T(8,128)(2,1)S(1)}, bf16[136,1024]{1,0:T(8,128)(2,1)}, u32[]{:S(2)}, u32[]{:S(2)}) collective-permute-start(bf16[136,1024]{1,0:T(8,128)(2,1)S(1)} %collective-permute-done.4.refs_5_), channel_id=1, source_target_pairs={{0,2},{2,0},{1,3},{3,1},{4,6},{6,4},{5,7},{7,5},{8,10},{10,8},{9,1... | collective-permute-start | bytes 835592 | tf_op jit(solution)/shard_map/ppermute | solution.py:22
  53.1 1.6 %copy-start.10 = (bf16[1,512,2048]{2,1,0:T(8,128)(2,1)S(1)}, bf16[1,512,2048]{2,1,0:T(8,128)(2,1)}, u32[]{:S(2)}) copy-start(bf16[1,512,2048]{2,1,0:T(8,128)(2,1)} %param.13) | copy-start | bytes 6291460
  64.4 28.0 %collective-permute-start.8 = (bf16[256,1024]{1,0:T(8,128)(2,1)}, bf16[256,1024]{1,0:T(8,128)(2,1)}, u32[]{:S(2)}, u32[]{:S(2)}) collective-permute-start(bf16[256,1024]{1,0:T(8,128)(2,1)} %get-tuple-element.40), channel_id=1, source_target_pairs={{0,1},{1,0},{2,3},{3,2},{4,5},{5,4},{6,7},{7,6},{8,9},{9,8},{10,11... | collective-permute-start | bytes 1572872 | tf_op jit(solution)/shard_map/ppermute | solution.py:22
  64.7 11.6 %all-to-all-start.2 = ((bf16[8,80,128]{2,1,0:T(8,128)(2,1)}), bf16[8,80,128]{2,1,0:T(8,128)(2,1)S(1)}, u32[]{:S(2)}, u32[]{:S(2)}) async-start(bf16[8,80,128]{2,1,0:T(8,128)(2,1)} %get-tuple-element.27), calls=%async_computation.2 | async-start | bytes 327680 | tf_op jit(solution)/shard_map/all_to_all | solution.py:444
  73.9 1.4 copy-start.8
  75.3 1.0 copy-start.26
  76.3 17.4 %collective-permute-start.11 = (bf16[256,1024]{1,0:T(8,128)(2,1)}, bf16[256,1024]{1,0:T(8,128)(2,1)}, u32[]{:S(2)}, u32[]{:S(2)}) collective-permute-start(bf16[256,1024]{1,0:T(8,128)(2,1)} %get-tuple-element.44), channel_id=1, source_target_pairs={{0,2},{2,0},{1,3},{3,1},{4,6},{6,4},{5,7},{7,5},{8,10},{10,8},{9,1... | collective-permute-start | bytes 1572872 | tf_op jit(solution)/shard_map/ppermute | solution.py:22
  76.3 1.2 copy-start.27
  77.5 1.7 %copy-start.29 = (bf16[1088,1088]{1,0:T(8,128)(2,1)S(1)}, bf16[1088,1088]{1,0:T(8,128)(2,1)}, u32[]{:S(2)}) copy-start(bf16[1088,1088]{1,0:T(8,128)(2,1)} %copy-done.28) | copy-start | bytes 7102468
  79.2 1.0 copy-start.31
  80.2 1.0 copy-start.33
  82.1 11.4 %copy-start.18 = (bf16[128,1024]{1,0:T(8,128)(2,1)S(1)}, bf16[128,1024]{1,0:T(8,128)(2,1)}, u32[]{:S(2)}) copy-start(bf16[128,1024]{1,0:T(8,128)(2,1)} %copy-done.17) | copy-start | bytes 786436
  86.3 8.4 %copy-start.16 = (bf16[128,1024]{1,0:T(8,128)(2,1)S(1)}, bf16[128,1024]{1,0:T(8,128)(2,1)}, u32[]{:S(2)}) copy-start(bf16[128,1024]{1,0:T(8,128)(2,1)} %copy-done.15) | copy-start | bytes 786436
  86.3 19.1 %all-to-all-start.3 = ((bf16[8,216,128]{2,1,0:T(8,128)(2,1)}), bf16[8,216,128]{2,1,0:T(8,128)(2,1)}, u32[]{:S(2)}, u32[]{:S(2)}) async-start(bf16[8,216,128]{2,1,0:T(8,128)(2,1)} %shard_map.123.slab_ref), calls=%async_computation.3 | async-start | bytes 884736 | tf_op jit(solution)/shard_map/all_to_all | solution.py:444
  92.4 3.9 %copy-start.9 = (bf16[8,136,1024]{2,1,0:T(8,128)(2,1)S(1)}, bf16[8,136,1024]{2,1,0:T(8,128)(2,1)}, u32[]{:S(2)}) copy-start(bf16[8,136,1024]{2,1,0:T(8,128)(2,1)} %copy-done.8) | copy-start | bytes 6684676
  93.6 7.7 %collective-permute-start.9 = (bf16[128,1024]{1,0:T(8,128)(2,1)S(1)}, bf16[128,1024]{1,0:T(8,128)(2,1)S(1)}, u32[]{:S(2)}, u32[]{:S(2)}) collective-permute-start(bf16[128,1024]{1,0:T(8,128)(2,1)S(1)} %fusion), channel_id=1, source_target_pairs={{0,2},{2,0},{1,3},{3,1},{4,6},{6,4},{5,7},{7,5},{8,10},{10,8},{9,1... | collective-permute-start | bytes 786440 | tf_op jit(solution)/shard_map/ppermute | solution.py:22
  94.8 9.4 %collective-permute-start.12 = (bf16[128,1024]{1,0:T(8,128)(2,1)S(1)}, bf16[128,1024]{1,0:T(8,128)(2,1)S(1)}, u32[]{:S(2)}, u32[]{:S(2)}) collective-permute-start(bf16[128,1024]{1,0:T(8,128)(2,1)S(1)} %fusion.1), channel_id=1, source_target_pairs={{0,1},{1,0},{2,3},{3,2},{4,5},{5,4},{6,7},{7,6},{8,9},{9,8},{10,11... | collective-permute-start | bytes 786440 | tf_op jit(solution)/shard_map/ppermute | solution.py:22
  98.4 3.7 %copy-start.11 = (bf16[8,192,128]{2,1,0:T(8,128)(2,1)}, bf16[8,192,128]{2,1,0:T(8,128)(2,1)S(1)}, u32[]{:S(2)}) copy-start(bf16[8,192,128]{2,1,0:T(8,128)(2,1)S(1)} %shard_map.126) | copy-start | bytes 1179652
  98.4 3.0 %copy-start.22 = (bf16[64,1024]{1,0:T(8,128)(2,1)S(1)}, bf16[64,1024]{1,0:T(8,128)(2,1)}, u32[]{:S(2)}) copy-start(bf16[64,1024]{1,0:T(8,128)(2,1)} %copy-done.21) | copy-start | bytes 393220
  99.7 5.3 %copy-start.37 = (f32[256,1024]{1,0:T(8,128)}, f32[256,1024]{1,0:T(8,128)S(1)}, u32[]{:S(2)}) copy-start(f32[256,1024]{1,0:T(8,128)S(1)} %convert_element_type.49) | copy-start | bytes 3145732
  99.7 4.5 %copy-start.20 = (bf16[64,1024]{1,0:T(8,128)(2,1)S(1)}, bf16[64,1024]{1,0:T(8,128)(2,1)}, u32[]{:S(2)}) copy-start(bf16[64,1024]{1,0:T(8,128)(2,1)} %copy-done.19) | copy-start | bytes 393220
  101.3 3.7 %copy-start.36 = (f32[256,1024]{1,0:T(8,128)}, f32[256,1024]{1,0:T(8,128)S(1)}, u32[]{:S(2)}) copy-start(f32[256,1024]{1,0:T(8,128)S(1)} %convert_element_type.57) | copy-start | bytes 3145732
  101.4 3.7 %copy-start.40 = (f32[128,1024]{1,0:T(8,128)}, f32[128,1024]{1,0:T(8,128)S(1)}, u32[]{:S(2)}) copy-start(f32[128,1024]{1,0:T(8,128)S(1)} %convert_element_type.52) | copy-start | bytes 1572868
  101.4 10.3 %copy-start.7 = (bf16[1,1024,512]{2,1,0:T(8,128)(2,1)S(1)}, bf16[1,1024,512]{2,1,0:T(8,128)(2,1)}, u32[]{:S(2)}) copy-start(bf16[1,1024,512]{2,1,0:T(8,128)(2,1)} %param.12) | copy-start | bytes 3145732
  102.1 8.5 %collective-permute-start.10 = (bf16[64,1024]{1,0:T(8,128)(2,1)}, bf16[64,1024]{1,0:T(8,128)(2,1)}, u32[]{:S(2)}, u32[]{:S(2)}) collective-permute-start(bf16[64,1024]{1,0:T(8,128)(2,1)} %fusion.4), channel_id=1, source_target_pairs={{0,4},{4,0},{1,5},{5,1},{2,6},{6,2},{3,7},{7,3},{8,12},{12,8},{9,1... | collective-permute-start | bytes 393224 | tf_op jit(solution)/shard_map/ppermute | solution.py:22
  105.1 26.5 %collective-permute-start.13 = (bf16[64,1024]{1,0:T(8,128)(2,1)}, bf16[64,1024]{1,0:T(8,128)(2,1)}, u32[]{:S(2)}, u32[]{:S(2)}) collective-permute-start(bf16[64,1024]{1,0:T(8,128)(2,1)} %fusion.2), channel_id=1, source_target_pairs={{0,4},{4,0},{1,5},{5,1},{2,6},{6,2},{3,7},{7,3},{8,12},{12,8},{9,1... | collective-permute-start | bytes 393224 | tf_op jit(solution)/shard_map/ppermute | solution.py:22
  105.4 28.1 %all-to-all-start.4 = ((bf16[8,192,128]{2,1,0:T(8,128)(2,1)}), bf16[8,192,128]{2,1,0:T(8,128)(2,1)}, u32[]{:S(2)}, u32[]{:S(2)}) async-start(bf16[8,192,128]{2,1,0:T(8,128)(2,1)} %copy-done.11), calls=%async_computation.4 | async-start | bytes 786432 | tf_op jit(solution)/shard_map/all_to_all | solution.py:444
  111.7 1.1 copy-start.13
  112.8 18.8 %copy-start.24 = (bf16[64,1024]{1,0:T(8,128)(2,1)S(1)}, bf16[64,1024]{1,0:T(8,128)(2,1)}, u32[]{:S(2)}) copy-start(bf16[64,1024]{1,0:T(8,128)(2,1)} %copy-done.23) | copy-start | bytes 393220
  112.8 18.8 %copy-start.39 = (f32[128,1024]{1,0:T(8,128)S(1)}, f32[128,1024]{1,0:T(8,128)}, u32[]{:S(2)}) copy-start(f32[128,1024]{1,0:T(8,128)} %copy-done.38) | copy-start | bytes 1572868
  115.9 29.9 %collective-permute-start.7 = (bf16[136,1024]{1,0:T(8,128)(2,1)}, bf16[136,1024]{1,0:T(8,128)(2,1)S(1)}, u32[]{:S(2)}, u32[]{:S(2)}) collective-permute-start(bf16[136,1024]{1,0:T(8,128)(2,1)} %shard_map.124), channel_id=1, source_target_pairs={{8,7},{9,6},{10,5},{11,4},{12,3},{13,2},{14,1},{15,0},{16,15},{17,... | collective-permute-start | bytes 835592 | tf_op jit(solution)/shard_map/ppermute | solution.py:562
  (14 other events, 10.6 us)

commit v3 on v2

--- a/solution.py
+++ b/solution.py
@@ -205,7 +205,7 @@
         in_specs=specs or [single] * len(operands),
         out_specs=tuple([single] * len(outs)),
         scratch_shapes=list(scratch),
-        compiler_params=pltpu.CompilerParams(vmem_limit_bytes=40 * 2**20),
+        compiler_params=pltpu.CompilerParams(vmem_limit_bytes=14 * 2**20),
         cost_estimate=pl.CostEstimate(flops=flops, bytes_accessed=moved, transcendentals=0),
     )(*operands)
 
@@ -249,56 +249,55 @@
     return field * row_scale, row_scale
 
 
-def project_kernel(act_ref, wq_ref, wk_ref, wv_ref, out_ref):
-    normed = normalize(act_ref[...])[0].astype(jnp.bfloat16)
-    rows = normed.shape[0]
-    query, key = dot(normed, wq_ref[...]), dot(normed, wk_ref[...])
-    value = dot(normed, wv_ref[...])
-    for pair in range(HEADS // 2):
-        lanes = slice(pair * 2 * HEAD_DIM, (pair + 1) * 2 * HEAD_DIM)
-        q, k, v = query[:, lanes], key[:, lanes], value[:, lanes]
-        q = q * lax.rsqrt(half_sums(q * q) / HEAD_DIM + EPSILON)
-        k = k * lax.rsqrt(half_sums(k * k) / HEAD_DIM + EPSILON)
-        first, last = v[:PACKED], v[rows - PACKED :]
-        low, low_v = low_lanes(q), low_lanes(first)
-        even = (jnp.where(low_v, first, swap(last)), jnp.where(low, q, swap(k)))
-        odd = (jnp.where(low_v, swap(first), last), jnp.where(low, swap(q), k))
-        for head, (upper, lower) in enumerate((even, odd)):
-            out_ref[2 * pair + head, :PACKED, :] = upper.astype(jnp.bfloat16)
-            out_ref[2 * pair + head, PACKED:, :] = lower.astype(jnp.bfloat16)
+def project_kernel(me_ref, *refs):
+    blocks, (wq_ref, wk_ref, wv_ref, normed_ref, back_ref, out_ref) = refs[:-6], refs[-6:]
+    odd = lax.rem(me_ref[0], 2) == 1
+    pair = pl.multiple_of(lax.div(me_ref[0], 2) * 2 * HEAD_DIM, 2 * HEAD_DIM)
+    weights = [ref[:, pl.ds(pair, 2 * HEAD_DIM)] for ref in (wq_ref, wk_ref, wv_ref)]
+    for m, block in enumerate(blocks):
+        normed = normalize(block[...])[0].astype(jnp.bfloat16)
+        q, k, v = [dot(normed, weight) for weight in weights]
+        low = low_lanes(q)
+        raw = jnp.where(low, jnp.where(odd, swap(q), q), jnp.where(odd, k, swap(k)))
+        scale = lax.rsqrt(half_sums(raw * raw) / HEAD_DIM + EPSILON)
+        unit = raw * scale
+        normed_ref[m] = normed
+        back_ref[m, :, : 2 * HEAD_DIM] = unit
+        back_ref[m, :, 2 * HEAD_DIM :] = scale
+        out_ref[m, :, : 2 * HEAD_DIM] = unit.astype(jnp.bfloat16)
+        out_ref[m, :, 2 * HEAD_DIM :] = jnp.where(odd, swap(v), v).astype(jnp.bfloat16)
 
 
 def tiles(tokens):
     size = 256
-    return [
-        (start, min(tokens, start + size), min(tokens, start + 2 * size))
-        for start in range(0, tokens, size)
-    ]
-
-
-def attend_kernel(slab_ref, row_ids, column_ids, prob_ref, qk_ref, v_ref, out_t_ref, out_ref):
-    parts, length, _ = slab_ref.shape
-    rows = length - PACKED
+    return [(start, min(tokens, start + size)) for start in range(0, tokens, size)]
+
+
+def attend_kernel(
+    me_ref, first_ref, last_ref, row_ids, column_ids, prob_ref, qk_ref, v_ref, out_t_ref, out_ref
+):
+    rows = first_ref.shape[1]
+    parts = 2 * first_ref.shape[0]
     tokens = parts * rows
-    slabs = [slab_ref[g].astype(jnp.float32) for g in range(parts)]
-    qk = jnp.concatenate([slab[PACKED:] for slab in slabs], axis=0).astype(jnp.bfloat16)
-    value = jnp.concatenate([unpack(slab[:PACKED], rows) for slab in slabs], axis=0)
-    value = value.astype(jnp.bfloat16)
+    slabs = [ref[m] for ref in (first_ref, last_ref) for m in range(parts // 2)]
+    whole = jnp.concatenate([slab.astype(jnp.float32) for slab in slabs], axis=0)
+    qk = whole[:, : 2 * HEAD_DIM].astype(jnp.bfloat16)
+    value = whole[:, 2 * HEAD_DIM : 3 * HEAD_DIM].astype(jnp.bfloat16)
     qk_ref[...] = qk
     v_ref[...] = value
     query, key = qk[:, :HEAD_DIM] * HEAD_DIM ** (-0.5), qk[:, HEAD_DIM:]
-    for start, stop, seen in tiles(tokens):
-        scores = dot(key[:seen], query[start:stop], ((1,), (1,)))
-        allowed = column_ids[:seen, :] <= row_ids[:, start:stop]
+    for start, stop in tiles(tokens):
+        scores = dot(key, query[start:stop], ((1,), (1,)))
+        allowed = column_ids[...] <= row_ids[:, start:stop]
         numerator = jnp.where(allowed, jnp.exp(scores), 0.0)
         probs = numerator * (1.0 / jnp.sum(numerator, axis=0, keepdims=True))
         probs = probs.astype(jnp.bfloat16)
-        prob_ref[:seen, start:stop] = probs
-        out_t = dot(value[:seen], probs, ((0,), (0,)))
+        prob_ref[:, start:stop] = probs
+        out_t = dot(value, probs, ((0,), (0,)))
         out_t_ref[:, start:stop] = out_t.astype(jnp.bfloat16).astype(jnp.float32)
     out = jnp.transpose(out_t_ref[...])
-    for g in range(parts):
-        out_ref[g] = pack(out[g * rows : (g + 1) * rows]).astype(jnp.bfloat16)
+    for m in range(parts):
+        out_ref[me_ref[0] ^ DISTANCES[m]] = pack(out[m * rows : (m + 1) * rows]).astype(jnp.bfloat16)
 
 
 def affine_kernel(slab_ref, act_ref, inc_ref, w_ref, att_ref, aff_ref, up_ref, out_ref):
@@ -321,49 +320,27 @@
         out_ref[h] = pack(block).astype(jnp.bfloat16)
 
 
+ORDER = ((1, 5, 3, 7), (2, 6), (4,), (0,))
+
+
 def out_term_kernel(me_ref, slab_ref, aff_ref, *out_refs):
-    heads = slab_ref.shape[0]
-    rows, width = aff_ref.shape[0], aff_ref.shape[1] // 2
+    heads, rows = slab_ref.shape[0], aff_ref.shape[0]
     columns = [
         unpack(slab_ref[me_ref[0] ^ m].astype(jnp.float32), rows) for m in range(heads)
     ]
-    for half, order in enumerate(ORDERS):
-        for out_ref, group in zip(out_refs[4 * half : 4 * half + 4], order):
-            left = jnp.concatenate([columns[m] for m in group], axis=1).astype(jnp.bfloat16)
-            right = aff_ref[:, half * width : (half + 1) * width]
-            out_ref[...] = dot(left, right, ((0,), (0,))).astype(jnp.bfloat16)
-
-
-ORDERS = (((1, 3, 5, 7), (2, 6), (4,), (0,)), ((2, 3, 6, 7), (1, 5), (4,), (0,)))
-
-
-def gathered_kernel(me_ref, *refs):
-    blocks, (wq_ref, wk_ref, normed_ref, back_ref) = refs[:HEADS], refs[HEADS:]
+    for out_ref, group in zip(out_refs, ORDER):
+        left = jnp.concatenate([columns[m] for m in group], axis=1).astype(jnp.bfloat16)
+        out_ref[...] = dot(left, aff_ref[...], ((0,), (0,))).astype(jnp.bfloat16)
+
+
+def backward_kernel(
+    me_ref, slab_ref, prob_ref, qk_ref, v_ref, out_t_ref, first_ref, last_ref, out_ref, gk_ref, gv_ref, gq_ref
+):
+    parts, rows = slab_ref.shape[0], first_ref.shape[1]
+    tokens = parts * rows
     me = me_ref[0]
-    odd = lax.rem(me, 2) == 1
-    pair = lax.div(me, 2)
-    weights = [None, None]
-    for i, ref in enumerate((wq_ref, wk_ref)):
-        weights[i] = ref[:, pl.ds(pl.multiple_of(pair * 2 * HEAD_DIM, 2 * HEAD_DIM), 2 * HEAD_DIM)]
-    for m, block in enumerate(blocks):
-        normed = normalize(block[...])[0].astype(jnp.bfloat16)
-        q, k = dot(normed, weights[0]), dot(normed, weights[1])
-        low = low_lanes(q)
-        raw = jnp.where(low, jnp.where(odd, swap(q), q), jnp.where(odd, k, swap(k)))
-        scale = lax.rsqrt(half_sums(raw * raw) / HEAD_DIM + EPSILON)
-        group = me ^ m
-        normed_ref[group] = normed
-        back_ref[group, :, : 2 * HEAD_DIM] = raw * scale
-        back_ref[group, :, 2 * HEAD_DIM :] = scale
-
-
-def backward_kernel(
-    slab_ref, prob_ref, qk_ref, v_ref, out_t_ref, back_ref, out_ref, gk_ref, gv_ref, gq_ref
-):
-    parts, rows = back_ref.shape[:2]
-    tokens = parts * rows
     grad_f = jnp.concatenate(
-        [unpack(slab_ref[g].astype(jnp.float32), rows) for g in range(parts)], axis=0
+        [unpack(slab_ref[me ^ DISTANCES[m]].astype(jnp.float32), rows) for m in range(parts)], axis=0
     )
     grad = grad_f.astype(jnp.bfloat16)
     grad_t = jnp.transpose(grad_f)
@@ -373,30 +350,32 @@
     query, key = qk[:, :HEAD_DIM], qk[:, HEAD_DIM:]
     gk_ref[...] = jnp.zeros_like(gk_ref)
     gv_ref[...] = jnp.zeros_like(gv_ref)
-    for start, stop, seen in tiles(tokens):
-        probs = prob_ref[:seen, start:stop]
-        grad_probs = dot(value[:seen], grad_t[:, start:stop])
+    for start, stop in tiles(tokens):
+        probs = prob_ref[:, start:stop]
+        grad_probs = dot(value, grad_t[:, start:stop])
         scores = probs.astype(jnp.float32) * (grad_probs - correction[:, start:stop])
         scores = scores.astype(jnp.bfloat16)
-        gv_ref[:seen, :] += dot(probs, grad[start:stop])
-        gk_ref[:seen, :] += dot(scores, query[start:stop])
-        gq_ref[:, start:stop] = dot(key[:seen], scores, ((0,), (0,)))
+        gv_ref[...] += dot(probs, grad[start:stop])
+        gk_ref[...] += dot(scores, query[start:stop])
+        gq_ref[:, start:stop] = dot(key, scores, ((0,), (0,)))
     grad_q = jnp.transpose(gq_ref[...])
-    for g in range(parts):
-        own = slice(g * rows, (g + 1) * rows)
+    for m in range(parts):
+        own = slice(m * rows, (m + 1) * rows)
+        back_ref, at = (first_ref, m) if m < parts // 2 else (last_ref, m - parts // 2)
         raw = jnp.concatenate([grad_q[own], gk_ref[own, :]], axis=1) * HEAD_DIM ** (-0.5)
-        unit, scale = back_ref[g, :, : 2 * HEAD_DIM], back_ref[g, :, 2 * HEAD_DIM :]
+        unit, scale = back_ref[at, :, : 2 * HEAD_DIM], back_ref[at, :, 2 * HEAD_DIM :]
         back = scale * (raw - unit * (half_sums(raw * unit) / HEAD_DIM))
-        out_ref[g, :PACKED, :] = pack(gv_ref[own, :]).astype(jnp.bfloat16)
-        out_ref[g, PACKED:, :] = back.astype(jnp.bfloat16)
-
-
-def weights_kernel(slab_ref, normed_ref, out_ref):
-    parts, rows, width = normed_ref.shape
+        out_ref[me ^ DISTANCES[m], :PACKED, :] = pack(gv_ref[own, :]).astype(jnp.bfloat16)
+        out_ref[me ^ DISTANCES[m], PACKED:, :] = back.astype(jnp.bfloat16)
+
+
+def weights_kernel(me_ref, slab_ref, first_ref, last_ref, out_ref):
+    half, rows, width = first_ref.shape
+    parts = 2 * half
     qk_sum = v_sum = 0.0
-    for g in range(parts):
-        slab = slab_ref[g].astype(jnp.float32)
-        normed = normed_ref[g]
+    for m in range(parts):
+        slab = slab_ref[me_ref[0] ^ DISTANCES[m]].astype(jnp.float32)
+        normed = first_ref[m] if m < half else last_ref[m - half]
         qk, v = slab[PACKED:].astype(jnp.bfloat16), unpack(slab[:PACKED], rows)
         qk_sum = qk_sum + dot(qk, normed, ((0,), (0,)))
         v_sum = v_sum + dot(v.astype(jnp.bfloat16), normed, ((0,), (0,)))
@@ -450,23 +429,27 @@
     near_far = partner(far, "seq", 1)
     side_near = partner(near, "seq", 0)
     last = partner(side_far, "seq", 1)
-    return block, side, near, side_near, far, side_far, near_far, last
+    return block, side, near, far, side_near, side_far, near_far, last
+
+
+DISTANCES = (0, 1, 2, 4, 3, 5, 6, 7)
 
 
 def wide(matrix):
     return matrix.astype(jnp.float32)
 
 
-def sum_to_owner(terms, bits):
-    first, second, third, keep = terms
+def low(matrix):
+    return matrix.astype(jnp.bfloat16)
+
+
+def sum_to_owner(first, second, third, keep):
     size = keep.shape[0]
-    got = wide(partner(first, "seq", bits[0]))
-    at = {0: got[:size], 1: got[size : 2 * size], 2: got[2 * size : 3 * size], 3: got[3 * size :]}
-    second = (wide(second) + jnp.concatenate([at[1], at[3]], axis=0)).astype(jnp.bfloat16)
-    third, keep = wide(third) + at[2], wide(keep) + at[0]
-    got = wide(partner(second, "seq", bits[1]))
-    third, keep = (third + got[size:]).astype(jnp.bfloat16), keep + got[:size]
-    return keep + wide(partner(third, "seq", bits[2]))
+    got = partner(first, "seq", 0)
+    more = partner(low(wide(second) + wide(got[2 * size :])), "seq", 1)
+    third = wide(third) + wide(got[size : 2 * size]) + wide(more[size:])
+    keep = wide(keep) + wide(got[:size]) + wide(more[:size])
+    return keep + wide(partner(low(third), "seq", 2))
 
 
 def head_shards(
@@ -485,11 +468,25 @@
     vmem = pl.BlockSpec(memory_space=pltpu.VMEM)
     f32 = jnp.float32
 
-    (slabs,) = call(
-        project_kernel, [shape(HEADS, length, 128)], [field, wq, wk, wv], 6 * rows * width * inner
-    )
-    slabs = exchange(slabs)
     blocks = spread(field)
+    order = me[0] ^ jnp.array(DISTANCES, jnp.int32)
+    ids = jnp.take(block_ids.reshape(parts, rows), order, axis=0).reshape(tokens)
+    half = parts // 2
+    pieces = [
+        call(
+            project_kernel,
+            [
+                shape(half, rows, width),
+                shape(half, rows, 256, dtype=f32),
+                shape(half, rows, 256),
+            ],
+            [me, *group, wq, wk, wv],
+            2 * half * rows * width * 512,
+            specs=[smem] + [vmem] * (half + 3),
+        )
+        for group in (blocks[:half], blocks[half:])
+    ]
+    normed, back, projected = zip(*pieces)
     probs, qk, value, out_t, packed = call(
         attend_kernel,
         [
@@ -499,8 +496,9 @@
             shape(HEAD_DIM, tokens, dtype=f32),
             shape(parts, PACKED, 128),
         ],
-        [slabs, block_ids[None, :], block_ids[:, None]],
+        [me, *projected, ids[None, :], ids[:, None]],
         4 * tokens * tokens * 256,
+        specs=[smem] + [vmem] * 4,
     )
     packed = exchange(packed)
     attended, grad_affine, scaled, grad_slabs = call(
@@ -517,23 +515,17 @@
     grad_slabs = exchange(grad_slabs)
     terms = call(
         out_term_kernel,
-        [shape(len(group) * HEAD_DIM, width) for order in ORDERS for group in order],
+        [shape(len(group) * HEAD_DIM, 2 * width) for group in ORDER],
         [me, packed, grad_affine],
         4 * rows * width * inner,
         specs=[smem, vmem, vmem],
     )
-    normed, back = call(
-        gathered_kernel,
-        [shape(parts, rows, width), shape(parts, rows, 256, dtype=f32)],
-        [me, *blocks, wq, wk],
-        4 * tokens * width * 128,
-        specs=[smem] + [vmem] * (HEADS + 2),
-    )
     (grads,) = call(
         backward_kernel,
         [shape(parts, length, 128)],
-        [grad_slabs, probs, qk, value, out_t, back],
+        [me, grad_slabs, probs, qk, value, out_t, *back],
         8 * tokens * tokens * 256,
+        specs=[smem] + [vmem] * 7,
         scratch=[
             pltpu.VMEM((tokens, HEAD_DIM), f32),
             pltpu.VMEM((tokens, HEAD_DIM), f32),
@@ -544,8 +536,9 @@
     (weight_terms,) = call(
         weights_kernel,
         [shape(parts, 3 * HEAD_DIM, width // parts)],
-        [grads, normed],
+        [me, grads, *normed],
         2 * tokens * width * 256,
+        specs=[smem] + [vmem] * 3,
     )
     weight_terms = exchange(weight_terms)
     (grad_input,) = call(
@@ -560,9 +553,7 @@
         for d in range(parts)
     ]
     moved = lax.ppermute(grad_input, ("section", "seq"), route)
-    grad_out = jnp.concatenate(
-        [sum_to_owner(terms[:4], (0, 1, 2)), sum_to_owner(terms[4:], (1, 0, 2))], axis=1
-    )
+    grad_out = sum_to_owner(*terms)
     grad_q, grad_k, grad_v = call(
         turn_kernel, [shape(1, width // parts, inner, dtype=f32)] * 3, [weight_terms]
     )

time: 148 us -> 150 us (1.014)
  the two profiles are of different devices: /device:TPU:9 before, /device:TPU:5 now
where the time goes in v3:
time: 150 us; the launch traced here: 149 us
  starting transfers between devices  35.1 us (23%)
  blocking collectives  34.7 us (23%)
  waiting for transfers between devices  30.8 us (21%)
  Pallas kernels  23.2 us (15%)
  local copies, waits for them, and re-layouts  18 us (12%)
  other arithmetic  6.03 us (4%)
    all_to_all x2, blocking collectives, exchange(): return lax.all_to_all(slabs, 'seq', split_axis=0, concat_axis=0, tiled=True)  34.7 us
    ppermute x10, waiting for transfers between devices, partner(): return lax.ppermute(block, axis, route)  26.9 us
    pallas_call x10, Pallas kernels, call(): pl.pallas_call(kernel, out_shape=tuple(outs), in_specs=specs or [single]...  23.2 us
    unnamed x56, local copies, waits for them, and re-layouts  15.5 us
    ppermute x1, starting transfers between devices, head_shards(): moved = lax.ppermute(grad_input, ('section', 'seq'), route)  14.7 us
    ppermute x10, starting transfers between devices, partner(): return lax.ppermute(block, axis, route)  12 us
    all_to_all x2, starting transfers between devices, exchange(): return lax.all_to_all(slabs, 'seq', split_axis=0, concat_axis=0, tiled=True)  8.39 us
    convert_element_type x2, other arithmetic, low(): return matrix.astype(jnp.bfloat16)  3.34 us
  transfers between devices with their start and end apart: 13, of which 5 were waited for; matrix products, arithmetic and copies ran while one was open for 4% of the time, Pallas kernels for 9%

profile of v3, /device:TPU:5, one launch (start us, length us, event | category | flops | bytes accessed | tf_op | source)
XLA Modules:
  0.0 148.7 jit_solution(17818552942142164564)
XLA Ops:
  0.6 2.4 %collective-permute-start.2 = (bf16[136,1024]{1,0:T(8,128)(2,1)}, bf16[136,1024]{1,0:T(8,128)(2,1)S(1)}, u32[]{:S(2)}, u32[]{:S(2)}) collective-permute-start(bf16[136,1024]{1,0:T(8,128)(2,1)} %bitcast.19), channel_id=1, source_target_pairs={{0,4},{4,0},{1,5},{5,1},{2,6},{6,2},{3,7},{7,3},{8,12},{12,8},{9,1... | collective-permute-start | bytes 835592 | tf_op jit(solution)/shard_map/ppermute | solution.py:22
  3.0 1.3 collective-permute-start.1
  4.3 1.2 collective-permute-start
  5.5 9.9 %collective-permute-done.2.refs_3_ = bf16[136,1024]{1,0:T(8,128)(2,1)S(1)} collective-permute-done((bf16[136,1024]{1,0:T(8,128)(2,1)}, bf16[136,1024]{1,0:T(8,128)(2,1)S(1)}, u32[]{:S(2)}, u32[]{:S(2)}) %collective-permute-start.2) | collective-permute-done | bytes 278560 | tf_op jit(solution)/shard_map/ppermute | solution.py:22
  15.4 1.2 collective-permute-start.4
  17.2 0.8 reshape.64
  18.6 1.6 %collective-permute-start.5 = (bf16[136,1024]{1,0:T(8,128)(2,1)S(1)}, bf16[136,1024]{1,0:T(8,128)(2,1)}, u32[]{:S(2)}, u32[]{:S(2)}) collective-permute-start(bf16[136,1024]{1,0:T(8,128)(2,1)S(1)} %collective-permute-done.2.refs_3_), channel_id=1, source_target_pairs={{0,2},{2,0},{1,3},{3,1},{4,6},{6,4},{5,7},{7,5},{8,10},{10,8},{9,1... | collective-permute-start | bytes 835592 | tf_op jit(solution)/shard_map/ppermute | solution.py:22
  20.4 1.6 %collective-permute-done.4.refs_1_ = bf16[136,1024]{1,0:T(8,128)(2,1)} collective-permute-done((bf16[136,1024]{1,0:T(8,128)(2,1)S(1)}, bf16[136,1024]{1,0:T(8,128)(2,1)}, u32[]{:S(2)}, u32[]{:S(2)}) %collective-permute-start.4) | collective-permute-done | bytes 278560 | tf_op jit(solution)/shard_map/ppermute | solution.py:22
  22.0 2.7 %collective-permute-start.6 = (bf16[136,1024]{1,0:T(8,128)(2,1)}, bf16[136,1024]{1,0:T(8,128)(2,1)}, u32[]{:S(2)}, u32[]{:S(2)}) collective-permute-start(bf16[136,1024]{1,0:T(8,128)(2,1)} %collective-permute-done.4.refs_1_), channel_id=1, source_target_pairs={{0,2},{2,0},{1,3},{3,1},{4,6},{6,4},{5,7},{7,5},{8,10},{10,8},{9,1... | collective-permute-start | bytes 835592 | tf_op jit(solution)/shard_map/ppermute | solution.py:22
  24.9 1.0 select_n.33.column_ids
  25.9 0.7 copy-done.20
  26.6 1.2 copy-done
  27.8 1.2 copy-done.2
  29.0 1.2 copy-done.4
  30.3 1.0 copy-done.6
  31.2 1.0 copy-done.21
  32.2 2.6 %shard_map.128 = (bf16[4,136,1024]{2,1,0:T(8,128)(2,1)S(1)}, f32[4,136,256]{2,1,0:T(8,128)S(1)}, bf16[4,136,256]{2,1,0:T(8,128)(2,1)S(1)}) custom-call(s32[1]{0:T(128)} %bitcast.1.me_ref, bf16[136,1024]{1,0:T(8,128)(2,1)S(1)} %bitcast.22, bf16[136,1024]{1,0:T(8,128)(2,1)S(1)} %copy-done.21, bf16[136,1024]{1,0:T(8,128)(2,1)} %collective-permute-done.1.refs_2_, ...), custom_call_target="tpu_custom_call" | custom-call | flops 570425344 | bytes 6209540 | tf_op jit(solution)/shard_map/pallas_call | solution.py:202
  34.8 1.0 copy-done.12
  35.9 2.8 %shard_map.129 = (bf16[4,136,1024]{2,1,0:T(8,128)(2,1)S(1)}, f32[4,136,256]{2,1,0:T(8,128)S(1)}, bf16[4,136,256]{2,1,0:T(8,128)(2,1)S(1)}) custom-call(s32[1]{0:T(128)} %bitcast.1.me_ref, bf16[136,1024]{1,0:T(8,128)(2,1)} %collective-permute-done.3.refs_0_, bf16[136,1024]{1,0:T(8,128)(2,1)} %collective-permute-done.4.refs_1_, ...), custom_call_target="tpu_custom_call" | custom-call | flops 570425344 | bytes 6209540 | tf_op jit(solution)/shard_map/pallas_call | solution.py:202
  38.6 1.0 copy-done.14
  39.6 3.3 %shard_map.130 = (bf16[1088,1088]{1,0:T(8,128)(2,1)S(1)}, bf16[1088,128]{1,0:T(8,128)(2,1)S(1)}, bf16[1088,64]{1,0:T(8,128)(2,1)S(1)}, f32[64,1088]{1,0:T(8,128)S(1)}, bf16[8,80,128]{2,1,0:T(8,128)(2,1)S(1)}) custom-call(s32[1]{0:T(128)} %bitcast.1.me_ref, bf16[4,136,256]{2,1,0:T(8,128)(2,1)S(1)} %get-tuple-element.26.first_ref, ...), custom_call_target="tpu_custom_call" | custom-call | flops 1212153856 | bytes 3793412 | tf_op jit(solution)/shard_map/pallas_call | solution.py:202
  42.9 11.7 %all_to_all.20.slab_ref = bf16[8,80,128]{2,1,0:T(8,128)(2,1)S(1)} all-to-all(bf16[8,80,128]{2,1,0:T(8,128)(2,1)S(1)} %get-tuple-element.28), channel_id=1, replica_groups=mesh['section'=4,'seq'=8] {'seq'}, dimensions={0} | all-to-all | bytes 327680 | tf_op jit(solution)/shard_map/all_to_all | solution.py:423
  54.6 1.9 %shard_map.131 = (bf16[136,512]{1,0:T(8,128)(2,1)}, bf16[136,2048]{1,0:T(8,128)(2,1)S(1)}, f32[136,1024]{1,0:T(8,128)S(1)}, bf16[8,80,128]{2,1,0:T(8,128)(2,1)S(1)}) custom-call(bf16[8,80,128]{2,1,0:T(8,128)(2,1)S(1)} %all_to_all.20.slab_ref, bf16[136,1024]{1,0:T(8,128)(2,1)S(1)} %bitcast.23, bf16[136,1024]{1,0:T(8,128)(2,1)S(1)} %bitcast.26, ...), custom_call_target="tpu_custom_call" | custom-call | flops 570425344 | bytes 4235264 | tf_op jit(solution)/shard_map/pallas_call | solution.py:202
  56.5 0.8 copy-done.16
  57.3 1.6 %shard_map.137 = (bf16[256,2048]{1,0:T(8,128)(2,1)}, bf16[128,2048]{1,0:T(8,128)(2,1)S(1)}, bf16[64,2048]{1,0:T(8,128)(2,1)S(1)}, bf16[64,2048]{1,0:T(8,128)(2,1)S(1)}) custom-call(s32[1]{0:T(128)} %bitcast.1.me_ref, bf16[8,80,128]{2,1,0:T(8,128)(2,1)S(1)} %all_to_all.20.slab_ref, bf16[136,2048]{1,0:T(8,128)(2,1)S(1)} %get-tuple-element.42.aff_ref), custom_call_target="tpu_custom_call" | custom-call | flops 285212672 | bytes 2818052 | tf_op jit(solution)/shard_map/pallas_call | solution.py:202
  58.9 0.8 copy-done.19
  59.7 0.7 copy-done.25
  60.4 23.1 %all_to_all.21.slab_ref = bf16[8,80,128]{2,1,0:T(8,128)(2,1)S(1)} all-to-all(bf16[8,80,128]{2,1,0:T(8,128)(2,1)S(1)} %get-tuple-element.29), channel_id=1, replica_groups=mesh['section'=4,'seq'=8] {'seq'}, dimensions={0} | all-to-all | bytes 327680 | tf_op jit(solution)/shard_map/all_to_all | solution.py:423
  83.5 3.9 %shard_map.132.slab_ref = bf16[8,216,128]{2,1,0:T(8,128)(2,1)S(1)} custom-call(s32[1]{0:T(128)} %bitcast.1.me_ref, bf16[8,80,128]{2,1,0:T(8,128)(2,1)S(1)} %all_to_all.21.slab_ref, bf16[1088,1088]{1,0:T(8,128)(2,1)S(1)} %get-tuple-element.30.prob_ref, bf16[1088,128]{1,0:T(8,128)(2,1)S(1)} %get-tuple-element.31.qk_ref, ...), custom_call_target="tpu_custom_call" | custom-call | flops 2424307712 | bytes 4784132 | tf_op jit(solution)/shard_map/pallas_call | solution.py:202
  87.4 0.8 copy-done.9
  88.2 4.3 %all-to-all-start.2 = ((bf16[8,216,128]{2,1,0:T(8,128)(2,1)}), bf16[8,216,128]{2,1,0:T(8,128)(2,1)}, u32[]{:S(2)}, u32[]{:S(2)}) async-start(bf16[8,216,128]{2,1,0:T(8,128)(2,1)} %copy-done.9), calls=%async_computation.2 | async-start | bytes 884736 | tf_op jit(solution)/shard_map/all_to_all | solution.py:423
  92.5 2.2 %add_convert_fusion = bf16[128,2048]{1,0:T(8,128)(2,1)} fusion(bf16[128,2048]{1,0:T(8,128)(2,1)} %copy-done.19, bf16[256,2048]{1,0:T(8,128)(2,1)} %collective-permute-done.8), kind=kLoop, calls=%fused_computation.1 | loop fusion | flops 1048576 | bytes 1572864 | tf_op jit(solution)/shard_map/convert_element_type | solution.py:443
  94.7 1.3 collective-permute-start.9
  96.1 1.0 copy-done.10
  97.1 1.2 copy-done.15
  98.3 1.1 shard_map.135
  99.4 0.7 copy-done.11
  100.2 0.8 all-to-all-done.2.slab_ref
  101.0 4.1 %all-to-all-start.3 = ((bf16[8,192,128]{2,1,0:T(8,128)(2,1)}), bf16[8,192,128]{2,1,0:T(8,128)(2,1)}, u32[]{:S(2)}, u32[]{:S(2)}) async-start(bf16[8,192,128]{2,1,0:T(8,128)(2,1)} %copy-done.11), calls=%async_computation.3 | async-start | bytes 786432 | tf_op jit(solution)/shard_map/all_to_all | solution.py:423
  105.1 1.0 copy-done.17
  106.2 3.1 %shard_map.133 = bf16[136,1024]{1,0:T(8,128)(2,1)} custom-call(bf16[8,216,128]{2,1,0:T(8,128)(2,1)} %all-to-all-done.2.slab_ref, bf16[1024,512]{1,0:T(8,128)(2,1)S(1)} %bitcast.12, bf16[1024,512]{1,0:T(8,128)(2,1)S(1)} %bitcast.15, bf16[1024,512]{1,0:T(8,128)(2,1)S(1)} %bitcast.18, bf16[136,1024]{1,0:T(8,128)(2,1)S(1)} %bitcast.24, f32[136,1024]{1,0:T(8,128)S(1)} %copy-done.17), custom_call_target="tpu_custom_call" | custom-call | flops 427819008 | bytes 4702208 | tf_op jit(solution)/shard_map/pallas_call | solution.py:202
  109.2 14.7 %collective-permute-start.7 = (bf16[136,1024]{1,0:T(8,128)(2,1)}, bf16[136,1024]{1,0:T(8,128)(2,1)S(1)}, u32[]{:S(2)}, u32[]{:S(2)}) collective-permute-start(bf16[136,1024]{1,0:T(8,128)(2,1)} %shard_map.133), channel_id=1, source_target_pairs={{8,7},{9,6},{10,5},{11,4},{12,3},{13,2},{14,1},{15,0},{16,15},{17,... | collective-permute-start | bytes 835592 | tf_op jit(solution)/shard_map/ppermute | solution.py:555
  124.0 1.1 add_convert_fusion.1
  125.3 2.0 %shard_map.136 = (f32[1,128,512]{2,1,0:T(8,128)}, f32[1,128,512]{2,1,0:T(8,128)}, f32[1,128,512]{2,1,0:T(8,128)}) custom-call(bf16[8,192,128]{2,1,0:T(8,128)(2,1)} %all-to-all-done.3.slab_ref), custom_call_target="tpu_custom_call" | custom-call | bytes 1179648 | tf_op jit(solution)/shard_map/pallas_call | solution.py:202
  127.3 3.1 %collective-permute-done.7.rows_ref = bf16[136,1024]{1,0:T(8,128)(2,1)S(1)} collective-permute-done((bf16[136,1024]{1,0:T(8,128)(2,1)}, bf16[136,1024]{1,0:T(8,128)(2,1)S(1)}, u32[]{:S(2)}, u32[]{:S(2)}) %collective-permute-start.7) | collective-permute-done | bytes 278560 | tf_op jit(solution)/shard_map/ppermute | solution.py:555
  130.4 1.0 shard_map.134
  131.4 15.4 %collective-permute-done.10 = bf16[64,2048]{1,0:T(8,128)(2,1)S(1)} collective-permute-done((bf16[64,2048]{1,0:T(8,128)(2,1)S(1)}, bf16[64,2048]{1,0:T(8,128)(2,1)S(1)}, u32[]{:S(2)}, u32[]{:S(2)}) %collective-permute-start.10) | collective-permute-done | bytes 262176 | tf_op jit(solution)/shard_map/ppermute | solution.py:22
  146.8 1.9 %add_bitcast_fusion = f32[1,64,2048]{2,1,0:T(8,128)} fusion(bf16[64,2048]{1,0:T(8,128)(2,1)S(1)} %collective-permute-done.10, bf16[64,2048]{1,0:T(8,128)(2,1)S(1)} %copy-done.24, bf16[128,2048]{1,0:T(8,128)(2,1)} %collective-permute-done.9, bf16[256,2048]{1,0:T(8,128)(2,1)} %collective-permute-done.8), kind=kLoop, calls=%fused_computation.2 | loop fusion | flops 917504 | bytes 1572864 | tf_op jit(solution)/shard_map/broadcast_in_dim | solution.py:563
  (57 shorter events, 1.9 us)
Async XLA Ops:
  0.6 14.7 %collective-permute-start.2 = (bf16[136,1024]{1,0:T(8,128)(2,1)}, bf16[136,1024]{1,0:T(8,128)(2,1)S(1)}, u32[]{:S(2)}, u32[]{:S(2)}) collective-permute-start(bf16[136,1024]{1,0:T(8,128)(2,1)} %bitcast.19), channel_id=1, source_target_pairs={{0,4},{4,0},{1,5},{5,1},{2,6},{6,2},{3,7},{7,3},{8,12},{12,8},{9,1... | collective-permute-start | bytes 835592 | tf_op jit(solution)/shard_map/ppermute | solution.py:22
  3.0 17.1 %collective-permute-start.1 = (bf16[136,1024]{1,0:T(8,128)(2,1)}, bf16[136,1024]{1,0:T(8,128)(2,1)}, u32[]{:S(2)}, u32[]{:S(2)}) collective-permute-start(bf16[136,1024]{1,0:T(8,128)(2,1)} %bitcast.20), channel_id=1, source_target_pairs={{0,2},{2,0},{1,3},{3,1},{4,6},{6,4},{5,7},{7,5},{8,10},{10,8},{9,1... | collective-permute-start | bytes 835592 | tf_op jit(solution)/shard_map/ppermute | solution.py:22
  4.3 21.6 %collective-permute-start = (bf16[136,1024]{1,0:T(8,128)(2,1)}, bf16[136,1024]{1,0:T(8,128)(2,1)S(1)}, u32[]{:S(2)}, u32[]{:S(2)}) collective-permute-start(bf16[136,1024]{1,0:T(8,128)(2,1)} %bitcast.21), channel_id=1, source_target_pairs={{0,1},{1,0},{2,3},{3,2},{4,5},{5,4},{6,7},{7,6},{8,9},{9,8},{10,11... | collective-permute-start | bytes 835592 | tf_op jit(solution)/shard_map/ppermute | solution.py:22
  15.4 6.7 %collective-permute-start.4 = (bf16[136,1024]{1,0:T(8,128)(2,1)S(1)}, bf16[136,1024]{1,0:T(8,128)(2,1)}, u32[]{:S(2)}, u32[]{:S(2)}) collective-permute-start(bf16[136,1024]{1,0:T(8,128)(2,1)S(1)} %collective-permute-done.2.refs_3_), channel_id=1, source_target_pairs={{0,1},{1,0},{2,3},{3,2},{4,5},{5,4},{6,7},{7,6},{8,9},{9,8},{10,11... | collective-permute-start | bytes 835592 | tf_op jit(solution)/shard_map/ppermute | solution.py:22
  18.6 17.2 %collective-permute-start.5 = (bf16[136,1024]{1,0:T(8,128)(2,1)S(1)}, bf16[136,1024]{1,0:T(8,128)(2,1)}, u32[]{:S(2)}, u32[]{:S(2)}) collective-permute-start(bf16[136,1024]{1,0:T(8,128)(2,1)S(1)} %collective-permute-done.2.refs_3_), channel_id=1, source_target_pairs={{0,2},{2,0},{1,3},{3,1},{4,6},{6,4},{5,7},{7,5},{8,10},{10,8},{9,1... | collective-permute-start | bytes 835592 | tf_op jit(solution)/shard_map/ppermute | solution.py:22
  20.2 15.7 %collective-permute-start.3 = (bf16[136,1024]{1,0:T(8,128)(2,1)}, bf16[136,1024]{1,0:T(8,128)(2,1)}, u32[]{:S(2)}, u32[]{:S(2)}) collective-permute-start(bf16[136,1024]{1,0:T(8,128)(2,1)} %collective-permute-done.1.refs_2_), channel_id=1, source_target_pairs={{0,1},{1,0},{2,3},{3,2},{4,5},{5,4},{6,7},{7,6},{8,9},{9,8},{10,11... | collective-permute-start | bytes 835592 | tf_op jit(solution)/shard_map/ppermute | solution.py:22
  22.0 13.8 %collective-permute-start.6 = (bf16[136,1024]{1,0:T(8,128)(2,1)}, bf16[136,1024]{1,0:T(8,128)(2,1)}, u32[]{:S(2)}, u32[]{:S(2)}) collective-permute-start(bf16[136,1024]{1,0:T(8,128)(2,1)} %collective-permute-done.4.refs_1_), channel_id=1, source_target_pairs={{0,2},{2,0},{1,3},{3,1},{4,6},{6,4},{5,7},{7,5},{8,10},{10,8},{9,1... | collective-permute-start | bytes 835592 | tf_op jit(solution)/shard_map/ppermute | solution.py:22
  25.9 0.7 copy-start.20
  26.6 1.2 copy-start
  27.8 1.2 copy-start.2
  29.0 1.2 copy-start.4
  30.3 1.0 copy-start.6
  31.2 1.0 copy-start.21
  32.2 3.7 %copy-start.1 = (bf16[1,1024,512]{2,1,0:T(8,128)(2,1)S(1)}, bf16[1,1024,512]{2,1,0:T(8,128)(2,1)}, u32[]{:S(2)}) copy-start(bf16[1,1024,512]{2,1,0:T(8,128)(2,1)} %param.11) | copy-start | bytes 3145732
  32.2 3.7 %copy-start.3 = (bf16[1,1024,512]{2,1,0:T(8,128)(2,1)S(1)}, bf16[1,1024,512]{2,1,0:T(8,128)(2,1)}, u32[]{:S(2)}) copy-start(bf16[1,1024,512]{2,1,0:T(8,128)(2,1)} %param.12) | copy-start | bytes 3145732
  32.2 3.7 %copy-start.5 = (bf16[1,1024,512]{2,1,0:T(8,128)(2,1)S(1)}, bf16[1,1024,512]{2,1,0:T(8,128)(2,1)}, u32[]{:S(2)}) copy-start(bf16[1,1024,512]{2,1,0:T(8,128)(2,1)} %param.13) | copy-start | bytes 3145732
  34.8 1.0 copy-start.12
  35.8 3.8 %copy-start.18 = (s32[1088,1]{1,0:T(8,128)S(1)}, s32[1088,1]{1,0:T(8,128)}, u32[]{:S(2)}) copy-start(s32[1088,1]{1,0:T(8,128)} %select_n.33.column_ids) | copy-start | bytes 13060
  38.6 1.0 copy-start.14
  39.6 15.0 %copy-start.7 = (bf16[1,136,1024]{2,1,0:T(8,128)(2,1)S(1)}, bf16[1,136,1024]{2,1,0:T(8,128)(2,1)}, u32[]{:S(2)}) copy-start(bf16[1,136,1024]{2,1,0:T(8,128)(2,1)} %param.9) | copy-start | bytes 835588
  39.6 15.0 %copy-start.8 = (bf16[1,512,2048]{2,1,0:T(8,128)(2,1)S(1)}, bf16[1,512,2048]{2,1,0:T(8,128)(2,1)}, u32[]{:S(2)}) copy-start(bf16[1,512,2048]{2,1,0:T(8,128)(2,1)} %param.14) | copy-start | bytes 6291460
  39.6 15.0 %copy-start.22 = (bf16[1,136,1024]{2,1,0:T(8,128)(2,1)S(1)}, bf16[1,136,1024]{2,1,0:T(8,128)(2,1)}, u32[]{:S(2)}) copy-start(bf16[1,136,1024]{2,1,0:T(8,128)(2,1)} %param.10) | copy-start | bytes 835588
  56.5 0.8 copy-start.16
  58.9 0.8 copy-start.19
  59.7 0.7 copy-start.25
  60.4 23.1 %copy-start.23 = (bf16[64,2048]{1,0:T(8,128)(2,1)}, bf16[64,2048]{1,0:T(8,128)(2,1)S(1)}, u32[]{:S(2)}) copy-start(bf16[64,2048]{1,0:T(8,128)(2,1)S(1)} %get-tuple-element.43) | copy-start | bytes 786436
  60.4 32.1 %collective-permute-start.8 = (bf16[256,2048]{1,0:T(8,128)(2,1)}, bf16[256,2048]{1,0:T(8,128)(2,1)}, u32[]{:S(2)}, u32[]{:S(2)}) collective-permute-start(bf16[256,2048]{1,0:T(8,128)(2,1)} %get-tuple-element.44), channel_id=1, source_target_pairs={{0,1},{1,0},{2,3},{3,2},{4,5},{5,4},{6,7},{7,6},{8,9},{9,8},{10,11... | collective-permute-start | bytes 3145736 | tf_op jit(solution)/shard_map/ppermute | solution.py:22
  87.4 0.8 copy-start.9
  88.2 12.8 %all-to-all-start.2 = ((bf16[8,216,128]{2,1,0:T(8,128)(2,1)}), bf16[8,216,128]{2,1,0:T(8,128)(2,1)}, u32[]{:S(2)}, u32[]{:S(2)}) async-start(bf16[8,216,128]{2,1,0:T(8,128)(2,1)} %copy-done.9), calls=%async_computation.2 | async-start | bytes 884736 | tf_op jit(solution)/shard_map/all_to_all | solution.py:423
  92.5 3.6 %copy-start.13 = (bf16[4,136,1024]{2,1,0:T(8,128)(2,1)S(1)}, bf16[4,136,1024]{2,1,0:T(8,128)(2,1)}, u32[]{:S(2)}) copy-start(bf16[4,136,1024]{2,1,0:T(8,128)(2,1)} %copy-done.12) | copy-start | bytes 3342340
  94.7 29.2 %collective-permute-start.9 = (bf16[128,2048]{1,0:T(8,128)(2,1)}, bf16[128,2048]{1,0:T(8,128)(2,1)}, u32[]{:S(2)}, u32[]{:S(2)}) collective-permute-start(bf16[128,2048]{1,0:T(8,128)(2,1)} %add_convert_fusion), channel_id=1, source_target_pairs={{0,2},{2,0},{1,3},{3,1},{4,6},{6,4},{5,7},{7,5},{8,10},{10,8},{9,1... | collective-permute-start | bytes 1572872 | tf_op jit(solution)/shard_map/ppermute | solution.py:22
  96.1 1.0 copy-start.10
  97.1 1.2 copy-start.15
  99.4 0.7 copy-start.11
  101.0 24.3 %all-to-all-start.3 = ((bf16[8,192,128]{2,1,0:T(8,128)(2,1)}), bf16[8,192,128]{2,1,0:T(8,128)(2,1)}, u32[]{:S(2)}, u32[]{:S(2)}) async-start(bf16[8,192,128]{2,1,0:T(8,128)(2,1)} %copy-done.11), calls=%async_computation.3 | async-start | bytes 786432 | tf_op jit(solution)/shard_map/all_to_all | solution.py:423
  105.1 1.1 copy-start.17
  106.2 17.8 %copy-start.26 = (bf16[64,2048]{1,0:T(8,128)(2,1)S(1)}, bf16[64,2048]{1,0:T(8,128)(2,1)}, u32[]{:S(2)}) copy-start(bf16[64,2048]{1,0:T(8,128)(2,1)} %copy-done.25) | copy-start | bytes 786436
  106.2 19.0 %copy-start.27 = (s32[1,136]{1,0:T(1,128)S(1)}, s32[1,136]{1,0:T(1,128)}, u32[]{:S(2)}) copy-start(s32[1,136]{1,0:T(1,128)} %param.16) | copy-start | bytes 1636
  109.2 37.5 %copy-start.24 = (bf16[64,2048]{1,0:T(8,128)(2,1)S(1)}, bf16[64,2048]{1,0:T(8,128)(2,1)}, u32[]{:S(2)}) copy-start(bf16[64,2048]{1,0:T(8,128)(2,1)} %copy-done.23) | copy-start | bytes 786436
  109.2 21.2 %collective-permute-start.7 = (bf16[136,1024]{1,0:T(8,128)(2,1)}, bf16[136,1024]{1,0:T(8,128)(2,1)S(1)}, u32[]{:S(2)}, u32[]{:S(2)}) collective-permute-start(bf16[136,1024]{1,0:T(8,128)(2,1)} %shard_map.133), channel_id=1, source_target_pairs={{8,7},{9,6},{10,5},{11,4},{12,3},{13,2},{14,1},{15,0},{16,15},{17,... | collective-permute-start | bytes 835592 | tf_op jit(solution)/shard_map/ppermute | solution.py:555
  125.1 21.6 %collective-permute-start.10 = (bf16[64,2048]{1,0:T(8,128)(2,1)S(1)}, bf16[64,2048]{1,0:T(8,128)(2,1)S(1)}, u32[]{:S(2)}, u32[]{:S(2)}) collective-permute-start(bf16[64,2048]{1,0:T(8,128)(2,1)S(1)} %add_convert_fusion.1), channel_id=1, source_target_pairs={{0,4},{4,0},{1,5},{5,1},{2,6},{6,2},{3,7},{7,3},{8,12},{12,8},{9,1... | collective-permute-start | bytes 786440 | tf_op jit(solution)/shard_map/ppermute | solution.py:22

commit v4 on v3

--- a/solution.py
+++ b/solution.py
@@ -194,24 +194,86 @@
 PACKED = 80
 
 
-def call(kernel, outs, operands, flops=0, specs=None, scratch=()):
-    moved = sum(x.size * x.dtype.itemsize for x in operands) + sum(
-        x.size * x.dtype.itemsize for x in outs
-    )
-    single = pl.BlockSpec(memory_space=pltpu.VMEM)
+class Fetched:
+    def __init__(self, source, ref, semaphore):
+        self.ref, self.shape, self.waiting = ref, ref.shape, True
+        self.copy = pltpu.make_async_copy(source, ref, semaphore)
+        self.copy.start()
+
+    def __getitem__(self, index):
+        if self.waiting:
+            self.copy.wait()
+            self.waiting = False
+        return self.ref[index]
+
+
+class Staged:
+    def __init__(self, target, ref, semaphores):
+        self.target, self.ref, self.semaphores = target, ref, semaphores
+        self.shape, self.copies = ref.shape, []
+
+    def __getitem__(self, index):
+        return self.ref[index]
+
+    def __setitem__(self, index, value):
+        self.ref[index] = value
+
+    def leave(self, index):
+        semaphore = self.semaphores.at[len(self.copies)]
+        copy = pltpu.make_async_copy(self.ref.at[index], self.target.at[index], semaphore)
+        copy.start()
+        self.copies.append(copy)
+
+
+def call(kernel, ins, outs, flops=0, scratch=()):
+    in_places, operands = zip(*ins)
+    out_places, results = zip(*outs)
+    spaces = {"s": pltpu.SMEM, "v": pltpu.VMEM, "h": pltpu.HBM, "r": pltpu.HBM}
+    staged = [x for place, x in zip(in_places + out_places, operands + results) if place == "h"]
+    count = in_places.count("h")
+
+    def body(*refs):
+        refs = list(refs)
+        n_in, n_out = len(operands), len(results)
+        arrays, rest = refs[: n_in + n_out], refs[n_in + n_out :]
+        buffers, (in_sems, out_sems), rest = (
+            rest[: len(staged)],
+            rest[len(staged) : len(staged) + 2],
+            rest[len(staged) + 2 :],
+        )
+        late, slot = [], 0
+        for i, place in enumerate(in_places + out_places):
+            if place != "h":
+                continue
+            if i < n_in:
+                arrays[i] = Fetched(arrays[i], buffers[slot], in_sems.at[slot])
+            else:
+                arrays[i] = Staged(arrays[i], buffers[slot], out_sems.at[slot - count])
+            late.append(arrays[i])
+            slot += 1
+        kernel(*arrays, *rest)
+        for item in late[count:]:
+            if not item.copies:
+                item.leave(slice(None))
+        for item in late[count:]:
+            for copy in item.copies:
+                copy.wait()
+
+    moved = sum(x.size * x.dtype.itemsize for x in operands + results)
     return pl.pallas_call(
-        kernel,
-        out_shape=tuple(outs),
-        in_specs=specs or [single] * len(operands),
-        out_specs=tuple([single] * len(outs)),
-        scratch_shapes=list(scratch),
-        compiler_params=pltpu.CompilerParams(vmem_limit_bytes=14 * 2**20),
+        body,
+        out_shape=results,
+        in_specs=[pl.BlockSpec(memory_space=spaces[place]) for place in in_places],
+        out_specs=tuple(pl.BlockSpec(memory_space=spaces[place]) for place in out_places),
+        scratch_shapes=[pltpu.VMEM(x.shape, x.dtype) for x in staged]
+        + [
+            pltpu.SemaphoreType.DMA((max(1, count),)),
+            pltpu.SemaphoreType.DMA((max(1, len(staged) - count), HEADS)),
+        ]
+        + list(scratch),
+        compiler_params=pltpu.CompilerParams(vmem_limit_bytes=58 * 2**20),
         cost_estimate=pl.CostEstimate(flops=flops, bytes_accessed=moved, transcendentals=0),
     )(*operands)
-
-
-def shape(*dims, dtype=jnp.bfloat16):
-    return jax.ShapeDtypeStruct(dims, dtype)
 
 
 def dot(left, right, contract=((1,), (0,))):
@@ -250,95 +312,119 @@
 
 
 def project_kernel(me_ref, *refs):
-    blocks, (wq_ref, wk_ref, wv_ref, normed_ref, back_ref, out_ref) = refs[:-6], refs[-6:]
+    count = len(refs) - 10
+    blocks, weight_refs = refs[:count], refs[count : count + 3]
+    normed_ref, back_ref, out_ref, *held, semaphores = refs[count + 3 :]
     odd = lax.rem(me_ref[0], 2) == 1
     pair = pl.multiple_of(lax.div(me_ref[0], 2) * 2 * HEAD_DIM, 2 * HEAD_DIM)
-    weights = [ref[:, pl.ds(pair, 2 * HEAD_DIM)] for ref in (wq_ref, wk_ref, wv_ref)]
+    copies = [
+        pltpu.make_async_copy(ref.at[:, pl.ds(pair, 2 * HEAD_DIM)], kept, semaphores.at[i])
+        for i, (ref, kept) in enumerate(zip(weight_refs, held))
+    ]
+    for copy in copies:
+        copy.start()
+    for copy in copies:
+        copy.wait()
+    weights = [kept[...] for kept in held]
     for m, block in enumerate(blocks):
         normed = normalize(block[...])[0].astype(jnp.bfloat16)
+        normed_ref[m] = normed
+        normed_ref.leave(m)
         q, k, v = [dot(normed, weight) for weight in weights]
         low = low_lanes(q)
         raw = jnp.where(low, jnp.where(odd, swap(q), q), jnp.where(odd, k, swap(k)))
         scale = lax.rsqrt(half_sums(raw * raw) / HEAD_DIM + EPSILON)
         unit = raw * scale
-        normed_ref[m] = normed
         back_ref[m, :, : 2 * HEAD_DIM] = unit
         back_ref[m, :, 2 * HEAD_DIM :] = scale
+        back_ref.leave(m)
         out_ref[m, :, : 2 * HEAD_DIM] = unit.astype(jnp.bfloat16)
         out_ref[m, :, 2 * HEAD_DIM :] = jnp.where(odd, swap(v), v).astype(jnp.bfloat16)
 
 
+TILE = 256
+
+
 def tiles(tokens):
-    size = 256
-    return [(start, min(tokens, start + size)) for start in range(0, tokens, size)]
+    starts = range(0, tokens, TILE)
+    return [(i, start, min(tokens, start + TILE)) for i, start in enumerate(starts)]
 
 
 def attend_kernel(
     me_ref, first_ref, last_ref, row_ids, column_ids, prob_ref, qk_ref, v_ref, out_t_ref, out_ref
 ):
     rows = first_ref.shape[1]
-    parts = 2 * first_ref.shape[0]
+    parts = first_ref.shape[0] + last_ref.shape[0]
     tokens = parts * rows
-    slabs = [ref[m] for ref in (first_ref, last_ref) for m in range(parts // 2)]
+    slabs = [ref[m] for ref in (first_ref, last_ref) for m in range(ref.shape[0])]
     whole = jnp.concatenate([slab.astype(jnp.float32) for slab in slabs], axis=0)
     qk = whole[:, : 2 * HEAD_DIM].astype(jnp.bfloat16)
     value = whole[:, 2 * HEAD_DIM : 3 * HEAD_DIM].astype(jnp.bfloat16)
     qk_ref[...] = qk
     v_ref[...] = value
+    qk_ref.leave(slice(None))
+    v_ref.leave(slice(None))
     query, key = qk[:, :HEAD_DIM] * HEAD_DIM ** (-0.5), qk[:, HEAD_DIM:]
-    for start, stop in tiles(tokens):
+    for i, start, stop in tiles(tokens):
         scores = dot(key, query[start:stop], ((1,), (1,)))
         allowed = column_ids[...] <= row_ids[:, start:stop]
         numerator = jnp.where(allowed, jnp.exp(scores), 0.0)
         probs = numerator * (1.0 / jnp.sum(numerator, axis=0, keepdims=True))
         probs = probs.astype(jnp.bfloat16)
-        prob_ref[:, start:stop] = probs
+        prob_ref[i, :, : stop - start] = probs
+        prob_ref.leave(i)
         out_t = dot(value, probs, ((0,), (0,)))
         out_t_ref[:, start:stop] = out_t.astype(jnp.bfloat16).astype(jnp.float32)
     out = jnp.transpose(out_t_ref[...])
     for m in range(parts):
-        out_ref[me_ref[0] ^ DISTANCES[m]] = pack(out[m * rows : (m + 1) * rows]).astype(jnp.bfloat16)
-
-
-def affine_kernel(slab_ref, act_ref, inc_ref, w_ref, att_ref, aff_ref, up_ref, out_ref):
+        group = me_ref[0] ^ DISTANCES[m]
+        out_ref[group] = pack(out[m * rows : (m + 1) * rows]).astype(jnp.bfloat16)
+
+
+def affine_kernel(slab_ref, act_ref, inc_ref, w_ref, aff_ref, up_ref, out_ref):
     heads = slab_ref.shape[0]
     rows, width = act_ref.shape
     attended = jnp.concatenate(
         [unpack(slab_ref[h].astype(jnp.float32), rows) for h in range(heads)], axis=1
     ).astype(jnp.bfloat16)
-    att_ref[...] = attended
     factor = jnp.exp(-dot(attended, w_ref[:, width:]))
     scaled = inc_ref[...].astype(jnp.float32) * factor
     up_ref[...] = scaled
+    up_ref.leave(slice(None))
     shift_part = dot(attended, w_ref[:, :width])
-    aff_ref[:, :width] = (-scaled).astype(jnp.bfloat16)
     latent_part = scaled * (act_ref[...].astype(jnp.float32) - shift_part)
-    aff_ref[:, width:] = (1.0 - latent_part).astype(jnp.bfloat16)
-    grad = dot(aff_ref[...], w_ref[...], ((1,), (1,)))
+    grad_affine = jnp.concatenate([-scaled, 1.0 - latent_part], axis=1).astype(jnp.bfloat16)
+    aff_ref[...] = grad_affine
+    grad = dot(grad_affine, w_ref[...], ((1,), (1,)))
     for h in range(heads):
         block = grad[:, h * HEAD_DIM : (h + 1) * HEAD_DIM]
         out_ref[h] = pack(block).astype(jnp.bfloat16)
 
 
-ORDER = ((1, 5, 3, 7), (2, 6), (4,), (0,))
+ORDERS = (((1, 5, 3, 7), (2, 6), (4,), (0,)), ((2, 6, 3, 7), (1, 5), (4,), (0,)))
 
 
 def out_term_kernel(me_ref, slab_ref, aff_ref, *out_refs):
     heads, rows = slab_ref.shape[0], aff_ref.shape[0]
+    width = aff_ref.shape[1] // 2
     columns = [
         unpack(slab_ref[me_ref[0] ^ m].astype(jnp.float32), rows) for m in range(heads)
     ]
-    for out_ref, group in zip(out_refs, ORDER):
-        left = jnp.concatenate([columns[m] for m in group], axis=1).astype(jnp.bfloat16)
-        out_ref[...] = dot(left, aff_ref[...], ((0,), (0,))).astype(jnp.bfloat16)
+    for half, order in enumerate(ORDERS):
+        right = aff_ref[:, half * width : (half + 1) * width]
+        for out_ref, group in zip(out_refs[4 * half : 4 * half + 4], order):
+            left = jnp.concatenate([columns[m] for m in group], axis=1).astype(jnp.bfloat16)
+            out_ref[...] = dot(left, right, ((0,), (0,))).astype(jnp.bfloat16)
+            out_ref.leave(slice(None))
 
 
 def backward_kernel(
-    me_ref, slab_ref, prob_ref, qk_ref, v_ref, out_t_ref, first_ref, last_ref, out_ref, gk_ref, gv_ref, gq_ref
+    me_ref, slab_ref, prob_ref, qk_ref, v_ref, out_t_ref, first_ref, last_ref, out_ref, *sums
 ):
-    parts, rows = slab_ref.shape[0], first_ref.shape[1]
+    parts, (early, rows) = slab_ref.shape[0], first_ref.shape[:2]
     tokens = parts * rows
     me = me_ref[0]
+    gk_ref, gv_ref, gq_ref = sums
     grad_f = jnp.concatenate(
         [unpack(slab_ref[me ^ DISTANCES[m]].astype(jnp.float32), rows) for m in range(parts)], axis=0
     )
@@ -350,8 +436,8 @@
     query, key = qk[:, :HEAD_DIM], qk[:, HEAD_DIM:]
     gk_ref[...] = jnp.zeros_like(gk_ref)
     gv_ref[...] = jnp.zeros_like(gv_ref)
-    for start, stop in tiles(tokens):
-        probs = prob_ref[:, start:stop]
+    for i, start, stop in tiles(tokens):
+        probs = prob_ref[i, :, : stop - start]
         grad_probs = dot(value, grad_t[:, start:stop])
         scores = probs.astype(jnp.float32) * (grad_probs - correction[:, start:stop])
         scores = scores.astype(jnp.bfloat16)
@@ -361,21 +447,22 @@
     grad_q = jnp.transpose(gq_ref[...])
     for m in range(parts):
         own = slice(m * rows, (m + 1) * rows)
-        back_ref, at = (first_ref, m) if m < parts // 2 else (last_ref, m - parts // 2)
+        back_ref, at = (first_ref, m) if m < early else (last_ref, m - early)
         raw = jnp.concatenate([grad_q[own], gk_ref[own, :]], axis=1) * HEAD_DIM ** (-0.5)
         unit, scale = back_ref[at, :, : 2 * HEAD_DIM], back_ref[at, :, 2 * HEAD_DIM :]
         back = scale * (raw - unit * (half_sums(raw * unit) / HEAD_DIM))
         out_ref[me ^ DISTANCES[m], :PACKED, :] = pack(gv_ref[own, :]).astype(jnp.bfloat16)
         out_ref[me ^ DISTANCES[m], PACKED:, :] = back.astype(jnp.bfloat16)
+        out_ref.leave(me ^ DISTANCES[m])
 
 
 def weights_kernel(me_ref, slab_ref, first_ref, last_ref, out_ref):
-    half, rows, width = first_ref.shape
-    parts = 2 * half
+    early, rows, width = first_ref.shape
+    parts = early + last_ref.shape[0]
     qk_sum = v_sum = 0.0
     for m in range(parts):
         slab = slab_ref[me_ref[0] ^ DISTANCES[m]].astype(jnp.float32)
-        normed = first_ref[m] if m < half else last_ref[m - half]
+        normed = first_ref[m] if m < early else last_ref[m - early]
         qk, v = slab[PACKED:].astype(jnp.bfloat16), unpack(slab[:PACKED], rows)
         qk_sum = qk_sum + dot(qk, normed, ((0,), (0,)))
         v_sum = v_sum + dot(v.astype(jnp.bfloat16), normed, ((0,), (0,)))
@@ -443,13 +530,16 @@
     return matrix.astype(jnp.bfloat16)
 
 
-def sum_to_owner(first, second, third, keep):
+def sum_to_owner(first, second, third, keep, bits):
     size = keep.shape[0]
-    got = partner(first, "seq", 0)
-    more = partner(low(wide(second) + wide(got[2 * size :])), "seq", 1)
+    got = partner(first, "seq", bits[0])
+    more = partner(low(wide(second) + wide(got[2 * size :])), "seq", bits[1])
     third = wide(third) + wide(got[size : 2 * size]) + wide(more[size:])
     keep = wide(keep) + wide(got[:size]) + wide(more[:size])
-    return keep + wide(partner(low(third), "seq", 2))
+    return keep + wide(partner(low(third), "seq", bits[2]))
+
+
+EARLY = 6
 
 
 def head_shards(
@@ -464,69 +554,68 @@
     inner = wq.shape[1]
     tokens = parts * rows
     length = PACKED + rows
-    smem = pl.BlockSpec(memory_space=pltpu.SMEM)
-    vmem = pl.BlockSpec(memory_space=pltpu.VMEM)
     f32 = jnp.float32
+
+    def out(place, *dims, dtype=jnp.bfloat16):
+        return place, jax.ShapeDtypeStruct(dims, dtype)
 
     blocks = spread(field)
     order = me[0] ^ jnp.array(DISTANCES, jnp.int32)
     ids = jnp.take(block_ids.reshape(parts, rows), order, axis=0).reshape(tokens)
-    half = parts // 2
     pieces = [
         call(
             project_kernel,
+            [("s", me), *[("h", block) for block in group], ("r", wq), ("r", wk), ("r", wv)],
             [
-                shape(half, rows, width),
-                shape(half, rows, 256, dtype=f32),
-                shape(half, rows, 256),
+                out("h", len(group), rows, width),
+                out("h", len(group), rows, 256, dtype=f32),
+                out("h", len(group), rows, 256),
             ],
-            [me, *group, wq, wk, wv],
-            2 * half * rows * width * 512,
-            specs=[smem] + [vmem] * (half + 3),
+            2 * len(group) * rows * width * 512,
+            [pltpu.VMEM((width, 2 * HEAD_DIM), jnp.bfloat16)] * 3
+            + [pltpu.SemaphoreType.DMA((3,))],
         )
-        for group in (blocks[:half], blocks[half:])
+        for group in (blocks[:EARLY], blocks[EARLY:])
     ]
     normed, back, projected = zip(*pieces)
     probs, qk, value, out_t, packed = call(
         attend_kernel,
+        [("s", me), *[("h", piece) for piece in projected], ("v", ids[None, :]), ("v", ids[:, None])],
         [
-            shape(tokens, tokens),
-            shape(tokens, 128),
-            shape(tokens, HEAD_DIM),
-            shape(HEAD_DIM, tokens, dtype=f32),
-            shape(parts, PACKED, 128),
+            out("h", len(tiles(tokens)), tokens, TILE),
+            out("h", tokens, 128),
+            out("h", tokens, HEAD_DIM),
+            out("h", HEAD_DIM, tokens, dtype=f32),
+            out("h", parts, PACKED, 128),
         ],
-        [me, *projected, ids[None, :], ids[:, None]],
         4 * tokens * tokens * 256,
-        specs=[smem] + [vmem] * 4,
     )
     packed = exchange(packed)
-    attended, grad_affine, scaled, grad_slabs = call(
+    grad_affine, scaled, grad_slabs = call(
         affine_kernel,
+        [("h", packed), ("h", field), ("h", upstream), ("h", wo)],
         [
-            shape(rows, inner),
-            shape(rows, 2 * width),
-            shape(rows, width, dtype=f32),
-            shape(HEADS, PACKED, 128),
+            out("h", rows, 2 * width),
+            out("h", rows, width, dtype=f32),
+            out("h", HEADS, PACKED, 128),
         ],
-        [packed, field, upstream, wo],
         8 * rows * width * inner,
     )
     grad_slabs = exchange(grad_slabs)
     terms = call(
         out_term_kernel,
-        [shape(len(group) * HEAD_DIM, 2 * width) for group in ORDER],
-        [me, packed, grad_affine],
+        [("s", me), ("h", packed), ("h", grad_affine)],
+        [out("h", len(group) * HEAD_DIM, width) for order in ORDERS for group in order],
         4 * rows * width * inner,
-        specs=[smem, vmem, vmem],
-    )
+    )
+    grad_slabs, terms = lax.optimization_barrier((grad_slabs, terms))
     (grads,) = call(
         backward_kernel,
-        [shape(parts, length, 128)],
-        [me, grad_slabs, probs, qk, value, out_t, *back],
+        [("s", me), ("h", grad_slabs), ("h", probs), ("h", qk), ("h", value), ("h", out_t)]
+        + [("h", piece) for piece in back],
+        [out("h", parts, length, 128)],
         8 * tokens * tokens * 256,
-        specs=[smem] + [vmem] * 7,
-        scratch=[
+        [
             pltpu.VMEM((tokens, HEAD_DIM), f32),
             pltpu.VMEM((tokens, HEAD_DIM), f32),
             pltpu.VMEM((HEAD_DIM, tokens), f32),
@@ -535,16 +624,15 @@
     token_grads = exchange(grads)
     (weight_terms,) = call(
         weights_kernel,
-        [shape(parts, 3 * HEAD_DIM, width // parts)],
-        [me, grads, *normed],
+        [("s", me), ("h", grads)] + [("h", piece) for piece in normed],
+        [out("h", parts, 3 * HEAD_DIM, width // parts)],
         2 * tokens * width * 256,
-        specs=[smem] + [vmem] * 3,
     )
     weight_terms = exchange(weight_terms)
     (grad_input,) = call(
         input_kernel,
-        [shape(rows, width)],
-        [token_grads, wq, wk, wv, field, scaled],
+        [("h", token_grads), ("h", wq), ("h", wk), ("h", wv), ("h", field), ("h", scaled)],
+        [out("h", rows, width)],
         6 * rows * width * inner,
     )
     route = [
@@ -553,12 +641,17 @@
         for d in range(parts)
     ]
     moved = lax.ppermute(grad_input, ("section", "seq"), route)
-    grad_out = sum_to_owner(*terms)
+    grad_out = jnp.concatenate(
+        [sum_to_owner(*terms[:4], (0, 1, 2)), sum_to_owner(*terms[4:], (1, 0, 2))], axis=1
+    )
     grad_q, grad_k, grad_v = call(
-        turn_kernel, [shape(1, width // parts, inner, dtype=f32)] * 3, [weight_terms]
+        turn_kernel, [("h", weight_terms)], [out("h", 1, width // parts, inner, dtype=f32)] * 3
     )
     (carry,) = call(
-        reorder_kernel, [shape(1, rows, width)], [flip_order[0][:, None], moved], 2 * rows * rows * width
+        reorder_kernel,
+        [("v", flip_order[0][:, None]), ("h", moved)],
+        [out("h", 1, rows, width)],
+        2 * rows * rows * width,
     )
     return (carry, grad_q, grad_k, grad_v, grad_out[None])
 

time: 150 us -> 168 us (1.12)
  waiting for transfers between devices: 30.8 us -> 56.1 us
  Pallas kernels: 23.2 us -> 45 us
  blocking collectives: 34.7 us -> 14.1 us
  local copies, waits for them, and re-layouts: 18 us -> 8.07 us
  starting transfers between devices: 35.1 us -> 39.9 us
  other arithmetic: 6.03 us -> 1.94 us
    pallas_call x10, Pallas kernels: 23.2 us -> 45 us  [call(): pl.pallas_call(body, out_shape=results, in_specs=[pl.BlockSpec(memory_spa...]
    all_to_all x2 -> x1, blocking collectives: 34.7 us -> 14.1 us  [exchange(): return lax.all_to_all(slabs, 'seq', split_axis=0, concat_axis=0, tiled=True)]
    ppermute x10 -> x13, waiting for transfers between devices: 26.9 us -> 46.7 us  [partner(): return lax.ppermute(block, axis, route)]
    unnamed x56 -> x38, local copies, waits for them, and re-layouts: 15.5 us -> 4.3 us
    all_to_all x2 -> x3, waiting for transfers between devices: 0.84 us -> 9.42 us  [exchange(): return lax.all_to_all(slabs, 'seq', split_axis=0, concat_axis=0, tiled=True)]
    ppermute x10 -> x13, starting transfers between devices: 12 us -> 18.9 us  [partner(): return lax.ppermute(block, axis, route)]
    ppermute x1, starting transfers between devices: 14.7 us -> 10.5 us  [head_shards(): moved = lax.ppermute(grad_input, ('section', 'seq'), route)]
    convert_element_type x2 -> x4, other arithmetic: 3.34 us -> 0.24 us  [low(): return matrix.astype(jnp.bfloat16)]
  transfers between devices with their start and end apart: 13 -> 17, of which waited for: 5 -> 9; matrix products, arithmetic and copies ran while one was open for 4% -> 3% of each run, Pallas kernels for 9% -> 10%
where the time goes in v4:
time: 168 us; the launch traced here: 166 us
  waiting for transfers between devices  56.1 us (33%)
  Pallas kernels  45 us (27%)
  starting transfers between devices  39.9 us (24%)
  blocking collectives  14.1 us (8%)
  local copies, waits for them, and re-layouts  8.07 us (5%)
  other arithmetic  1.94 us (1%)
    ppermute x13, waiting for transfers between devices, partner(): return lax.ppermute(block, axis, route)  46.7 us
    pallas_call x10, Pallas kernels, call(): pl.pallas_call(body, out_shape=results, in_specs=[pl.BlockSpec(memory_spa...  45 us
    ppermute x13, starting transfers between devices, partner(): return lax.ppermute(block, axis, route)  18.9 us
    all_to_all x1, blocking collectives, exchange(): return lax.all_to_all(slabs, 'seq', split_axis=0, concat_axis=0, tiled=True)  14.1 us
    all_to_all x3, starting transfers between devices, exchange(): return lax.all_to_all(slabs, 'seq', split_axis=0, concat_axis=0, tiled=True)  10.5 us
    ppermute x1, starting transfers between devices, head_shards(): moved = lax.ppermute(grad_input, ('section', 'seq'), route)  10.5 us
    all_to_all x3, waiting for transfers between devices, exchange(): return lax.all_to_all(slabs, 'seq', split_axis=0, concat_axis=0, tiled=True)  9.42 us
    unnamed x38, local copies, waits for them, and re-layouts  4.3 us
  transfers between devices with their start and end apart: 17, of which 9 were waited for; matrix products, arithmetic and copies ran while one was open for 3% of the time, Pallas kernels for 10%

profile of v4, /device:TPU:5, one launch (start us, length us, event | category | flops | bytes accessed | tf_op | source)
XLA Modules:
  0.0 166.2 jit_solution(15908490532766858409)
XLA Ops:
  0.6 2.4 %collective-permute-start.2 = (bf16[136,1024]{1,0:T(8,128)(2,1)}, bf16[136,1024]{1,0:T(8,128)(2,1)S(1)}, u32[]{:S(2)}, u32[]{:S(2)}) collective-permute-start(bf16[136,1024]{1,0:T(8,128)(2,1)} %bitcast.19), channel_id=1, source_target_pairs={{0,4},{4,0},{1,5},{5,1},{2,6},{6,2},{3,7},{7,3},{8,12},{12,8},{9,1... | collective-permute-start | bytes 835592 | tf_op jit(solution)/shard_map/ppermute | solution.py:22
  3.0 1.3 collective-permute-start.1
  4.3 1.2 collective-permute-start
  5.5 9.9 %collective-permute-done.2.refs_4_ = bf16[136,1024]{1,0:T(8,128)(2,1)S(1)} collective-permute-done((bf16[136,1024]{1,0:T(8,128)(2,1)}, bf16[136,1024]{1,0:T(8,128)(2,1)S(1)}, u32[]{:S(2)}, u32[]{:S(2)}) %collective-permute-start.2) | collective-permute-done | bytes 278560 | tf_op jit(solution)/shard_map/ppermute | solution.py:22
  15.4 1.2 collective-permute-start.4
  16.6 0.7 compare_and_fusion
  17.6 0.8 reshape.64
  18.4 0.6 gather_fusion
  18.9 1.6 collective-permute-start.5
  20.5 1.5 collective-permute-done.4.refs_6_
  21.9 2.7 %collective-permute-start.6 = (bf16[136,1024]{1,0:T(8,128)(2,1)S(1)}, bf16[136,1024]{1,0:T(8,128)(2,1)S(1)}, u32[]{:S(2)}, u32[]{:S(2)}) collective-permute-start(bf16[136,1024]{1,0:T(8,128)(2,1)S(1)} %collective-permute-done.4.refs_6_), channel_id=1, source_target_pairs={{0,2},{2,0},{1,3},{3,1},{4,6},{6,4},{5,7},{7,5},{8,10},{10,8},{9,1... | collective-permute-start | bytes 835592 | tf_op jit(solution)/shard_map/ppermute | solution.py:22
  24.7 1.0 select_n.33.refs_4_
  25.7 0.7 select_n.31.refs_3_
  26.4 1.5 collective-permute-done.3.refs_5_
  27.9 0.7 copy-done.6
  28.6 7.0 %shard_map.128 = (bf16[6,136,1024]{2,1,0:T(8,128)(2,1)}, f32[6,136,256]{2,1,0:T(8,128)}, bf16[6,136,256]{2,1,0:T(8,128)(2,1)}) custom-call(s32[1]{0:T(128)} %bitcast.1.refs_0_, bf16[136,1024]{1,0:T(8,128)(2,1)} %bitcast.22, bf16[136,1024]{1,0:T(8,128)(2,1)} %copy-done.4, bf16[136,1024]{1,0:T(8,128)(2,1)} %copy-done.3, bf16[136,1024]{1,0:T(8,128)(2,1)} %copy-done.2, ...), custom_call_target="tpu_custom_call" | custom-call | flops 855638016 | bytes 7741444 | tf_op jit(solution)/shard_map/pallas_call | solution.py:263
  35.7 0.7 copy-done.8
  36.4 0.7 copy-done.9
  37.1 3.7 %shard_map.129 = (bf16[2,136,1024]{2,1,0:T(8,128)(2,1)}, f32[2,136,256]{2,1,0:T(8,128)}, bf16[2,136,256]{2,1,0:T(8,128)(2,1)}) custom-call(s32[1]{0:T(128)} %bitcast.1.refs_0_, bf16[136,1024]{1,0:T(8,128)(2,1)} %copy-done.8, bf16[136,1024]{1,0:T(8,128)(2,1)} %copy-done.9, bf16[1024,512]{1,0:T(8,128)(2,1)} %bitcast.11, bf16[1024,512]{1,0:T(8,128)(2,1)} %bitcast.14, ...), custom_call_target="tpu_custom_call" | custom-call | flops 285212672 | bytes 4677636 | tf_op jit(solution)/shard_map/pallas_call | solution.py:263
  40.8 6.5 %shard_map.130 = (bf16[5,1088,256]{2,1,0:T(8,128)(2,1)}, bf16[1088,128]{1,0:T(8,128)(2,1)}, bf16[1088,64]{1,0:T(8,128)(2,1)}, f32[64,1088]{1,0:T(8,128)}, bf16[8,80,128]{2,1,0:T(8,128)(2,1)}) custom-call(s32[1]{0:T(128)} %bitcast.1.refs_0_, bf16[6,136,256]{2,1,0:T(8,128)(2,1)} %get-tuple-element.39.refs_1_, bf16[2,136,256]{2,1,0:T(8,128)(2,1)} %get-tuple-element.40.refs_2_, ...), custom_call_target="tpu_custom_call" | custom-call | flops 1212153856 | bytes 4211204 | tf_op jit(solution)/shard_map/pallas_call | solution.py:263
  47.3 14.1 %all_to_all.20.refs_0_.refs_1_ = bf16[8,80,128]{2,1,0:T(8,128)(2,1)} all-to-all(bf16[8,80,128]{2,1,0:T(8,128)(2,1)} %get-tuple-element.41), channel_id=1, replica_groups=mesh['section'=4,'seq'=8] {'seq'}, dimensions={0} | all-to-all | bytes 327680 | tf_op jit(solution)/shard_map/all_to_all | solution.py:510
  61.4 4.4 %shard_map.131 = (bf16[136,2048]{1,0:T(8,128)(2,1)}, f32[136,1024]{1,0:T(8,128)}, bf16[8,80,128]{2,1,0:T(8,128)(2,1)}) custom-call(bf16[8,80,128]{2,1,0:T(8,128)(2,1)} %all_to_all.20.refs_0_.refs_1_, bf16[136,1024]{1,0:T(8,128)(2,1)} %bitcast.23, bf16[136,1024]{1,0:T(8,128)(2,1)} %bitcast.26, bf16[512,2048]{1,0:T(8,128)(2,1)} %bitcast.25), custom_call_target="tpu_custom_call" | custom-call | flops 570425344 | bytes 4096000 | tf_op jit(solution)/shard_map/pallas_call | solution.py:263
  65.8 3.6 %all-to-all-start.1 = ((bf16[8,80,128]{2,1,0:T(8,128)(2,1)}), bf16[8,80,128]{2,1,0:T(8,128)(2,1)S(1)}, u32[]{:S(2)}, u32[]{:S(2)}) async-start(bf16[8,80,128]{2,1,0:T(8,128)(2,1)} %get-tuple-element.42), calls=%async_computation.1 | async-start | bytes 327680 | tf_op jit(solution)/shard_map/all_to_all | solution.py:510
  69.4 3.4 %shard_map.132 = (bf16[256,1024]{1,0:T(8,128)(2,1)}, bf16[128,1024]{1,0:T(8,128)(2,1)}, bf16[64,1024]{1,0:T(8,128)(2,1)}, bf16[64,1024]{1,0:T(8,128)(2,1)}, bf16...) custom-call(s32[1]{0:T(128)} %bitcast.1.refs_0_, ...), custom_call_target="tpu_custom_call" | custom-call | flops 285212672 | bytes 2818052 | tf_op jit(solution)/shard_map/pallas_call | solution.py:263
  72.8 2.7 %all-to-all-done.1.refs_1_ = bf16[8,80,128]{2,1,0:T(8,128)(2,1)S(1)} async-done(((bf16[8,80,128]{2,1,0:T(8,128)(2,1)}), bf16[8,80,128]{2,1,0:T(8,128)(2,1)S(1)}, u32[]{:S(2)}, u32[]{:S(2)}) %all-to-all-start.1) | async-done | bytes 163872 | tf_op jit(solution)/shard_map/all_to_all | solution.py:510
  75.5 0.7 copy-done.12
  76.2 6.6 %shard_map.133.refs_1_ = bf16[8,216,128]{2,1,0:T(8,128)(2,1)} custom-call(s32[1]{0:T(128)} %bitcast.1.refs_0_, bf16[8,80,128]{2,1,0:T(8,128)(2,1)} %copy-done.12, bf16[5,1088,256]{2,1,0:T(8,128)(2,1)} %get-tuple-element.53.refs_2_, bf16[1088,128]{1,0:T(8,128)(2,1)} %get-tuple-element.54.refs_3_, bf16[1088,64]{1,0:T(8,128)(2,1)} %get-tuple-element.55.refs_4_, ...), custom_call_target="tpu_custom_call" | custom-call | flops 2424307712 | bytes 5201924 | tf_op jit(solution)/shard_map/pallas_call | solution.py:263
  82.8 3.7 %shard_map.136 = bf16[8,192,128]{2,1,0:T(8,128)(2,1)} custom-call(s32[1]{0:T(128)} %bitcast.1.refs_0_, bf16[8,216,128]{2,1,0:T(8,128)(2,1)} %shard_map.133.refs_1_, bf16[6,136,1024]{2,1,0:T(8,128)(2,1)} %get-tuple-element.60.refs_2_, bf16[2,136,1024]{2,1,0:T(8,128)(2,1)} %get-tuple-element.61.refs_3_), custom_call_target="tpu_custom_call" | custom-call | flops 570425344 | bytes 3063812 | tf_op jit(solution)/shard_map/pallas_call | solution.py:263
  86.5 3.5 %all-to-all-start.3 = ((bf16[8,192,128]{2,1,0:T(8,128)(2,1)}), bf16[8,192,128]{2,1,0:T(8,128)(2,1)S(1)}, u32[]{:S(2)}, u32[]{:S(2)}) async-start(bf16[8,192,128]{2,1,0:T(8,128)(2,1)} %shard_map.136), calls=%async_computation.3 | async-start | bytes 786432 | tf_op jit(solution)/shard_map/all_to_all | solution.py:510
  89.9 1.4 collective-permute-start.8
  91.3 6.7 %all-to-all-done.3.refs_0_ = bf16[8,192,128]{2,1,0:T(8,128)(2,1)S(1)} async-done(((bf16[8,192,128]{2,1,0:T(8,128)(2,1)}), bf16[8,192,128]{2,1,0:T(8,128)(2,1)S(1)}, u32[]{:S(2)}, u32[]{:S(2)}) %all-to-all-start.3) | async-done | bytes 393248 | tf_op jit(solution)/shard_map/all_to_all | solution.py:510
  98.0 3.5 %all-to-all-start.2 = ((bf16[8,216,128]{2,1,0:T(8,128)(2,1)}), bf16[8,216,128]{2,1,0:T(8,128)(2,1)S(1)}, u32[]{:S(2)}, u32[]{:S(2)}) async-start(bf16[8,216,128]{2,1,0:T(8,128)(2,1)} %shard_map.133.refs_1_), calls=%async_computation.2 | async-start | bytes 884736 | tf_op jit(solution)/shard_map/all_to_all | solution.py:510
  101.5 1.4 collective-permute-start.11
  102.8 0.7 copy.15.refs_0_
  103.6 1.4 collective-permute-done.8
  105.0 1.7 %collective-permute-start.9 = (bf16[128,1024]{1,0:T(8,128)(2,1)S(1)}, bf16[128,1024]{1,0:T(8,128)(2,1)S(1)}, u32[]{:S(2)}, u32[]{:S(2)}) collective-permute-start(bf16[128,1024]{1,0:T(8,128)(2,1)S(1)} %add_convert_fusion.1), channel_id=1, source_target_pairs={{0,2},{2,0},{1,3},{3,1},{4,6},{6,4},{5,7},{7,5},{8,10},{10,8},{9,1... | collective-permute-start | bytes 786440 | tf_op jit(solution)/shard_map/ppermute | solution.py:22
  106.7 12.5 %collective-permute-done.11 = bf16[256,1024]{1,0:T(8,128)(2,1)S(1)} collective-permute-done((bf16[256,1024]{1,0:T(8,128)(2,1)S(1)}, bf16[256,1024]{1,0:T(8,128)(2,1)S(1)}, u32[]{:S(2)}, u32[]{:S(2)}) %collective-permute-start.11) | collective-permute-done | bytes 524320 | tf_op jit(solution)/shard_map/ppermute | solution.py:22
  119.2 1.5 collective-permute-start.12
  120.7 2.2 %shard_map.137 = (f32[1,128,512]{2,1,0:T(8,128)}, f32[1,128,512]{2,1,0:T(8,128)}, f32[1,128,512]{2,1,0:T(8,128)}) custom-call(bf16[8,192,128]{2,1,0:T(8,128)(2,1)} %copy-done.1), custom_call_target="tpu_custom_call" | custom-call | bytes 1179648 | tf_op jit(solution)/shard_map/pallas_call | solution.py:263
  122.9 0.8 copy-done
  123.7 4.7 %shard_map.134 = bf16[136,1024]{1,0:T(8,128)(2,1)} custom-call(bf16[8,216,128]{2,1,0:T(8,128)(2,1)} %copy-done, bf16[1024,512]{1,0:T(8,128)(2,1)} %bitcast.12, bf16[1024,512]{1,0:T(8,128)(2,1)} %bitcast.15, bf16[1024,512]{1,0:T(8,128)(2,1)} %bitcast.18, bf16[136,1024]{1,0:T(8,128)(2,1)} %bitcast.24, f32[136,1024]{1,0:T(8,128)} %get-tuple-element.59.refs_5_), custom_call_target="tpu_custom_call" | custom-call | flops 427819008 | bytes 4702208 | tf_op jit(solution)/shard_map/pallas_call | solution.py:263
  128.3 10.5 %collective-permute-start.7 = (bf16[136,1024]{1,0:T(8,128)(2,1)}, bf16[136,1024]{1,0:T(8,128)(2,1)S(1)}, u32[]{:S(2)}, u32[]{:S(2)}) collective-permute-start(bf16[136,1024]{1,0:T(8,128)(2,1)} %shard_map.134), channel_id=1, source_target_pairs={{8,7},{9,6},{10,5},{11,4},{12,3},{13,2},{14,1},{15,0},{16,15},{17,... | collective-permute-start | bytes 835592 | tf_op jit(solution)/shard_map/ppermute | solution.py:643
  139.1 2.4 %collective-permute-start.13 = (bf16[64,1024]{1,0:T(8,128)(2,1)S(1)}, bf16[64,1024]{1,0:T(8,128)(2,1)S(1)}, u32[]{:S(2)}, u32[]{:S(2)}) collective-permute-start(bf16[64,1024]{1,0:T(8,128)(2,1)S(1)} %add_convert_fusion.2), channel_id=1, source_target_pairs={{0,4},{4,0},{1,5},{5,1},{2,6},{6,2},{3,7},{7,3},{8,12},{12,8},{9,1... | collective-permute-start | bytes 393224 | tf_op jit(solution)/shard_map/ppermute | solution.py:22
  141.5 17.3 %collective-permute-done.10 = bf16[64,1024]{1,0:T(8,128)(2,1)S(1)} collective-permute-done((bf16[64,1024]{1,0:T(8,128)(2,1)S(1)}, bf16[64,1024]{1,0:T(8,128)(2,1)S(1)}, u32[]{:S(2)}, u32[]{:S(2)}) %collective-permute-start.10) | collective-permute-done | bytes 131104 | tf_op jit(solution)/shard_map/ppermute | solution.py:22
  158.8 2.7 %collective-permute-done.13 = bf16[64,1024]{1,0:T(8,128)(2,1)S(1)} collective-permute-done((bf16[64,1024]{1,0:T(8,128)(2,1)S(1)}, bf16[64,1024]{1,0:T(8,128)(2,1)S(1)}, u32[]{:S(2)}, u32[]{:S(2)}) %collective-permute-start.13) | collective-permute-done | bytes 131104 | tf_op jit(solution)/shard_map/ppermute | solution.py:22
  161.6 0.8 maximum_bitcast_fusion
  162.5 0.7 copy-done.7
  163.2 2.9 %shard_map.135 = bf16[1,136,1024]{2,1,0:T(8,128)(2,1)} custom-call(s32[136,1]{1,0:T(8,128)} %copy.15.refs_0_, bf16[136,1024]{1,0:T(8,128)(2,1)} %copy-done.7), custom_call_target="tpu_custom_call" | custom-call | flops 37879808 | bytes 557600 | tf_op jit(solution)/shard_map/pallas_call | solution.py:263
  (50 shorter events, 0.9 us)
Async XLA Ops:
  0.6 14.7 %collective-permute-start.2 = (bf16[136,1024]{1,0:T(8,128)(2,1)}, bf16[136,1024]{1,0:T(8,128)(2,1)S(1)}, u32[]{:S(2)}, u32[]{:S(2)}) collective-permute-start(bf16[136,1024]{1,0:T(8,128)(2,1)} %bitcast.19), channel_id=1, source_target_pairs={{0,4},{4,0},{1,5},{5,1},{2,6},{6,2},{3,7},{7,3},{8,12},{12,8},{9,1... | collective-permute-start | bytes 835592 | tf_op jit(solution)/shard_map/ppermute | solution.py:22
  3.0 14.2 %collective-permute-start.1 = (bf16[136,1024]{1,0:T(8,128)(2,1)}, bf16[136,1024]{1,0:T(8,128)(2,1)S(1)}, u32[]{:S(2)}, u32[]{:S(2)}) collective-permute-start(bf16[136,1024]{1,0:T(8,128)(2,1)} %bitcast.20), channel_id=1, source_target_pairs={{0,2},{2,0},{1,3},{3,1},{4,6},{6,4},{5,7},{7,5},{8,10},{10,8},{9,1... | collective-permute-start | bytes 835592 | tf_op jit(solution)/shard_map/ppermute | solution.py:22
  4.3 22.1 %collective-permute-start = (bf16[136,1024]{1,0:T(8,128)(2,1)}, bf16[136,1024]{1,0:T(8,128)(2,1)S(1)}, u32[]{:S(2)}, u32[]{:S(2)}) collective-permute-start(bf16[136,1024]{1,0:T(8,128)(2,1)} %bitcast.21), channel_id=1, source_target_pairs={{0,1},{1,0},{2,3},{3,2},{4,5},{5,4},{6,7},{7,6},{8,9},{9,8},{10,11... | collective-permute-start | bytes 835592 | tf_op jit(solution)/shard_map/ppermute | solution.py:22
  15.4 12.5 %copy-start.2 = (bf16[136,1024]{1,0:T(8,128)(2,1)}, bf16[136,1024]{1,0:T(8,128)(2,1)S(1)}, u32[]{:S(2)}) copy-start(bf16[136,1024]{1,0:T(8,128)(2,1)S(1)} %collective-permute-done.2.refs_4_) | copy-start | bytes 835588
  15.4 6.6 %collective-permute-start.4 = (bf16[136,1024]{1,0:T(8,128)(2,1)S(1)}, bf16[136,1024]{1,0:T(8,128)(2,1)S(1)}, u32[]{:S(2)}, u32[]{:S(2)}) collective-permute-start(bf16[136,1024]{1,0:T(8,128)(2,1)S(1)} %collective-permute-done.2.refs_4_), channel_id=1, source_target_pairs={{0,1},{1,0},{2,3},{3,2},{4,5},{5,4},{6,7},{7,6},{8,9},{9,8},{10,11... | collective-permute-start | bytes 835592 | tf_op jit(solution)/shard_map/ppermute | solution.py:22
  17.2 10.7 %copy-start.3 = (bf16[136,1024]{1,0:T(8,128)(2,1)}, bf16[136,1024]{1,0:T(8,128)(2,1)S(1)}, u32[]{:S(2)}) copy-start(bf16[136,1024]{1,0:T(8,128)(2,1)S(1)} %collective-permute-done.1.refs_3_) | copy-start | bytes 835588
  17.2 10.7 %collective-permute-start.3 = (bf16[136,1024]{1,0:T(8,128)(2,1)S(1)}, bf16[136,1024]{1,0:T(8,128)(2,1)S(1)}, u32[]{:S(2)}, u32[]{:S(2)}) collective-permute-start(bf16[136,1024]{1,0:T(8,128)(2,1)S(1)} %collective-permute-done.1.refs_3_), channel_id=1, source_target_pairs={{0,1},{1,0},{2,3},{3,2},{4,5},{5,4},{6,7},{7,6},{8,9},{9,8},{10,11... | collective-permute-start | bytes 835592 | tf_op jit(solution)/shard_map/ppermute | solution.py:22
  18.9 16.7 %collective-permute-start.5 = (bf16[136,1024]{1,0:T(8,128)(2,1)S(1)}, bf16[136,1024]{1,0:T(8,128)(2,1)S(1)}, u32[]{:S(2)}, u32[]{:S(2)}) collective-permute-start(bf16[136,1024]{1,0:T(8,128)(2,1)S(1)} %collective-permute-done.2.refs_4_), channel_id=1, source_target_pairs={{0,2},{2,0},{1,3},{3,1},{4,6},{6,4},{5,7},{7,5},{8,10},{10,8},{9,1... | collective-permute-start | bytes 835592 | tf_op jit(solution)/shard_map/ppermute | solution.py:22
  21.9 6.0 %copy-start.5 = (bf16[136,1024]{1,0:T(8,128)(2,1)}, bf16[136,1024]{1,0:T(8,128)(2,1)S(1)}, u32[]{:S(2)}) copy-start(bf16[136,1024]{1,0:T(8,128)(2,1)S(1)} %collective-permute-done.4.refs_6_) | copy-start | bytes 835588
  21.9 13.7 %collective-permute-start.6 = (bf16[136,1024]{1,0:T(8,128)(2,1)S(1)}, bf16[136,1024]{1,0:T(8,128)(2,1)S(1)}, u32[]{:S(2)}, u32[]{:S(2)}) collective-permute-start(bf16[136,1024]{1,0:T(8,128)(2,1)S(1)} %collective-permute-done.4.refs_6_), channel_id=1, source_target_pairs={{0,2},{2,0},{1,3},{3,1},{4,6},{6,4},{5,7},{7,5},{8,10},{10,8},{9,1... | collective-permute-start | bytes 835592 | tf_op jit(solution)/shard_map/ppermute | solution.py:22
  26.4 1.6 copy-start.4
  27.9 0.7 copy-start.6
  35.6 0.7 copy-start.8
  36.4 0.7 copy-start.9
  65.8 9.8 %all-to-all-start.1 = ((bf16[8,80,128]{2,1,0:T(8,128)(2,1)}), bf16[8,80,128]{2,1,0:T(8,128)(2,1)S(1)}, u32[]{:S(2)}, u32[]{:S(2)}) async-start(bf16[8,80,128]{2,1,0:T(8,128)(2,1)} %get-tuple-element.42), calls=%async_computation.1 | async-start | bytes 327680 | tf_op jit(solution)/shard_map/all_to_all | solution.py:510
  75.5 0.7 copy-start.12
  82.8 18.7 %copy-start.18 = (bf16[256,1024]{1,0:T(8,128)(2,1)S(1)}, bf16[256,1024]{1,0:T(8,128)(2,1)}, u32[]{:S(2)}) copy-start(bf16[256,1024]{1,0:T(8,128)(2,1)} %get-tuple-element.70) | copy-start | bytes 1572868
  82.8 20.1 %copy-start.17 = (s32[1,136]{1,0:T(1,128)S(1)}, s32[1,136]{1,0:T(1,128)}, u32[]{:S(2)}) copy-start(s32[1,136]{1,0:T(1,128)} %param.16) | copy-start | bytes 1636
  82.8 22.1 %copy-start.11 = (bf16[128,1024]{1,0:T(8,128)(2,1)S(1)}, bf16[128,1024]{1,0:T(8,128)(2,1)}, u32[]{:S(2)}) copy-start(bf16[128,1024]{1,0:T(8,128)(2,1)} %get-tuple-element.67) | copy-start | bytes 786436
  82.8 36.3 %copy-start.10 = (bf16[128,1024]{1,0:T(8,128)(2,1)S(1)}, bf16[128,1024]{1,0:T(8,128)(2,1)}, u32[]{:S(2)}) copy-start(bf16[128,1024]{1,0:T(8,128)(2,1)} %get-tuple-element.71) | copy-start | bytes 786436
  86.5 11.5 %all-to-all-start.3 = ((bf16[8,192,128]{2,1,0:T(8,128)(2,1)}), bf16[8,192,128]{2,1,0:T(8,128)(2,1)S(1)}, u32[]{:S(2)}, u32[]{:S(2)}) async-start(bf16[8,192,128]{2,1,0:T(8,128)(2,1)} %shard_map.136), calls=%async_computation.3 | async-start | bytes 786432 | tf_op jit(solution)/shard_map/all_to_all | solution.py:510
  89.9 15.0 %collective-permute-start.8 = (bf16[256,1024]{1,0:T(8,128)(2,1)}, bf16[256,1024]{1,0:T(8,128)(2,1)S(1)}, u32[]{:S(2)}, u32[]{:S(2)}) collective-permute-start(bf16[256,1024]{1,0:T(8,128)(2,1)} %get-tuple-element.66), channel_id=1, source_target_pairs={{0,1},{1,0},{2,3},{3,2},{4,5},{5,4},{6,7},{7,6},{8,9},{9,8},{10,11... | collective-permute-start | bytes 1572872 | tf_op jit(solution)/shard_map/ppermute | solution.py:22
  98.0 22.7 %copy-start.1 = (bf16[8,192,128]{2,1,0:T(8,128)(2,1)}, bf16[8,192,128]{2,1,0:T(8,128)(2,1)S(1)}, u32[]{:S(2)}) copy-start(bf16[8,192,128]{2,1,0:T(8,128)(2,1)S(1)} %all-to-all-done.3.refs_0_) | copy-start | bytes 1179652
  98.0 24.9 %all-to-all-start.2 = ((bf16[8,216,128]{2,1,0:T(8,128)(2,1)}), bf16[8,216,128]{2,1,0:T(8,128)(2,1)S(1)}, u32[]{:S(2)}, u32[]{:S(2)}) async-start(bf16[8,216,128]{2,1,0:T(8,128)(2,1)} %shard_map.133.refs_1_), calls=%async_computation.2 | async-start | bytes 884736 | tf_op jit(solution)/shard_map/all_to_all | solution.py:510
  101.5 17.7 %collective-permute-start.11 = (bf16[256,1024]{1,0:T(8,128)(2,1)S(1)}, bf16[256,1024]{1,0:T(8,128)(2,1)S(1)}, u32[]{:S(2)}, u32[]{:S(2)}) collective-permute-start(bf16[256,1024]{1,0:T(8,128)(2,1)S(1)} %copy-done.18), channel_id=1, source_target_pairs={{0,2},{2,0},{1,3},{3,1},{4,6},{6,4},{5,7},{7,5},{8,10},{10,8},{9,1... | collective-permute-start | bytes 1572872 | tf_op jit(solution)/shard_map/ppermute | solution.py:22
  105.0 33.8 %collective-permute-start.9 = (bf16[128,1024]{1,0:T(8,128)(2,1)S(1)}, bf16[128,1024]{1,0:T(8,128)(2,1)S(1)}, u32[]{:S(2)}, u32[]{:S(2)}) collective-permute-start(bf16[128,1024]{1,0:T(8,128)(2,1)S(1)} %add_convert_fusion.1), channel_id=1, source_target_pairs={{0,2},{2,0},{1,3},{3,1},{4,6},{6,4},{5,7},{7,5},{8,10},{10,8},{9,1... | collective-permute-start | bytes 786440 | tf_op jit(solution)/shard_map/ppermute | solution.py:22
  119.2 19.8 %collective-permute-start.12 = (bf16[128,1024]{1,0:T(8,128)(2,1)S(1)}, bf16[128,1024]{1,0:T(8,128)(2,1)S(1)}, u32[]{:S(2)}, u32[]{:S(2)}) collective-permute-start(bf16[128,1024]{1,0:T(8,128)(2,1)S(1)} %add_convert_fusion), channel_id=1, source_target_pairs={{0,1},{1,0},{2,3},{3,2},{4,5},{5,4},{6,7},{7,6},{8,9},{9,8},{10,11... | collective-permute-start | bytes 786440 | tf_op jit(solution)/shard_map/ppermute | solution.py:22
  122.9 0.8 copy-start
  123.7 15.2 %copy-start.16 = (bf16[64,1024]{1,0:T(8,128)(2,1)S(1)}, bf16[64,1024]{1,0:T(8,128)(2,1)}, u32[]{:S(2)}) copy-start(bf16[64,1024]{1,0:T(8,128)(2,1)} %get-tuple-element.68) | copy-start | bytes 393220
  123.7 15.3 %copy-start.15 = (bf16[64,1024]{1,0:T(8,128)(2,1)S(1)}, bf16[64,1024]{1,0:T(8,128)(2,1)}, u32[]{:S(2)}) copy-start(bf16[64,1024]{1,0:T(8,128)(2,1)} %get-tuple-element.72) | copy-start | bytes 393220
  123.7 35.1 %copy-start.14 = (bf16[64,1024]{1,0:T(8,128)(2,1)S(1)}, bf16[64,1024]{1,0:T(8,128)(2,1)}, u32[]{:S(2)}) copy-start(bf16[64,1024]{1,0:T(8,128)(2,1)} %get-tuple-element.65) | copy-start | bytes 393220
  123.7 37.9 %copy-start.13 = (bf16[64,1024]{1,0:T(8,128)(2,1)S(1)}, bf16[64,1024]{1,0:T(8,128)(2,1)}, u32[]{:S(2)}) copy-start(bf16[64,1024]{1,0:T(8,128)(2,1)} %get-tuple-element.69) | copy-start | bytes 393220
  128.3 34.1 %collective-permute-start.7 = (bf16[136,1024]{1,0:T(8,128)(2,1)}, bf16[136,1024]{1,0:T(8,128)(2,1)S(1)}, u32[]{:S(2)}, u32[]{:S(2)}) collective-permute-start(bf16[136,1024]{1,0:T(8,128)(2,1)} %shard_map.134), channel_id=1, source_target_pairs={{8,7},{9,6},{10,5},{11,4},{12,3},{13,2},{14,1},{15,0},{16,15},{17,... | collective-permute-start | bytes 835592 | tf_op jit(solution)/shard_map/ppermute | solution.py:643
  138.9 19.9 %collective-permute-start.10 = (bf16[64,1024]{1,0:T(8,128)(2,1)S(1)}, bf16[64,1024]{1,0:T(8,128)(2,1)S(1)}, u32[]{:S(2)}, u32[]{:S(2)}) collective-permute-start(bf16[64,1024]{1,0:T(8,128)(2,1)S(1)} %add_convert_fusion.3), channel_id=1, source_target_pairs={{0,4},{4,0},{1,5},{5,1},{2,6},{6,2},{3,7},{7,3},{8,12},{12,8},{9,1... | collective-permute-start | bytes 393224 | tf_op jit(solution)/shard_map/ppermute | solution.py:22
  139.1 22.5 %collective-permute-start.13 = (bf16[64,1024]{1,0:T(8,128)(2,1)S(1)}, bf16[64,1024]{1,0:T(8,128)(2,1)S(1)}, u32[]{:S(2)}, u32[]{:S(2)}) collective-permute-start(bf16[64,1024]{1,0:T(8,128)(2,1)S(1)} %add_convert_fusion.2), channel_id=1, source_target_pairs={{0,4},{4,0},{1,5},{5,1},{2,6},{6,2},{3,7},{7,3},{8,12},{12,8},{9,1... | collective-permute-start | bytes 393224 | tf_op jit(solution)/shard_map/ppermute | solution.py:22
  162.5 0.7 copy-start.7

commit v5 on v3

--- a/solution.py
+++ b/solution.py
@@ -194,24 +194,18 @@
 PACKED = 80
 
 
-def call(kernel, outs, operands, flops=0, specs=None, scratch=()):
-    moved = sum(x.size * x.dtype.itemsize for x in operands) + sum(
-        x.size * x.dtype.itemsize for x in outs
-    )
-    single = pl.BlockSpec(memory_space=pltpu.VMEM)
+def call(kernel, ins, outs, scratch=()):
+    spaces = {"s": pltpu.SMEM, "v": pltpu.VMEM, "a": pl.ANY}
+    places, operands = zip(*ins)
     return pl.pallas_call(
         kernel,
         out_shape=tuple(outs),
-        in_specs=specs or [single] * len(operands),
-        out_specs=tuple([single] * len(outs)),
+        in_specs=[pl.BlockSpec(memory_space=spaces[place]) for place in places],
+        out_specs=(pl.BlockSpec(memory_space=pltpu.VMEM),) * len(outs),
         scratch_shapes=list(scratch),
         compiler_params=pltpu.CompilerParams(vmem_limit_bytes=14 * 2**20),
-        cost_estimate=pl.CostEstimate(flops=flops, bytes_accessed=moved, transcendentals=0),
+        cost_estimate=pl.CostEstimate(flops=1024, bytes_accessed=1024, transcendentals=0),
     )(*operands)
-
-
-def shape(*dims, dtype=jnp.bfloat16):
-    return jax.ShapeDtypeStruct(dims, dtype)
 
 
 def dot(left, right, contract=((1,), (0,))):
@@ -249,40 +243,46 @@
     return field * row_scale, row_scale
 
 
-def project_kernel(me_ref, *refs):
-    blocks, (wq_ref, wk_ref, wv_ref, normed_ref, back_ref, out_ref) = refs[:-6], refs[-6:]
-    odd = lax.rem(me_ref[0], 2) == 1
-    pair = pl.multiple_of(lax.div(me_ref[0], 2) * 2 * HEAD_DIM, 2 * HEAD_DIM)
-    weights = [ref[:, pl.ds(pair, 2 * HEAD_DIM)] for ref in (wq_ref, wk_ref, wv_ref)]
+def project(block, weight):
+    normed = normalize(block)[0].astype(jnp.bfloat16)
+    product = dot(normed, weight)
+    raw, value = product[:, : 2 * HEAD_DIM], product[:, 2 * HEAD_DIM :]
+    scale = lax.rsqrt(half_sums(raw * raw) / HEAD_DIM + EPSILON)
+    return normed, raw * scale, scale, value
+
+
+def project_kernel(*refs):
+    blocks, (weight_ref, normed_ref, unit_ref, scale_ref, value_ref) = refs[:-5], refs[-5:]
     for m, block in enumerate(blocks):
-        normed = normalize(block[...])[0].astype(jnp.bfloat16)
-        q, k, v = [dot(normed, weight) for weight in weights]
-        low = low_lanes(q)
-        raw = jnp.where(low, jnp.where(odd, swap(q), q), jnp.where(odd, k, swap(k)))
-        scale = lax.rsqrt(half_sums(raw * raw) / HEAD_DIM + EPSILON)
-        unit = raw * scale
-        normed_ref[m] = normed
-        back_ref[m, :, : 2 * HEAD_DIM] = unit
-        back_ref[m, :, 2 * HEAD_DIM :] = scale
-        out_ref[m, :, : 2 * HEAD_DIM] = unit.astype(jnp.bfloat16)
-        out_ref[m, :, 2 * HEAD_DIM :] = jnp.where(odd, swap(v), v).astype(jnp.bfloat16)
+        made = project(block[...], weight_ref[...])
+        for ref, part in zip((normed_ref, unit_ref, scale_ref, value_ref), made):
+            ref[m] = part.astype(ref.dtype)
+
+
+TILE = 256
 
 
 def tiles(tokens):
-    size = 256
-    return [(start, min(tokens, start + size)) for start in range(0, tokens, size)]
+    starts = range(0, tokens, TILE)
+    return [(start, min(tokens, start + TILE)) for start in starts]
 
 
 def attend_kernel(
-    me_ref, first_ref, last_ref, row_ids, column_ids, prob_ref, qk_ref, v_ref, out_t_ref, out_ref
+    me_ref, unit_ref, value_ref, near_ref, last_ref, weight_ref, row_ids, column_ids, *out_refs
 ):
-    rows = first_ref.shape[1]
-    parts = 2 * first_ref.shape[0]
+    normed_ref, late_unit, late_scale, prob_ref, qk_ref, v_ref, out_t_ref, out_ref = out_refs
+    early, rows = unit_ref.shape[:2]
+    units = [unit_ref[m] for m in range(early)]
+    values = [value_ref[m] for m in range(early)]
+    for m, ref in enumerate((near_ref, last_ref)):
+        normed, unit, scale, value = project(ref[...], weight_ref[...])
+        normed_ref[m], late_unit[m], late_scale[m] = normed, unit, scale
+        units.append(unit)
+        values.append(value)
+    parts = len(units)
     tokens = parts * rows
-    slabs = [ref[m] for ref in (first_ref, last_ref) for m in range(parts // 2)]
-    whole = jnp.concatenate([slab.astype(jnp.float32) for slab in slabs], axis=0)
-    qk = whole[:, : 2 * HEAD_DIM].astype(jnp.bfloat16)
-    value = whole[:, 2 * HEAD_DIM : 3 * HEAD_DIM].astype(jnp.bfloat16)
+    qk = jnp.concatenate(units, axis=0).astype(jnp.bfloat16)
+    value = jnp.concatenate(values, axis=0).astype(jnp.bfloat16)
     qk_ref[...] = qk
     v_ref[...] = value
     query, key = qk[:, :HEAD_DIM] * HEAD_DIM ** (-0.5), qk[:, HEAD_DIM:]
@@ -297,48 +297,51 @@
         out_t_ref[:, start:stop] = out_t.astype(jnp.bfloat16).astype(jnp.float32)
     out = jnp.transpose(out_t_ref[...])
     for m in range(parts):
-        out_ref[me_ref[0] ^ DISTANCES[m]] = pack(out[m * rows : (m + 1) * rows]).astype(jnp.bfloat16)
-
-
-def affine_kernel(slab_ref, act_ref, inc_ref, w_ref, att_ref, aff_ref, up_ref, out_ref):
+        group = me_ref[0] ^ DISTANCES[m]
+        out_ref[group] = pack(out[m * rows : (m + 1) * rows]).astype(jnp.bfloat16)
+
+
+def affine_kernel(slab_ref, act_ref, inc_ref, w_ref, aff_ref, up_ref, out_ref):
     heads = slab_ref.shape[0]
     rows, width = act_ref.shape
     attended = jnp.concatenate(
         [unpack(slab_ref[h].astype(jnp.float32), rows) for h in range(heads)], axis=1
     ).astype(jnp.bfloat16)
-    att_ref[...] = attended
     factor = jnp.exp(-dot(attended, w_ref[:, width:]))
     scaled = inc_ref[...].astype(jnp.float32) * factor
     up_ref[...] = scaled
     shift_part = dot(attended, w_ref[:, :width])
-    aff_ref[:, :width] = (-scaled).astype(jnp.bfloat16)
     latent_part = scaled * (act_ref[...].astype(jnp.float32) - shift_part)
-    aff_ref[:, width:] = (1.0 - latent_part).astype(jnp.bfloat16)
-    grad = dot(aff_ref[...], w_ref[...], ((1,), (1,)))
+    grad_affine = jnp.concatenate([-scaled, 1.0 - latent_part], axis=1).astype(jnp.bfloat16)
+    aff_ref[...] = grad_affine
+    grad = dot(grad_affine, w_ref[...], ((1,), (1,)))
     for h in range(heads):
         block = grad[:, h * HEAD_DIM : (h + 1) * HEAD_DIM]
         out_ref[h] = pack(block).astype(jnp.bfloat16)
 
 
-ORDER = ((1, 5, 3, 7), (2, 6), (4,), (0,))
+ORDERS = (((1, 5, 3, 7), (2, 6), (4,), (0,)), ((2, 6, 3, 7), (1, 5), (4,), (0,)))
 
 
 def out_term_kernel(me_ref, slab_ref, aff_ref, *out_refs):
     heads, rows = slab_ref.shape[0], aff_ref.shape[0]
+    width = aff_ref.shape[1] // 2
     columns = [
         unpack(slab_ref[me_ref[0] ^ m].astype(jnp.float32), rows) for m in range(heads)
     ]
-    for out_ref, group in zip(out_refs, ORDER):
-        left = jnp.concatenate([columns[m] for m in group], axis=1).astype(jnp.bfloat16)
-        out_ref[...] = dot(left, aff_ref[...], ((0,), (0,))).astype(jnp.bfloat16)
-
-
-def backward_kernel(
-    me_ref, slab_ref, prob_ref, qk_ref, v_ref, out_t_ref, first_ref, last_ref, out_ref, gk_ref, gv_ref, gq_ref
-):
-    parts, rows = slab_ref.shape[0], first_ref.shape[1]
+    for half, order in enumerate(ORDERS):
+        right = aff_ref[:, half * width : (half + 1) * width]
+        for out_ref, group in zip(out_refs[4 * half : 4 * half + 4], order):
+            left = jnp.concatenate([columns[m] for m in group], axis=1).astype(jnp.bfloat16)
+            out_ref[...] = dot(left, right, ((0,), (0,))).astype(jnp.bfloat16)
+
+
+def backward_kernel(me_ref, slab_ref, prob_ref, qk_ref, v_ref, out_t_ref, *refs):
+    early, late, (out_ref, gk_ref, gv_ref, gq_ref) = refs[:3], refs[3:6], refs[6:]
+    parts, rows = slab_ref.shape[0], early[0].shape[1]
     tokens = parts * rows
     me = me_ref[0]
+    first = early[0].shape[0]
     grad_f = jnp.concatenate(
         [unpack(slab_ref[me ^ DISTANCES[m]].astype(jnp.float32), rows) for m in range(parts)], axis=0
     )
@@ -359,38 +362,54 @@
         gk_ref[...] += dot(scores, query[start:stop])
         gq_ref[:, start:stop] = dot(key, scores, ((0,), (0,)))
     grad_q = jnp.transpose(gq_ref[...])
+    qk_sum = v_sum = 0.0
     for m in range(parts):
         own = slice(m * rows, (m + 1) * rows)
-        back_ref, at = (first_ref, m) if m < parts // 2 else (last_ref, m - parts // 2)
+        normed, unit, scale = [
+            early[i][m] if m < first else late[i][m - first] for i in range(3)
+        ]
         raw = jnp.concatenate([grad_q[own], gk_ref[own, :]], axis=1) * HEAD_DIM ** (-0.5)
-        unit, scale = back_ref[at, :, : 2 * HEAD_DIM], back_ref[at, :, 2 * HEAD_DIM :]
         back = scale * (raw - unit * (half_sums(raw * unit) / HEAD_DIM))
-        out_ref[me ^ DISTANCES[m], :PACKED, :] = pack(gv_ref[own, :]).astype(jnp.bfloat16)
-        out_ref[me ^ DISTANCES[m], PACKED:, :] = back.astype(jnp.bfloat16)
-
-
-def weights_kernel(me_ref, slab_ref, first_ref, last_ref, out_ref):
-    half, rows, width = first_ref.shape
-    parts = 2 * half
-    qk_sum = v_sum = 0.0
-    for m in range(parts):
-        slab = slab_ref[me_ref[0] ^ DISTANCES[m]].astype(jnp.float32)
-        normed = first_ref[m] if m < half else last_ref[m - half]
-        qk, v = slab[PACKED:].astype(jnp.bfloat16), unpack(slab[:PACKED], rows)
-        qk_sum = qk_sum + dot(qk, normed, ((0,), (0,)))
-        v_sum = v_sum + dot(v.astype(jnp.bfloat16), normed, ((0,), (0,)))
-    step = width // parts
+        back, grad_v = back.astype(jnp.bfloat16), gv_ref[own, :]
+        out_ref[me ^ DISTANCES[m], :PACKED, :] = pack(grad_v).astype(jnp.bfloat16)
+        out_ref[me ^ DISTANCES[m], PACKED : PACKED + rows, :] = back
+        qk_sum = qk_sum + dot(back, normed, ((0,), (0,)))
+        v_sum = v_sum + dot(grad_v.astype(jnp.bfloat16), normed, ((0,), (0,)))
+    step = qk_sum.shape[1] // parts
+    middle = PACKED + rows + 2 * HEAD_DIM
     for g in range(parts):
         own = slice(g * step, (g + 1) * step)
-        out_ref[g, : 2 * HEAD_DIM, :] = qk_sum[:, own].astype(jnp.bfloat16)
-        out_ref[g, 2 * HEAD_DIM :, :] = v_sum[:, own].astype(jnp.bfloat16)
+        out_ref[g, PACKED + rows : middle, :] = qk_sum[:, own].astype(jnp.bfloat16)
+        out_ref[g, middle:, :] = v_sum[:, own].astype(jnp.bfloat16)
 
 
 def turn_kernel(slab_ref, *out_refs):
+    start = slab_ref.shape[1] - 3 * HEAD_DIM
     for i, out_ref in enumerate(out_refs):
-        own = slice(i * HEAD_DIM, (i + 1) * HEAD_DIM)
+        own = slice(start + i * HEAD_DIM, start + (i + 1) * HEAD_DIM)
         heads = [slab_ref[h, own, :].astype(jnp.float32) for h in range(slab_ref.shape[0])]
         out_ref[0] = jnp.transpose(jnp.concatenate(heads, axis=0))
+
+
+def second_sum_kernel(*refs):
+    for second, got, out in zip(refs[0:2], refs[2:4], refs[5:7]):
+        start = got.shape[0] - second.shape[0]
+        out[...] = low(wide(second[...]) + wide(got[start:, :]))
+
+
+def third_sum_kernel(*refs):
+    for i in range(2):
+        third, keep, got, more = [ref[...] for ref in refs[i:8:2]]
+        size = third.shape[0]
+        leaving, staying = refs[9 + i], refs[11 + i]
+        leaving[...] = low(wide(third) + wide(got[size : 2 * size]) + wide(more[size:]))
+        staying[...] = wide(keep) + wide(got[:size]) + wide(more[:size])
+
+
+def last_sum_kernel(keep_a, keep_b, got_a, got_b, out_ref):
+    for i, (keep, got) in enumerate(((keep_a, got_a), (keep_b, got_b))):
+        width = keep.shape[1]
+        out_ref[0, :, i * width : (i + 1) * width] = keep[...] + wide(got[...])
 
 
 def input_kernel(slab_ref, wq_ref, wk_ref, wv_ref, act_ref, up_ref, out_ref):
@@ -398,8 +417,9 @@
     unit, row_scale = normalize(act_ref[...])
     queries, keys, values = [], [], []
     for pair in range(HEADS // 2):
-        even = slab_ref[2 * pair].astype(jnp.float32)
-        odd = slab_ref[2 * pair + 1].astype(jnp.float32)
+        even, odd = [
+            slab_ref[2 * pair + i, : PACKED + rows, :].astype(jnp.float32) for i in range(2)
+        ]
         low = low_lanes(even[PACKED:])
         queries.append(jnp.where(low, even[PACKED:], swap(odd[PACKED:])))
         keys.append(jnp.where(low, swap(even[PACKED:]), odd[PACKED:]))
@@ -443,13 +463,7 @@
     return matrix.astype(jnp.bfloat16)
 
 
-def sum_to_owner(first, second, third, keep):
-    size = keep.shape[0]
-    got = partner(first, "seq", 0)
-    more = partner(low(wide(second) + wide(got[2 * size :])), "seq", 1)
-    third = wide(third) + wide(got[size : 2 * size]) + wide(more[size:])
-    keep = wide(keep) + wide(got[:size]) + wide(more[:size])
-    return keep + wide(partner(low(third), "seq", 2))
+EARLY = 6
 
 
 def head_shards(
@@ -463,89 +477,88 @@
     rows, width = field.shape
     inner = wq.shape[1]
     tokens = parts * rows
-    length = PACKED + rows
-    smem = pl.BlockSpec(memory_space=pltpu.SMEM)
-    vmem = pl.BlockSpec(memory_space=pltpu.VMEM)
     f32 = jnp.float32
+
+    def out(*dims, dtype=jnp.bfloat16):
+        return jax.ShapeDtypeStruct(dims, dtype)
 
     blocks = spread(field)
     order = me[0] ^ jnp.array(DISTANCES, jnp.int32)
     ids = jnp.take(block_ids.reshape(parts, rows), order, axis=0).reshape(tokens)
-    half = parts // 2
-    pieces = [
-        call(
-            project_kernel,
-            [
-                shape(half, rows, width),
-                shape(half, rows, 256, dtype=f32),
-                shape(half, rows, 256),
-            ],
-            [me, *group, wq, wk, wv],
-            2 * half * rows * width * 512,
-            specs=[smem] + [vmem] * (half + 3),
-        )
-        for group in (blocks[:half], blocks[half:])
-    ]
-    normed, back, projected = zip(*pieces)
-    probs, qk, value, out_t, packed = call(
+    weight = jnp.concatenate(
+        [lax.dynamic_slice_in_dim(w, me[0] * HEAD_DIM, HEAD_DIM, axis=1) for w in (wq, wk, wv)],
+        axis=1,
+    )
+    pair = 2 * HEAD_DIM
+    normed, unit, unit_scale, projected = call(
+        project_kernel,
+        [("v", block) for block in blocks[:EARLY]] + [("v", weight)],
+        [
+            out(EARLY, rows, width),
+            out(EARLY, rows, pair, dtype=f32),
+            out(EARLY, rows, pair, dtype=f32),
+            out(EARLY, rows, HEAD_DIM, dtype=f32),
+        ],
+    )
+    late = parts - EARLY
+    *late_parts, probs, qk, value, out_t, packed = call(
         attend_kernel,
+        [("s", me), ("v", unit), ("v", projected), *[("v", block) for block in blocks[EARLY:]]]
+        + [("v", weight), ("v", ids[None, :]), ("v", ids[:, None])],
         [
-            shape(tokens, tokens),
-            shape(tokens, 128),
-            shape(tokens, HEAD_DIM),
-            shape(HEAD_DIM, tokens, dtype=f32),
-            shape(parts, PACKED, 128),
+            out(late, rows, width),
+            out(late, rows, pair, dtype=f32),
+            out(late, rows, pair, dtype=f32),
+            out(tokens, tokens),
+            out(tokens, pair),
+            out(tokens, HEAD_DIM),
+            out(HEAD_DIM, tokens, dtype=f32),
+            out(parts, PACKED, 128),
         ],
-        [me, *projected, ids[None, :], ids[:, None]],
-        4 * tokens * tokens * 256,
-        specs=[smem] + [vmem] * 4,
     )
     packed = exchange(packed)
-    attended, grad_affine, scaled, grad_slabs = call(
+    grad_affine, scaled, grad_slabs = call(
         affine_kernel,
-        [
-            shape(rows, inner),
-            shape(rows, 2 * width),
-            shape(rows, width, dtype=f32),
-            shape(HEADS, PACKED, 128),
-        ],
-        [packed, field, upstream, wo],
-        8 * rows * width * inner,
+        [("v", packed), ("v", field), ("v", upstream), ("v", wo)],
+        [out(rows, 2 * width), out(rows, width, dtype=f32), out(HEADS, PACKED, 128)],
     )
     grad_slabs = exchange(grad_slabs)
     terms = call(
         out_term_kernel,
-        [shape(len(group) * HEAD_DIM, 2 * width) for group in ORDER],
-        [me, packed, grad_affine],
-        4 * rows * width * inner,
-        specs=[smem, vmem, vmem],
-    )
+        [("s", me), ("v", packed), ("v", grad_affine)],
+        [out(len(group) * HEAD_DIM, width) for order in ORDERS for group in order],
+    )
+    grad_slabs, terms = lax.optimization_barrier((grad_slabs, terms))
+    first, second, third, keep = zip(terms[:4], terms[4:])
+    got = [partner(part, "seq", bit) for bit, part in enumerate(first)]
     (grads,) = call(
         backward_kernel,
-        [shape(parts, length, 128)],
-        [me, grad_slabs, probs, qk, value, out_t, *back],
-        8 * tokens * tokens * 256,
-        specs=[smem] + [vmem] * 7,
-        scratch=[
+        [("s", me), ("v", grad_slabs), ("v", probs), ("v", qk), ("v", value), ("v", out_t)]
+        + [("v", x) for x in (normed, unit, unit_scale, *late_parts)],
+        [out(parts, PACKED + rows + 3 * HEAD_DIM, 128)],
+        [
             pltpu.VMEM((tokens, HEAD_DIM), f32),
             pltpu.VMEM((tokens, HEAD_DIM), f32),
             pltpu.VMEM((HEAD_DIM, tokens), f32),
         ],
     )
-    token_grads = exchange(grads)
-    (weight_terms,) = call(
-        weights_kernel,
-        [shape(parts, 3 * HEAD_DIM, width // parts)],
-        [me, grads, *normed],
-        2 * tokens * width * 256,
-        specs=[smem] + [vmem] * 3,
-    )
-    weight_terms = exchange(weight_terms)
+    slabs = exchange(grads)
+    leaving = call(
+        second_sum_kernel,
+        [("v", x) for x in (*second, *got)] + [("a", grads)],
+        [out(*second[0].shape)] * 2,
+    )
+    more = [partner(part, "seq", 1 - bit) for bit, part in enumerate(leaving)]
+    *leaving, keep_a, keep_b = call(
+        third_sum_kernel,
+        [("v", x) for x in (*third, *keep, *got, *more)] + [("a", slabs)],
+        [out(*third[0].shape)] * 2 + [out(*keep[0].shape, dtype=f32)] * 2,
+    )
+    rest = [partner(part, "seq", 2) for part in leaving]
     (grad_input,) = call(
         input_kernel,
-        [shape(rows, width)],
-        [token_grads, wq, wk, wv, field, scaled],
-        6 * rows * width * inner,
+        [("v", x) for x in (slabs, wq, wk, wv, field, scaled)],
+        [out(rows, width)],
     )
     route = [
         (s * parts + d, (s - 1) * parts + parts - 1 - d)
@@ -553,14 +566,18 @@
         for d in range(parts)
     ]
     moved = lax.ppermute(grad_input, ("section", "seq"), route)
-    grad_out = sum_to_owner(*terms)
     grad_q, grad_k, grad_v = call(
-        turn_kernel, [shape(1, width // parts, inner, dtype=f32)] * 3, [weight_terms]
+        turn_kernel, [("v", slabs)], [out(1, width // parts, inner, dtype=f32)] * 3
+    )
+    (grad_out,) = call(
+        last_sum_kernel,
+        [("v", x) for x in (keep_a, keep_b, *rest)],
+        [out(1, keep_a.shape[0], 2 * width, dtype=f32)],
     )
     (carry,) = call(
-        reorder_kernel, [shape(1, rows, width)], [flip_order[0][:, None], moved], 2 * rows * rows * width
-    )
-    return (carry, grad_q, grad_k, grad_v, grad_out[None])
+        reorder_kernel, [("v", flip_order[0][:, None]), ("v", moved)], [out(1, rows, width)]
+    )
+    return (carry, grad_q, grad_k, grad_v, grad_out)
 
 
 def solution(mesh):

time: 150 us -> 157 us (1.047)
  blocking collectives: 34.7 us -> 13.4 us
  waiting for transfers between devices: 30.8 us -> 51.2 us
  local copies, waits for them, and re-layouts: 18 us -> 30.8 us
  other arithmetic: 6.03 us -> 0.99 us
    ppermute x10 -> x13, waiting for transfers between devices: 26.9 us -> 51.2 us  [partner(): return lax.ppermute(block, axis, route)]
    all_to_all x2 -> x1, blocking collectives: 34.7 us -> 13.4 us  [exchange(): return lax.all_to_all(slabs, 'seq', split_axis=0, concat_axis=0, tiled=True)]
    unnamed x56 -> x84, local copies, waits for them, and re-layouts: 15.5 us -> 26.7 us
    ppermute x1, starting transfers between devices: 14.7 us -> 8.89 us  [head_shards(): moved = lax.ppermute(grad_input, ('section', 'seq'), route)]
    ppermute x10 -> x13, starting transfers between devices: 12 us -> 17.4 us  [partner(): return lax.ppermute(block, axis, route)]
    convert_element_type x2 -> x0, other arithmetic: 3.34 us -> none  [low(): return matrix.astype(jnp.bfloat16)]
    ppermute x1, waiting for transfers between devices: 3.08 us -> 0.01 us  [head_shards(): moved = lax.ppermute(grad_input, ('section', 'seq'), route)]
    dynamic_slice x0 -> x2, local copies, waits for them, and re-layouts: none -> 2.33 us  [head_shards(): lax.dynamic_slice_in_dim(w, me[0] * HEAD_DIM, HEAD_DIM, axis=1)]
  transfers between devices with their start and end apart: 13 -> 16, of which waited for: 5 -> 6; matrix products, arithmetic and copies ran while one was open for 4% -> 3% of each run, Pallas kernels for 9% -> 6%
where the time goes in v5:
time: 157 us; the launch traced here: 156 us
  waiting for transfers between devices  51.2 us (33%)
  starting transfers between devices  35.1 us (22%)
  local copies, waits for them, and re-layouts  30.8 us (20%)
  Pallas kernels  23.6 us (15%)
  blocking collectives  13.4 us (9%)
    ppermute x13, waiting for transfers between devices, partner(): return lax.ppermute(block, axis, route)  51.2 us
    unnamed x84, local copies, waits for them, and re-layouts  26.7 us
    pallas_call x11, Pallas kernels, call(): pl.pallas_call(kernel, out_shape=tuple(outs), in_specs=[pl.BlockSpec(memo...  23.6 us
    ppermute x13, starting transfers between devices, partner(): return lax.ppermute(block, axis, route)  17.4 us
    all_to_all x1, blocking collectives, exchange(): return lax.all_to_all(slabs, 'seq', split_axis=0, concat_axis=0, tiled=True)  13.4 us
    ppermute x1, starting transfers between devices, head_shards(): moved = lax.ppermute(grad_input, ('section', 'seq'), route)  8.89 us
    all_to_all x2, starting transfers between devices, exchange(): return lax.all_to_all(slabs, 'seq', split_axis=0, concat_axis=0, tiled=True)  8.87 us
  transfers between devices with their start and end apart: 16, of which 6 were waited for; matrix products, arithmetic and copies ran while one was open for 3% of the time, Pallas kernels for 6%

profile of v5, /device:TPU:5, one launch (start us, length us, event | category | flops | bytes accessed | tf_op | source)
XLA Modules:
  0.0 156.1 jit_solution(9850086808817873226)
XLA Ops:
  0.6 2.4 %collective-permute-start.2 = (bf16[136,1024]{1,0:T(8,128)(2,1)}, bf16[136,1024]{1,0:T(8,128)(2,1)S(1)}, u32[]{:S(2)}, u32[]{:S(2)}) collective-permute-start(bf16[136,1024]{1,0:T(8,128)(2,1)} %bitcast.14), channel_id=1, source_target_pairs={{0,4},{4,0},{1,5},{5,1},{2,6},{6,2},{3,7},{7,3},{8,12},{12,8},{9,1... | collective-permute-start | bytes 835592 | tf_op jit(solution)/shard_map/ppermute | solution.py:22
  3.0 1.3 collective-permute-start.1
  4.3 1.2 collective-permute-start
  6.2 9.2 %collective-permute-done.2.refs_3_ = bf16[136,1024]{1,0:T(8,128)(2,1)S(1)} collective-permute-done((bf16[136,1024]{1,0:T(8,128)(2,1)}, bf16[136,1024]{1,0:T(8,128)(2,1)S(1)}, u32[]{:S(2)}, u32[]{:S(2)}) %collective-permute-start.2) | collective-permute-done | bytes 278560 | tf_op jit(solution)/shard_map/ppermute | solution.py:22
  15.4 1.2 collective-permute-start.4
  18.0 1.5 collective-permute-start.5
  19.8 2.3 %collective-permute-done.4.refs_5_ = bf16[136,1024]{1,0:T(8,128)(2,1)} collective-permute-done((bf16[136,1024]{1,0:T(8,128)(2,1)S(1)}, bf16[136,1024]{1,0:T(8,128)(2,1)}, u32[]{:S(2)}, u32[]{:S(2)}) %collective-permute-start.4) | collective-permute-done | bytes 278560 | tf_op jit(solution)/shard_map/ppermute | solution.py:22
  22.0 2.7 %collective-permute-start.6 = (bf16[136,1024]{1,0:T(8,128)(2,1)}, bf16[136,1024]{1,0:T(8,128)(2,1)}, u32[]{:S(2)}, u32[]{:S(2)}) collective-permute-start(bf16[136,1024]{1,0:T(8,128)(2,1)} %collective-permute-done.4.refs_5_), channel_id=1, source_target_pairs={{0,2},{2,0},{1,3},{3,1},{4,6},{6,4},{5,7},{7,5},{8,10},{10,8},{9,1... | collective-permute-start | bytes 835592 | tf_op jit(solution)/shard_map/ppermute | solution.py:22
  24.7 1.1 dynamic-slice_bitcast_fusion.2
  26.1 1.3 dynamic-slice_bitcast_fusion
  29.1 1.0 copy-done.16
  30.0 1.0 copy-done.22
  31.0 2.1 %shard_map.128 = (bf16[6,136,1024]{2,1,0:T(8,128)(2,1)S(1)}, f32[6,136,128]{2,1,0:T(8,128)S(1)}, f32[6,136,128]{2,1,0:T(8,128)S(1)}, f32[6,136,64]{2,1,0:T(8,128)S(1)}) custom-call(bf16[136,1024]{1,0:T(8,128)(2,1)S(1)} %bitcast.17, bf16[136,1024]{1,0:T(8,128)(2,1)S(1)} %copy-done.16, bf16[136,1024]{1,0:T(8,128)(2,1)S(1)} %collective-permute-done.1.refs_2_, ...), custom_call_target="tpu_custom_call" | custom-call | flops 1024 | bytes 1024 | tf_op jit(solution)/shard_map/pallas_call | solution.py:200
  33.1 5.0 %shard_map.129 = (bf16[2,136,1024]{2,1,0:T(8,128)(2,1)S(1)}, f32[2,136,128]{2,1,0:T(8,128)S(1)}, f32[2,136,128]{2,1,0:T(8,128)S(1)}, bf16[1088,1088]{1,0:T(8,128...) custom-call(s32[1]{0:T(128)} %bitcast.1.me_ref, ...), custom_call_target="tpu_custom_call" | custom-call | flops 1024 | bytes 1024 | tf_op jit(solution)/shard_map/pallas_call | solution.py:200
  38.1 1.4 copy-done.1
  41.1 13.4 %all_to_all.15.slab_ref = bf16[8,80,128]{2,1,0:T(8,128)(2,1)S(1)} all-to-all(bf16[8,80,128]{2,1,0:T(8,128)(2,1)S(1)} %get-tuple-element.48), channel_id=1, replica_groups=mesh['section'=4,'seq'=8] {'seq'}, dimensions={0} | all-to-all | bytes 327680 | tf_op jit(solution)/shard_map/all_to_all | solution.py:443
  54.5 2.1 %shard_map.130 = (bf16[136,2048]{1,0:T(8,128)(2,1)S(1)}, f32[136,1024]{1,0:T(8,128)S(1)}, bf16[8,80,128]{2,1,0:T(8,128)(2,1)}) custom-call(bf16[8,80,128]{2,1,0:T(8,128)(2,1)S(1)} %all_to_all.15.slab_ref, bf16[136,1024]{1,0:T(8,128)(2,1)S(1)} %bitcast.18, bf16[136,1024]{1,0:T(8,128)(2,1)S(1)} %bitcast.24, bf16[512,2048]{1,0:T(8,128)(2,1)S(1)} %bitcast.20), custom_call_target="tpu_custom_call" | custom-call | flops 1024 | bytes 1024 | tf_op jit(solution)/shard_map/pallas_call | solution.py:200
  58.3 3.6 %all-to-all-start.1 = ((bf16[8,80,128]{2,1,0:T(8,128)(2,1)}), bf16[8,80,128]{2,1,0:T(8,128)(2,1)S(1)}, u32[]{:S(2)}, u32[]{:S(2)}) async-start(bf16[8,80,128]{2,1,0:T(8,128)(2,1)} %get-tuple-element.49), calls=%async_computation.1 | async-start | bytes 327680 | tf_op jit(solution)/shard_map/all_to_all | solution.py:443
  61.9 1.0 copy-done.10
  62.9 1.8 %shard_map.131 = (bf16[256,1024]{1,0:T(8,128)(2,1)}, bf16[128,1024]{1,0:T(8,128)(2,1)S(1)}, bf16[64,1024]{1,0:T(8,128)(2,1)S(1)}, bf16[64,1024]{1,0:T(8,128)(2,1...) custom-call(s32[1]{0:T(128)} %bitcast.1.me_ref, ...), custom_call_target="tpu_custom_call" | custom-call | flops 1024 | bytes 1024 | tf_op jit(solution)/shard_map/pallas_call | solution.py:200
  69.5 1.7 %copy-done.2 = bf16[1088,1088]{1,0:T(8,128)(2,1)S(1)} copy-done((bf16[1088,1088]{1,0:T(8,128)(2,1)S(1)}, bf16[1088,1088]{1,0:T(8,128)(2,1)}, u32[]{:S(2)}) %copy-start.2) | copy-done | bytes 2367512
  71.2 1.1 copy-done.12
  72.3 1.0 copy-done.14
  73.3 1.0 copy-done.18
  74.3 1.0 copy-done.20
  75.2 0.9 copy-done.29
  76.1 0.9 copy-done.31
  77.0 5.9 %shard_map.132.refs_4_ = bf16[8,408,128]{2,1,0:T(8,128)(2,1)} custom-call(s32[1]{0:T(128)} %bitcast.1.me_ref, bf16[8,80,128]{2,1,0:T(8,128)(2,1)S(1)} %all-to-all-done.1.slab_ref, bf16[1088,1088]{1,0:T(8,128)(2,1)S(1)} %copy-done.2, bf16[1088,128]{1,0:T(8,128)(2,1)S(1)} %copy-done.18, bf16[1088,64]{1,0:T(8,128)(2,1)S(1)} %copy-done.20, ...), custom_call_target="tpu_custom_call" | custom-call | flops 1024 | bytes 1024 | tf_op jit(solution)/shard_map/pallas_call | solution.py:200
  82.9 5.3 %all-to-all-start.2 = ((bf16[8,408,128]{2,1,0:T(8,128)(2,1)}), bf16[8,408,128]{2,1,0:T(8,128)(2,1)S(1)}, u32[]{:S(2)}, u32[]{:S(2)}) async-start(bf16[8,408,128]{2,1,0:T(8,128)(2,1)} %shard_map.132.refs_4_), calls=%async_computation.2 | async-start | bytes 1671168 | tf_op jit(solution)/shard_map/all_to_all | solution.py:443
  88.2 1.5 collective-permute-start.8
  89.7 1.2 collective-permute-start.9
  90.9 18.3 %collective-permute-done.8.refs_2_.refs_4_ = bf16[256,1024]{1,0:T(8,128)(2,1)S(1)} collective-permute-done((bf16[256,1024]{1,0:T(8,128)(2,1)}, bf16[256,1024]{1,0:T(8,128)(2,1)S(1)}, u32[]{:S(2)}, u32[]{:S(2)}) %collective-permute-start.8) | collective-permute-done | bytes 524320 | tf_op jit(solution)/shard_map/ppermute | solution.py:22
  109.2 3.3 %collective-permute-done.9.refs_3_.refs_5_ = bf16[256,1024]{1,0:T(8,128)(2,1)S(1)} collective-permute-done((bf16[256,1024]{1,0:T(8,128)(2,1)}, bf16[256,1024]{1,0:T(8,128)(2,1)S(1)}, u32[]{:S(2)}, u32[]{:S(2)}) %collective-permute-start.9) | collective-permute-done | bytes 524320 | tf_op jit(solution)/shard_map/ppermute | solution.py:22
  112.5 0.9 copy-done.25
  113.4 0.9 copy-done.27
  114.4 0.9 shard_map.136
  115.5 1.6 %collective-permute-start.11 = (bf16[128,1024]{1,0:T(8,128)(2,1)}, bf16[128,1024]{1,0:T(8,128)(2,1)}, u32[]{:S(2)}, u32[]{:S(2)}) collective-permute-start(bf16[128,1024]{1,0:T(8,128)(2,1)} %get-tuple-element.82), channel_id=1, source_target_pairs={{0,1},{1,0},{2,3},{3,2},{4,5},{5,4},{6,7},{7,6},{8,9},{9,8},{10,11... | collective-permute-start | bytes 786440 | tf_op jit(solution)/shard_map/ppermute | solution.py:22
  117.1 1.2 copy-done.5
  118.3 1.2 copy-done.6
  119.5 1.1 copy-done.8
  120.6 1.3 shard_map.133
  121.9 8.9 %collective-permute-start.7 = (bf16[136,1024]{1,0:T(8,128)(2,1)S(1)}, bf16[136,1024]{1,0:T(8,128)(2,1)S(1)}, u32[]{:S(2)}, u32[]{:S(2)}) collective-permute-start(bf16[136,1024]{1,0:T(8,128)(2,1)S(1)} %shard_map.133), channel_id=1, source_target_pairs={{8,7},{9,6},{10,5},{11,4},{12,3},{13,2},{14,1},{15,0},{16,15},{17,... | collective-permute-start | bytes 835592 | tf_op jit(solution)/shard_map/ppermute | solution.py:568
  130.9 1.8 %shard_map.137 = (bf16[64,1024]{1,0:T(8,128)(2,1)}, bf16[64,1024]{1,0:T(8,128)(2,1)}, f32[64,1024]{1,0:T(8,128)S(1)}, f32[64,1024]{1,0:T(8,128)S(1)}) custom-call(bf16[64,1024]{1,0:T(8,128)(2,1)S(1)} %copy-done.33, bf16[64,1024]{1,0:T(8,128)(2,1)S(1)} %copy-done.37, bf16[64,1024]{1,0:T(8,128)(2,1)S(1)} %copy-done.35, bf16[64,1024]{1,0:T(8,128)(2,1)S(1)} %copy-done.39, ...), custom_call_target="tpu_custom_call" | custom-call | flops 1024 | bytes 1024 | tf_op jit(solution)/shard_map/pallas_call | solution.py:200
  132.7 2.4 %collective-permute-start.13 = (bf16[64,1024]{1,0:T(8,128)(2,1)}, bf16[64,1024]{1,0:T(8,128)(2,1)S(1)}, u32[]{:S(2)}, u32[]{:S(2)}) collective-permute-start(bf16[64,1024]{1,0:T(8,128)(2,1)} %get-tuple-element.86), channel_id=1, source_target_pairs={{0,4},{4,0},{1,5},{5,1},{2,6},{6,2},{3,7},{7,3},{8,12},{12,8},{9,1... | collective-permute-start | bytes 393224 | tf_op jit(solution)/shard_map/ppermute | solution.py:22
  135.2 1.0 shard_map.135
  136.2 15.3 %collective-permute-done.12.got_a = bf16[64,1024]{1,0:T(8,128)(2,1)S(1)} collective-permute-done((bf16[64,1024]{1,0:T(8,128)(2,1)}, bf16[64,1024]{1,0:T(8,128)(2,1)S(1)}, u32[]{:S(2)}, u32[]{:S(2)}) %collective-permute-start.12) | collective-permute-done | bytes 131104 | tf_op jit(solution)/shard_map/ppermute | solution.py:22
  151.5 2.8 %collective-permute-done.13.got_b = bf16[64,1024]{1,0:T(8,128)(2,1)S(1)} collective-permute-done((bf16[64,1024]{1,0:T(8,128)(2,1)}, bf16[64,1024]{1,0:T(8,128)(2,1)S(1)}, u32[]{:S(2)}, u32[]{:S(2)}) %collective-permute-start.13) | collective-permute-done | bytes 131104 | tf_op jit(solution)/shard_map/ppermute | solution.py:22
  155.1 1.0 shard_map.134
  (91 shorter events, 13.6 us)
Async XLA Ops:
  0.6 28.4 %copy-start = (bf16[1,136,1024]{2,1,0:T(8,128)(2,1)S(1)}, bf16[1,136,1024]{2,1,0:T(8,128)(2,1)}, u32[]{:S(2)}) copy-start(bf16[1,136,1024]{2,1,0:T(8,128)(2,1)} %param.9) | copy-start | bytes 835588
  0.6 14.7 %collective-permute-start.2 = (bf16[136,1024]{1,0:T(8,128)(2,1)}, bf16[136,1024]{1,0:T(8,128)(2,1)S(1)}, u32[]{:S(2)}, u32[]{:S(2)}) collective-permute-start(bf16[136,1024]{1,0:T(8,128)(2,1)} %bitcast.14), channel_id=1, source_target_pairs={{0,4},{4,0},{1,5},{5,1},{2,6},{6,2},{3,7},{7,3},{8,12},{12,8},{9,1... | collective-permute-start | bytes 835592 | tf_op jit(solution)/shard_map/ppermute | solution.py:22
  3.0 16.5 %collective-permute-start.1 = (bf16[136,1024]{1,0:T(8,128)(2,1)}, bf16[136,1024]{1,0:T(8,128)(2,1)S(1)}, u32[]{:S(2)}, u32[]{:S(2)}) collective-permute-start(bf16[136,1024]{1,0:T(8,128)(2,1)} %bitcast.15), channel_id=1, source_target_pairs={{0,2},{2,0},{1,3},{3,1},{4,6},{6,4},{5,7},{7,5},{8,10},{10,8},{9,1... | collective-permute-start | bytes 835592 | tf_op jit(solution)/shard_map/ppermute | solution.py:22
  4.3 23.3 %collective-permute-start = (bf16[136,1024]{1,0:T(8,128)(2,1)}, bf16[136,1024]{1,0:T(8,128)(2,1)S(1)}, u32[]{:S(2)}, u32[]{:S(2)}) collective-permute-start(bf16[136,1024]{1,0:T(8,128)(2,1)} %bitcast.16), channel_id=1, source_target_pairs={{0,1},{1,0},{2,3},{3,2},{4,5},{5,4},{6,7},{7,6},{8,9},{9,8},{10,11... | collective-permute-start | bytes 835592 | tf_op jit(solution)/shard_map/ppermute | solution.py:22
  15.4 6.7 %collective-permute-start.4 = (bf16[136,1024]{1,0:T(8,128)(2,1)S(1)}, bf16[136,1024]{1,0:T(8,128)(2,1)}, u32[]{:S(2)}, u32[]{:S(2)}) collective-permute-start(bf16[136,1024]{1,0:T(8,128)(2,1)S(1)} %collective-permute-done.2.refs_3_), channel_id=1, source_target_pairs={{0,1},{1,0},{2,3},{3,2},{4,5},{5,4},{6,7},{7,6},{8,9},{9,8},{10,11... | collective-permute-start | bytes 835592 | tf_op jit(solution)/shard_map/ppermute | solution.py:22
  18.0 15.1 %collective-permute-start.5 = (bf16[136,1024]{1,0:T(8,128)(2,1)S(1)}, bf16[136,1024]{1,0:T(8,128)(2,1)}, u32[]{:S(2)}, u32[]{:S(2)}) collective-permute-start(bf16[136,1024]{1,0:T(8,128)(2,1)S(1)} %collective-permute-done.2.refs_3_), channel_id=1, source_target_pairs={{0,2},{2,0},{1,3},{3,1},{4,6},{6,4},{5,7},{7,5},{8,10},{10,8},{9,1... | collective-permute-start | bytes 835592 | tf_op jit(solution)/shard_map/ppermute | solution.py:22
  19.5 8.9 %collective-permute-start.3 = (bf16[136,1024]{1,0:T(8,128)(2,1)S(1)}, bf16[136,1024]{1,0:T(8,128)(2,1)S(1)}, u32[]{:S(2)}, u32[]{:S(2)}) collective-permute-start(bf16[136,1024]{1,0:T(8,128)(2,1)S(1)} %collective-permute-done.1.refs_2_), channel_id=1, source_target_pairs={{0,1},{1,0},{2,3},{3,2},{4,5},{5,4},{6,7},{7,6},{8,9},{9,8},{10,11... | collective-permute-start | bytes 835592 | tf_op jit(solution)/shard_map/ppermute | solution.py:22
  22.0 11.1 %collective-permute-start.6 = (bf16[136,1024]{1,0:T(8,128)(2,1)}, bf16[136,1024]{1,0:T(8,128)(2,1)}, u32[]{:S(2)}, u32[]{:S(2)}) collective-permute-start(bf16[136,1024]{1,0:T(8,128)(2,1)} %collective-permute-done.4.refs_5_), channel_id=1, source_target_pairs={{0,2},{2,0},{1,3},{3,1},{4,6},{6,4},{5,7},{7,5},{8,10},{10,8},{9,1... | collective-permute-start | bytes 835592 | tf_op jit(solution)/shard_map/ppermute | solution.py:22
  27.4 27.2 %copy-start.23 = (bf16[1,136,1024]{2,1,0:T(8,128)(2,1)S(1)}, bf16[1,136,1024]{2,1,0:T(8,128)(2,1)}, u32[]{:S(2)}) copy-start(bf16[1,136,1024]{2,1,0:T(8,128)(2,1)} %param.10) | copy-start | bytes 835588
  27.6 26.9 %copy-start.3 = (bf16[1,512,2048]{2,1,0:T(8,128)(2,1)S(1)}, bf16[1,512,2048]{2,1,0:T(8,128)(2,1)}, u32[]{:S(2)}) copy-start(bf16[1,512,2048]{2,1,0:T(8,128)(2,1)} %param.14) | copy-start | bytes 6291460
  29.1 1.0 copy-start.16
  30.0 1.0 copy-start.22
  33.1 23.5 %copy-start.13 = (f32[6,136,128]{2,1,0:T(8,128)}, f32[6,136,128]{2,1,0:T(8,128)S(1)}, u32[]{:S(2)}) copy-start(f32[6,136,128]{2,1,0:T(8,128)S(1)} %get-tuple-element.65.refs_2_) | copy-start | bytes 1253380
  38.1 1.4 copy-start.1
  41.1 15.5 %copy-start.17 = (bf16[1088,128]{1,0:T(8,128)(2,1)}, bf16[1088,128]{1,0:T(8,128)(2,1)S(1)}, u32[]{:S(2)}) copy-start(bf16[1088,128]{1,0:T(8,128)(2,1)S(1)} %get-tuple-element.61.qk_ref) | copy-start | bytes 835588
  41.1 15.5 %copy-start.28 = (f32[2,136,128]{2,1,0:T(8,128)}, f32[2,136,128]{2,1,0:T(8,128)S(1)}, u32[]{:S(2)}) copy-start(f32[2,136,128]{2,1,0:T(8,128)S(1)} %get-tuple-element.67.refs_4_) | copy-start | bytes 417796
  41.1 15.5 %copy-start.30 = (f32[2,136,128]{2,1,0:T(8,128)}, f32[2,136,128]{2,1,0:T(8,128)S(1)}, u32[]{:S(2)}) copy-start(f32[2,136,128]{2,1,0:T(8,128)S(1)} %get-tuple-element.68.refs_5_) | copy-start | bytes 417796
  56.6 0.8 copy-start.7
  57.5 0.8 copy-start.9
  58.3 11.2 %all-to-all-start.1 = ((bf16[8,80,128]{2,1,0:T(8,128)(2,1)}), bf16[8,80,128]{2,1,0:T(8,128)(2,1)S(1)}, u32[]{:S(2)}, u32[]{:S(2)}) async-start(bf16[8,80,128]{2,1,0:T(8,128)(2,1)} %get-tuple-element.49), calls=%async_computation.1 | async-start | bytes 327680 | tf_op jit(solution)/shard_map/all_to_all | solution.py:443
  61.9 1.1 copy-start.10
  68.7 0.8 copy-start.40
  69.5 1.7 %copy-start.2 = (bf16[1088,1088]{1,0:T(8,128)(2,1)S(1)}, bf16[1088,1088]{1,0:T(8,128)(2,1)}, u32[]{:S(2)}) copy-start(bf16[1088,1088]{1,0:T(8,128)(2,1)} %copy-done.1) | copy-start | bytes 7102468
  71.2 1.1 copy-start.12
  72.3 1.0 copy-start.14
  73.3 1.0 copy-start.18
  74.3 1.0 copy-start.20
  75.2 0.9 copy-start.29
  76.1 0.9 copy-start.31
  82.9 34.2 %copy-start.4 = (bf16[1,1024,512]{2,1,0:T(8,128)(2,1)S(1)}, bf16[1,1024,512]{2,1,0:T(8,128)(2,1)}, u32[]{:S(2)}) copy-start(bf16[1,1024,512]{2,1,0:T(8,128)(2,1)} %param.11) | copy-start | bytes 3145732
  82.9 34.2 %all-to-all-start.2 = ((bf16[8,408,128]{2,1,0:T(8,128)(2,1)}), bf16[8,408,128]{2,1,0:T(8,128)(2,1)S(1)}, u32[]{:S(2)}, u32[]{:S(2)}) async-start(bf16[8,408,128]{2,1,0:T(8,128)(2,1)} %shard_map.132.refs_4_), calls=%async_computation.2 | async-start | bytes 1671168 | tf_op jit(solution)/shard_map/all_to_all | solution.py:443
  88.2 21.0 %collective-permute-start.8 = (bf16[256,1024]{1,0:T(8,128)(2,1)}, bf16[256,1024]{1,0:T(8,128)(2,1)S(1)}, u32[]{:S(2)}, u32[]{:S(2)}) collective-permute-start(bf16[256,1024]{1,0:T(8,128)(2,1)} %get-tuple-element.77), channel_id=1, source_target_pairs={{0,1},{1,0},{2,3},{3,2},{4,5},{5,4},{6,7},{7,6},{8,9},{9,8},{10,11... | collective-permute-start | bytes 1572872 | tf_op jit(solution)/shard_map/ppermute | solution.py:22
  89.7 22.8 %collective-permute-start.9 = (bf16[256,1024]{1,0:T(8,128)(2,1)}, bf16[256,1024]{1,0:T(8,128)(2,1)S(1)}, u32[]{:S(2)}, u32[]{:S(2)}) collective-permute-start(bf16[256,1024]{1,0:T(8,128)(2,1)} %copy-done.40), channel_id=1, source_target_pairs={{0,2},{2,0},{1,3},{3,1},{4,6},{6,4},{5,7},{7,5},{8,10},{10,8},{9,1... | collective-permute-start | bytes 1572872 | tf_op jit(solution)/shard_map/ppermute | solution.py:22
  112.5 1.0 copy-start.25
  113.4 0.9 copy-start.27
  115.2 15.6 %collective-permute-start.10 = (bf16[128,1024]{1,0:T(8,128)(2,1)}, bf16[128,1024]{1,0:T(8,128)(2,1)}, u32[]{:S(2)}, u32[]{:S(2)}) collective-permute-start(bf16[128,1024]{1,0:T(8,128)(2,1)} %get-tuple-element.81), channel_id=1, source_target_pairs={{0,2},{2,0},{1,3},{3,1},{4,6},{6,4},{5,7},{7,5},{8,10},{10,8},{9,1... | collective-permute-start | bytes 786440 | tf_op jit(solution)/shard_map/ppermute | solution.py:22
  115.5 15.4 %collective-permute-start.11 = (bf16[128,1024]{1,0:T(8,128)(2,1)}, bf16[128,1024]{1,0:T(8,128)(2,1)}, u32[]{:S(2)}, u32[]{:S(2)}) collective-permute-start(bf16[128,1024]{1,0:T(8,128)(2,1)} %get-tuple-element.82), channel_id=1, source_target_pairs={{0,1},{1,0},{2,3},{3,2},{4,5},{5,4},{6,7},{7,6},{8,9},{9,8},{10,11... | collective-permute-start | bytes 786440 | tf_op jit(solution)/shard_map/ppermute | solution.py:22
  117.1 1.2 copy-start.5
  118.3 1.2 copy-start.6
  119.5 1.1 copy-start.8
  120.6 10.3 %copy-start.33 = (bf16[64,1024]{1,0:T(8,128)(2,1)S(1)}, bf16[64,1024]{1,0:T(8,128)(2,1)}, u32[]{:S(2)}) copy-start(bf16[64,1024]{1,0:T(8,128)(2,1)} %copy-done.32) | copy-start | bytes 393220
  120.6 10.3 %copy-start.35 = (bf16[64,1024]{1,0:T(8,128)(2,1)S(1)}, bf16[64,1024]{1,0:T(8,128)(2,1)}, u32[]{:S(2)}) copy-start(bf16[64,1024]{1,0:T(8,128)(2,1)} %copy-done.34) | copy-start | bytes 393220
  120.6 10.3 %copy-start.37 = (bf16[64,1024]{1,0:T(8,128)(2,1)S(1)}, bf16[64,1024]{1,0:T(8,128)(2,1)}, u32[]{:S(2)}) copy-start(bf16[64,1024]{1,0:T(8,128)(2,1)} %copy-done.36) | copy-start | bytes 393220
  120.6 10.3 %copy-start.39 = (bf16[64,1024]{1,0:T(8,128)(2,1)S(1)}, bf16[64,1024]{1,0:T(8,128)(2,1)}, u32[]{:S(2)}) copy-start(bf16[64,1024]{1,0:T(8,128)(2,1)} %copy-done.38) | copy-start | bytes 393220
  121.9 13.1 %copy-start.41 = (s32[1,136]{1,0:T(1,128)S(1)}, s32[1,136]{1,0:T(1,128)}, u32[]{:S(2)}) copy-start(s32[1,136]{1,0:T(1,128)} %param.16) | copy-start | bytes 1636
  121.9 33.2 %collective-permute-start.7 = (bf16[136,1024]{1,0:T(8,128)(2,1)S(1)}, bf16[136,1024]{1,0:T(8,128)(2,1)S(1)}, u32[]{:S(2)}, u32[]{:S(2)}) collective-permute-start(bf16[136,1024]{1,0:T(8,128)(2,1)S(1)} %shard_map.133), channel_id=1, source_target_pairs={{8,7},{9,6},{10,5},{11,4},{12,3},{13,2},{14,1},{15,0},{16,15},{17,... | collective-permute-start | bytes 835592 | tf_op jit(solution)/shard_map/ppermute | solution.py:568
  132.7 18.8 %collective-permute-start.12 = (bf16[64,1024]{1,0:T(8,128)(2,1)}, bf16[64,1024]{1,0:T(8,128)(2,1)S(1)}, u32[]{:S(2)}, u32[]{:S(2)}) collective-permute-start(bf16[64,1024]{1,0:T(8,128)(2,1)} %get-tuple-element.85), channel_id=1, source_target_pairs={{0,4},{4,0},{1,5},{5,1},{2,6},{6,2},{3,7},{7,3},{8,12},{12,8},{9,1... | collective-permute-start | bytes 393224 | tf_op jit(solution)/shard_map/ppermute | solution.py:22
  132.7 21.6 %collective-permute-start.13 = (bf16[64,1024]{1,0:T(8,128)(2,1)}, bf16[64,1024]{1,0:T(8,128)(2,1)S(1)}, u32[]{:S(2)}, u32[]{:S(2)}) collective-permute-start(bf16[64,1024]{1,0:T(8,128)(2,1)} %get-tuple-element.86), channel_id=1, source_target_pairs={{0,4},{4,0},{1,5},{5,1},{2,6},{6,2},{3,7},{7,3},{8,12},{12,8},{9,1... | collective-permute-start | bytes 393224 | tf_op jit(solution)/shard_map/ppermute | solution.py:22
  (10 other events, 7.0 us)

commit v6 on v5

--- a/solution.py
+++ b/solution.py
@@ -194,7 +194,7 @@
 PACKED = 80
 
 
-def call(kernel, ins, outs, scratch=()):
+def call(kernel, microseconds, ins, outs, scratch=()):
     spaces = {"s": pltpu.SMEM, "v": pltpu.VMEM, "a": pl.ANY}
     places, operands = zip(*ins)
     return pl.pallas_call(
@@ -204,7 +204,9 @@
         out_specs=(pl.BlockSpec(memory_space=pltpu.VMEM),) * len(outs),
         scratch_shapes=list(scratch),
         compiler_params=pltpu.CompilerParams(vmem_limit_bytes=14 * 2**20),
-        cost_estimate=pl.CostEstimate(flops=1024, bytes_accessed=1024, transcendentals=0),
+        cost_estimate=pl.CostEstimate(
+            flops=int(microseconds * 1e9), bytes_accessed=1024, transcendentals=0
+        ),
     )(*operands)
 
 
@@ -251,6 +253,25 @@
     return normed, raw * scale, scale, value
 
 
+def select_kernel(me_ref, wq_ref, wk_ref, wv_ref, out_ref, *scratch):
+    held, semaphores = scratch[:3], scratch[3]
+    odd = lax.rem(me_ref[0], 2) == 1
+    pair = pl.multiple_of(lax.div(me_ref[0], 2) * 2 * HEAD_DIM, 2 * HEAD_DIM)
+    copies = [
+        pltpu.make_async_copy(ref.at[:, pl.ds(pair, 2 * HEAD_DIM)], kept, semaphores.at[i])
+        for i, (ref, kept) in enumerate(zip((wq_ref, wk_ref, wv_ref), held))
+    ]
+    for copy in copies:
+        copy.start()
+    for copy in copies:
+        copy.wait()
+    q, k, v = [wide(kept[...]) for kept in held]
+    lower = low_lanes(q)
+    qk = jnp.where(lower, jnp.where(odd, swap(q), q), jnp.where(odd, k, swap(k)))
+    out_ref[:, : 2 * HEAD_DIM] = low(qk)
+    out_ref[:, 2 * HEAD_DIM :] = low(jnp.where(odd, swap(v), v)[:, :HEAD_DIM])
+
+
 def project_kernel(*refs):
     blocks, (weight_ref, normed_ref, unit_ref, scale_ref, value_ref) = refs[:-5], refs[-5:]
     for m, block in enumerate(blocks):
@@ -268,9 +289,9 @@
 
 
 def attend_kernel(
-    me_ref, unit_ref, value_ref, near_ref, last_ref, weight_ref, row_ids, column_ids, *out_refs
+    unit_ref, value_ref, near_ref, last_ref, weight_ref, row_ids, column_ids, *out_refs
 ):
-    normed_ref, late_unit, late_scale, prob_ref, qk_ref, v_ref, out_t_ref, out_ref = out_refs
+    normed_ref, late_unit, late_scale, prob_ref, qk_ref, v_ref, out_t_ref = out_refs[:7]
     early, rows = unit_ref.shape[:2]
     units = [unit_ref[m] for m in range(early)]
     values = [value_ref[m] for m in range(early)]
@@ -296,17 +317,18 @@
         out_t = dot(value, probs, ((0,), (0,)))
         out_t_ref[:, start:stop] = out_t.astype(jnp.bfloat16).astype(jnp.float32)
     out = jnp.transpose(out_t_ref[...])
-    for m in range(parts):
-        group = me_ref[0] ^ DISTANCES[m]
-        out_ref[group] = pack(out[m * rows : (m + 1) * rows]).astype(jnp.bfloat16)
-
-
-def affine_kernel(slab_ref, act_ref, inc_ref, w_ref, aff_ref, up_ref, out_ref):
-    heads = slab_ref.shape[0]
+    for m, out_ref in enumerate(out_refs[7:]):
+        out_ref[...] = low(pack(out[m * rows : (m + 1) * rows]))
+
+
+def affine_kernel(me_ref, *refs):
+    slabs, (act_ref, inc_ref, w_ref, aff_ref, up_ref) = refs[:HEADS], refs[HEADS : HEADS + 5]
+    out_refs, held_ref = refs[HEADS + 5 : -1], refs[-1]
     rows, width = act_ref.shape
-    attended = jnp.concatenate(
-        [unpack(slab_ref[h].astype(jnp.float32), rows) for h in range(heads)], axis=1
-    ).astype(jnp.bfloat16)
+    for m, slab in enumerate(slabs):
+        held_ref[me_ref[0] ^ DISTANCES[m]] = slab[...]
+    attended = jnp.concatenate([unpack(wide(held_ref[h]), rows) for h in range(HEADS)], axis=1)
+    attended = low(attended)
     factor = jnp.exp(-dot(attended, w_ref[:, width:]))
     scaled = inc_ref[...].astype(jnp.float32) * factor
     up_ref[...] = scaled
@@ -315,20 +337,19 @@
     grad_affine = jnp.concatenate([-scaled, 1.0 - latent_part], axis=1).astype(jnp.bfloat16)
     aff_ref[...] = grad_affine
     grad = dot(grad_affine, w_ref[...], ((1,), (1,)))
-    for h in range(heads):
-        block = grad[:, h * HEAD_DIM : (h + 1) * HEAD_DIM]
-        out_ref[h] = pack(block).astype(jnp.bfloat16)
+    for h in range(HEADS):
+        held_ref[h] = low(pack(grad[:, h * HEAD_DIM : (h + 1) * HEAD_DIM]))
+    for m, out_ref in enumerate(out_refs):
+        out_ref[...] = held_ref[me_ref[0] ^ DISTANCES[m]]
 
 
 ORDERS = (((1, 5, 3, 7), (2, 6), (4,), (0,)), ((2, 6, 3, 7), (1, 5), (4,), (0,)))
 
 
-def out_term_kernel(me_ref, slab_ref, aff_ref, *out_refs):
-    heads, rows = slab_ref.shape[0], aff_ref.shape[0]
-    width = aff_ref.shape[1] // 2
-    columns = [
-        unpack(slab_ref[me_ref[0] ^ m].astype(jnp.float32), rows) for m in range(heads)
-    ]
+def out_term_kernel(*refs):
+    slabs, aff_ref, out_refs = refs[:HEADS], refs[HEADS], refs[HEADS + 1 :]
+    rows, width = aff_ref.shape[0], aff_ref.shape[1] // 2
+    columns = {m: unpack(wide(slab[...]), rows) for m, slab in zip(DISTANCES, slabs)}
     for half, order in enumerate(ORDERS):
         right = aff_ref[:, half * width : (half + 1) * width]
         for out_ref, group in zip(out_refs[4 * half : 4 * half + 4], order):
@@ -336,16 +357,14 @@
             out_ref[...] = dot(left, right, ((0,), (0,))).astype(jnp.bfloat16)
 
 
-def backward_kernel(me_ref, slab_ref, prob_ref, qk_ref, v_ref, out_t_ref, *refs):
-    early, late, (out_ref, gk_ref, gv_ref, gq_ref) = refs[:3], refs[3:6], refs[6:]
-    parts, rows = slab_ref.shape[0], early[0].shape[1]
-    tokens = parts * rows
-    me = me_ref[0]
-    first = early[0].shape[0]
-    grad_f = jnp.concatenate(
-        [unpack(slab_ref[me ^ DISTANCES[m]].astype(jnp.float32), rows) for m in range(parts)], axis=0
-    )
+def backward_kernel(me_ref, *refs):
+    slabs, (prob_ref, qk_ref, v_ref, out_t_ref) = refs[:HEADS], refs[HEADS : HEADS + 4]
+    early, late = refs[HEADS + 4 : HEADS + 7], refs[HEADS + 7 : HEADS + 10]
+    out_refs, (gk_ref, gv_ref, gq_ref, held_ref) = refs[HEADS + 10 : -4], refs[-4:]
+    first, rows = early[0].shape[:2]
+    grad_f = jnp.concatenate([unpack(wide(slab[...]), rows) for slab in slabs], axis=0)
     grad = grad_f.astype(jnp.bfloat16)
+    tokens = grad_f.shape[0]
     grad_t = jnp.transpose(grad_f)
     correction = jnp.sum(grad_t * out_t_ref[...], axis=0, keepdims=True)
     grad_t = grad_t.astype(jnp.bfloat16)
@@ -363,7 +382,7 @@
         gq_ref[:, start:stop] = dot(key, scores, ((0,), (0,)))
     grad_q = jnp.transpose(gq_ref[...])
     qk_sum = v_sum = 0.0
-    for m in range(parts):
+    for m, out_ref in enumerate(out_refs):
         own = slice(m * rows, (m + 1) * rows)
         normed, unit, scale = [
             early[i][m] if m < first else late[i][m - first] for i in range(3)
@@ -371,23 +390,26 @@
         raw = jnp.concatenate([grad_q[own], gk_ref[own, :]], axis=1) * HEAD_DIM ** (-0.5)
         back = scale * (raw - unit * (half_sums(raw * unit) / HEAD_DIM))
         back, grad_v = back.astype(jnp.bfloat16), gv_ref[own, :]
-        out_ref[me ^ DISTANCES[m], :PACKED, :] = pack(grad_v).astype(jnp.bfloat16)
-        out_ref[me ^ DISTANCES[m], PACKED : PACKED + rows, :] = back
+        out_ref[:PACKED, :] = low(pack(grad_v))
+        out_ref[PACKED : PACKED + rows, :] = back
         qk_sum = qk_sum + dot(back, normed, ((0,), (0,)))
         v_sum = v_sum + dot(grad_v.astype(jnp.bfloat16), normed, ((0,), (0,)))
-    step = qk_sum.shape[1] // parts
-    middle = PACKED + rows + 2 * HEAD_DIM
-    for g in range(parts):
+    step = qk_sum.shape[1] // HEADS
+    for g in range(HEADS):
         own = slice(g * step, (g + 1) * step)
-        out_ref[g, PACKED + rows : middle, :] = qk_sum[:, own].astype(jnp.bfloat16)
-        out_ref[g, middle:, :] = v_sum[:, own].astype(jnp.bfloat16)
-
-
-def turn_kernel(slab_ref, *out_refs):
-    start = slab_ref.shape[1] - 3 * HEAD_DIM
+        held_ref[g] = low(jnp.concatenate([qk_sum[:, own], v_sum[:, own]], axis=0))
+    for m, out_ref in enumerate(out_refs):
+        out_ref[PACKED + rows :, :] = held_ref[me_ref[0] ^ DISTANCES[m]]
+
+
+def turn_kernel(me_ref, *refs):
+    slabs, out_refs, held_ref = refs[:HEADS], refs[HEADS:-1], refs[-1]
+    start = slabs[0].shape[0] - 3 * HEAD_DIM
+    for m, slab in enumerate(slabs):
+        held_ref[me_ref[0] ^ DISTANCES[m]] = slab[start:, :]
     for i, out_ref in enumerate(out_refs):
-        own = slice(start + i * HEAD_DIM, start + (i + 1) * HEAD_DIM)
-        heads = [slab_ref[h, own, :].astype(jnp.float32) for h in range(slab_ref.shape[0])]
+        own = slice(i * HEAD_DIM, (i + 1) * HEAD_DIM)
+        heads = [wide(held_ref[h, own, :]) for h in range(HEADS)]
         out_ref[0] = jnp.transpose(jnp.concatenate(heads, axis=0))
 
 
@@ -401,7 +423,7 @@
     for i in range(2):
         third, keep, got, more = [ref[...] for ref in refs[i:8:2]]
         size = third.shape[0]
-        leaving, staying = refs[9 + i], refs[11 + i]
+        leaving, staying = refs[8 + i], refs[10 + i]
         leaving[...] = low(wide(third) + wide(got[size : 2 * size]) + wide(more[size:]))
         staying[...] = wide(keep) + wide(got[:size]) + wide(more[:size])
 
@@ -412,17 +434,19 @@
         out_ref[0, :, i * width : (i + 1) * width] = keep[...] + wide(got[...])
 
 
-def input_kernel(slab_ref, wq_ref, wk_ref, wv_ref, act_ref, up_ref, out_ref):
+def input_kernel(me_ref, *refs):
+    slabs, (wq_ref, wk_ref, wv_ref, act_ref, up_ref, out_ref) = refs[:HEADS], refs[HEADS:-1]
+    held_ref = refs[-1]
     rows = act_ref.shape[0]
+    for m, slab in enumerate(slabs):
+        held_ref[me_ref[0] ^ DISTANCES[m]] = slab[: PACKED + rows, :]
     unit, row_scale = normalize(act_ref[...])
     queries, keys, values = [], [], []
     for pair in range(HEADS // 2):
-        even, odd = [
-            slab_ref[2 * pair + i, : PACKED + rows, :].astype(jnp.float32) for i in range(2)
-        ]
-        low = low_lanes(even[PACKED:])
-        queries.append(jnp.where(low, even[PACKED:], swap(odd[PACKED:])))
-        keys.append(jnp.where(low, swap(even[PACKED:]), odd[PACKED:]))
+        even, odd = [wide(held_ref[2 * pair + i]) for i in range(2)]
+        lower = low_lanes(even[PACKED:])
+        queries.append(jnp.where(lower, even[PACKED:], swap(odd[PACKED:])))
+        keys.append(jnp.where(lower, swap(even[PACKED:]), odd[PACKED:]))
         values += [unpack(even[:PACKED], rows), unpack(odd[:PACKED], rows)]
     total = 0.0
     for parts, ref in ((queries, wq_ref), (keys, wk_ref), (values, wv_ref)):
@@ -439,8 +463,13 @@
     out_ref[0] = dot(chosen, rows_ref[...]).astype(jnp.bfloat16)
 
 
+def hop(block, distance):
+    route = [(i, i ^ distance) for i in range(lax.axis_size("seq"))]
+    return lax.ppermute(block, "seq", route)
+
+
 def exchange(slabs):
-    return lax.all_to_all(slabs, "seq", split_axis=0, concat_axis=0, tiled=True)
+    return [hop(slab, m) if m else slab for m, slab in zip(DISTANCES, slabs)]
 
 
 def spread(block):
@@ -485,13 +514,17 @@
     blocks = spread(field)
     order = me[0] ^ jnp.array(DISTANCES, jnp.int32)
     ids = jnp.take(block_ids.reshape(parts, rows), order, axis=0).reshape(tokens)
-    weight = jnp.concatenate(
-        [lax.dynamic_slice_in_dim(w, me[0] * HEAD_DIM, HEAD_DIM, axis=1) for w in (wq, wk, wv)],
-        axis=1,
+    (weight,) = call(
+        select_kernel,
+        1.5,
+        [("s", me), ("a", wq), ("a", wk), ("a", wv)],
+        [out(width, 3 * HEAD_DIM)],
+        [pltpu.VMEM((width, 2 * HEAD_DIM), jnp.bfloat16)] * 3 + [pltpu.SemaphoreType.DMA((3,))],
     )
     pair = 2 * HEAD_DIM
     normed, unit, unit_scale, projected = call(
         project_kernel,
+        2,
         [("v", block) for block in blocks[:EARLY]] + [("v", weight)],
         [
             out(EARLY, rows, width),
@@ -501,9 +534,10 @@
         ],
     )
     late = parts - EARLY
-    *late_parts, probs, qk, value, out_t, packed = call(
+    made = call(
         attend_kernel,
-        [("s", me), ("v", unit), ("v", projected), *[("v", block) for block in blocks[EARLY:]]]
+        5,
+        [("v", unit), ("v", projected), *[("v", block) for block in blocks[EARLY:]]]
         + [("v", weight), ("v", ids[None, :]), ("v", ids[:, None])],
         [
             out(late, rows, width),
@@ -513,52 +547,63 @@
             out(tokens, pair),
             out(tokens, HEAD_DIM),
             out(HEAD_DIM, tokens, dtype=f32),
-            out(parts, PACKED, 128),
-        ],
-    )
+        ]
+        + [out(PACKED, 128)] * parts,
+    )
+    late_parts, (probs, qk, value, out_t), packed = made[:3], made[3:7], made[7:]
     packed = exchange(packed)
-    grad_affine, scaled, grad_slabs = call(
+    grad_affine, scaled, *grad_slabs = call(
         affine_kernel,
-        [("v", packed), ("v", field), ("v", upstream), ("v", wo)],
-        [out(rows, 2 * width), out(rows, width, dtype=f32), out(HEADS, PACKED, 128)],
+        2,
+        [("s", me)] + [("v", x) for x in (*packed, field, upstream, wo)],
+        [out(rows, 2 * width), out(rows, width, dtype=f32)] + [out(PACKED, 128)] * HEADS,
+        [pltpu.VMEM((HEADS, PACKED, 128), jnp.bfloat16)],
     )
     grad_slabs = exchange(grad_slabs)
     terms = call(
         out_term_kernel,
-        [("s", me), ("v", packed), ("v", grad_affine)],
+        2,
+        [("v", x) for x in (*packed, grad_affine)],
         [out(len(group) * HEAD_DIM, width) for order in ORDERS for group in order],
     )
     grad_slabs, terms = lax.optimization_barrier((grad_slabs, terms))
     first, second, third, keep = zip(terms[:4], terms[4:])
     got = [partner(part, "seq", bit) for bit, part in enumerate(first)]
-    (grads,) = call(
+    grads = call(
         backward_kernel,
-        [("s", me), ("v", grad_slabs), ("v", probs), ("v", qk), ("v", value), ("v", out_t)]
+        6,
+        [("s", me)]
+        + [("v", x) for x in (*grad_slabs, probs, qk, value, out_t)]
         + [("v", x) for x in (normed, unit, unit_scale, *late_parts)],
-        [out(parts, PACKED + rows + 3 * HEAD_DIM, 128)],
+        [out(PACKED + rows + 3 * HEAD_DIM, 128)] * parts,
         [
             pltpu.VMEM((tokens, HEAD_DIM), f32),
             pltpu.VMEM((tokens, HEAD_DIM), f32),
             pltpu.VMEM((HEAD_DIM, tokens), f32),
+            pltpu.VMEM((HEADS, 3 * HEAD_DIM, 128), jnp.bfloat16),
         ],
     )
     slabs = exchange(grads)
     leaving = call(
         second_sum_kernel,
-        [("v", x) for x in (*second, *got)] + [("a", grads)],
+        1,
+        [("v", x) for x in (*second, *got)] + [("a", grads[0])],
         [out(*second[0].shape)] * 2,
     )
     more = [partner(part, "seq", 1 - bit) for bit, part in enumerate(leaving)]
     *leaving, keep_a, keep_b = call(
         third_sum_kernel,
-        [("v", x) for x in (*third, *keep, *got, *more)] + [("a", slabs)],
+        2,
+        [("v", x) for x in (*third, *keep, *got, *more)],
         [out(*third[0].shape)] * 2 + [out(*keep[0].shape, dtype=f32)] * 2,
     )
     rest = [partner(part, "seq", 2) for part in leaving]
     (grad_input,) = call(
         input_kernel,
-        [("v", x) for x in (slabs, wq, wk, wv, field, scaled)],
+        1.5,
+        [("s", me)] + [("v", x) for x in (*slabs, wq, wk, wv, field, scaled)],
         [out(rows, width)],
+        [pltpu.VMEM((HEADS, PACKED + rows, 128), jnp.bfloat16)],
     )
     route = [
         (s * parts + d, (s - 1) * parts + parts - 1 - d)
@@ -567,15 +612,20 @@
     ]
     moved = lax.ppermute(grad_input, ("section", "seq"), route)
     grad_q, grad_k, grad_v = call(
-        turn_kernel, [("v", slabs)], [out(1, width // parts, inner, dtype=f32)] * 3
+        turn_kernel,
+        1,
+        [("s", me)] + [("v", x) for x in slabs],
+        [out(1, width // parts, inner, dtype=f32)] * 3,
+        [pltpu.VMEM((HEADS, 3 * HEAD_DIM, 128), jnp.bfloat16)],
     )
     (grad_out,) = call(
         last_sum_kernel,
+        1,
         [("v", x) for x in (keep_a, keep_b, *rest)],
         [out(1, keep_a.shape[0], 2 * width, dtype=f32)],
     )
     (carry,) = call(
-        reorder_kernel, [("v", flip_order[0][:, None]), ("v", moved)], [out(1, rows, width)]
+        reorder_kernel, 1, [("v", flip_order[0][:, None]), ("v", moved)], [out(1, rows, width)]
     )
     return (carry, grad_q, grad_k, grad_v, grad_out)
 

time: 157 us -> 140 us (0.89)
  starting transfers between devices: 35.1 us -> 60.8 us
  local copies, waits for them, and re-layouts: 30.8 us -> 15.3 us
  blocking collectives: 13.4 us -> 0 us
  waiting for transfers between devices: 51.2 us -> 39.3 us
    ppermute x0 -> x21, starting transfers between devices: none -> 30.6 us  [hop(): return lax.ppermute(block, 'seq', route)]
    ppermute x13, waiting for transfers between devices: 51.2 us -> 25 us  [partner(): return lax.ppermute(block, axis, route)]
    ppermute x0 -> x21, waiting for transfers between devices: none -> 13.6 us  [hop(): return lax.ppermute(block, 'seq', route)]
    all_to_all x1 -> x0, blocking collectives: 13.4 us -> none  [exchange(): return lax.all_to_all(slabs, 'seq', split_axis=0, concat_axis=0, tiled=True)]
    unnamed x84 -> x70, local copies, waits for them, and re-layouts: 26.7 us -> 13.6 us
    all_to_all x2 -> x0, starting transfers between devices: 8.87 us -> none  [exchange(): return lax.all_to_all(slabs, 'seq', split_axis=0, concat_axis=0, tiled=True)]
    ppermute x1, starting transfers between devices: 8.89 us -> 15.3 us  [head_shards(): moved = lax.ppermute(grad_input, ('section', 'seq'), route)]
    ppermute x13, starting transfers between devices: 17.4 us -> 14.9 us  [partner(): return lax.ppermute(block, axis, route)]
  transfers between devices with their start and end apart: 16 -> 35, of which waited for: 6 -> 14; matrix products, arithmetic and copies ran while one was open for 3% -> 2% of each run, Pallas kernels for 6% -> 12%
where the time goes in v6:
time: 140 us; the launch traced here: 139 us
  starting transfers between devices  60.8 us (43%)
  waiting for transfers between devices  39.3 us (28%)
  Pallas kernels  22.3 us (16%)
  local copies, waits for them, and re-layouts  15.3 us (11%)
    ppermute x21, starting transfers between devices, hop(): return lax.ppermute(block, 'seq', route)  30.6 us
    ppermute x13, waiting for transfers between devices, partner(): return lax.ppermute(block, axis, route)  25 us
    pallas_call x12, Pallas kernels, call(): pl.pallas_call(kernel, out_shape=tuple(outs), in_specs=[pl.BlockSpec(memo...  22.3 us
    ppermute x1, starting transfers between devices, head_shards(): moved = lax.ppermute(grad_input, ('section', 'seq'), route)  15.3 us
    ppermute x13, starting transfers between devices, partner(): return lax.ppermute(block, axis, route)  14.9 us
    ppermute x21, waiting for transfers between devices, hop(): return lax.ppermute(block, 'seq', route)  13.6 us
    unnamed x70, local copies, waits for them, and re-layouts  13.6 us
  transfers between devices with their start and end apart: 35, of which 14 were waited for; matrix products, arithmetic and copies ran while one was open for 2% of the time, Pallas kernels for 12%

profile of v6, /device:TPU:5, one launch (start us, length us, event | category | flops | bytes accessed | tf_op | source)
XLA Modules:
  0.0 139.4 jit_solution(1341188887660379131)
XLA Ops:
  0.6 2.4 %collective-permute-start.2 = (bf16[136,1024]{1,0:T(8,128)(2,1)}, bf16[136,1024]{1,0:T(8,128)(2,1)S(1)}, u32[]{:S(2)}, u32[]{:S(2)}) collective-permute-start(bf16[136,1024]{1,0:T(8,128)(2,1)} %bitcast.16), channel_id=1, source_target_pairs={{0,4},{4,0},{1,5},{5,1},{2,6},{6,2},{3,7},{7,3},{8,12},{12,8},{9,1... | collective-permute-start | bytes 835592 | tf_op jit(solution)/shard_map/ppermute | solution.py:22
  3.0 1.3 collective-permute-start.1
  4.3 1.2 collective-permute-start
  6.2 9.2 %collective-permute-done.2.refs_3_ = bf16[136,1024]{1,0:T(8,128)(2,1)S(1)} collective-permute-done((bf16[136,1024]{1,0:T(8,128)(2,1)}, bf16[136,1024]{1,0:T(8,128)(2,1)S(1)}, u32[]{:S(2)}, u32[]{:S(2)}) %collective-permute-start.2) | collective-permute-done | bytes 278560 | tf_op jit(solution)/shard_map/ppermute | solution.py:22
  15.4 1.2 collective-permute-start.4
  18.6 1.6 %collective-permute-start.5 = (bf16[136,1024]{1,0:T(8,128)(2,1)S(1)}, bf16[136,1024]{1,0:T(8,128)(2,1)S(1)}, u32[]{:S(2)}, u32[]{:S(2)}) collective-permute-start(bf16[136,1024]{1,0:T(8,128)(2,1)S(1)} %collective-permute-done.2.refs_3_), channel_id=1, source_target_pairs={{0,2},{2,0},{1,3},{3,1},{4,6},{6,4},{5,7},{7,5},{8,10},{10,8},{9,1... | collective-permute-start | bytes 835592 | tf_op jit(solution)/shard_map/ppermute | solution.py:22
  20.2 1.7 %collective-permute-done.4.refs_5_ = bf16[136,1024]{1,0:T(8,128)(2,1)S(1)} collective-permute-done((bf16[136,1024]{1,0:T(8,128)(2,1)S(1)}, bf16[136,1024]{1,0:T(8,128)(2,1)S(1)}, u32[]{:S(2)}, u32[]{:S(2)}) %collective-permute-start.4) | collective-permute-done | bytes 278560 | tf_op jit(solution)/shard_map/ppermute | solution.py:22
  21.9 2.7 %collective-permute-start.6 = (bf16[136,1024]{1,0:T(8,128)(2,1)S(1)}, bf16[136,1024]{1,0:T(8,128)(2,1)S(1)}, u32[]{:S(2)}, u32[]{:S(2)}) collective-permute-start(bf16[136,1024]{1,0:T(8,128)(2,1)S(1)} %collective-permute-done.4.refs_5_), channel_id=1, source_target_pairs={{0,2},{2,0},{1,3},{3,1},{4,6},{6,4},{5,7},{7,5},{8,10},{10,8},{9,1... | collective-permute-start | bytes 835592 | tf_op jit(solution)/shard_map/ppermute | solution.py:22
  24.6 1.2 copy-done.1
  25.8 1.2 copy-done.3
  27.0 1.2 copy-done.5
  29.2 1.1 shard_map.129
  31.1 3.8 %shard_map.130 = (bf16[2,136,1024]{2,1,0:T(8,128)(2,1)S(1)}, f32[2,136,128]{2,1,0:T(8,128)S(1)}, f32[2,136,128]{2,1,0:T(8,128)S(1)}, bf16[1088,1088]{1,0:T(8,128...) custom-call(f32[6,136,128]{2,1,0:T(8,128)S(1)} %get-tuple-element.75, ...), custom_call_target="tpu_custom_call" | custom-call | flops 5000000000 | bytes 1024 | tf_op jit(solution)/shard_map/pallas_call | solution.py:200
  34.9 3.2 %collective-permute-start.10 = (bf16[80,128]{1,0:T(8,128)(2,1)S(1)}, bf16[80,128]{1,0:T(8,128)(2,1)S(1)}, u32[]{:S(2)}, u32[]{:S(2)}) collective-permute-start(bf16[80,128]{1,0:T(8,128)(2,1)S(1)} %get-tuple-element.81), channel_id=1, source_target_pairs={{0,3},{1,2},{2,1},{3,0},{4,7},{5,6},{6,5},{7,4},{8,11},{9,10},{10,... | collective-permute-start | bytes 61448 | tf_op jit(solution)/shard_map/ppermute | solution.py:468
  38.1 3.0 %collective-permute-start.11 = (bf16[80,128]{1,0:T(8,128)(2,1)S(1)}, bf16[80,128]{1,0:T(8,128)(2,1)S(1)}, u32[]{:S(2)}, u32[]{:S(2)}) collective-permute-start(bf16[80,128]{1,0:T(8,128)(2,1)S(1)} %get-tuple-element.82), channel_id=1, source_target_pairs={{0,5},{1,4},{2,7},{3,6},{4,1},{5,0},{6,3},{7,2},{8,13},{9,12},{10,... | collective-permute-start | bytes 61448 | tf_op jit(solution)/shard_map/ppermute | solution.py:468
  41.1 4.2 %collective-permute-start.13 = (bf16[80,128]{1,0:T(8,128)(2,1)S(1)}, bf16[80,128]{1,0:T(8,128)(2,1)S(1)}, u32[]{:S(2)}, u32[]{:S(2)}) collective-permute-start(bf16[80,128]{1,0:T(8,128)(2,1)S(1)} %get-tuple-element.84), channel_id=1, source_target_pairs={{0,7},{1,6},{2,5},{3,4},{4,3},{5,2},{6,1},{7,0},{8,15},{9,14},{10,... | collective-permute-start | bytes 61448 | tf_op jit(solution)/shard_map/ppermute | solution.py:468
  46.6 1.5 %collective-permute-done.7.refs_1_ = bf16[80,128]{1,0:T(8,128)(2,1)S(1)} collective-permute-done((bf16[80,128]{1,0:T(8,128)(2,1)S(1)}, bf16[80,128]{1,0:T(8,128)(2,1)S(1)}, u32[]{:S(2)}, u32[]{:S(2)}) %collective-permute-start.7) | collective-permute-done | bytes 20512 | tf_op jit(solution)/shard_map/ppermute | solution.py:468
  48.4 1.0 collective-permute-done.9.refs_3_
  49.4 1.5 %shard_map.131 = (bf16[136,2048]{1,0:T(8,128)(2,1)S(1)}, f32[136,1024]{1,0:T(8,128)S(1)}, bf16[80,128]{1,0:T(8,128)(2,1)S(1)}, bf16[80,128]{1,0:T(8,128)(2,1)S(1...) custom-call(s32[1]{0:T(128)} %bitcast.1.me_ref, ...), custom_call_target="tpu_custom_call" | custom-call | flops 2000000000 | bytes 1024 | tf_op jit(solution)/shard_map/pallas_call | solution.py:200
  51.0 1.3 collective-permute-start.14
  52.2 1.1 collective-permute-start.15
  53.7 3.3 %collective-permute-start.18 = (bf16[80,128]{1,0:T(8,128)(2,1)S(1)}, bf16[80,128]{1,0:T(8,128)(2,1)S(1)}, u32[]{:S(2)}, u32[]{:S(2)}) collective-permute-start(bf16[80,128]{1,0:T(8,128)(2,1)S(1)} %get-tuple-element.90), channel_id=1, source_target_pairs={{0,5},{1,4},{2,7},{3,6},{4,1},{5,0},{6,3},{7,2},{8,13},{9,12},{10,... | collective-permute-start | bytes 61448 | tf_op jit(solution)/shard_map/ppermute | solution.py:468
  57.0 1.0 collective-permute-start.19
  58.0 2.2 %collective-permute-start.20 = (bf16[80,128]{1,0:T(8,128)(2,1)S(1)}, bf16[80,128]{1,0:T(8,128)(2,1)S(1)}, u32[]{:S(2)}, u32[]{:S(2)}) collective-permute-start(bf16[80,128]{1,0:T(8,128)(2,1)S(1)} %get-tuple-element.92), channel_id=1, source_target_pairs={{0,7},{1,6},{2,5},{3,4},{4,3},{5,2},{6,1},{7,0},{8,15},{9,14},{10,... | collective-permute-start | bytes 61448 | tf_op jit(solution)/shard_map/ppermute | solution.py:468
  60.2 1.1 shard_map.132
  64.0 5.8 %shard_map.133 = (bf16[408,128]{1,0:T(8,128)(2,1)S(1)}, bf16[408,128]{1,0:T(8,128)(2,1)S(1)}, bf16[408,128]{1,0:T(8,128)(2,1)S(1)}, bf16[408,128]{1,0:T(8,128)(2...) custom-call(s32[1]{0:T(128)} %bitcast.1.me_ref, ...), custom_call_target="tpu_custom_call" | custom-call | flops 6000000000 | bytes 1024 | tf_op jit(solution)/shard_map/pallas_call | solution.py:200
  69.9 0.9 collective-permute-start.21
  70.8 1.4 %collective-permute-start.22 = (bf16[408,128]{1,0:T(8,128)(2,1)S(1)}, bf16[408,128]{1,0:T(8,128)(2,1)S(1)}, u32[]{:S(2)}, u32[]{:S(2)}) collective-permute-start(bf16[408,128]{1,0:T(8,128)(2,1)S(1)} %get-tuple-element.121), channel_id=1, source_target_pairs={{0,2},{1,3},{2,0},{3,1},{4,6},{5,7},{6,4},{7,5},{8,10},{9,11},{10,... | collective-permute-start | bytes 313352 | tf_op jit(solution)/shard_map/ppermute | solution.py:468
  72.2 1.1 collective-permute-start.23
  73.3 1.4 %collective-permute-start.24 = (bf16[408,128]{1,0:T(8,128)(2,1)S(1)}, bf16[408,128]{1,0:T(8,128)(2,1)S(1)}, u32[]{:S(2)}, u32[]{:S(2)}) collective-permute-start(bf16[408,128]{1,0:T(8,128)(2,1)S(1)} %get-tuple-element.123), channel_id=1, source_target_pairs={{0,3},{1,2},{2,1},{3,0},{4,7},{5,6},{6,5},{7,4},{8,11},{9,10},{10,... | collective-permute-start | bytes 313352 | tf_op jit(solution)/shard_map/ppermute | solution.py:468
  74.7 1.0 shard_map.137
  76.4 1.1 collective-permute-start.32
  78.2 1.6 %collective-permute-start.25 = (bf16[408,128]{1,0:T(8,128)(2,1)}, bf16[408,128]{1,0:T(8,128)(2,1)}, u32[]{:S(2)}, u32[]{:S(2)}) collective-permute-start(bf16[408,128]{1,0:T(8,128)(2,1)} %get-tuple-element.124), channel_id=1, source_target_pairs={{0,5},{1,4},{2,7},{3,6},{4,1},{5,0},{6,3},{7,2},{8,13},{9,12},{10,... | collective-permute-start | bytes 313352 | tf_op jit(solution)/shard_map/ppermute | solution.py:468
  80.5 1.9 %collective-permute-start.26 = (bf16[408,128]{1,0:T(8,128)(2,1)}, bf16[408,128]{1,0:T(8,128)(2,1)}, u32[]{:S(2)}, u32[]{:S(2)}) collective-permute-start(bf16[408,128]{1,0:T(8,128)(2,1)} %get-tuple-element.125), channel_id=1, source_target_pairs={{0,6},{1,7},{2,4},{3,5},{4,2},{5,3},{6,0},{7,1},{8,14},{9,15},{10,... | collective-permute-start | bytes 313352 | tf_op jit(solution)/shard_map/ppermute | solution.py:468
  83.0 2.0 %collective-permute-start.27 = (bf16[408,128]{1,0:T(8,128)(2,1)}, bf16[408,128]{1,0:T(8,128)(2,1)}, u32[]{:S(2)}, u32[]{:S(2)}) collective-permute-start(bf16[408,128]{1,0:T(8,128)(2,1)} %get-tuple-element.126), channel_id=1, source_target_pairs={{0,7},{1,6},{2,5},{3,4},{4,3},{5,2},{6,1},{7,0},{8,15},{9,14},{10,... | collective-permute-start | bytes 313352 | tf_op jit(solution)/shard_map/ppermute | solution.py:468
  85.1 2.2 %collective-permute-done.25.refs_5_ = bf16[408,128]{1,0:T(8,128)(2,1)} collective-permute-done((bf16[408,128]{1,0:T(8,128)(2,1)}, bf16[408,128]{1,0:T(8,128)(2,1)}, u32[]{:S(2)}, u32[]{:S(2)}) %collective-permute-start.25) | collective-permute-done | bytes 104480 | tf_op jit(solution)/shard_map/ppermute | solution.py:468
  87.4 4.6 %collective-permute-done.26.refs_6_ = bf16[408,128]{1,0:T(8,128)(2,1)} collective-permute-done((bf16[408,128]{1,0:T(8,128)(2,1)}, bf16[408,128]{1,0:T(8,128)(2,1)}, u32[]{:S(2)}, u32[]{:S(2)}) %collective-permute-start.26) | collective-permute-done | bytes 104480 | tf_op jit(solution)/shard_map/ppermute | solution.py:468
  92.0 2.5 %collective-permute-done.27.refs_7_ = bf16[408,128]{1,0:T(8,128)(2,1)} collective-permute-done((bf16[408,128]{1,0:T(8,128)(2,1)}, bf16[408,128]{1,0:T(8,128)(2,1)}, u32[]{:S(2)}, u32[]{:S(2)}) %collective-permute-start.27) | collective-permute-done | bytes 104480 | tf_op jit(solution)/shard_map/ppermute | solution.py:468
  95.4 0.9 copy-done.16
  98.1 1.1 copy-done.22
  100.1 2.5 %shard_map.134 = bf16[136,1024]{1,0:T(8,128)(2,1)S(1)} custom-call(s32[1]{0:T(128)} %bitcast.1.me_ref, bf16[408,128]{1,0:T(8,128)(2,1)S(1)} %copy-done.24, bf16[408,128]{1,0:T(8,128)(2,1)S(1)} %copy-done.14, bf16[408,128]{1,0:T(8,128)(2,1)S(1)} %copy-done.16, bf16[408,128]{1,0:T(8,128)(2,1)S(1)} %copy-done.18, bf16[408,128]{1,0:T(8,128)(2,1)S(1)} %copy-done.20, ...), custom_call_target="tpu_custom_call" | custom-call | flops 1500000000 | bytes 1024 | tf_op jit(solution)/shard_map/pallas_call | solution.py:200
  102.5 15.3 %collective-permute-start.28 = (bf16[136,1024]{1,0:T(8,128)(2,1)S(1)}, bf16[136,1024]{1,0:T(8,128)(2,1)S(1)}, u32[]{:S(2)}, u32[]{:S(2)}) collective-permute-start(bf16[136,1024]{1,0:T(8,128)(2,1)S(1)} %shard_map.134), channel_id=1, source_target_pairs={{8,7},{9,6},{10,5},{11,4},{12,3},{13,2},{14,1},{15,0},{16,15},{17,... | collective-permute-start | bytes 835592 | tf_op jit(solution)/shard_map/ppermute | solution.py:613
  117.9 1.2 shard_map.138
  119.3 2.4 %collective-permute-start.34 = (bf16[64,1024]{1,0:T(8,128)(2,1)S(1)}, bf16[64,1024]{1,0:T(8,128)(2,1)S(1)}, u32[]{:S(2)}, u32[]{:S(2)}) collective-permute-start(bf16[64,1024]{1,0:T(8,128)(2,1)S(1)} %get-tuple-element.144), channel_id=1, source_target_pairs={{0,4},{4,0},{1,5},{5,1},{2,6},{6,2},{3,7},{7,3},{8,12},{12,8},{9,1... | collective-permute-start | bytes 393224 | tf_op jit(solution)/shard_map/ppermute | solution.py:22
  121.6 2.0 %shard_map.136 = (f32[1,128,512]{2,1,0:T(8,128)}, f32[1,128,512]{2,1,0:T(8,128)}, f32[1,128,512]{2,1,0:T(8,128)}) custom-call(s32[1]{0:T(128)} %bitcast.1.me_ref, bf16[408,128]{1,0:T(8,128)(2,1)S(1)} %copy-done.25, bf16[408,128]{1,0:T(8,128)(2,1)S(1)} %copy-done.14, bf16[408,128]{1,0:T(8,128)(2,1)S(1)} %copy-done.16, bf16[408,128]{1,0:T(8,128)(2,1)S(1)} %copy-done.18, ...), custom_call_target="tpu_custom_call" | custom-call | flops 1000000000 | bytes 1024 | tf_op jit(solution)/shard_map/pallas_call | solution.py:200
  124.4 1.0 shard_map.135
  125.4 11.4 %collective-permute-done.33.got_a = bf16[64,1024]{1,0:T(8,128)(2,1)S(1)} collective-permute-done((bf16[64,1024]{1,0:T(8,128)(2,1)S(1)}, bf16[64,1024]{1,0:T(8,128)(2,1)S(1)}, u32[]{:S(2)}, u32[]{:S(2)}) %collective-permute-start.33) | collective-permute-done | bytes 131104 | tf_op jit(solution)/shard_map/ppermute | solution.py:22
  136.8 1.8 %collective-permute-done.34.got_b = bf16[64,1024]{1,0:T(8,128)(2,1)S(1)} collective-permute-done((bf16[64,1024]{1,0:T(8,128)(2,1)S(1)}, bf16[64,1024]{1,0:T(8,128)(2,1)S(1)}, u32[]{:S(2)}, u32[]{:S(2)}) %collective-permute-start.34) | collective-permute-done | bytes 131104 | tf_op jit(solution)/shard_map/ppermute | solution.py:22
  (112 shorter events, 17.1 us)
Async XLA Ops:
  0.6 14.7 %collective-permute-start.2 = (bf16[136,1024]{1,0:T(8,128)(2,1)}, bf16[136,1024]{1,0:T(8,128)(2,1)S(1)}, u32[]{:S(2)}, u32[]{:S(2)}) collective-permute-start(bf16[136,1024]{1,0:T(8,128)(2,1)} %bitcast.16), channel_id=1, source_target_pairs={{0,4},{4,0},{1,5},{5,1},{2,6},{6,2},{3,7},{7,3},{8,12},{12,8},{9,1... | collective-permute-start | bytes 835592 | tf_op jit(solution)/shard_map/ppermute | solution.py:22
  3.0 14.9 %collective-permute-start.1 = (bf16[136,1024]{1,0:T(8,128)(2,1)}, bf16[136,1024]{1,0:T(8,128)(2,1)S(1)}, u32[]{:S(2)}, u32[]{:S(2)}) collective-permute-start(bf16[136,1024]{1,0:T(8,128)(2,1)} %bitcast.17), channel_id=1, source_target_pairs={{0,2},{2,0},{1,3},{3,1},{4,6},{6,4},{5,7},{7,5},{8,10},{10,8},{9,1... | collective-permute-start | bytes 835592 | tf_op jit(solution)/shard_map/ppermute | solution.py:22
  4.3 24.4 %collective-permute-start = (bf16[136,1024]{1,0:T(8,128)(2,1)}, bf16[136,1024]{1,0:T(8,128)(2,1)S(1)}, u32[]{:S(2)}, u32[]{:S(2)}) collective-permute-start(bf16[136,1024]{1,0:T(8,128)(2,1)} %bitcast.18), channel_id=1, source_target_pairs={{0,1},{1,0},{2,3},{3,2},{4,5},{5,4},{6,7},{7,6},{8,9},{9,8},{10,11... | collective-permute-start | bytes 835592 | tf_op jit(solution)/shard_map/ppermute | solution.py:22
  15.4 6.6 %collective-permute-start.4 = (bf16[136,1024]{1,0:T(8,128)(2,1)S(1)}, bf16[136,1024]{1,0:T(8,128)(2,1)S(1)}, u32[]{:S(2)}, u32[]{:S(2)}) collective-permute-start(bf16[136,1024]{1,0:T(8,128)(2,1)S(1)} %collective-permute-done.2.refs_3_), channel_id=1, source_target_pairs={{0,1},{1,0},{2,3},{3,2},{4,5},{5,4},{6,7},{7,6},{8,9},{9,8},{10,11... | collective-permute-start | bytes 835592 | tf_op jit(solution)/shard_map/ppermute | solution.py:22
  17.9 10.8 %collective-permute-start.3 = (bf16[136,1024]{1,0:T(8,128)(2,1)S(1)}, bf16[136,1024]{1,0:T(8,128)(2,1)S(1)}, u32[]{:S(2)}, u32[]{:S(2)}) collective-permute-start(bf16[136,1024]{1,0:T(8,128)(2,1)S(1)} %collective-permute-done.1.refs_2_), channel_id=1, source_target_pairs={{0,1},{1,0},{2,3},{3,2},{4,5},{5,4},{6,7},{7,6},{8,9},{9,8},{10,11... | collective-permute-start | bytes 835592 | tf_op jit(solution)/shard_map/ppermute | solution.py:22
  18.6 11.7 %collective-permute-start.5 = (bf16[136,1024]{1,0:T(8,128)(2,1)S(1)}, bf16[136,1024]{1,0:T(8,128)(2,1)S(1)}, u32[]{:S(2)}, u32[]{:S(2)}) collective-permute-start(bf16[136,1024]{1,0:T(8,128)(2,1)S(1)} %collective-permute-done.2.refs_3_), channel_id=1, source_target_pairs={{0,2},{2,0},{1,3},{3,1},{4,6},{6,4},{5,7},{7,5},{8,10},{10,8},{9,1... | collective-permute-start | bytes 835592 | tf_op jit(solution)/shard_map/ppermute | solution.py:22
  21.9 9.2 %collective-permute-start.6 = (bf16[136,1024]{1,0:T(8,128)(2,1)S(1)}, bf16[136,1024]{1,0:T(8,128)(2,1)S(1)}, u32[]{:S(2)}, u32[]{:S(2)}) collective-permute-start(bf16[136,1024]{1,0:T(8,128)(2,1)S(1)} %collective-permute-done.4.refs_5_), channel_id=1, source_target_pairs={{0,2},{2,0},{1,3},{3,1},{4,6},{6,4},{5,7},{7,5},{8,10},{10,8},{9,1... | collective-permute-start | bytes 835592 | tf_op jit(solution)/shard_map/ppermute | solution.py:22
  31.1 18.3 %copy-start = (bf16[1,512,2048]{2,1,0:T(8,128)(2,1)S(1)}, bf16[1,512,2048]{2,1,0:T(8,128)(2,1)}, u32[]{:S(2)}) copy-start(bf16[1,512,2048]{2,1,0:T(8,128)(2,1)} %param.14) | copy-start | bytes 6291460
  31.1 18.3 %copy-start.11 = (bf16[1,136,1024]{2,1,0:T(8,128)(2,1)S(1)}, bf16[1,136,1024]{2,1,0:T(8,128)(2,1)}, u32[]{:S(2)}) copy-start(bf16[1,136,1024]{2,1,0:T(8,128)(2,1)} %param.10) | copy-start | bytes 835588
  34.9 10.6 %collective-permute-start.10 = (bf16[80,128]{1,0:T(8,128)(2,1)S(1)}, bf16[80,128]{1,0:T(8,128)(2,1)S(1)}, u32[]{:S(2)}, u32[]{:S(2)}) collective-permute-start(bf16[80,128]{1,0:T(8,128)(2,1)S(1)} %get-tuple-element.81), channel_id=1, source_target_pairs={{0,3},{1,2},{2,1},{3,0},{4,7},{5,6},{6,5},{7,4},{8,11},{9,10},{10,... | collective-permute-start | bytes 61448 | tf_op jit(solution)/shard_map/ppermute | solution.py:468
  38.1 7.4 %collective-permute-start.11 = (bf16[80,128]{1,0:T(8,128)(2,1)S(1)}, bf16[80,128]{1,0:T(8,128)(2,1)S(1)}, u32[]{:S(2)}, u32[]{:S(2)}) collective-permute-start(bf16[80,128]{1,0:T(8,128)(2,1)S(1)} %get-tuple-element.82), channel_id=1, source_target_pairs={{0,5},{1,4},{2,7},{3,6},{4,1},{5,0},{6,3},{7,2},{8,13},{9,12},{10,... | collective-permute-start | bytes 61448 | tf_op jit(solution)/shard_map/ppermute | solution.py:468
  41.0 4.8 %collective-permute-start.12 = (bf16[80,128]{1,0:T(8,128)(2,1)S(1)}, bf16[80,128]{1,0:T(8,128)(2,1)S(1)}, u32[]{:S(2)}, u32[]{:S(2)}) collective-permute-start(bf16[80,128]{1,0:T(8,128)(2,1)S(1)} %get-tuple-element.83), channel_id=1, source_target_pairs={{0,6},{1,7},{2,4},{3,5},{4,2},{5,3},{6,0},{7,1},{8,14},{9,15},{10,... | collective-permute-start | bytes 61448 | tf_op jit(solution)/shard_map/ppermute | solution.py:468
  41.1 5.6 %collective-permute-start.13 = (bf16[80,128]{1,0:T(8,128)(2,1)S(1)}, bf16[80,128]{1,0:T(8,128)(2,1)S(1)}, u32[]{:S(2)}, u32[]{:S(2)}) collective-permute-start(bf16[80,128]{1,0:T(8,128)(2,1)S(1)} %get-tuple-element.84), channel_id=1, source_target_pairs={{0,7},{1,6},{2,5},{3,4},{4,3},{5,2},{6,1},{7,0},{8,15},{9,14},{10,... | collective-permute-start | bytes 61448 | tf_op jit(solution)/shard_map/ppermute | solution.py:468
  45.2 2.9 %collective-permute-start.7 = (bf16[80,128]{1,0:T(8,128)(2,1)S(1)}, bf16[80,128]{1,0:T(8,128)(2,1)S(1)}, u32[]{:S(2)}, u32[]{:S(2)}) collective-permute-start(bf16[80,128]{1,0:T(8,128)(2,1)S(1)} %get-tuple-element.78), channel_id=1, source_target_pairs={{0,1},{1,0},{2,3},{3,2},{4,5},{5,4},{6,7},{7,6},{8,9},{9,8},{10,11... | collective-permute-start | bytes 61448 | tf_op jit(solution)/shard_map/ppermute | solution.py:468
  45.5 2.9 %collective-permute-start.8 = (bf16[80,128]{1,0:T(8,128)(2,1)S(1)}, bf16[80,128]{1,0:T(8,128)(2,1)S(1)}, u32[]{:S(2)}, u32[]{:S(2)}) collective-permute-start(bf16[80,128]{1,0:T(8,128)(2,1)S(1)} %get-tuple-element.79), channel_id=1, source_target_pairs={{0,2},{1,3},{2,0},{3,1},{4,6},{5,7},{6,4},{7,5},{8,10},{9,11},{10,... | collective-permute-start | bytes 61448 | tf_op jit(solution)/shard_map/ppermute | solution.py:468
  45.5 3.9 %collective-permute-start.9 = (bf16[80,128]{1,0:T(8,128)(2,1)S(1)}, bf16[80,128]{1,0:T(8,128)(2,1)S(1)}, u32[]{:S(2)}, u32[]{:S(2)}) collective-permute-start(bf16[80,128]{1,0:T(8,128)(2,1)S(1)} %get-tuple-element.80), channel_id=1, source_target_pairs={{0,4},{1,5},{2,6},{3,7},{4,0},{5,1},{6,2},{7,3},{8,12},{9,13},{10,... | collective-permute-start | bytes 61448 | tf_op jit(solution)/shard_map/ppermute | solution.py:468
  51.0 6.0 %collective-permute-start.14 = (bf16[80,128]{1,0:T(8,128)(2,1)S(1)}, bf16[80,128]{1,0:T(8,128)(2,1)S(1)}, u32[]{:S(2)}, u32[]{:S(2)}) collective-permute-start(bf16[80,128]{1,0:T(8,128)(2,1)S(1)} %get-tuple-element.86), channel_id=1, source_target_pairs={{0,1},{1,0},{2,3},{3,2},{4,5},{5,4},{6,7},{7,6},{8,9},{9,8},{10,11... | collective-permute-start | bytes 61448 | tf_op jit(solution)/shard_map/ppermute | solution.py:468
  52.2 5.8 %collective-permute-start.15 = (bf16[80,128]{1,0:T(8,128)(2,1)S(1)}, bf16[80,128]{1,0:T(8,128)(2,1)S(1)}, u32[]{:S(2)}, u32[]{:S(2)}) collective-permute-start(bf16[80,128]{1,0:T(8,128)(2,1)S(1)} %get-tuple-element.87), channel_id=1, source_target_pairs={{0,2},{1,3},{2,0},{3,1},{4,6},{5,7},{6,4},{7,5},{8,10},{9,11},{10,... | collective-permute-start | bytes 61448 | tf_op jit(solution)/shard_map/ppermute | solution.py:468
  53.3 9.3 %collective-permute-start.16 = (bf16[80,128]{1,0:T(8,128)(2,1)S(1)}, bf16[80,128]{1,0:T(8,128)(2,1)S(1)}, u32[]{:S(2)}, u32[]{:S(2)}) collective-permute-start(bf16[80,128]{1,0:T(8,128)(2,1)S(1)} %get-tuple-element.88), channel_id=1, source_target_pairs={{0,4},{1,5},{2,6},{3,7},{4,0},{5,1},{6,2},{7,3},{8,12},{9,13},{10,... | collective-permute-start | bytes 61448 | tf_op jit(solution)/shard_map/ppermute | solution.py:468
  53.6 9.1 %collective-permute-start.17 = (bf16[80,128]{1,0:T(8,128)(2,1)S(1)}, bf16[80,128]{1,0:T(8,128)(2,1)S(1)}, u32[]{:S(2)}, u32[]{:S(2)}) collective-permute-start(bf16[80,128]{1,0:T(8,128)(2,1)S(1)} %get-tuple-element.89), channel_id=1, source_target_pairs={{0,3},{1,2},{2,1},{3,0},{4,7},{5,6},{6,5},{7,4},{8,11},{9,10},{10,... | collective-permute-start | bytes 61448 | tf_op jit(solution)/shard_map/ppermute | solution.py:468
  53.7 9.0 %collective-permute-start.18 = (bf16[80,128]{1,0:T(8,128)(2,1)S(1)}, bf16[80,128]{1,0:T(8,128)(2,1)S(1)}, u32[]{:S(2)}, u32[]{:S(2)}) collective-permute-start(bf16[80,128]{1,0:T(8,128)(2,1)S(1)} %get-tuple-element.90), channel_id=1, source_target_pairs={{0,5},{1,4},{2,7},{3,6},{4,1},{5,0},{6,3},{7,2},{8,13},{9,12},{10,... | collective-permute-start | bytes 61448 | tf_op jit(solution)/shard_map/ppermute | solution.py:468
  57.0 5.7 %collective-permute-start.19 = (bf16[80,128]{1,0:T(8,128)(2,1)S(1)}, bf16[80,128]{1,0:T(8,128)(2,1)S(1)}, u32[]{:S(2)}, u32[]{:S(2)}) collective-permute-start(bf16[80,128]{1,0:T(8,128)(2,1)S(1)} %get-tuple-element.91), channel_id=1, source_target_pairs={{0,6},{1,7},{2,4},{3,5},{4,2},{5,3},{6,0},{7,1},{8,14},{9,15},{10,... | collective-permute-start | bytes 61448 | tf_op jit(solution)/shard_map/ppermute | solution.py:468
  58.0 5.3 %collective-permute-start.20 = (bf16[80,128]{1,0:T(8,128)(2,1)S(1)}, bf16[80,128]{1,0:T(8,128)(2,1)S(1)}, u32[]{:S(2)}, u32[]{:S(2)}) collective-permute-start(bf16[80,128]{1,0:T(8,128)(2,1)S(1)} %get-tuple-element.92), channel_id=1, source_target_pairs={{0,7},{1,6},{2,5},{3,4},{4,3},{5,2},{6,1},{7,0},{8,15},{9,14},{10,... | collective-permute-start | bytes 61448 | tf_op jit(solution)/shard_map/ppermute | solution.py:468
  63.3 10.0 %collective-permute-start.29 = (bf16[256,1024]{1,0:T(8,128)(2,1)S(1)}, bf16[256,1024]{1,0:T(8,128)(2,1)S(1)}, u32[]{:S(2)}, u32[]{:S(2)}) collective-permute-start(bf16[256,1024]{1,0:T(8,128)(2,1)S(1)} %get-tuple-element.135), channel_id=1, source_target_pairs={{0,1},{1,0},{2,3},{3,2},{4,5},{5,4},{6,7},{7,6},{8,9},{9,8},{10,11... | collective-permute-start | bytes 1572872 | tf_op jit(solution)/shard_map/ppermute | solution.py:22
  64.0 10.8 %collective-permute-start.30 = (bf16[256,1024]{1,0:T(8,128)(2,1)S(1)}, bf16[256,1024]{1,0:T(8,128)(2,1)S(1)}, u32[]{:S(2)}, u32[]{:S(2)}) collective-permute-start(bf16[256,1024]{1,0:T(8,128)(2,1)S(1)} %get-tuple-element.136), channel_id=1, source_target_pairs={{0,2},{2,0},{1,3},{3,1},{4,6},{6,4},{5,7},{7,5},{8,10},{10,8},{9,1... | collective-permute-start | bytes 1572872 | tf_op jit(solution)/shard_map/ppermute | solution.py:22
  69.8 15.2 %copy-start.34 = (s32[1,136]{1,0:T(1,128)S(1)}, s32[1,136]{1,0:T(1,128)}, u32[]{:S(2)}) copy-start(s32[1,136]{1,0:T(1,128)} %param.16) | copy-start | bytes 1636
  69.8 24.7 %copy-start.2 = (bf16[1,1024,512]{2,1,0:T(8,128)(2,1)S(1)}, bf16[1,1024,512]{2,1,0:T(8,128)(2,1)}, u32[]{:S(2)}) copy-start(bf16[1,1024,512]{2,1,0:T(8,128)(2,1)} %param.11) | copy-start | bytes 3145732
  69.8 24.7 %copy-start.4 = (bf16[1,1024,512]{2,1,0:T(8,128)(2,1)S(1)}, bf16[1,1024,512]{2,1,0:T(8,128)(2,1)}, u32[]{:S(2)}) copy-start(bf16[1,1024,512]{2,1,0:T(8,128)(2,1)} %param.12) | copy-start | bytes 3145732
  69.8 24.6 %copy-start.6 = (bf16[1,1024,512]{2,1,0:T(8,128)(2,1)S(1)}, bf16[1,1024,512]{2,1,0:T(8,128)(2,1)}, u32[]{:S(2)}) copy-start(bf16[1,1024,512]{2,1,0:T(8,128)(2,1)} %param.13) | copy-start | bytes 3145732
  69.9 5.9 %collective-permute-start.21 = (bf16[408,128]{1,0:T(8,128)(2,1)S(1)}, bf16[408,128]{1,0:T(8,128)(2,1)S(1)}, u32[]{:S(2)}, u32[]{:S(2)}) collective-permute-start(bf16[408,128]{1,0:T(8,128)(2,1)S(1)} %get-tuple-element.120), channel_id=1, source_target_pairs={{0,1},{1,0},{2,3},{3,2},{4,5},{5,4},{6,7},{7,6},{8,9},{9,8},{10,11... | collective-permute-start | bytes 313352 | tf_op jit(solution)/shard_map/ppermute | solution.py:468
  70.8 6.8 %collective-permute-start.22 = (bf16[408,128]{1,0:T(8,128)(2,1)S(1)}, bf16[408,128]{1,0:T(8,128)(2,1)S(1)}, u32[]{:S(2)}, u32[]{:S(2)}) collective-permute-start(bf16[408,128]{1,0:T(8,128)(2,1)S(1)} %get-tuple-element.121), channel_id=1, source_target_pairs={{0,2},{1,3},{2,0},{3,1},{4,6},{5,7},{6,4},{7,5},{8,10},{9,11},{10,... | collective-permute-start | bytes 313352 | tf_op jit(solution)/shard_map/ppermute | solution.py:468
  72.2 7.6 %collective-permute-start.23 = (bf16[408,128]{1,0:T(8,128)(2,1)S(1)}, bf16[408,128]{1,0:T(8,128)(2,1)S(1)}, u32[]{:S(2)}, u32[]{:S(2)}) collective-permute-start(bf16[408,128]{1,0:T(8,128)(2,1)S(1)} %get-tuple-element.122), channel_id=1, source_target_pairs={{0,4},{1,5},{2,6},{3,7},{4,0},{5,1},{6,2},{7,3},{8,12},{9,13},{10,... | collective-permute-start | bytes 313352 | tf_op jit(solution)/shard_map/ppermute | solution.py:468
  73.3 9.1 %collective-permute-start.24 = (bf16[408,128]{1,0:T(8,128)(2,1)S(1)}, bf16[408,128]{1,0:T(8,128)(2,1)S(1)}, u32[]{:S(2)}, u32[]{:S(2)}) collective-permute-start(bf16[408,128]{1,0:T(8,128)(2,1)S(1)} %get-tuple-element.123), channel_id=1, source_target_pairs={{0,3},{1,2},{2,1},{3,0},{4,7},{5,6},{6,5},{7,4},{8,11},{9,10},{10,... | collective-permute-start | bytes 313352 | tf_op jit(solution)/shard_map/ppermute | solution.py:468
  75.7 42.2 %collective-permute-start.31 = (bf16[128,1024]{1,0:T(8,128)(2,1)}, bf16[128,1024]{1,0:T(8,128)(2,1)}, u32[]{:S(2)}, u32[]{:S(2)}) collective-permute-start(bf16[128,1024]{1,0:T(8,128)(2,1)} %get-tuple-element.139), channel_id=1, source_target_pairs={{0,2},{2,0},{1,3},{3,1},{4,6},{6,4},{5,7},{7,5},{8,10},{10,8},{9,1... | collective-permute-start | bytes 786440 | tf_op jit(solution)/shard_map/ppermute | solution.py:22
  76.4 41.4 %collective-permute-start.32 = (bf16[128,1024]{1,0:T(8,128)(2,1)}, bf16[128,1024]{1,0:T(8,128)(2,1)}, u32[]{:S(2)}, u32[]{:S(2)}) collective-permute-start(bf16[128,1024]{1,0:T(8,128)(2,1)} %get-tuple-element.140), channel_id=1, source_target_pairs={{0,1},{1,0},{2,3},{3,2},{4,5},{5,4},{6,7},{7,6},{8,9},{9,8},{10,11... | collective-permute-start | bytes 786440 | tf_op jit(solution)/shard_map/ppermute | solution.py:22
  78.2 9.2 %collective-permute-start.25 = (bf16[408,128]{1,0:T(8,128)(2,1)}, bf16[408,128]{1,0:T(8,128)(2,1)}, u32[]{:S(2)}, u32[]{:S(2)}) collective-permute-start(bf16[408,128]{1,0:T(8,128)(2,1)} %get-tuple-element.124), channel_id=1, source_target_pairs={{0,5},{1,4},{2,7},{3,6},{4,1},{5,0},{6,3},{7,2},{8,13},{9,12},{10,... | collective-permute-start | bytes 313352 | tf_op jit(solution)/shard_map/ppermute | solution.py:468
  80.5 11.5 %collective-permute-start.26 = (bf16[408,128]{1,0:T(8,128)(2,1)}, bf16[408,128]{1,0:T(8,128)(2,1)}, u32[]{:S(2)}, u32[]{:S(2)}) collective-permute-start(bf16[408,128]{1,0:T(8,128)(2,1)} %get-tuple-element.125), channel_id=1, source_target_pairs={{0,6},{1,7},{2,4},{3,5},{4,2},{5,3},{6,0},{7,1},{8,14},{9,15},{10,... | collective-permute-start | bytes 313352 | tf_op jit(solution)/shard_map/ppermute | solution.py:468
  83.0 11.5 %collective-permute-start.27 = (bf16[408,128]{1,0:T(8,128)(2,1)}, bf16[408,128]{1,0:T(8,128)(2,1)}, u32[]{:S(2)}, u32[]{:S(2)}) collective-permute-start(bf16[408,128]{1,0:T(8,128)(2,1)} %get-tuple-element.126), channel_id=1, source_target_pairs={{0,7},{1,6},{2,5},{3,4},{4,3},{5,2},{6,1},{7,0},{8,15},{9,14},{10,... | collective-permute-start | bytes 313352 | tf_op jit(solution)/shard_map/ppermute | solution.py:468
  100.0 17.9 %copy-start.8 = (bf16[256,1024]{1,0:T(8,128)(2,1)S(1)}, bf16[256,1024]{1,0:T(8,128)(2,1)}, u32[]{:S(2)}) copy-start(bf16[256,1024]{1,0:T(8,128)(2,1)} %copy-done.7) | copy-start | bytes 1572868
  100.0 17.9 %copy-start.10 = (bf16[256,1024]{1,0:T(8,128)(2,1)S(1)}, bf16[256,1024]{1,0:T(8,128)(2,1)}, u32[]{:S(2)}) copy-start(bf16[256,1024]{1,0:T(8,128)(2,1)} %copy-done.9) | copy-start | bytes 1572868
  100.0 17.9 %copy-start.27 = (bf16[64,1024]{1,0:T(8,128)(2,1)S(1)}, bf16[64,1024]{1,0:T(8,128)(2,1)}, u32[]{:S(2)}) copy-start(bf16[64,1024]{1,0:T(8,128)(2,1)} %copy-done.26) | copy-start | bytes 393220
  100.0 17.9 %copy-start.29 = (bf16[64,1024]{1,0:T(8,128)(2,1)S(1)}, bf16[64,1024]{1,0:T(8,128)(2,1)}, u32[]{:S(2)}) copy-start(bf16[64,1024]{1,0:T(8,128)(2,1)} %copy-done.28) | copy-start | bytes 393220
  100.0 17.9 %copy-start.31 = (bf16[64,1024]{1,0:T(8,128)(2,1)S(1)}, bf16[64,1024]{1,0:T(8,128)(2,1)}, u32[]{:S(2)}) copy-start(bf16[64,1024]{1,0:T(8,128)(2,1)} %copy-done.30) | copy-start | bytes 393220
  100.0 17.9 %copy-start.33 = (bf16[64,1024]{1,0:T(8,128)(2,1)S(1)}, bf16[64,1024]{1,0:T(8,128)(2,1)}, u32[]{:S(2)}) copy-start(bf16[64,1024]{1,0:T(8,128)(2,1)} %copy-done.32) | copy-start | bytes 393220
  102.5 19.1 %copy-start.25 = (bf16[408,128]{1,0:T(8,128)(2,1)S(1)}, bf16[408,128]{1,0:T(8,128)(2,1)}, u32[]{:S(2)}) copy-start(bf16[408,128]{1,0:T(8,128)(2,1)} %copy-done.23) | copy-start | bytes 313348
  102.5 21.8 %collective-permute-start.28 = (bf16[136,1024]{1,0:T(8,128)(2,1)S(1)}, bf16[136,1024]{1,0:T(8,128)(2,1)S(1)}, u32[]{:S(2)}, u32[]{:S(2)}) collective-permute-start(bf16[136,1024]{1,0:T(8,128)(2,1)S(1)} %shard_map.134), channel_id=1, source_target_pairs={{8,7},{9,6},{10,5},{11,4},{12,3},{13,2},{14,1},{15,0},{16,15},{17,... | collective-permute-start | bytes 835592 | tf_op jit(solution)/shard_map/ppermute | solution.py:613
  119.2 17.6 %collective-permute-start.33 = (bf16[64,1024]{1,0:T(8,128)(2,1)S(1)}, bf16[64,1024]{1,0:T(8,128)(2,1)S(1)}, u32[]{:S(2)}, u32[]{:S(2)}) collective-permute-start(bf16[64,1024]{1,0:T(8,128)(2,1)S(1)} %get-tuple-element.143), channel_id=1, source_target_pairs={{0,4},{4,0},{1,5},{5,1},{2,6},{6,2},{3,7},{7,3},{8,12},{12,8},{9,1... | collective-permute-start | bytes 393224 | tf_op jit(solution)/shard_map/ppermute | solution.py:22
  119.3 19.4 %collective-permute-start.34 = (bf16[64,1024]{1,0:T(8,128)(2,1)S(1)}, bf16[64,1024]{1,0:T(8,128)(2,1)S(1)}, u32[]{:S(2)}, u32[]{:S(2)}) collective-permute-start(bf16[64,1024]{1,0:T(8,128)(2,1)S(1)} %get-tuple-element.144), channel_id=1, source_target_pairs={{0,4},{4,0},{1,5},{5,1},{2,6},{6,2},{3,7},{7,3},{8,12},{12,8},{9,1... | collective-permute-start | bytes 393224 | tf_op jit(solution)/shard_map/ppermute | solution.py:22
  (22 other events, 76.0 us)

commit v7 on v6

--- a/solution.py
+++ b/solution.py
@@ -435,7 +435,7 @@
 
 
 def input_kernel(me_ref, *refs):
-    slabs, (wq_ref, wk_ref, wv_ref, act_ref, up_ref, out_ref) = refs[:HEADS], refs[HEADS:-1]
+    slabs, (wq_ref, wk_ref, wv_ref, act_ref, up_ref, _, out_ref) = refs[:HEADS], refs[HEADS:-1]
     held_ref = refs[-1]
     rows = act_ref.shape[0]
     for m, slab in enumerate(slabs):
@@ -458,9 +458,9 @@
 
 def reorder_kernel(order_ref, rows_ref, out_ref):
     rows = rows_ref.shape[0]
-    chosen = lax.broadcasted_iota(jnp.int32, (rows, rows), 1) == order_ref[...]
-    chosen = jnp.where(chosen, 1.0, 0.0).astype(jnp.bfloat16)
-    out_ref[0] = dot(chosen, rows_ref[...]).astype(jnp.bfloat16)
+    chosen = lax.broadcasted_iota(jnp.int32, (rows, rows), 0) == order_ref[...]
+    chosen = low(jnp.where(chosen, 1.0, 0.0))
+    out_ref[0] = low(dot(chosen, rows_ref[...], ((0,), (0,))))
 
 
 def hop(block, distance):
@@ -601,7 +601,7 @@
     (grad_input,) = call(
         input_kernel,
         1.5,
-        [("s", me)] + [("v", x) for x in (*slabs, wq, wk, wv, field, scaled)],
+        [("s", me)] + [("v", x) for x in (*slabs, wq, wk, wv, field, scaled)] + [("a", leaving[0])],
         [out(rows, width)],
         [pltpu.VMEM((HEADS, PACKED + rows, 128), jnp.bfloat16)],
     )
@@ -625,7 +625,7 @@
         [out(1, keep_a.shape[0], 2 * width, dtype=f32)],
     )
     (carry,) = call(
-        reorder_kernel, 1, [("v", flip_order[0][:, None]), ("v", moved)], [out(1, rows, width)]
+        reorder_kernel, 1, [("v", flip_order), ("v", moved)], [out(1, rows, width)]
     )
     return (carry, grad_q, grad_k, grad_v, grad_out)
 

time: 140 us -> 141 us (level)
  waiting for transfers between devices: 39.3 us -> 53.1 us
  local copies, waits for them, and re-layouts: 15.3 us -> 5.79 us
  Pallas kernels: 22.3 us -> 17.7 us
  starting transfers between devices: 60.8 us -> 62.7 us
    ppermute x13, waiting for transfers between devices: 25 us -> 35.8 us  [partner(): return lax.ppermute(block, axis, route)]
    unnamed x70 -> x20, local copies, waits for them, and re-layouts: 13.6 us -> 4.15 us
    pallas_call x12, Pallas kernels: 22.3 us -> 17.7 us  [call(): pl.pallas_call(kernel, out_shape=tuple(outs), in_specs=[pl.BlockSpec(memo...]
    ppermute x21, waiting for transfers between devices: 13.6 us -> 17.3 us  [hop(): return lax.ppermute(block, 'seq', route)]
  transfers between devices with their start and end apart: 35 -> 35, of which waited for: 14 -> 15; matrix products, arithmetic and copies ran while one was open for 2% -> 2% of each run, Pallas kernels for 12% -> 7%
where the time goes in v7:
time: 141 us
  starting transfers between devices  62.7 us (44%)
  waiting for transfers between devices  53.1 us (38%)
  Pallas kernels  17.7 us (13%)
  local copies, waits for them, and re-layouts  5.79 us (4%)
    ppermute x13, waiting for transfers between devices, partner(): return lax.ppermute(block, axis, route)  35.8 us
    ppermute x21, starting transfers between devices, hop(): return lax.ppermute(block, 'seq', route)  31.2 us
    pallas_call x12, Pallas kernels, call(): pl.pallas_call(kernel, out_shape=tuple(outs), in_specs=[pl.BlockSpec(memo...  17.7 us
    ppermute x21, waiting for transfers between devices, hop(): return lax.ppermute(block, 'seq', route)  17.3 us
    ppermute x1, starting transfers between devices, head_shards(): moved = lax.ppermute(grad_input, ('section', 'seq'), route)  16.4 us
    ppermute x13, starting transfers between devices, partner(): return lax.ppermute(block, axis, route)  15.1 us
    unnamed x20, local copies, waits for them, and re-layouts  4.15 us
  transfers between devices with their start and end apart: 35, of which 15 were waited for; matrix products, arithmetic and copies ran while one was open for 2% of the time, Pallas kernels for 7%

profile of v7, /device:TPU:5, one launch (start us, length us, event | category | flops | bytes accessed | tf_op | source)
XLA Modules:
  0.0 140.9 jit_solution(15731985950592495147)
XLA Ops:
  0.6 2.4 %collective-permute-start.2 = (bf16[136,1024]{1,0:T(8,128)(2,1)}, bf16[136,1024]{1,0:T(8,128)(2,1)S(1)}, u32[]{:S(2)}, u32[]{:S(2)}) collective-permute-start(bf16[136,1024]{1,0:T(8,128)(2,1)} %bitcast.15), channel_id=1, source_target_pairs={{0,4},{4,0},{1,5},{5,1},{2,6},{6,2},{3,7},{7,3},{8,12},{12,8},{9,1... | collective-permute-start | bytes 835592 | tf_op jit(solution)/shard_map/ppermute | solution.py:22
  3.0 1.3 collective-permute-start.1
  4.3 1.2 collective-permute-start
  6.2 9.2 %collective-permute-done.2.refs_3_ = bf16[136,1024]{1,0:T(8,128)(2,1)S(1)} collective-permute-done((bf16[136,1024]{1,0:T(8,128)(2,1)}, bf16[136,1024]{1,0:T(8,128)(2,1)S(1)}, u32[]{:S(2)}, u32[]{:S(2)}) %collective-permute-start.2) | collective-permute-done | bytes 278560 | tf_op jit(solution)/shard_map/ppermute | solution.py:22
  15.4 1.2 collective-permute-start.4
  16.6 0.8 reshape.64
  18.6 1.6 %collective-permute-start.5 = (bf16[136,1024]{1,0:T(8,128)(2,1)S(1)}, bf16[136,1024]{1,0:T(8,128)(2,1)S(1)}, u32[]{:S(2)}, u32[]{:S(2)}) collective-permute-start(bf16[136,1024]{1,0:T(8,128)(2,1)S(1)} %collective-permute-done.2.refs_3_), channel_id=1, source_target_pairs={{0,2},{2,0},{1,3},{3,1},{4,6},{6,4},{5,7},{7,5},{8,10},{10,8},{9,1... | collective-permute-start | bytes 835592 | tf_op jit(solution)/shard_map/ppermute | solution.py:22
  20.2 1.7 %collective-permute-done.4.refs_5_ = bf16[136,1024]{1,0:T(8,128)(2,1)S(1)} collective-permute-done((bf16[136,1024]{1,0:T(8,128)(2,1)S(1)}, bf16[136,1024]{1,0:T(8,128)(2,1)S(1)}, u32[]{:S(2)}, u32[]{:S(2)}) %collective-permute-start.4) | collective-permute-done | bytes 278560 | tf_op jit(solution)/shard_map/ppermute | solution.py:22
  21.9 2.7 %collective-permute-start.6 = (bf16[136,1024]{1,0:T(8,128)(2,1)S(1)}, bf16[136,1024]{1,0:T(8,128)(2,1)S(1)}, u32[]{:S(2)}, u32[]{:S(2)}) collective-permute-start(bf16[136,1024]{1,0:T(8,128)(2,1)S(1)} %collective-permute-done.4.refs_5_), channel_id=1, source_target_pairs={{0,2},{2,0},{1,3},{3,1},{4,6},{6,4},{5,7},{7,5},{8,10},{10,8},{9,1... | collective-permute-start | bytes 835592 | tf_op jit(solution)/shard_map/ppermute | solution.py:22
  24.6 1.2 copy-done.1
  25.8 1.2 copy-done.3
  27.0 1.2 copy-done.5
  29.2 1.1 shard_map.129
  30.3 0.8 collective-permute-done.6.last_ref
  31.1 3.8 %shard_map.130 = (bf16[2,136,1024]{2,1,0:T(8,128)(2,1)S(1)}, f32[2,136,128]{2,1,0:T(8,128)S(1)}, f32[2,136,128]{2,1,0:T(8,128)S(1)}, bf16[1088,1088]{1,0:T(8,128...) custom-call(f32[6,136,128]{2,1,0:T(8,128)S(1)} %get-tuple-element.75, ...), custom_call_target="tpu_custom_call" | custom-call | flops 5000000000 | bytes 1024 | tf_op jit(solution)/shard_map/pallas_call | solution.py:200
  34.9 1.3 collective-permute-start.7
  36.2 2.2 %collective-permute-start.8 = (bf16[80,128]{1,0:T(8,128)(2,1)S(1)}, bf16[80,128]{1,0:T(8,128)(2,1)S(1)}, u32[]{:S(2)}, u32[]{:S(2)}) collective-permute-start(bf16[80,128]{1,0:T(8,128)(2,1)S(1)} %get-tuple-element.79), channel_id=1, source_target_pairs={{0,2},{1,3},{2,0},{3,1},{4,6},{5,7},{6,4},{7,5},{8,10},{9,11},{10,... | collective-permute-start | bytes 61448 | tf_op jit(solution)/shard_map/ppermute | solution.py:468
  38.4 3.0 %collective-permute-start.9 = (bf16[80,128]{1,0:T(8,128)(2,1)S(1)}, bf16[80,128]{1,0:T(8,128)(2,1)S(1)}, u32[]{:S(2)}, u32[]{:S(2)}) collective-permute-start(bf16[80,128]{1,0:T(8,128)(2,1)S(1)} %get-tuple-element.80), channel_id=1, source_target_pairs={{0,4},{1,5},{2,6},{3,7},{4,0},{5,1},{6,2},{7,3},{8,12},{9,13},{10,... | collective-permute-start | bytes 61448 | tf_op jit(solution)/shard_map/ppermute | solution.py:468
  41.6 0.9 collective-permute-start.11
  42.5 3.3 %collective-permute-start.12 = (bf16[80,128]{1,0:T(8,128)(2,1)S(1)}, bf16[80,128]{1,0:T(8,128)(2,1)S(1)}, u32[]{:S(2)}, u32[]{:S(2)}) collective-permute-start(bf16[80,128]{1,0:T(8,128)(2,1)S(1)} %get-tuple-element.83), channel_id=1, source_target_pairs={{0,6},{1,7},{2,4},{3,5},{4,2},{5,3},{6,0},{7,1},{8,14},{9,15},{10,... | collective-permute-start | bytes 61448 | tf_op jit(solution)/shard_map/ppermute | solution.py:468
  46.0 1.3 collective-permute-done.12.refs_6_
  47.3 3.9 %collective-permute-done.13.refs_7_ = bf16[80,128]{1,0:T(8,128)(2,1)S(1)} collective-permute-done((bf16[80,128]{1,0:T(8,128)(2,1)S(1)}, bf16[80,128]{1,0:T(8,128)(2,1)S(1)}, u32[]{:S(2)}, u32[]{:S(2)}) %collective-permute-start.13) | collective-permute-done | bytes 20512 | tf_op jit(solution)/shard_map/ppermute | solution.py:468
  51.2 1.5 %shard_map.131 = (bf16[136,2048]{1,0:T(8,128)(2,1)S(1)}, f32[136,1024]{1,0:T(8,128)S(1)}, bf16[80,128]{1,0:T(8,128)(2,1)S(1)}, bf16[80,128]{1,0:T(8,128)(2,1)S(1...) custom-call(s32[1]{0:T(128)} %bitcast.me_ref, ...), custom_call_target="tpu_custom_call" | custom-call | flops 2000000000 | bytes 1024 | tf_op jit(solution)/shard_map/pallas_call | solution.py:200
  53.6 1.8 %collective-permute-start.17 = (bf16[80,128]{1,0:T(8,128)(2,1)S(1)}, bf16[80,128]{1,0:T(8,128)(2,1)S(1)}, u32[]{:S(2)}, u32[]{:S(2)}) collective-permute-start(bf16[80,128]{1,0:T(8,128)(2,1)S(1)} %get-tuple-element.89), channel_id=1, source_target_pairs={{0,3},{1,2},{2,1},{3,0},{4,7},{5,6},{6,5},{7,4},{8,11},{9,10},{10,... | collective-permute-start | bytes 61448 | tf_op jit(solution)/shard_map/ppermute | solution.py:468
  55.4 2.3 %collective-permute-start.18 = (bf16[80,128]{1,0:T(8,128)(2,1)S(1)}, bf16[80,128]{1,0:T(8,128)(2,1)S(1)}, u32[]{:S(2)}, u32[]{:S(2)}) collective-permute-start(bf16[80,128]{1,0:T(8,128)(2,1)S(1)} %get-tuple-element.90), channel_id=1, source_target_pairs={{0,5},{1,4},{2,7},{3,6},{4,1},{5,0},{6,3},{7,2},{8,13},{9,12},{10,... | collective-permute-start | bytes 61448 | tf_op jit(solution)/shard_map/ppermute | solution.py:468
  58.1 3.8 %collective-permute-start.20 = (bf16[80,128]{1,0:T(8,128)(2,1)S(1)}, bf16[80,128]{1,0:T(8,128)(2,1)S(1)}, u32[]{:S(2)}, u32[]{:S(2)}) collective-permute-start(bf16[80,128]{1,0:T(8,128)(2,1)S(1)} %get-tuple-element.92), channel_id=1, source_target_pairs={{0,7},{1,6},{2,5},{3,4},{4,3},{5,2},{6,1},{7,0},{8,15},{9,14},{10,... | collective-permute-start | bytes 61448 | tf_op jit(solution)/shard_map/ppermute | solution.py:468
  61.9 1.1 shard_map.132
  63.4 0.9 collective-permute-start.28
  64.4 5.2 %shard_map.133 = (bf16[408,128]{1,0:T(8,128)(2,1)S(1)}, bf16[408,128]{1,0:T(8,128)(2,1)S(1)}, bf16[408,128]{1,0:T(8,128)(2,1)S(1)}, bf16[408,128]{1,0:T(8,128)(2...) custom-call(s32[1]{0:T(128)} %bitcast.me_ref, ...), custom_call_target="tpu_custom_call" | custom-call | flops 6000000000 | bytes 1024 | tf_op jit(solution)/shard_map/pallas_call | solution.py:200
  69.5 2.4 %collective-permute-done.28.refs_2_.refs_4_ = bf16[256,1024]{1,0:T(8,128)(2,1)S(1)} collective-permute-done((bf16[256,1024]{1,0:T(8,128)(2,1)S(1)}, bf16[256,1024]{1,0:T(8,128)(2,1)S(1)}, u32[]{:S(2)}, u32[]{:S(2)}) %collective-permute-start.28) | collective-permute-done | bytes 524320 | tf_op jit(solution)/shard_map/ppermute | solution.py:22
  71.9 0.9 collective-permute-done.29.refs_3_.refs_5_
  73.3 0.8 collective-permute-start.31
  74.7 1.2 collective-permute-start.22
  76.0 2.3 %collective-permute-start.23 = (bf16[408,128]{1,0:T(8,128)(2,1)S(1)}, bf16[408,128]{1,0:T(8,128)(2,1)S(1)}, u32[]{:S(2)}, u32[]{:S(2)}) collective-permute-start(bf16[408,128]{1,0:T(8,128)(2,1)S(1)} %get-tuple-element.122), channel_id=1, source_target_pairs={{0,4},{1,5},{2,6},{3,7},{4,0},{5,1},{6,2},{7,3},{8,12},{9,13},{10,... | collective-permute-start | bytes 313352 | tf_op jit(solution)/shard_map/ppermute | solution.py:468
  78.3 5.6 %collective-permute-done.21.refs_1_ = bf16[408,128]{1,0:T(8,128)(2,1)S(1)} collective-permute-done((bf16[408,128]{1,0:T(8,128)(2,1)S(1)}, bf16[408,128]{1,0:T(8,128)(2,1)S(1)}, u32[]{:S(2)}, u32[]{:S(2)}) %collective-permute-start.21) | collective-permute-done | bytes 104480 | tf_op jit(solution)/shard_map/ppermute | solution.py:468
  83.9 0.8 collective-permute-done.22.refs_2_
  84.7 3.4 %collective-permute-start.25 = (bf16[408,128]{1,0:T(8,128)(2,1)S(1)}, bf16[408,128]{1,0:T(8,128)(2,1)S(1)}, u32[]{:S(2)}, u32[]{:S(2)}) collective-permute-start(bf16[408,128]{1,0:T(8,128)(2,1)S(1)} %get-tuple-element.124), channel_id=1, source_target_pairs={{0,5},{1,4},{2,7},{3,6},{4,1},{5,0},{6,3},{7,2},{8,13},{9,12},{10,... | collective-permute-start | bytes 313352 | tf_op jit(solution)/shard_map/ppermute | solution.py:468
  88.4 3.2 %collective-permute-start.27 = (bf16[408,128]{1,0:T(8,128)(2,1)S(1)}, bf16[408,128]{1,0:T(8,128)(2,1)S(1)}, u32[]{:S(2)}, u32[]{:S(2)}) collective-permute-start(bf16[408,128]{1,0:T(8,128)(2,1)S(1)} %get-tuple-element.126), channel_id=1, source_target_pairs={{0,7},{1,6},{2,5},{3,4},{4,3},{5,2},{6,1},{7,0},{8,15},{9,14},{10,... | collective-permute-start | bytes 313352 | tf_op jit(solution)/shard_map/ppermute | solution.py:468
  91.8 2.8 %collective-permute-done.26.refs_6_ = bf16[408,128]{1,0:T(8,128)(2,1)S(1)} collective-permute-done((bf16[408,128]{1,0:T(8,128)(2,1)S(1)}, bf16[408,128]{1,0:T(8,128)(2,1)S(1)}, u32[]{:S(2)}, u32[]{:S(2)}) %collective-permute-start.26) | collective-permute-done | bytes 104480 | tf_op jit(solution)/shard_map/ppermute | solution.py:468
  94.5 2.4 %collective-permute-done.27.refs_7_ = bf16[408,128]{1,0:T(8,128)(2,1)S(1)} collective-permute-done((bf16[408,128]{1,0:T(8,128)(2,1)S(1)}, bf16[408,128]{1,0:T(8,128)(2,1)S(1)}, u32[]{:S(2)}, u32[]{:S(2)}) %collective-permute-start.27) | collective-permute-done | bytes 104480 | tf_op jit(solution)/shard_map/ppermute | solution.py:468
  97.0 1.4 shard_map.136
  98.3 16.4 %collective-permute-start.32 = (bf16[136,1024]{1,0:T(8,128)(2,1)S(1)}, bf16[136,1024]{1,0:T(8,128)(2,1)S(1)}, u32[]{:S(2)}, u32[]{:S(2)}) collective-permute-start(bf16[136,1024]{1,0:T(8,128)(2,1)S(1)} %shard_map.136), channel_id=1, source_target_pairs={{8,7},{9,6},{10,5},{11,4},{12,3},{13,2},{14,1},{15,0},{16,15},{17,... | collective-permute-start | bytes 835592 | tf_op jit(solution)/shard_map/ppermute | solution.py:613
  115.5 1.7 %collective-permute-start.33 = (bf16[64,1024]{1,0:T(8,128)(2,1)S(1)}, bf16[64,1024]{1,0:T(8,128)(2,1)S(1)}, u32[]{:S(2)}, u32[]{:S(2)}) collective-permute-start(bf16[64,1024]{1,0:T(8,128)(2,1)S(1)} %get-tuple-element.138.refs_13_), channel_id=1, source_target_pairs={{0,4},{4,0},{1,5},{5,1},{2,6},{6,2},{3,7},{7,3},{8,12},{12,8},{9,1... | collective-permute-start | bytes 393224 | tf_op jit(solution)/shard_map/ppermute | solution.py:22
  117.2 1.0 shard_map.138
  118.2 18.1 %collective-permute-done.34.got_b = bf16[64,1024]{1,0:T(8,128)(2,1)S(1)} collective-permute-done((bf16[64,1024]{1,0:T(8,128)(2,1)S(1)}, bf16[64,1024]{1,0:T(8,128)(2,1)S(1)}, u32[]{:S(2)}, u32[]{:S(2)}) %collective-permute-start.34) | collective-permute-done | bytes 131104 | tf_op jit(solution)/shard_map/ppermute | solution.py:22
  136.3 2.7 %collective-permute-done.33.got_a = bf16[64,1024]{1,0:T(8,128)(2,1)S(1)} collective-permute-done((bf16[64,1024]{1,0:T(8,128)(2,1)S(1)}, bf16[64,1024]{1,0:T(8,128)(2,1)S(1)}, u32[]{:S(2)}, u32[]{:S(2)}) %collective-permute-start.33) | collective-permute-done | bytes 131104 | tf_op jit(solution)/shard_map/ppermute | solution.py:22
  139.0 0.8 shard_map.139
  139.9 1.0 shard_map.137
  (61 shorter events, 7.3 us)
Async XLA Ops:
  0.6 14.7 %collective-permute-start.2 = (bf16[136,1024]{1,0:T(8,128)(2,1)}, bf16[136,1024]{1,0:T(8,128)(2,1)S(1)}, u32[]{:S(2)}, u32[]{:S(2)}) collective-permute-start(bf16[136,1024]{1,0:T(8,128)(2,1)} %bitcast.15), channel_id=1, source_target_pairs={{0,4},{4,0},{1,5},{5,1},{2,6},{6,2},{3,7},{7,3},{8,12},{12,8},{9,1... | collective-permute-start | bytes 835592 | tf_op jit(solution)/shard_map/ppermute | solution.py:22
  3.0 14.9 %collective-permute-start.1 = (bf16[136,1024]{1,0:T(8,128)(2,1)}, bf16[136,1024]{1,0:T(8,128)(2,1)S(1)}, u32[]{:S(2)}, u32[]{:S(2)}) collective-permute-start(bf16[136,1024]{1,0:T(8,128)(2,1)} %bitcast.16), channel_id=1, source_target_pairs={{0,2},{2,0},{1,3},{3,1},{4,6},{6,4},{5,7},{7,5},{8,10},{10,8},{9,1... | collective-permute-start | bytes 835592 | tf_op jit(solution)/shard_map/ppermute | solution.py:22
  4.3 24.4 %collective-permute-start = (bf16[136,1024]{1,0:T(8,128)(2,1)}, bf16[136,1024]{1,0:T(8,128)(2,1)S(1)}, u32[]{:S(2)}, u32[]{:S(2)}) collective-permute-start(bf16[136,1024]{1,0:T(8,128)(2,1)} %bitcast.17), channel_id=1, source_target_pairs={{0,1},{1,0},{2,3},{3,2},{4,5},{5,4},{6,7},{7,6},{8,9},{9,8},{10,11... | collective-permute-start | bytes 835592 | tf_op jit(solution)/shard_map/ppermute | solution.py:22
  15.4 6.6 %collective-permute-start.4 = (bf16[136,1024]{1,0:T(8,128)(2,1)S(1)}, bf16[136,1024]{1,0:T(8,128)(2,1)S(1)}, u32[]{:S(2)}, u32[]{:S(2)}) collective-permute-start(bf16[136,1024]{1,0:T(8,128)(2,1)S(1)} %collective-permute-done.2.refs_3_), channel_id=1, source_target_pairs={{0,1},{1,0},{2,3},{3,2},{4,5},{5,4},{6,7},{7,6},{8,9},{9,8},{10,11... | collective-permute-start | bytes 835592 | tf_op jit(solution)/shard_map/ppermute | solution.py:22
  17.9 10.8 %collective-permute-start.3 = (bf16[136,1024]{1,0:T(8,128)(2,1)S(1)}, bf16[136,1024]{1,0:T(8,128)(2,1)S(1)}, u32[]{:S(2)}, u32[]{:S(2)}) collective-permute-start(bf16[136,1024]{1,0:T(8,128)(2,1)S(1)} %collective-permute-done.1.refs_2_), channel_id=1, source_target_pairs={{0,1},{1,0},{2,3},{3,2},{4,5},{5,4},{6,7},{7,6},{8,9},{9,8},{10,11... | collective-permute-start | bytes 835592 | tf_op jit(solution)/shard_map/ppermute | solution.py:22
  18.6 11.7 %collective-permute-start.5 = (bf16[136,1024]{1,0:T(8,128)(2,1)S(1)}, bf16[136,1024]{1,0:T(8,128)(2,1)S(1)}, u32[]{:S(2)}, u32[]{:S(2)}) collective-permute-start(bf16[136,1024]{1,0:T(8,128)(2,1)S(1)} %collective-permute-done.2.refs_3_), channel_id=1, source_target_pairs={{0,2},{2,0},{1,3},{3,1},{4,6},{6,4},{5,7},{7,5},{8,10},{10,8},{9,1... | collective-permute-start | bytes 835592 | tf_op jit(solution)/shard_map/ppermute | solution.py:22
  21.9 9.2 %collective-permute-start.6 = (bf16[136,1024]{1,0:T(8,128)(2,1)S(1)}, bf16[136,1024]{1,0:T(8,128)(2,1)S(1)}, u32[]{:S(2)}, u32[]{:S(2)}) collective-permute-start(bf16[136,1024]{1,0:T(8,128)(2,1)S(1)} %collective-permute-done.4.refs_5_), channel_id=1, source_target_pairs={{0,2},{2,0},{1,3},{3,1},{4,6},{6,4},{5,7},{7,5},{8,10},{10,8},{9,1... | collective-permute-start | bytes 835592 | tf_op jit(solution)/shard_map/ppermute | solution.py:22
  24.6 1.2 copy-start.1
  25.8 1.2 copy-start.3
  27.0 1.2 copy-start.5
  28.3 1.0 copy-start.8
  31.1 20.0 %copy-start = (bf16[1,512,2048]{2,1,0:T(8,128)(2,1)S(1)}, bf16[1,512,2048]{2,1,0:T(8,128)(2,1)}, u32[]{:S(2)}) copy-start(bf16[1,512,2048]{2,1,0:T(8,128)(2,1)} %param.14) | copy-start | bytes 6291460
  31.1 20.0 %copy-start.7 = (bf16[1,136,1024]{2,1,0:T(8,128)(2,1)S(1)}, bf16[1,136,1024]{2,1,0:T(8,128)(2,1)}, u32[]{:S(2)}) copy-start(bf16[1,136,1024]{2,1,0:T(8,128)(2,1)} %param.10) | copy-start | bytes 835588
  34.9 7.6 %collective-permute-start.7 = (bf16[80,128]{1,0:T(8,128)(2,1)S(1)}, bf16[80,128]{1,0:T(8,128)(2,1)S(1)}, u32[]{:S(2)}, u32[]{:S(2)}) collective-permute-start(bf16[80,128]{1,0:T(8,128)(2,1)S(1)} %get-tuple-element.78), channel_id=1, source_target_pairs={{0,1},{1,0},{2,3},{3,2},{4,5},{5,4},{6,7},{7,6},{8,9},{9,8},{10,11... | collective-permute-start | bytes 61448 | tf_op jit(solution)/shard_map/ppermute | solution.py:468
  36.2 9.6 %collective-permute-start.8 = (bf16[80,128]{1,0:T(8,128)(2,1)S(1)}, bf16[80,128]{1,0:T(8,128)(2,1)S(1)}, u32[]{:S(2)}, u32[]{:S(2)}) collective-permute-start(bf16[80,128]{1,0:T(8,128)(2,1)S(1)} %get-tuple-element.79), channel_id=1, source_target_pairs={{0,2},{1,3},{2,0},{3,1},{4,6},{5,7},{6,4},{7,5},{8,10},{9,11},{10,... | collective-permute-start | bytes 61448 | tf_op jit(solution)/shard_map/ppermute | solution.py:468
  38.4 7.5 %collective-permute-start.9 = (bf16[80,128]{1,0:T(8,128)(2,1)S(1)}, bf16[80,128]{1,0:T(8,128)(2,1)S(1)}, u32[]{:S(2)}, u32[]{:S(2)}) collective-permute-start(bf16[80,128]{1,0:T(8,128)(2,1)S(1)} %get-tuple-element.80), channel_id=1, source_target_pairs={{0,4},{1,5},{2,6},{3,7},{4,0},{5,1},{6,2},{7,3},{8,12},{9,13},{10,... | collective-permute-start | bytes 61448 | tf_op jit(solution)/shard_map/ppermute | solution.py:468
  41.4 4.5 %collective-permute-start.10 = (bf16[80,128]{1,0:T(8,128)(2,1)S(1)}, bf16[80,128]{1,0:T(8,128)(2,1)S(1)}, u32[]{:S(2)}, u32[]{:S(2)}) collective-permute-start(bf16[80,128]{1,0:T(8,128)(2,1)S(1)} %get-tuple-element.81), channel_id=1, source_target_pairs={{0,3},{1,2},{2,1},{3,0},{4,7},{5,6},{6,5},{7,4},{8,11},{9,10},{10,... | collective-permute-start | bytes 61448 | tf_op jit(solution)/shard_map/ppermute | solution.py:468
  41.6 4.4 %collective-permute-start.11 = (bf16[80,128]{1,0:T(8,128)(2,1)S(1)}, bf16[80,128]{1,0:T(8,128)(2,1)S(1)}, u32[]{:S(2)}, u32[]{:S(2)}) collective-permute-start(bf16[80,128]{1,0:T(8,128)(2,1)S(1)} %get-tuple-element.82), channel_id=1, source_target_pairs={{0,5},{1,4},{2,7},{3,6},{4,1},{5,0},{6,3},{7,2},{8,13},{9,12},{10,... | collective-permute-start | bytes 61448 | tf_op jit(solution)/shard_map/ppermute | solution.py:468
  42.5 4.8 %collective-permute-start.12 = (bf16[80,128]{1,0:T(8,128)(2,1)S(1)}, bf16[80,128]{1,0:T(8,128)(2,1)S(1)}, u32[]{:S(2)}, u32[]{:S(2)}) collective-permute-start(bf16[80,128]{1,0:T(8,128)(2,1)S(1)} %get-tuple-element.83), channel_id=1, source_target_pairs={{0,6},{1,7},{2,4},{3,5},{4,2},{5,3},{6,0},{7,1},{8,14},{9,15},{10,... | collective-permute-start | bytes 61448 | tf_op jit(solution)/shard_map/ppermute | solution.py:468
  45.8 5.3 %collective-permute-start.13 = (bf16[80,128]{1,0:T(8,128)(2,1)S(1)}, bf16[80,128]{1,0:T(8,128)(2,1)S(1)}, u32[]{:S(2)}, u32[]{:S(2)}) collective-permute-start(bf16[80,128]{1,0:T(8,128)(2,1)S(1)} %get-tuple-element.84), channel_id=1, source_target_pairs={{0,7},{1,6},{2,5},{3,4},{4,3},{5,2},{6,1},{7,0},{8,15},{9,14},{10,... | collective-permute-start | bytes 61448 | tf_op jit(solution)/shard_map/ppermute | solution.py:468
  52.7 5.1 %collective-permute-start.14 = (bf16[80,128]{1,0:T(8,128)(2,1)S(1)}, bf16[80,128]{1,0:T(8,128)(2,1)S(1)}, u32[]{:S(2)}, u32[]{:S(2)}) collective-permute-start(bf16[80,128]{1,0:T(8,128)(2,1)S(1)} %get-tuple-element.86), channel_id=1, source_target_pairs={{0,1},{1,0},{2,3},{3,2},{4,5},{5,4},{6,7},{7,6},{8,9},{9,8},{10,11... | collective-permute-start | bytes 61448 | tf_op jit(solution)/shard_map/ppermute | solution.py:468
  53.0 5.1 %collective-permute-start.15 = (bf16[80,128]{1,0:T(8,128)(2,1)S(1)}, bf16[80,128]{1,0:T(8,128)(2,1)S(1)}, u32[]{:S(2)}, u32[]{:S(2)}) collective-permute-start(bf16[80,128]{1,0:T(8,128)(2,1)S(1)} %get-tuple-element.87), channel_id=1, source_target_pairs={{0,2},{1,3},{2,0},{3,1},{4,6},{5,7},{6,4},{7,5},{8,10},{9,11},{10,... | collective-permute-start | bytes 61448 | tf_op jit(solution)/shard_map/ppermute | solution.py:468
  53.0 10.1 %collective-permute-start.16 = (bf16[80,128]{1,0:T(8,128)(2,1)S(1)}, bf16[80,128]{1,0:T(8,128)(2,1)S(1)}, u32[]{:S(2)}, u32[]{:S(2)}) collective-permute-start(bf16[80,128]{1,0:T(8,128)(2,1)S(1)} %get-tuple-element.88), channel_id=1, source_target_pairs={{0,4},{1,5},{2,6},{3,7},{4,0},{5,1},{6,2},{7,3},{8,12},{9,13},{10,... | collective-permute-start | bytes 61448 | tf_op jit(solution)/shard_map/ppermute | solution.py:468
  53.6 9.4 %collective-permute-start.17 = (bf16[80,128]{1,0:T(8,128)(2,1)S(1)}, bf16[80,128]{1,0:T(8,128)(2,1)S(1)}, u32[]{:S(2)}, u32[]{:S(2)}) collective-permute-start(bf16[80,128]{1,0:T(8,128)(2,1)S(1)} %get-tuple-element.89), channel_id=1, source_target_pairs={{0,3},{1,2},{2,1},{3,0},{4,7},{5,6},{6,5},{7,4},{8,11},{9,10},{10,... | collective-permute-start | bytes 61448 | tf_op jit(solution)/shard_map/ppermute | solution.py:468
  55.4 7.7 %collective-permute-start.18 = (bf16[80,128]{1,0:T(8,128)(2,1)S(1)}, bf16[80,128]{1,0:T(8,128)(2,1)S(1)}, u32[]{:S(2)}, u32[]{:S(2)}) collective-permute-start(bf16[80,128]{1,0:T(8,128)(2,1)S(1)} %get-tuple-element.90), channel_id=1, source_target_pairs={{0,5},{1,4},{2,7},{3,6},{4,1},{5,0},{6,3},{7,2},{8,13},{9,12},{10,... | collective-permute-start | bytes 61448 | tf_op jit(solution)/shard_map/ppermute | solution.py:468
  57.7 5.4 %collective-permute-start.19 = (bf16[80,128]{1,0:T(8,128)(2,1)S(1)}, bf16[80,128]{1,0:T(8,128)(2,1)S(1)}, u32[]{:S(2)}, u32[]{:S(2)}) collective-permute-start(bf16[80,128]{1,0:T(8,128)(2,1)S(1)} %get-tuple-element.91), channel_id=1, source_target_pairs={{0,6},{1,7},{2,4},{3,5},{4,2},{5,3},{6,0},{7,1},{8,14},{9,15},{10,... | collective-permute-start | bytes 61448 | tf_op jit(solution)/shard_map/ppermute | solution.py:468
  58.1 5.3 %collective-permute-start.20 = (bf16[80,128]{1,0:T(8,128)(2,1)S(1)}, bf16[80,128]{1,0:T(8,128)(2,1)S(1)}, u32[]{:S(2)}, u32[]{:S(2)}) collective-permute-start(bf16[80,128]{1,0:T(8,128)(2,1)S(1)} %get-tuple-element.92), channel_id=1, source_target_pairs={{0,7},{1,6},{2,5},{3,4},{4,3},{5,2},{6,1},{7,0},{8,15},{9,14},{10,... | collective-permute-start | bytes 61448 | tf_op jit(solution)/shard_map/ppermute | solution.py:468
  63.4 8.5 %collective-permute-start.28 = (bf16[256,1024]{1,0:T(8,128)(2,1)S(1)}, bf16[256,1024]{1,0:T(8,128)(2,1)S(1)}, u32[]{:S(2)}, u32[]{:S(2)}) collective-permute-start(bf16[256,1024]{1,0:T(8,128)(2,1)S(1)} %get-tuple-element.132), channel_id=1, source_target_pairs={{0,1},{1,0},{2,3},{3,2},{4,5},{5,4},{6,7},{7,6},{8,9},{9,8},{10,11... | collective-permute-start | bytes 1572872 | tf_op jit(solution)/shard_map/ppermute | solution.py:22
  64.4 8.5 %collective-permute-start.29 = (bf16[256,1024]{1,0:T(8,128)(2,1)S(1)}, bf16[256,1024]{1,0:T(8,128)(2,1)S(1)}, u32[]{:S(2)}, u32[]{:S(2)}) collective-permute-start(bf16[256,1024]{1,0:T(8,128)(2,1)S(1)} %get-tuple-element.133), channel_id=1, source_target_pairs={{0,2},{2,0},{1,3},{3,1},{4,6},{6,4},{5,7},{7,5},{8,10},{10,8},{9,1... | collective-permute-start | bytes 1572872 | tf_op jit(solution)/shard_map/ppermute | solution.py:22
  73.0 15.1 %collective-permute-start.30 = (bf16[128,1024]{1,0:T(8,128)(2,1)S(1)}, bf16[128,1024]{1,0:T(8,128)(2,1)S(1)}, u32[]{:S(2)}, u32[]{:S(2)}) collective-permute-start(bf16[128,1024]{1,0:T(8,128)(2,1)S(1)} %get-tuple-element.136), channel_id=1, source_target_pairs={{0,2},{2,0},{1,3},{3,1},{4,6},{6,4},{5,7},{7,5},{8,10},{10,8},{9,1... | collective-permute-start | bytes 786440 | tf_op jit(solution)/shard_map/ppermute | solution.py:22
  73.3 15.1 %collective-permute-start.31 = (bf16[128,1024]{1,0:T(8,128)(2,1)S(1)}, bf16[128,1024]{1,0:T(8,128)(2,1)S(1)}, u32[]{:S(2)}, u32[]{:S(2)}) collective-permute-start(bf16[128,1024]{1,0:T(8,128)(2,1)S(1)} %get-tuple-element.137), channel_id=1, source_target_pairs={{0,1},{1,0},{2,3},{3,2},{4,5},{5,4},{6,7},{7,6},{8,9},{9,8},{10,11... | collective-permute-start | bytes 786440 | tf_op jit(solution)/shard_map/ppermute | solution.py:22
  74.1 9.8 %collective-permute-start.21 = (bf16[408,128]{1,0:T(8,128)(2,1)S(1)}, bf16[408,128]{1,0:T(8,128)(2,1)S(1)}, u32[]{:S(2)}, u32[]{:S(2)}) collective-permute-start(bf16[408,128]{1,0:T(8,128)(2,1)S(1)} %get-tuple-element.120), channel_id=1, source_target_pairs={{0,1},{1,0},{2,3},{3,2},{4,5},{5,4},{6,7},{7,6},{8,9},{9,8},{10,11... | collective-permute-start | bytes 313352 | tf_op jit(solution)/shard_map/ppermute | solution.py:468
  74.7 10.0 %collective-permute-start.22 = (bf16[408,128]{1,0:T(8,128)(2,1)S(1)}, bf16[408,128]{1,0:T(8,128)(2,1)S(1)}, u32[]{:S(2)}, u32[]{:S(2)}) collective-permute-start(bf16[408,128]{1,0:T(8,128)(2,1)S(1)} %get-tuple-element.121), channel_id=1, source_target_pairs={{0,2},{1,3},{2,0},{3,1},{4,6},{5,7},{6,4},{7,5},{8,10},{9,11},{10,... | collective-permute-start | bytes 313352 | tf_op jit(solution)/shard_map/ppermute | solution.py:468
  76.0 15.8 %collective-permute-start.23 = (bf16[408,128]{1,0:T(8,128)(2,1)S(1)}, bf16[408,128]{1,0:T(8,128)(2,1)S(1)}, u32[]{:S(2)}, u32[]{:S(2)}) collective-permute-start(bf16[408,128]{1,0:T(8,128)(2,1)S(1)} %get-tuple-element.122), channel_id=1, source_target_pairs={{0,4},{1,5},{2,6},{3,7},{4,0},{5,1},{6,2},{7,3},{8,12},{9,13},{10,... | collective-permute-start | bytes 313352 | tf_op jit(solution)/shard_map/ppermute | solution.py:468
  83.9 7.9 %collective-permute-start.24 = (bf16[408,128]{1,0:T(8,128)(2,1)S(1)}, bf16[408,128]{1,0:T(8,128)(2,1)S(1)}, u32[]{:S(2)}, u32[]{:S(2)}) collective-permute-start(bf16[408,128]{1,0:T(8,128)(2,1)S(1)} %get-tuple-element.123), channel_id=1, source_target_pairs={{0,3},{1,2},{2,1},{3,0},{4,7},{5,6},{6,5},{7,4},{8,11},{9,10},{10,... | collective-permute-start | bytes 313352 | tf_op jit(solution)/shard_map/ppermute | solution.py:468
  84.7 7.1 %collective-permute-start.25 = (bf16[408,128]{1,0:T(8,128)(2,1)S(1)}, bf16[408,128]{1,0:T(8,128)(2,1)S(1)}, u32[]{:S(2)}, u32[]{:S(2)}) collective-permute-start(bf16[408,128]{1,0:T(8,128)(2,1)S(1)} %get-tuple-element.124), channel_id=1, source_target_pairs={{0,5},{1,4},{2,7},{3,6},{4,1},{5,0},{6,3},{7,2},{8,13},{9,12},{10,... | collective-permute-start | bytes 313352 | tf_op jit(solution)/shard_map/ppermute | solution.py:468
  88.1 6.4 %collective-permute-start.26 = (bf16[408,128]{1,0:T(8,128)(2,1)S(1)}, bf16[408,128]{1,0:T(8,128)(2,1)S(1)}, u32[]{:S(2)}, u32[]{:S(2)}) collective-permute-start(bf16[408,128]{1,0:T(8,128)(2,1)S(1)} %get-tuple-element.125), channel_id=1, source_target_pairs={{0,6},{1,7},{2,4},{3,5},{4,2},{5,3},{6,0},{7,1},{8,14},{9,15},{10,... | collective-permute-start | bytes 313352 | tf_op jit(solution)/shard_map/ppermute | solution.py:468
  88.3 8.6 %copy-start.2 = (bf16[1,1024,512]{2,1,0:T(8,128)(2,1)S(1)}, bf16[1,1024,512]{2,1,0:T(8,128)(2,1)}, u32[]{:S(2)}) copy-start(bf16[1,1024,512]{2,1,0:T(8,128)(2,1)} %param.11) | copy-start | bytes 3145732
  88.3 8.6 %copy-start.4 = (bf16[1,1024,512]{2,1,0:T(8,128)(2,1)S(1)}, bf16[1,1024,512]{2,1,0:T(8,128)(2,1)}, u32[]{:S(2)}) copy-start(bf16[1,1024,512]{2,1,0:T(8,128)(2,1)} %param.12) | copy-start | bytes 3145732
  88.3 8.6 %copy-start.6 = (bf16[1,1024,512]{2,1,0:T(8,128)(2,1)S(1)}, bf16[1,1024,512]{2,1,0:T(8,128)(2,1)}, u32[]{:S(2)}) copy-start(bf16[1,1024,512]{2,1,0:T(8,128)(2,1)} %param.13) | copy-start | bytes 3145732
  88.4 8.6 %collective-permute-start.27 = (bf16[408,128]{1,0:T(8,128)(2,1)S(1)}, bf16[408,128]{1,0:T(8,128)(2,1)S(1)}, u32[]{:S(2)}, u32[]{:S(2)}) collective-permute-start(bf16[408,128]{1,0:T(8,128)(2,1)S(1)} %get-tuple-element.126), channel_id=1, source_target_pairs={{0,7},{1,6},{2,5},{3,4},{4,3},{5,2},{6,1},{7,0},{8,15},{9,14},{10,... | collective-permute-start | bytes 313352 | tf_op jit(solution)/shard_map/ppermute | solution.py:468
  98.3 41.5 %collective-permute-start.32 = (bf16[136,1024]{1,0:T(8,128)(2,1)S(1)}, bf16[136,1024]{1,0:T(8,128)(2,1)S(1)}, u32[]{:S(2)}, u32[]{:S(2)}) collective-permute-start(bf16[136,1024]{1,0:T(8,128)(2,1)S(1)} %shard_map.136), channel_id=1, source_target_pairs={{8,7},{9,6},{10,5},{11,4},{12,3},{13,2},{14,1},{15,0},{16,15},{17,... | collective-permute-start | bytes 835592 | tf_op jit(solution)/shard_map/ppermute | solution.py:613
  114.8 21.5 %collective-permute-start.34 = (bf16[64,1024]{1,0:T(8,128)(2,1)S(1)}, bf16[64,1024]{1,0:T(8,128)(2,1)S(1)}, u32[]{:S(2)}, u32[]{:S(2)}) collective-permute-start(bf16[64,1024]{1,0:T(8,128)(2,1)S(1)} %get-tuple-element.144), channel_id=1, source_target_pairs={{0,4},{4,0},{1,5},{5,1},{2,6},{6,2},{3,7},{7,3},{8,12},{12,8},{9,1... | collective-permute-start | bytes 393224 | tf_op jit(solution)/shard_map/ppermute | solution.py:22
  115.5 23.5 %collective-permute-start.33 = (bf16[64,1024]{1,0:T(8,128)(2,1)S(1)}, bf16[64,1024]{1,0:T(8,128)(2,1)S(1)}, u32[]{:S(2)}, u32[]{:S(2)}) collective-permute-start(bf16[64,1024]{1,0:T(8,128)(2,1)S(1)} %get-tuple-element.138.refs_13_), channel_id=1, source_target_pairs={{0,4},{4,0},{1,5},{5,1},{2,6},{6,2},{3,7},{7,3},{8,12},{12,8},{9,1... | collective-permute-start | bytes 393224 | tf_op jit(solution)/shard_map/ppermute | solution.py:22
  118.2 21.6 %copy-start.9 = (s32[1,136]{1,0:T(1,128)S(1)}, s32[1,136]{1,0:T(1,128)}, u32[]{:S(2)}) copy-start(s32[1,136]{1,0:T(1,128)} %order_ref.1) | copy-start | bytes 1636

commit v8 on v7

--- a/solution.py
+++ b/solution.py
@@ -331,7 +331,7 @@
     attended = low(attended)
     factor = jnp.exp(-dot(attended, w_ref[:, width:]))
     scaled = inc_ref[...].astype(jnp.float32) * factor
-    up_ref[...] = scaled
+    up_ref[...] = low(scaled)
     shift_part = dot(attended, w_ref[:, :width])
     latent_part = scaled * (act_ref[...].astype(jnp.float32) - shift_part)
     grad_affine = jnp.concatenate([-scaled, 1.0 - latent_part], axis=1).astype(jnp.bfloat16)
@@ -382,7 +382,7 @@
         gq_ref[:, start:stop] = dot(key, scores, ((0,), (0,)))
     grad_q = jnp.transpose(gq_ref[...])
     qk_sum = v_sum = 0.0
-    for m, out_ref in enumerate(out_refs):
+    for m in range(HEADS):
         own = slice(m * rows, (m + 1) * rows)
         normed, unit, scale = [
             early[i][m] if m < first else late[i][m - first] for i in range(3)
@@ -390,8 +390,9 @@
         raw = jnp.concatenate([grad_q[own], gk_ref[own, :]], axis=1) * HEAD_DIM ** (-0.5)
         back = scale * (raw - unit * (half_sums(raw * unit) / HEAD_DIM))
         back, grad_v = back.astype(jnp.bfloat16), gv_ref[own, :]
-        out_ref[:PACKED, :] = low(pack(grad_v))
-        out_ref[PACKED : PACKED + rows, :] = back
+        mirrored = out_refs[DISTANCES.index(DISTANCES[m] ^ HEADS - 1)]
+        mirrored[:PACKED, :] = low(pack(grad_v))
+        mirrored[PACKED : PACKED + rows, :] = back
         qk_sum = qk_sum + dot(back, normed, ((0,), (0,)))
         v_sum = v_sum + dot(grad_v.astype(jnp.bfloat16), normed, ((0,), (0,)))
     step = qk_sum.shape[1] // HEADS
@@ -414,7 +415,7 @@
 
 
 def second_sum_kernel(*refs):
-    for second, got, out in zip(refs[0:2], refs[2:4], refs[5:7]):
+    for second, got, out in zip(refs[0:2], refs[2:4], refs[-2:]):
         start = got.shape[0] - second.shape[0]
         out[...] = low(wide(second[...]) + wide(got[start:, :]))
 
@@ -423,7 +424,7 @@
     for i in range(2):
         third, keep, got, more = [ref[...] for ref in refs[i:8:2]]
         size = third.shape[0]
-        leaving, staying = refs[8 + i], refs[10 + i]
+        leaving, staying = refs[9 + i], refs[11 + i]
         leaving[...] = low(wide(third) + wide(got[size : 2 * size]) + wide(more[size:]))
         staying[...] = wide(keep) + wide(got[:size]) + wide(more[:size])
 
@@ -453,7 +454,7 @@
         left = jnp.concatenate(parts, axis=1).astype(jnp.bfloat16)
         total = total + dot(left, ref[...], ((1,), (1,)))
     total = total - unit * jnp.mean(total * unit, axis=-1, keepdims=True)
-    out_ref[...] = (up_ref[...] + row_scale * total).astype(jnp.bfloat16)
+    out_ref[...] = (wide(up_ref[...]) + row_scale * total).astype(jnp.bfloat16)
 
 
 def reorder_kernel(order_ref, rows_ref, out_ref):
@@ -499,7 +500,6 @@
     activations, incoming, w_query, w_key, w_value, w_out, block_ids, flip_order
 ):
     parts = lax.axis_size("seq")
-    sections = lax.axis_size("section")
     me = lax.axis_index("seq").astype(jnp.int32).reshape(1)
     field, upstream = activations[0], incoming[0]
     wq, wk, wv, wo = w_query[0], w_key[0], w_value[0], w_out[0]
@@ -556,7 +556,7 @@
         affine_kernel,
         2,
         [("s", me)] + [("v", x) for x in (*packed, field, upstream, wo)],
-        [out(rows, 2 * width), out(rows, width, dtype=f32)] + [out(PACKED, 128)] * HEADS,
+        [out(rows, 2 * width), out(rows, width)] + [out(PACKED, 128)] * HEADS,
         [pltpu.VMEM((HEADS, PACKED, 128), jnp.bfloat16)],
     )
     grad_slabs = exchange(grad_slabs)
@@ -566,7 +566,8 @@
         [("v", x) for x in (*packed, grad_affine)],
         [out(len(group) * HEAD_DIM, width) for order in ORDERS for group in order],
     )
-    grad_slabs, terms = lax.optimization_barrier((grad_slabs, terms))
+    grad_slabs, terms, scaled = lax.optimization_barrier((grad_slabs, terms, scaled))
+    scaled = hop(scaled, parts - 1)
     first, second, third, keep = zip(terms[:4], terms[4:])
     got = [partner(part, "seq", bit) for bit, part in enumerate(first)]
     grads = call(
@@ -587,30 +588,25 @@
     leaving = call(
         second_sum_kernel,
         1,
-        [("v", x) for x in (*second, *got)] + [("a", grads[0])],
+        [("v", x) for x in (*second, *got)] + [("a", x) for x in (*slabs[1:3], scaled)],
         [out(*second[0].shape)] * 2,
     )
     more = [partner(part, "seq", 1 - bit) for bit, part in enumerate(leaving)]
     *leaving, keep_a, keep_b = call(
         third_sum_kernel,
         2,
-        [("v", x) for x in (*third, *keep, *got, *more)],
+        [("v", x) for x in (*third, *keep, *got, *more)] + [("a", slabs[5])],
         [out(*third[0].shape)] * 2 + [out(*keep[0].shape, dtype=f32)] * 2,
     )
     rest = [partner(part, "seq", 2) for part in leaving]
     (grad_input,) = call(
         input_kernel,
         1.5,
-        [("s", me)] + [("v", x) for x in (*slabs, wq, wk, wv, field, scaled)] + [("a", leaving[0])],
+        [("s", me)] + [("v", x) for x in (*slabs, wq, wk, wv, blocks[-1], scaled)] + [("a", leaving[0])],
         [out(rows, width)],
         [pltpu.VMEM((HEADS, PACKED + rows, 128), jnp.bfloat16)],
     )
-    route = [
-        (s * parts + d, (s - 1) * parts + parts - 1 - d)
-        for s in range(1, sections)
-        for d in range(parts)
-    ]
-    moved = lax.ppermute(grad_input, ("section", "seq"), route)
+    moved = to_previous(grad_input)
     grad_q, grad_k, grad_v = call(
         turn_kernel,
         1,

time: 141 us -> 133 us (0.943)
  waiting for transfers between devices: 53.1 us -> 44.3 us
    ppermute x13, waiting for transfers between devices: 35.8 us -> 25 us  [partner(): return lax.ppermute(block, axis, route)]
    ppermute x1, starting transfers between devices: 16.4 us -> 13.1 us  [shifted(): return lax.ppermute(block, axis, route)]
    ppermute x21 -> x22, starting transfers between devices: 31.2 us -> 34 us  [hop(): return lax.ppermute(block, 'seq', route)]
    ppermute x21 -> x22, waiting for transfers between devices: 17.3 us -> 19.3 us  [hop(): return lax.ppermute(block, 'seq', route)]
  transfers between devices with their start and end apart: 35 -> 36, of which waited for: 15 -> 15; matrix products, arithmetic and copies ran while one was open for 2% -> 2% of each run, Pallas kernels for 7% -> 8%
where the time goes in v8:
time: 133 us; the launch traced here: 131 us
  starting transfers between devices  62.2 us (47%)
  waiting for transfers between devices  44.3 us (33%)
  Pallas kernels  17.7 us (13%)
  local copies, waits for them, and re-layouts  5.79 us (4%)
    ppermute x22, starting transfers between devices, hop(): return lax.ppermute(block, 'seq', route)  34 us
    ppermute x13, waiting for transfers between devices, partner(): return lax.ppermute(block, axis, route)  25 us
    ppermute x22, waiting for transfers between devices, hop(): return lax.ppermute(block, 'seq', route)  19.3 us
    pallas_call x12, Pallas kernels, call(): pl.pallas_call(kernel, out_shape=tuple(outs), in_specs=[pl.BlockSpec(memo...  17.7 us
    ppermute x13, starting transfers between devices, partner(): return lax.ppermute(block, axis, route)  15 us
    ppermute x1, starting transfers between devices, shifted(): return lax.ppermute(block, axis, route)  13.1 us
    unnamed x20, local copies, waits for them, and re-layouts  4.15 us
  transfers between devices with their start and end apart: 36, of which 15 were waited for; matrix products, arithmetic and copies ran while one was open for 2% of the time, Pallas kernels for 8%

profile of v8, /device:TPU:5, one launch (start us, length us, event | category | flops | bytes accessed | tf_op | source)
XLA Modules:
  0.0 131.5 jit_solution(4621378056556494015)
XLA Ops:
  0.6 2.4 %collective-permute-start.2 = (bf16[136,1024]{1,0:T(8,128)(2,1)}, bf16[136,1024]{1,0:T(8,128)(2,1)S(1)}, u32[]{:S(2)}, u32[]{:S(2)}) collective-permute-start(bf16[136,1024]{1,0:T(8,128)(2,1)} %bitcast.14), channel_id=1, source_target_pairs={{0,4},{4,0},{1,5},{5,1},{2,6},{6,2},{3,7},{7,3},{8,12},{12,8},{9,1... | collective-permute-start | bytes 835592 | tf_op jit(solution)/shard_map/ppermute | solution.py:22
  3.0 1.3 collective-permute-start.1
  4.3 1.2 collective-permute-start
  6.2 9.2 %collective-permute-done.2.refs_3_ = bf16[136,1024]{1,0:T(8,128)(2,1)S(1)} collective-permute-done((bf16[136,1024]{1,0:T(8,128)(2,1)}, bf16[136,1024]{1,0:T(8,128)(2,1)S(1)}, u32[]{:S(2)}, u32[]{:S(2)}) %collective-permute-start.2) | collective-permute-done | bytes 278560 | tf_op jit(solution)/shard_map/ppermute | solution.py:22
  15.4 1.2 collective-permute-start.4
  16.6 0.8 reshape.64
  18.6 1.6 %collective-permute-start.5 = (bf16[136,1024]{1,0:T(8,128)(2,1)S(1)}, bf16[136,1024]{1,0:T(8,128)(2,1)S(1)}, u32[]{:S(2)}, u32[]{:S(2)}) collective-permute-start(bf16[136,1024]{1,0:T(8,128)(2,1)S(1)} %collective-permute-done.2.refs_3_), channel_id=1, source_target_pairs={{0,2},{2,0},{1,3},{3,1},{4,6},{6,4},{5,7},{7,5},{8,10},{10,8},{9,1... | collective-permute-start | bytes 835592 | tf_op jit(solution)/shard_map/ppermute | solution.py:22
  20.2 1.7 %collective-permute-done.4.refs_5_ = bf16[136,1024]{1,0:T(8,128)(2,1)S(1)} collective-permute-done((bf16[136,1024]{1,0:T(8,128)(2,1)S(1)}, bf16[136,1024]{1,0:T(8,128)(2,1)S(1)}, u32[]{:S(2)}, u32[]{:S(2)}) %collective-permute-start.4) | collective-permute-done | bytes 278560 | tf_op jit(solution)/shard_map/ppermute | solution.py:22
  21.9 2.7 %collective-permute-start.6 = (bf16[136,1024]{1,0:T(8,128)(2,1)S(1)}, bf16[136,1024]{1,0:T(8,128)(2,1)S(1)}, u32[]{:S(2)}, u32[]{:S(2)}) collective-permute-start(bf16[136,1024]{1,0:T(8,128)(2,1)S(1)} %collective-permute-done.4.refs_5_), channel_id=1, source_target_pairs={{0,2},{2,0},{1,3},{3,1},{4,6},{6,4},{5,7},{7,5},{8,10},{10,8},{9,1... | collective-permute-start | bytes 835592 | tf_op jit(solution)/shard_map/ppermute | solution.py:22
  24.6 1.2 copy-done.1
  25.8 1.2 copy-done.3
  27.0 1.2 copy-done.5
  29.2 1.1 shard_map.129
  30.4 0.8 collective-permute-done.6.last_ref.refs_11_
  31.1 3.8 %shard_map.130 = (bf16[2,136,1024]{2,1,0:T(8,128)(2,1)S(1)}, f32[2,136,128]{2,1,0:T(8,128)S(1)}, f32[2,136,128]{2,1,0:T(8,128)S(1)}, bf16[1088,1088]{1,0:T(8,128...) custom-call(f32[6,136,128]{2,1,0:T(8,128)S(1)} %get-tuple-element.76, ...), custom_call_target="tpu_custom_call" | custom-call | flops 5000000000 | bytes 1024 | tf_op jit(solution)/shard_map/pallas_call | solution.py:200
  34.9 1.3 collective-permute-start.7
  36.2 2.2 %collective-permute-start.8 = (bf16[80,128]{1,0:T(8,128)(2,1)S(1)}, bf16[80,128]{1,0:T(8,128)(2,1)S(1)}, u32[]{:S(2)}, u32[]{:S(2)}) collective-permute-start(bf16[80,128]{1,0:T(8,128)(2,1)S(1)} %get-tuple-element.80), channel_id=1, source_target_pairs={{0,2},{1,3},{2,0},{3,1},{4,6},{5,7},{6,4},{7,5},{8,10},{9,11},{10,... | collective-permute-start | bytes 61448 | tf_op jit(solution)/shard_map/ppermute | solution.py:469
  38.4 3.0 %collective-permute-start.9 = (bf16[80,128]{1,0:T(8,128)(2,1)S(1)}, bf16[80,128]{1,0:T(8,128)(2,1)S(1)}, u32[]{:S(2)}, u32[]{:S(2)}) collective-permute-start(bf16[80,128]{1,0:T(8,128)(2,1)S(1)} %get-tuple-element.81), channel_id=1, source_target_pairs={{0,4},{1,5},{2,6},{3,7},{4,0},{5,1},{6,2},{7,3},{8,12},{9,13},{10,... | collective-permute-start | bytes 61448 | tf_op jit(solution)/shard_map/ppermute | solution.py:469
  41.6 0.9 collective-permute-start.11
  42.5 3.3 %collective-permute-start.12 = (bf16[80,128]{1,0:T(8,128)(2,1)S(1)}, bf16[80,128]{1,0:T(8,128)(2,1)S(1)}, u32[]{:S(2)}, u32[]{:S(2)}) collective-permute-start(bf16[80,128]{1,0:T(8,128)(2,1)S(1)} %get-tuple-element.84), channel_id=1, source_target_pairs={{0,6},{1,7},{2,4},{3,5},{4,2},{5,3},{6,0},{7,1},{8,14},{9,15},{10,... | collective-permute-start | bytes 61448 | tf_op jit(solution)/shard_map/ppermute | solution.py:469
  46.0 1.3 collective-permute-done.12.refs_6_
  47.3 3.8 %collective-permute-done.13.refs_7_ = bf16[80,128]{1,0:T(8,128)(2,1)S(1)} collective-permute-done((bf16[80,128]{1,0:T(8,128)(2,1)S(1)}, bf16[80,128]{1,0:T(8,128)(2,1)S(1)}, u32[]{:S(2)}, u32[]{:S(2)}) %collective-permute-start.13) | collective-permute-done | bytes 20512 | tf_op jit(solution)/shard_map/ppermute | solution.py:469
  51.2 1.5 %shard_map.131 = (bf16[136,2048]{1,0:T(8,128)(2,1)S(1)}, bf16[136,1024]{1,0:T(8,128)(2,1)S(1)}, bf16[80,128]{1,0:T(8,128)(2,1)S(1)}, bf16[80,128]{1,0:T(8,128)(2...) custom-call(s32[1]{0:T(128)} %bitcast.me_ref, ...), custom_call_target="tpu_custom_call" | custom-call | flops 2000000000 | bytes 1024 | tf_op jit(solution)/shard_map/pallas_call | solution.py:200
  53.6 1.8 %collective-permute-start.17 = (bf16[80,128]{1,0:T(8,128)(2,1)S(1)}, bf16[80,128]{1,0:T(8,128)(2,1)S(1)}, u32[]{:S(2)}, u32[]{:S(2)}) collective-permute-start(bf16[80,128]{1,0:T(8,128)(2,1)S(1)} %get-tuple-element.90), channel_id=1, source_target_pairs={{0,3},{1,2},{2,1},{3,0},{4,7},{5,6},{6,5},{7,4},{8,11},{9,10},{10,... | collective-permute-start | bytes 61448 | tf_op jit(solution)/shard_map/ppermute | solution.py:469
  55.4 2.3 %collective-permute-start.18 = (bf16[80,128]{1,0:T(8,128)(2,1)S(1)}, bf16[80,128]{1,0:T(8,128)(2,1)S(1)}, u32[]{:S(2)}, u32[]{:S(2)}) collective-permute-start(bf16[80,128]{1,0:T(8,128)(2,1)S(1)} %get-tuple-element.91), channel_id=1, source_target_pairs={{0,5},{1,4},{2,7},{3,6},{4,1},{5,0},{6,3},{7,2},{8,13},{9,12},{10,... | collective-permute-start | bytes 61448 | tf_op jit(solution)/shard_map/ppermute | solution.py:469
  58.1 3.8 %collective-permute-start.20 = (bf16[80,128]{1,0:T(8,128)(2,1)S(1)}, bf16[80,128]{1,0:T(8,128)(2,1)S(1)}, u32[]{:S(2)}, u32[]{:S(2)}) collective-permute-start(bf16[80,128]{1,0:T(8,128)(2,1)S(1)} %get-tuple-element.93), channel_id=1, source_target_pairs={{0,7},{1,6},{2,5},{3,4},{4,3},{5,2},{6,1},{7,0},{8,15},{9,14},{10,... | collective-permute-start | bytes 61448 | tf_op jit(solution)/shard_map/ppermute | solution.py:469
  61.9 1.1 shard_map.132
  63.4 3.8 %collective-permute-start.28 = (bf16[136,1024]{1,0:T(8,128)(2,1)S(1)}, bf16[136,1024]{1,0:T(8,128)(2,1)S(1)}, u32[]{:S(2)}, u32[]{:S(2)}) collective-permute-start(bf16[136,1024]{1,0:T(8,128)(2,1)S(1)} %get-tuple-element.129), channel_id=1, source_target_pairs={{0,7},{1,6},{2,5},{3,4},{4,3},{5,2},{6,1},{7,0},{8,15},{9,14},{10,... | collective-permute-start | bytes 835592 | tf_op jit(solution)/shard_map/ppermute | solution.py:469
  67.5 5.1 %shard_map.133 = (bf16[408,128]{1,0:T(8,128)(2,1)S(1)}, bf16[408,128]{1,0:T(8,128)(2,1)S(1)}, bf16[408,128]{1,0:T(8,128)(2,1)S(1)}, bf16[408,128]{1,0:T(8,128)(2...) custom-call(s32[1]{0:T(128)} %bitcast.me_ref, ...), custom_call_target="tpu_custom_call" | custom-call | flops 6000000000 | bytes 1024 | tf_op jit(solution)/shard_map/pallas_call | solution.py:200
  72.7 1.3 collective-permute-start.21
  74.0 1.5 %collective-permute-start.22 = (bf16[408,128]{1,0:T(8,128)(2,1)S(1)}, bf16[408,128]{1,0:T(8,128)(2,1)S(1)}, u32[]{:S(2)}, u32[]{:S(2)}) collective-permute-start(bf16[408,128]{1,0:T(8,128)(2,1)S(1)} %get-tuple-element.123), channel_id=1, source_target_pairs={{0,2},{1,3},{2,0},{3,1},{4,6},{5,7},{6,4},{7,5},{8,10},{9,11},{10,... | collective-permute-start | bytes 313352 | tf_op jit(solution)/shard_map/ppermute | solution.py:469
  75.4 6.9 %collective-permute-done.21.refs_4_.refs_1_ = bf16[408,128]{1,0:T(8,128)(2,1)S(1)} collective-permute-done((bf16[408,128]{1,0:T(8,128)(2,1)S(1)}, bf16[408,128]{1,0:T(8,128)(2,1)S(1)}, u32[]{:S(2)}, u32[]{:S(2)}) %collective-permute-start.21) | collective-permute-done | bytes 104480 | tf_op jit(solution)/shard_map/ppermute | solution.py:469
  82.6 1.7 %collective-permute-start.32 = (bf16[128,1024]{1,0:T(8,128)(2,1)S(1)}, bf16[128,1024]{1,0:T(8,128)(2,1)S(1)}, u32[]{:S(2)}, u32[]{:S(2)}) collective-permute-start(bf16[128,1024]{1,0:T(8,128)(2,1)S(1)} %get-tuple-element.139), channel_id=1, source_target_pairs={{0,1},{1,0},{2,3},{3,2},{4,5},{5,4},{6,7},{7,6},{8,9},{9,8},{10,11... | collective-permute-start | bytes 786440 | tf_op jit(solution)/shard_map/ppermute | solution.py:22
  84.3 1.2 collective-permute-start.25
  85.5 1.0 collective-permute-start.23
  86.4 2.5 %collective-permute-start.24 = (bf16[408,128]{1,0:T(8,128)(2,1)S(1)}, bf16[408,128]{1,0:T(8,128)(2,1)S(1)}, u32[]{:S(2)}, u32[]{:S(2)}) collective-permute-start(bf16[408,128]{1,0:T(8,128)(2,1)S(1)} %get-tuple-element.125), channel_id=1, source_target_pairs={{0,3},{1,2},{2,1},{3,0},{4,7},{5,6},{6,5},{7,4},{8,11},{9,10},{10,... | collective-permute-start | bytes 313352 | tf_op jit(solution)/shard_map/ppermute | solution.py:469
  88.9 2.1 %collective-permute-done.25.refs_8_.refs_5_ = bf16[408,128]{1,0:T(8,128)(2,1)S(1)} collective-permute-done((bf16[408,128]{1,0:T(8,128)(2,1)S(1)}, bf16[408,128]{1,0:T(8,128)(2,1)S(1)}, u32[]{:S(2)}, u32[]{:S(2)}) %collective-permute-start.25) | collective-permute-done | bytes 104480 | tf_op jit(solution)/shard_map/ppermute | solution.py:469
  91.0 2.2 %collective-permute-done.31.refs_6_ = bf16[128,1024]{1,0:T(8,128)(2,1)S(1)} collective-permute-done((bf16[128,1024]{1,0:T(8,128)(2,1)S(1)}, bf16[128,1024]{1,0:T(8,128)(2,1)S(1)}, u32[]{:S(2)}, u32[]{:S(2)}) %collective-permute-start.31) | collective-permute-done | bytes 262176 | tf_op jit(solution)/shard_map/ppermute | solution.py:22
  93.2 2.6 %collective-permute-start.27 = (bf16[408,128]{1,0:T(8,128)(2,1)S(1)}, bf16[408,128]{1,0:T(8,128)(2,1)S(1)}, u32[]{:S(2)}, u32[]{:S(2)}) collective-permute-start(bf16[408,128]{1,0:T(8,128)(2,1)S(1)} %get-tuple-element.128), channel_id=1, source_target_pairs={{0,7},{1,6},{2,5},{3,4},{4,3},{5,2},{6,1},{7,0},{8,15},{9,14},{10,... | collective-permute-start | bytes 313352 | tf_op jit(solution)/shard_map/ppermute | solution.py:469
  96.5 4.1 %collective-permute-done.27.refs_7_ = bf16[408,128]{1,0:T(8,128)(2,1)S(1)} collective-permute-done((bf16[408,128]{1,0:T(8,128)(2,1)S(1)}, bf16[408,128]{1,0:T(8,128)(2,1)S(1)}, u32[]{:S(2)}, u32[]{:S(2)}) %collective-permute-start.27) | collective-permute-done | bytes 104480 | tf_op jit(solution)/shard_map/ppermute | solution.py:469
  100.6 1.4 %shard_map.136 = bf16[136,1024]{1,0:T(8,128)(2,1)S(1)} custom-call(s32[1]{0:T(128)} %bitcast.me_ref, bf16[408,128]{1,0:T(8,128)(2,1)S(1)} %get-tuple-element.121.refs_0_, bf16[408,128]{1,0:T(8,128)(2,1)S(1)} %collective-permute-done.21.refs_4_.refs_1_, bf16[408,128]{1,0:T(8,128)(2,1)S(1)} %collective-permute-done.22.refs_5_.refs_2_, ...), custom_call_target="tpu_custom_call" | custom-call | flops 1500000000 | bytes 1024 | tf_op jit(solution)/shard_map/pallas_call | solution.py:200
  102.0 13.1 %collective-permute-start.33 = (bf16[136,1024]{1,0:T(8,128)(2,1)S(1)}, bf16[136,1024]{1,0:T(8,128)(2,1)S(1)}, u32[]{:S(2)}, u32[]{:S(2)}) collective-permute-start(bf16[136,1024]{1,0:T(8,128)(2,1)S(1)} %shard_map.136), channel_id=1, source_target_pairs={{8,0},{16,8},{24,16},{9,1},{17,9},{25,17},{10,2},{18,10},{26,18},{... | collective-permute-start | bytes 835592 | tf_op jit(solution)/shard_map/ppermute | solution.py:28
  115.1 1.9 %collective-permute-start.35 = (bf16[64,1024]{1,0:T(8,128)(2,1)S(1)}, bf16[64,1024]{1,0:T(8,128)(2,1)S(1)}, u32[]{:S(2)}, u32[]{:S(2)}) collective-permute-start(bf16[64,1024]{1,0:T(8,128)(2,1)S(1)} %get-tuple-element.146), channel_id=1, source_target_pairs={{0,4},{4,0},{1,5},{5,1},{2,6},{6,2},{3,7},{7,3},{8,12},{12,8},{9,1... | collective-permute-start | bytes 393224 | tf_op jit(solution)/shard_map/ppermute | solution.py:22
  117.5 1.0 shard_map.138
  118.5 8.3 %collective-permute-done.35.got_b = bf16[64,1024]{1,0:T(8,128)(2,1)S(1)} collective-permute-done((bf16[64,1024]{1,0:T(8,128)(2,1)S(1)}, bf16[64,1024]{1,0:T(8,128)(2,1)S(1)}, u32[]{:S(2)}, u32[]{:S(2)}) %collective-permute-start.35) | collective-permute-done | bytes 131104 | tf_op jit(solution)/shard_map/ppermute | solution.py:22
  126.8 2.8 %collective-permute-done.34.got_a = bf16[64,1024]{1,0:T(8,128)(2,1)S(1)} collective-permute-done((bf16[64,1024]{1,0:T(8,128)(2,1)S(1)}, bf16[64,1024]{1,0:T(8,128)(2,1)S(1)}, u32[]{:S(2)}, u32[]{:S(2)}) %collective-permute-start.34) | collective-permute-done | bytes 131104 | tf_op jit(solution)/shard_map/ppermute | solution.py:22
  129.6 0.8 shard_map.139
  130.5 1.0 shard_map.137
  (63 shorter events, 6.6 us)
Async XLA Ops:
  0.6 14.7 %collective-permute-start.2 = (bf16[136,1024]{1,0:T(8,128)(2,1)}, bf16[136,1024]{1,0:T(8,128)(2,1)S(1)}, u32[]{:S(2)}, u32[]{:S(2)}) collective-permute-start(bf16[136,1024]{1,0:T(8,128)(2,1)} %bitcast.14), channel_id=1, source_target_pairs={{0,4},{4,0},{1,5},{5,1},{2,6},{6,2},{3,7},{7,3},{8,12},{12,8},{9,1... | collective-permute-start | bytes 835592 | tf_op jit(solution)/shard_map/ppermute | solution.py:22
  3.0 14.9 %collective-permute-start.1 = (bf16[136,1024]{1,0:T(8,128)(2,1)}, bf16[136,1024]{1,0:T(8,128)(2,1)S(1)}, u32[]{:S(2)}, u32[]{:S(2)}) collective-permute-start(bf16[136,1024]{1,0:T(8,128)(2,1)} %bitcast.15), channel_id=1, source_target_pairs={{0,2},{2,0},{1,3},{3,1},{4,6},{6,4},{5,7},{7,5},{8,10},{10,8},{9,1... | collective-permute-start | bytes 835592 | tf_op jit(solution)/shard_map/ppermute | solution.py:22
  4.3 24.4 %collective-permute-start = (bf16[136,1024]{1,0:T(8,128)(2,1)}, bf16[136,1024]{1,0:T(8,128)(2,1)S(1)}, u32[]{:S(2)}, u32[]{:S(2)}) collective-permute-start(bf16[136,1024]{1,0:T(8,128)(2,1)} %bitcast.16), channel_id=1, source_target_pairs={{0,1},{1,0},{2,3},{3,2},{4,5},{5,4},{6,7},{7,6},{8,9},{9,8},{10,11... | collective-permute-start | bytes 835592 | tf_op jit(solution)/shard_map/ppermute | solution.py:22
  15.4 6.6 %collective-permute-start.4 = (bf16[136,1024]{1,0:T(8,128)(2,1)S(1)}, bf16[136,1024]{1,0:T(8,128)(2,1)S(1)}, u32[]{:S(2)}, u32[]{:S(2)}) collective-permute-start(bf16[136,1024]{1,0:T(8,128)(2,1)S(1)} %collective-permute-done.2.refs_3_), channel_id=1, source_target_pairs={{0,1},{1,0},{2,3},{3,2},{4,5},{5,4},{6,7},{7,6},{8,9},{9,8},{10,11... | collective-permute-start | bytes 835592 | tf_op jit(solution)/shard_map/ppermute | solution.py:22
  17.9 10.8 %collective-permute-start.3 = (bf16[136,1024]{1,0:T(8,128)(2,1)S(1)}, bf16[136,1024]{1,0:T(8,128)(2,1)S(1)}, u32[]{:S(2)}, u32[]{:S(2)}) collective-permute-start(bf16[136,1024]{1,0:T(8,128)(2,1)S(1)} %collective-permute-done.1.refs_2_), channel_id=1, source_target_pairs={{0,1},{1,0},{2,3},{3,2},{4,5},{5,4},{6,7},{7,6},{8,9},{9,8},{10,11... | collective-permute-start | bytes 835592 | tf_op jit(solution)/shard_map/ppermute | solution.py:22
  18.6 11.7 %collective-permute-start.5 = (bf16[136,1024]{1,0:T(8,128)(2,1)S(1)}, bf16[136,1024]{1,0:T(8,128)(2,1)S(1)}, u32[]{:S(2)}, u32[]{:S(2)}) collective-permute-start(bf16[136,1024]{1,0:T(8,128)(2,1)S(1)} %collective-permute-done.2.refs_3_), channel_id=1, source_target_pairs={{0,2},{2,0},{1,3},{3,1},{4,6},{6,4},{5,7},{7,5},{8,10},{10,8},{9,1... | collective-permute-start | bytes 835592 | tf_op jit(solution)/shard_map/ppermute | solution.py:22
  21.9 9.2 %collective-permute-start.6 = (bf16[136,1024]{1,0:T(8,128)(2,1)S(1)}, bf16[136,1024]{1,0:T(8,128)(2,1)S(1)}, u32[]{:S(2)}, u32[]{:S(2)}) collective-permute-start(bf16[136,1024]{1,0:T(8,128)(2,1)S(1)} %collective-permute-done.4.refs_5_), channel_id=1, source_target_pairs={{0,2},{2,0},{1,3},{3,1},{4,6},{6,4},{5,7},{7,5},{8,10},{10,8},{9,1... | collective-permute-start | bytes 835592 | tf_op jit(solution)/shard_map/ppermute | solution.py:22
  24.6 1.2 copy-start.1
  25.8 1.2 copy-start.3
  27.0 1.2 copy-start.5
  28.3 1.0 copy-start.7
  31.1 20.0 %copy-start = (bf16[1,512,2048]{2,1,0:T(8,128)(2,1)S(1)}, bf16[1,512,2048]{2,1,0:T(8,128)(2,1)}, u32[]{:S(2)}) copy-start(bf16[1,512,2048]{2,1,0:T(8,128)(2,1)} %param.14) | copy-start | bytes 6291460
  31.1 20.0 %copy-start.8 = (bf16[1,136,1024]{2,1,0:T(8,128)(2,1)S(1)}, bf16[1,136,1024]{2,1,0:T(8,128)(2,1)}, u32[]{:S(2)}) copy-start(bf16[1,136,1024]{2,1,0:T(8,128)(2,1)} %param.10) | copy-start | bytes 835588
  34.9 7.6 %collective-permute-start.7 = (bf16[80,128]{1,0:T(8,128)(2,1)S(1)}, bf16[80,128]{1,0:T(8,128)(2,1)S(1)}, u32[]{:S(2)}, u32[]{:S(2)}) collective-permute-start(bf16[80,128]{1,0:T(8,128)(2,1)S(1)} %get-tuple-element.79), channel_id=1, source_target_pairs={{0,1},{1,0},{2,3},{3,2},{4,5},{5,4},{6,7},{7,6},{8,9},{9,8},{10,11... | collective-permute-start | bytes 61448 | tf_op jit(solution)/shard_map/ppermute | solution.py:469
  36.2 9.7 %collective-permute-start.8 = (bf16[80,128]{1,0:T(8,128)(2,1)S(1)}, bf16[80,128]{1,0:T(8,128)(2,1)S(1)}, u32[]{:S(2)}, u32[]{:S(2)}) collective-permute-start(bf16[80,128]{1,0:T(8,128)(2,1)S(1)} %get-tuple-element.80), channel_id=1, source_target_pairs={{0,2},{1,3},{2,0},{3,1},{4,6},{5,7},{6,4},{7,5},{8,10},{9,11},{10,... | collective-permute-start | bytes 61448 | tf_op jit(solution)/shard_map/ppermute | solution.py:469
  38.4 7.5 %collective-permute-start.9 = (bf16[80,128]{1,0:T(8,128)(2,1)S(1)}, bf16[80,128]{1,0:T(8,128)(2,1)S(1)}, u32[]{:S(2)}, u32[]{:S(2)}) collective-permute-start(bf16[80,128]{1,0:T(8,128)(2,1)S(1)} %get-tuple-element.81), channel_id=1, source_target_pairs={{0,4},{1,5},{2,6},{3,7},{4,0},{5,1},{6,2},{7,3},{8,12},{9,13},{10,... | collective-permute-start | bytes 61448 | tf_op jit(solution)/shard_map/ppermute | solution.py:469
  41.4 4.5 %collective-permute-start.10 = (bf16[80,128]{1,0:T(8,128)(2,1)S(1)}, bf16[80,128]{1,0:T(8,128)(2,1)S(1)}, u32[]{:S(2)}, u32[]{:S(2)}) collective-permute-start(bf16[80,128]{1,0:T(8,128)(2,1)S(1)} %get-tuple-element.82), channel_id=1, source_target_pairs={{0,3},{1,2},{2,1},{3,0},{4,7},{5,6},{6,5},{7,4},{8,11},{9,10},{10,... | collective-permute-start | bytes 61448 | tf_op jit(solution)/shard_map/ppermute | solution.py:469
  41.6 4.4 %collective-permute-start.11 = (bf16[80,128]{1,0:T(8,128)(2,1)S(1)}, bf16[80,128]{1,0:T(8,128)(2,1)S(1)}, u32[]{:S(2)}, u32[]{:S(2)}) collective-permute-start(bf16[80,128]{1,0:T(8,128)(2,1)S(1)} %get-tuple-element.83), channel_id=1, source_target_pairs={{0,5},{1,4},{2,7},{3,6},{4,1},{5,0},{6,3},{7,2},{8,13},{9,12},{10,... | collective-permute-start | bytes 61448 | tf_op jit(solution)/shard_map/ppermute | solution.py:469
  42.5 4.8 %collective-permute-start.12 = (bf16[80,128]{1,0:T(8,128)(2,1)S(1)}, bf16[80,128]{1,0:T(8,128)(2,1)S(1)}, u32[]{:S(2)}, u32[]{:S(2)}) collective-permute-start(bf16[80,128]{1,0:T(8,128)(2,1)S(1)} %get-tuple-element.84), channel_id=1, source_target_pairs={{0,6},{1,7},{2,4},{3,5},{4,2},{5,3},{6,0},{7,1},{8,14},{9,15},{10,... | collective-permute-start | bytes 61448 | tf_op jit(solution)/shard_map/ppermute | solution.py:469
  45.8 5.3 %collective-permute-start.13 = (bf16[80,128]{1,0:T(8,128)(2,1)S(1)}, bf16[80,128]{1,0:T(8,128)(2,1)S(1)}, u32[]{:S(2)}, u32[]{:S(2)}) collective-permute-start(bf16[80,128]{1,0:T(8,128)(2,1)S(1)} %get-tuple-element.85), channel_id=1, source_target_pairs={{0,7},{1,6},{2,5},{3,4},{4,3},{5,2},{6,1},{7,0},{8,15},{9,14},{10,... | collective-permute-start | bytes 61448 | tf_op jit(solution)/shard_map/ppermute | solution.py:469
  52.7 5.1 %collective-permute-start.14 = (bf16[80,128]{1,0:T(8,128)(2,1)S(1)}, bf16[80,128]{1,0:T(8,128)(2,1)S(1)}, u32[]{:S(2)}, u32[]{:S(2)}) collective-permute-start(bf16[80,128]{1,0:T(8,128)(2,1)S(1)} %get-tuple-element.87), channel_id=1, source_target_pairs={{0,1},{1,0},{2,3},{3,2},{4,5},{5,4},{6,7},{7,6},{8,9},{9,8},{10,11... | collective-permute-start | bytes 61448 | tf_op jit(solution)/shard_map/ppermute | solution.py:469
  53.0 5.1 %collective-permute-start.15 = (bf16[80,128]{1,0:T(8,128)(2,1)S(1)}, bf16[80,128]{1,0:T(8,128)(2,1)S(1)}, u32[]{:S(2)}, u32[]{:S(2)}) collective-permute-start(bf16[80,128]{1,0:T(8,128)(2,1)S(1)} %get-tuple-element.88), channel_id=1, source_target_pairs={{0,2},{1,3},{2,0},{3,1},{4,6},{5,7},{6,4},{7,5},{8,10},{9,11},{10,... | collective-permute-start | bytes 61448 | tf_op jit(solution)/shard_map/ppermute | solution.py:469
  53.0 10.1 %collective-permute-start.16 = (bf16[80,128]{1,0:T(8,128)(2,1)S(1)}, bf16[80,128]{1,0:T(8,128)(2,1)S(1)}, u32[]{:S(2)}, u32[]{:S(2)}) collective-permute-start(bf16[80,128]{1,0:T(8,128)(2,1)S(1)} %get-tuple-element.89), channel_id=1, source_target_pairs={{0,4},{1,5},{2,6},{3,7},{4,0},{5,1},{6,2},{7,3},{8,12},{9,13},{10,... | collective-permute-start | bytes 61448 | tf_op jit(solution)/shard_map/ppermute | solution.py:469
  53.6 9.4 %collective-permute-start.17 = (bf16[80,128]{1,0:T(8,128)(2,1)S(1)}, bf16[80,128]{1,0:T(8,128)(2,1)S(1)}, u32[]{:S(2)}, u32[]{:S(2)}) collective-permute-start(bf16[80,128]{1,0:T(8,128)(2,1)S(1)} %get-tuple-element.90), channel_id=1, source_target_pairs={{0,3},{1,2},{2,1},{3,0},{4,7},{5,6},{6,5},{7,4},{8,11},{9,10},{10,... | collective-permute-start | bytes 61448 | tf_op jit(solution)/shard_map/ppermute | solution.py:469
  55.4 7.7 %collective-permute-start.18 = (bf16[80,128]{1,0:T(8,128)(2,1)S(1)}, bf16[80,128]{1,0:T(8,128)(2,1)S(1)}, u32[]{:S(2)}, u32[]{:S(2)}) collective-permute-start(bf16[80,128]{1,0:T(8,128)(2,1)S(1)} %get-tuple-element.91), channel_id=1, source_target_pairs={{0,5},{1,4},{2,7},{3,6},{4,1},{5,0},{6,3},{7,2},{8,13},{9,12},{10,... | collective-permute-start | bytes 61448 | tf_op jit(solution)/shard_map/ppermute | solution.py:469
  57.7 5.4 %collective-permute-start.19 = (bf16[80,128]{1,0:T(8,128)(2,1)S(1)}, bf16[80,128]{1,0:T(8,128)(2,1)S(1)}, u32[]{:S(2)}, u32[]{:S(2)}) collective-permute-start(bf16[80,128]{1,0:T(8,128)(2,1)S(1)} %get-tuple-element.92), channel_id=1, source_target_pairs={{0,6},{1,7},{2,4},{3,5},{4,2},{5,3},{6,0},{7,1},{8,14},{9,15},{10,... | collective-permute-start | bytes 61448 | tf_op jit(solution)/shard_map/ppermute | solution.py:469
  58.1 5.3 %collective-permute-start.20 = (bf16[80,128]{1,0:T(8,128)(2,1)S(1)}, bf16[80,128]{1,0:T(8,128)(2,1)S(1)}, u32[]{:S(2)}, u32[]{:S(2)}) collective-permute-start(bf16[80,128]{1,0:T(8,128)(2,1)S(1)} %get-tuple-element.93), channel_id=1, source_target_pairs={{0,7},{1,6},{2,5},{3,4},{4,3},{5,2},{6,1},{7,0},{8,15},{9,14},{10,... | collective-permute-start | bytes 61448 | tf_op jit(solution)/shard_map/ppermute | solution.py:469
  63.4 19.0 %collective-permute-start.28 = (bf16[136,1024]{1,0:T(8,128)(2,1)S(1)}, bf16[136,1024]{1,0:T(8,128)(2,1)S(1)}, u32[]{:S(2)}, u32[]{:S(2)}) collective-permute-start(bf16[136,1024]{1,0:T(8,128)(2,1)S(1)} %get-tuple-element.129), channel_id=1, source_target_pairs={{0,7},{1,6},{2,5},{3,4},{4,3},{5,2},{6,1},{7,0},{8,15},{9,14},{10,... | collective-permute-start | bytes 835592 | tf_op jit(solution)/shard_map/ppermute | solution.py:469
  67.3 15.1 %collective-permute-start.29 = (bf16[256,1024]{1,0:T(8,128)(2,1)S(1)}, bf16[256,1024]{1,0:T(8,128)(2,1)S(1)}, u32[]{:S(2)}, u32[]{:S(2)}) collective-permute-start(bf16[256,1024]{1,0:T(8,128)(2,1)S(1)} %get-tuple-element.134), channel_id=1, source_target_pairs={{0,1},{1,0},{2,3},{3,2},{4,5},{5,4},{6,7},{7,6},{8,9},{9,8},{10,11... | collective-permute-start | bytes 1572872 | tf_op jit(solution)/shard_map/ppermute | solution.py:22
  67.5 14.9 %collective-permute-start.30 = (bf16[256,1024]{1,0:T(8,128)(2,1)S(1)}, bf16[256,1024]{1,0:T(8,128)(2,1)S(1)}, u32[]{:S(2)}, u32[]{:S(2)}) collective-permute-start(bf16[256,1024]{1,0:T(8,128)(2,1)S(1)} %get-tuple-element.135), channel_id=1, source_target_pairs={{0,2},{2,0},{1,3},{3,1},{4,6},{6,4},{5,7},{7,5},{8,10},{10,8},{9,1... | collective-permute-start | bytes 1572872 | tf_op jit(solution)/shard_map/ppermute | solution.py:22
  72.7 9.6 %collective-permute-start.21 = (bf16[408,128]{1,0:T(8,128)(2,1)S(1)}, bf16[408,128]{1,0:T(8,128)(2,1)S(1)}, u32[]{:S(2)}, u32[]{:S(2)}) collective-permute-start(bf16[408,128]{1,0:T(8,128)(2,1)S(1)} %get-tuple-element.122), channel_id=1, source_target_pairs={{0,1},{1,0},{2,3},{3,2},{4,5},{5,4},{6,7},{7,6},{8,9},{9,8},{10,11... | collective-permute-start | bytes 313352 | tf_op jit(solution)/shard_map/ppermute | solution.py:469
  74.0 8.4 %collective-permute-start.22 = (bf16[408,128]{1,0:T(8,128)(2,1)S(1)}, bf16[408,128]{1,0:T(8,128)(2,1)S(1)}, u32[]{:S(2)}, u32[]{:S(2)}) collective-permute-start(bf16[408,128]{1,0:T(8,128)(2,1)S(1)} %get-tuple-element.123), channel_id=1, source_target_pairs={{0,2},{1,3},{2,0},{3,1},{4,6},{5,7},{6,4},{7,5},{8,10},{9,11},{10,... | collective-permute-start | bytes 313352 | tf_op jit(solution)/shard_map/ppermute | solution.py:469
  82.5 10.7 %collective-permute-start.31 = (bf16[128,1024]{1,0:T(8,128)(2,1)S(1)}, bf16[128,1024]{1,0:T(8,128)(2,1)S(1)}, u32[]{:S(2)}, u32[]{:S(2)}) collective-permute-start(bf16[128,1024]{1,0:T(8,128)(2,1)S(1)} %get-tuple-element.138), channel_id=1, source_target_pairs={{0,2},{2,0},{1,3},{3,1},{4,6},{6,4},{5,7},{7,5},{8,10},{10,8},{9,1... | collective-permute-start | bytes 786440 | tf_op jit(solution)/shard_map/ppermute | solution.py:22
  82.6 13.2 %collective-permute-start.32 = (bf16[128,1024]{1,0:T(8,128)(2,1)S(1)}, bf16[128,1024]{1,0:T(8,128)(2,1)S(1)}, u32[]{:S(2)}, u32[]{:S(2)}) collective-permute-start(bf16[128,1024]{1,0:T(8,128)(2,1)S(1)} %get-tuple-element.139), channel_id=1, source_target_pairs={{0,1},{1,0},{2,3},{3,2},{4,5},{5,4},{6,7},{7,6},{8,9},{9,8},{10,11... | collective-permute-start | bytes 786440 | tf_op jit(solution)/shard_map/ppermute | solution.py:22
  84.3 6.8 %collective-permute-start.25 = (bf16[408,128]{1,0:T(8,128)(2,1)S(1)}, bf16[408,128]{1,0:T(8,128)(2,1)S(1)}, u32[]{:S(2)}, u32[]{:S(2)}) collective-permute-start(bf16[408,128]{1,0:T(8,128)(2,1)S(1)} %get-tuple-element.126), channel_id=1, source_target_pairs={{0,5},{1,4},{2,7},{3,6},{4,1},{5,0},{6,3},{7,2},{8,13},{9,12},{10,... | collective-permute-start | bytes 313352 | tf_op jit(solution)/shard_map/ppermute | solution.py:469
  85.5 10.6 %collective-permute-start.23 = (bf16[408,128]{1,0:T(8,128)(2,1)S(1)}, bf16[408,128]{1,0:T(8,128)(2,1)S(1)}, u32[]{:S(2)}, u32[]{:S(2)}) collective-permute-start(bf16[408,128]{1,0:T(8,128)(2,1)S(1)} %get-tuple-element.124), channel_id=1, source_target_pairs={{0,4},{1,5},{2,6},{3,7},{4,0},{5,1},{6,2},{7,3},{8,12},{9,13},{10,... | collective-permute-start | bytes 313352 | tf_op jit(solution)/shard_map/ppermute | solution.py:469
  86.4 9.6 %collective-permute-start.24 = (bf16[408,128]{1,0:T(8,128)(2,1)S(1)}, bf16[408,128]{1,0:T(8,128)(2,1)S(1)}, u32[]{:S(2)}, u32[]{:S(2)}) collective-permute-start(bf16[408,128]{1,0:T(8,128)(2,1)S(1)} %get-tuple-element.125), channel_id=1, source_target_pairs={{0,3},{1,2},{2,1},{3,0},{4,7},{5,6},{6,5},{7,4},{8,11},{9,10},{10,... | collective-permute-start | bytes 313352 | tf_op jit(solution)/shard_map/ppermute | solution.py:469
  91.0 5.4 %collective-permute-start.26 = (bf16[408,128]{1,0:T(8,128)(2,1)S(1)}, bf16[408,128]{1,0:T(8,128)(2,1)S(1)}, u32[]{:S(2)}, u32[]{:S(2)}) collective-permute-start(bf16[408,128]{1,0:T(8,128)(2,1)S(1)} %get-tuple-element.127), channel_id=1, source_target_pairs={{0,6},{1,7},{2,4},{3,5},{4,2},{5,3},{6,0},{7,1},{8,14},{9,15},{10,... | collective-permute-start | bytes 313352 | tf_op jit(solution)/shard_map/ppermute | solution.py:469
  93.2 7.3 %copy-start.2 = (bf16[1,1024,512]{2,1,0:T(8,128)(2,1)S(1)}, bf16[1,1024,512]{2,1,0:T(8,128)(2,1)}, u32[]{:S(2)}) copy-start(bf16[1,1024,512]{2,1,0:T(8,128)(2,1)} %param.11) | copy-start | bytes 3145732
  93.2 7.3 %copy-start.4 = (bf16[1,1024,512]{2,1,0:T(8,128)(2,1)S(1)}, bf16[1,1024,512]{2,1,0:T(8,128)(2,1)}, u32[]{:S(2)}) copy-start(bf16[1,1024,512]{2,1,0:T(8,128)(2,1)} %param.12) | copy-start | bytes 3145732
  93.2 7.3 %copy-start.6 = (bf16[1,1024,512]{2,1,0:T(8,128)(2,1)S(1)}, bf16[1,1024,512]{2,1,0:T(8,128)(2,1)}, u32[]{:S(2)}) copy-start(bf16[1,1024,512]{2,1,0:T(8,128)(2,1)} %param.13) | copy-start | bytes 3145732
  93.2 7.3 %collective-permute-start.27 = (bf16[408,128]{1,0:T(8,128)(2,1)S(1)}, bf16[408,128]{1,0:T(8,128)(2,1)S(1)}, u32[]{:S(2)}, u32[]{:S(2)}) collective-permute-start(bf16[408,128]{1,0:T(8,128)(2,1)S(1)} %get-tuple-element.128), channel_id=1, source_target_pairs={{0,7},{1,6},{2,5},{3,4},{4,3},{5,2},{6,1},{7,0},{8,15},{9,14},{10,... | collective-permute-start | bytes 313352 | tf_op jit(solution)/shard_map/ppermute | solution.py:469
  102.0 28.5 %collective-permute-start.33 = (bf16[136,1024]{1,0:T(8,128)(2,1)S(1)}, bf16[136,1024]{1,0:T(8,128)(2,1)S(1)}, u32[]{:S(2)}, u32[]{:S(2)}) collective-permute-start(bf16[136,1024]{1,0:T(8,128)(2,1)S(1)} %shard_map.136), channel_id=1, source_target_pairs={{8,0},{16,8},{24,16},{9,1},{17,9},{25,17},{10,2},{18,10},{26,18},{... | collective-permute-start | bytes 835592 | tf_op jit(solution)/shard_map/ppermute | solution.py:28
  115.1 11.7 %collective-permute-start.35 = (bf16[64,1024]{1,0:T(8,128)(2,1)S(1)}, bf16[64,1024]{1,0:T(8,128)(2,1)S(1)}, u32[]{:S(2)}, u32[]{:S(2)}) collective-permute-start(bf16[64,1024]{1,0:T(8,128)(2,1)S(1)} %get-tuple-element.146), channel_id=1, source_target_pairs={{0,4},{4,0},{1,5},{5,1},{2,6},{6,2},{3,7},{7,3},{8,12},{12,8},{9,1... | collective-permute-start | bytes 393224 | tf_op jit(solution)/shard_map/ppermute | solution.py:22
  117.0 12.6 %collective-permute-start.34 = (bf16[64,1024]{1,0:T(8,128)(2,1)S(1)}, bf16[64,1024]{1,0:T(8,128)(2,1)S(1)}, u32[]{:S(2)}, u32[]{:S(2)}) collective-permute-start(bf16[64,1024]{1,0:T(8,128)(2,1)S(1)} %get-tuple-element.140.refs_13_), channel_id=1, source_target_pairs={{0,4},{4,0},{1,5},{5,1},{2,6},{6,2},{3,7},{7,3},{8,12},{12,8},{9,1... | collective-permute-start | bytes 393224 | tf_op jit(solution)/shard_map/ppermute | solution.py:22
  118.5 11.9 %copy-start.9 = (s32[1,136]{1,0:T(1,128)S(1)}, s32[1,136]{1,0:T(1,128)}, u32[]{:S(2)}) copy-start(s32[1,136]{1,0:T(1,128)} %order_ref.1) | copy-start | bytes 1636

commit v9 on v8

--- a/solution.py
+++ b/solution.py
@@ -289,7 +289,7 @@
 
 
 def attend_kernel(
-    unit_ref, value_ref, near_ref, last_ref, weight_ref, row_ids, column_ids, *out_refs
+    me_ref, unit_ref, value_ref, near_ref, last_ref, weight_ref, row_ids, column_ids, *out_refs
 ):
     normed_ref, late_unit, late_scale, prob_ref, qk_ref, v_ref, out_t_ref = out_refs[:7]
     early, rows = unit_ref.shape[:2]
@@ -317,52 +317,40 @@
         out_t = dot(value, probs, ((0,), (0,)))
         out_t_ref[:, start:stop] = out_t.astype(jnp.bfloat16).astype(jnp.float32)
     out = jnp.transpose(out_t_ref[...])
-    for m, out_ref in enumerate(out_refs[7:]):
-        out_ref[...] = low(pack(out[m * rows : (m + 1) * rows]))
-
-
-def affine_kernel(me_ref, *refs):
-    slabs, (act_ref, inc_ref, w_ref, aff_ref, up_ref) = refs[:HEADS], refs[HEADS : HEADS + 5]
-    out_refs, held_ref = refs[HEADS + 5 : -1], refs[-1]
+    for m, distance in enumerate(DISTANCES):
+        out_refs[7][me_ref[0] ^ distance] = low(pack(out[m * rows : (m + 1) * rows]))
+
+
+def affine_kernel(me_ref, slab_ref, act_ref, inc_ref, w_ref, up_ref, out_ref, *term_refs):
     rows, width = act_ref.shape
-    for m, slab in enumerate(slabs):
-        held_ref[me_ref[0] ^ DISTANCES[m]] = slab[...]
-    attended = jnp.concatenate([unpack(wide(held_ref[h]), rows) for h in range(HEADS)], axis=1)
-    attended = low(attended)
+    columns = [unpack(wide(slab_ref[h]), rows) for h in range(HEADS)]
+    attended = low(jnp.concatenate(columns, axis=1))
     factor = jnp.exp(-dot(attended, w_ref[:, width:]))
     scaled = inc_ref[...].astype(jnp.float32) * factor
     up_ref[...] = low(scaled)
     shift_part = dot(attended, w_ref[:, :width])
     latent_part = scaled * (act_ref[...].astype(jnp.float32) - shift_part)
     grad_affine = jnp.concatenate([-scaled, 1.0 - latent_part], axis=1).astype(jnp.bfloat16)
-    aff_ref[...] = grad_affine
     grad = dot(grad_affine, w_ref[...], ((1,), (1,)))
     for h in range(HEADS):
-        held_ref[h] = low(pack(grad[:, h * HEAD_DIM : (h + 1) * HEAD_DIM]))
-    for m, out_ref in enumerate(out_refs):
-        out_ref[...] = held_ref[me_ref[0] ^ DISTANCES[m]]
+        out_ref[h] = low(pack(grad[:, h * HEAD_DIM : (h + 1) * HEAD_DIM]))
+    columns = [unpack(wide(slab_ref[me_ref[0] ^ m]), rows) for m in range(HEADS)]
+    for half, order in enumerate(ORDERS):
+        right = grad_affine[:, half * width : (half + 1) * width]
+        for term_ref, group in zip(term_refs[4 * half : 4 * half + 4], order):
+            left = low(jnp.concatenate([columns[m] for m in group], axis=1))
+            term_ref[...] = low(dot(left, right, ((0,), (0,))))
 
 
 ORDERS = (((1, 5, 3, 7), (2, 6), (4,), (0,)), ((2, 6, 3, 7), (1, 5), (4,), (0,)))
 
 
-def out_term_kernel(*refs):
-    slabs, aff_ref, out_refs = refs[:HEADS], refs[HEADS], refs[HEADS + 1 :]
-    rows, width = aff_ref.shape[0], aff_ref.shape[1] // 2
-    columns = {m: unpack(wide(slab[...]), rows) for m, slab in zip(DISTANCES, slabs)}
-    for half, order in enumerate(ORDERS):
-        right = aff_ref[:, half * width : (half + 1) * width]
-        for out_ref, group in zip(out_refs[4 * half : 4 * half + 4], order):
-            left = jnp.concatenate([columns[m] for m in group], axis=1).astype(jnp.bfloat16)
-            out_ref[...] = dot(left, right, ((0,), (0,))).astype(jnp.bfloat16)
-
-
-def backward_kernel(me_ref, *refs):
-    slabs, (prob_ref, qk_ref, v_ref, out_t_ref) = refs[:HEADS], refs[HEADS : HEADS + 4]
-    early, late = refs[HEADS + 4 : HEADS + 7], refs[HEADS + 7 : HEADS + 10]
-    out_refs, (gk_ref, gv_ref, gq_ref, held_ref) = refs[HEADS + 10 : -4], refs[-4:]
+def backward_kernel(me_ref, slab_ref, prob_ref, qk_ref, v_ref, out_t_ref, *refs):
+    early, late, out_refs = refs[:3], refs[3:6], refs[6:-4]
+    gk_ref, gv_ref, gq_ref, held_ref = refs[-4:]
     first, rows = early[0].shape[:2]
-    grad_f = jnp.concatenate([unpack(wide(slab[...]), rows) for slab in slabs], axis=0)
+    slabs = [wide(slab_ref[me_ref[0] ^ distance]) for distance in DISTANCES]
+    grad_f = jnp.concatenate([unpack(slab, rows) for slab in slabs], axis=0)
     grad = grad_f.astype(jnp.bfloat16)
     tokens = grad_f.shape[0]
     grad_t = jnp.transpose(grad_f)
@@ -473,6 +461,10 @@
     return [hop(slab, m) if m else slab for m, slab in zip(DISTANCES, slabs)]
 
 
+def switch(slabs):
+    return lax.all_to_all(slabs, "seq", split_axis=0, concat_axis=0, tiled=True)
+
+
 def spread(block):
     side, near, far = [partner(block, "seq", bit) for bit in range(3)]
     side_far = partner(far, "seq", 0)
@@ -537,7 +529,7 @@
     made = call(
         attend_kernel,
         5,
-        [("v", unit), ("v", projected), *[("v", block) for block in blocks[EARLY:]]]
+        [("s", me), ("v", unit), ("v", projected), *[("v", block) for block in blocks[EARLY:]]]
         + [("v", weight), ("v", ids[None, :]), ("v", ids[:, None])],
         [
             out(late, rows, width),
@@ -548,24 +540,17 @@
             out(tokens, HEAD_DIM),
             out(HEAD_DIM, tokens, dtype=f32),
         ]
-        + [out(PACKED, 128)] * parts,
-    )
-    late_parts, (probs, qk, value, out_t), packed = made[:3], made[3:7], made[7:]
-    packed = exchange(packed)
-    grad_affine, scaled, *grad_slabs = call(
+        + [out(parts, PACKED, 128)],
+    )
+    late_parts, (probs, qk, value, out_t), packed = made[:3], made[3:7], switch(made[7])
+    scaled, grad_slabs, *terms = call(
         affine_kernel,
-        2,
-        [("s", me)] + [("v", x) for x in (*packed, field, upstream, wo)],
-        [out(rows, 2 * width), out(rows, width)] + [out(PACKED, 128)] * HEADS,
-        [pltpu.VMEM((HEADS, PACKED, 128), jnp.bfloat16)],
-    )
-    grad_slabs = exchange(grad_slabs)
-    terms = call(
-        out_term_kernel,
-        2,
-        [("v", x) for x in (*packed, grad_affine)],
-        [out(len(group) * HEAD_DIM, width) for order in ORDERS for group in order],
-    )
+        3,
+        [("s", me)] + [("v", x) for x in (packed, field, upstream, wo)],
+        [out(rows, width), out(HEADS, PACKED, 128)]
+        + [out(len(group) * HEAD_DIM, width) for order in ORDERS for group in order],
+    )
+    grad_slabs = switch(grad_slabs)
     grad_slabs, terms, scaled = lax.optimization_barrier((grad_slabs, terms, scaled))
     scaled = hop(scaled, parts - 1)
     first, second, third, keep = zip(terms[:4], terms[4:])
@@ -574,7 +559,7 @@
         backward_kernel,
         6,
         [("s", me)]
-        + [("v", x) for x in (*grad_slabs, probs, qk, value, out_t)]
+        + [("v", x) for x in (grad_slabs, probs, qk, value, out_t)]
         + [("v", x) for x in (normed, unit, unit_scale, *late_parts)],
         [out(PACKED + rows + 3 * HEAD_DIM, 128)] * parts,
         [
@@ -606,6 +591,13 @@
         [out(rows, width)],
         [pltpu.VMEM((HEADS, PACKED + rows, 128), jnp.bfloat16)],
     )
+    (grad_out,) = call(
+        last_sum_kernel,
+        1,
+        [("v", x) for x in (keep_a, keep_b, *rest)],
+        [out(1, keep_a.shape[0], 2 * width, dtype=f32)],
+    )
+    grad_input, grad_out = lax.optimization_barrier((grad_input, grad_out))
     moved = to_previous(grad_input)
     grad_q, grad_k, grad_v = call(
         turn_kernel,
@@ -613,12 +605,6 @@
         [("s", me)] + [("v", x) for x in slabs],
         [out(1, width // parts, inner, dtype=f32)] * 3,
         [pltpu.VMEM((HEADS, 3 * HEAD_DIM, 128), jnp.bfloat16)],
-    )
-    (grad_out,) = call(
-        last_sum_kernel,
-        1,
-        [("v", x) for x in (keep_a, keep_b, *rest)],
-        [out(1, keep_a.shape[0], 2 * width, dtype=f32)],
     )
     (carry,) = call(
         reorder_kernel, 1, [("v", flip_order), ("v", moved)], [out(1, rows, width)]

time: 133 us -> 126 us (0.947)
  the two profiles are of different devices: /device:TPU:5 before, /device:TPU:1 now
where the time goes in v9:
time: 126 us
  waiting for transfers between devices  49.3 us (39%)
  starting transfers between devices  30.2 us (24%)
  blocking collectives  21.9 us (17%)
  Pallas kernels  16.8 us (13%)
  local copies, waits for them, and re-layouts  5.79 us (5%)
    ppermute x13, waiting for transfers between devices, partner(): return lax.ppermute(block, axis, route)  28.3 us
    all_to_all x2, blocking collectives, switch(): return lax.all_to_all(slabs, 'seq', split_axis=0, concat_axis=0, tiled=True)  21.9 us
    pallas_call x11, Pallas kernels, call(): pl.pallas_call(kernel, out_shape=tuple(outs), in_specs=[pl.BlockSpec(memo...  16.8 us
    ppermute x8, waiting for transfers between devices, hop(): return lax.ppermute(block, 'seq', route)  16.7 us
    ppermute x13, starting transfers between devices, partner(): return lax.ppermute(block, axis, route)  14.3 us
    ppermute x8, starting transfers between devices, hop(): return lax.ppermute(block, 'seq', route)  12 us
    ppermute x1, waiting for transfers between devices, shifted(): return lax.ppermute(block, axis, route)  4.32 us
    unnamed x20, local copies, waits for them, and re-layouts  4.15 us
  transfers between devices with their start and end apart: 22, of which 11 were waited for; matrix products, arithmetic and copies ran while one was open for 2% of the time, Pallas kernels for 7%

profile of v9, /device:TPU:1, one launch (start us, length us, event | category | flops | bytes accessed | tf_op | source)
XLA Modules:
  0.0 125.6 jit_solution(7761631312041311186)
XLA Ops:
  0.6 3.2 %collective-permute-start.2 = (bf16[136,1024]{1,0:T(8,128)(2,1)}, bf16[136,1024]{1,0:T(8,128)(2,1)S(1)}, u32[]{:S(2)}, u32[]{:S(2)}) collective-permute-start(bf16[136,1024]{1,0:T(8,128)(2,1)} %bitcast.14), channel_id=1, source_target_pairs={{0,4},{4,0},{1,5},{5,1},{2,6},{6,2},{3,7},{7,3},{8,12},{12,8},{9,1... | collective-permute-start | bytes 835592 | tf_op jit(solution)/shard_map/ppermute | solution.py:22
  3.8 1.3 %collective-permute-start.1 = (bf16[136,1024]{1,0:T(8,128)(2,1)}, bf16[136,1024]{1,0:T(8,128)(2,1)S(1)}, u32[]{:S(2)}, u32[]{:S(2)}) collective-permute-start(bf16[136,1024]{1,0:T(8,128)(2,1)} %bitcast.15), channel_id=1, source_target_pairs={{0,2},{2,0},{1,3},{3,1},{4,6},{6,4},{5,7},{7,5},{8,10},{10,8},{9,1... | collective-permute-start | bytes 835592 | tf_op jit(solution)/shard_map/ppermute | solution.py:22
  5.1 1.2 collective-permute-start
  6.3 0.7 compare_and_fusion
  7.0 9.4 %collective-permute-done.2.refs_3_ = bf16[136,1024]{1,0:T(8,128)(2,1)S(1)} collective-permute-done((bf16[136,1024]{1,0:T(8,128)(2,1)}, bf16[136,1024]{1,0:T(8,128)(2,1)S(1)}, u32[]{:S(2)}, u32[]{:S(2)}) %collective-permute-start.2) | collective-permute-done | bytes 278560 | tf_op jit(solution)/shard_map/ppermute | solution.py:22
  16.4 1.0 collective-permute-start.4
  17.4 0.8 reshape.64
  18.2 0.6 gather_fusion
  18.8 0.6 collective-permute-start.3
  19.7 1.3 %collective-permute-start.5 = (bf16[136,1024]{1,0:T(8,128)(2,1)S(1)}, bf16[136,1024]{1,0:T(8,128)(2,1)S(1)}, u32[]{:S(2)}, u32[]{:S(2)}) collective-permute-start(bf16[136,1024]{1,0:T(8,128)(2,1)S(1)} %collective-permute-done.2.refs_3_), channel_id=1, source_target_pairs={{0,2},{2,0},{1,3},{3,1},{4,6},{6,4},{5,7},{7,5},{8,10},{10,8},{9,1... | collective-permute-start | bytes 835592 | tf_op jit(solution)/shard_map/ppermute | solution.py:22
  21.0 2.3 %collective-permute-done.4.refs_5_ = bf16[136,1024]{1,0:T(8,128)(2,1)S(1)} collective-permute-done((bf16[136,1024]{1,0:T(8,128)(2,1)S(1)}, bf16[136,1024]{1,0:T(8,128)(2,1)S(1)}, u32[]{:S(2)}, u32[]{:S(2)}) %collective-permute-start.4) | collective-permute-done | bytes 278560 | tf_op jit(solution)/shard_map/ppermute | solution.py:22
  23.3 2.1 %collective-permute-start.6 = (bf16[136,1024]{1,0:T(8,128)(2,1)S(1)}, bf16[136,1024]{1,0:T(8,128)(2,1)S(1)}, u32[]{:S(2)}, u32[]{:S(2)}) collective-permute-start(bf16[136,1024]{1,0:T(8,128)(2,1)S(1)} %collective-permute-done.4.refs_5_), channel_id=1, source_target_pairs={{0,2},{2,0},{1,3},{3,1},{4,6},{6,4},{5,7},{7,5},{8,10},{10,8},{9,1... | collective-permute-start | bytes 835592 | tf_op jit(solution)/shard_map/ppermute | solution.py:22
  25.4 1.2 copy-done.1
  26.6 1.2 copy-done.3
  27.9 1.2 copy-done.5
  29.1 0.5 shard_map.128.refs_6_.weight_ref
  29.6 0.5 copy-done.7
  30.0 1.1 shard_map.129
  31.2 1.2 collective-permute-done.6.last_ref.refs_11_
  32.3 3.8 %shard_map.130 = (bf16[2,136,1024]{2,1,0:T(8,128)(2,1)S(1)}, f32[2,136,128]{2,1,0:T(8,128)S(1)}, f32[2,136,128]{2,1,0:T(8,128)S(1)}, bf16[1088,1088]{1,0:T(8,128...) custom-call(s32[1]{0:T(128)} %bitcast.me_ref, ...), custom_call_target="tpu_custom_call" | custom-call | flops 5000000000 | bytes 1024 | tf_op jit(solution)/shard_map/pallas_call | solution.py:200
  36.1 13.1 %all_to_all.10.slab_ref = bf16[8,80,128]{2,1,0:T(8,128)(2,1)S(1)} all-to-all(bf16[8,80,128]{2,1,0:T(8,128)(2,1)S(1)} %get-tuple-element.58), channel_id=1, replica_groups=mesh['section'=4,'seq'=8] {'seq'}, dimensions={0} | all-to-all | bytes 327680 | tf_op jit(solution)/shard_map/all_to_all | solution.py:465
  49.2 2.0 %shard_map.131 = (bf16[136,1024]{1,0:T(8,128)(2,1)S(1)}, bf16[8,80,128]{2,1,0:T(8,128)(2,1)S(1)}, bf16[256,1024]{1,0:T(8,128)(2,1)S(1)}, bf16[128,1024]{1,0:T(8,...) custom-call(s32[1]{0:T(128)} %bitcast.me_ref, ...), custom_call_target="tpu_custom_call" | custom-call | flops 3000000000 | bytes 1024 | tf_op jit(solution)/shard_map/pallas_call | solution.py:200
  51.2 8.8 %all_to_all.11.slab_ref = bf16[8,80,128]{2,1,0:T(8,128)(2,1)S(1)} all-to-all(bf16[8,80,128]{2,1,0:T(8,128)(2,1)S(1)} %get-tuple-element.59), channel_id=1, replica_groups=mesh['section'=4,'seq'=8] {'seq'}, dimensions={0} | all-to-all | bytes 327680 | tf_op jit(solution)/shard_map/all_to_all | solution.py:465
  60.0 0.9 collective-permute-start.14
  60.9 0.5 collective-permute-start.15
  61.5 5.0 %shard_map.132 = (bf16[408,128]{1,0:T(8,128)(2,1)S(1)}, bf16[408,128]{1,0:T(8,128)(2,1)S(1)}, bf16[408,128]{1,0:T(8,128)(2,1)S(1)}, bf16[408,128]{1,0:T(8,128)(2...) custom-call(s32[1]{0:T(128)} %bitcast.me_ref, ...), custom_call_target="tpu_custom_call" | custom-call | flops 6000000000 | bytes 1024 | tf_op jit(solution)/shard_map/pallas_call | solution.py:200
  66.5 0.9 collective-permute-start.7
  67.4 1.5 %collective-permute-start.8 = (bf16[408,128]{1,0:T(8,128)(2,1)S(1)}, bf16[408,128]{1,0:T(8,128)(2,1)S(1)}, u32[]{:S(2)}, u32[]{:S(2)}) collective-permute-start(bf16[408,128]{1,0:T(8,128)(2,1)S(1)} %get-tuple-element.81), channel_id=1, source_target_pairs={{0,2},{1,3},{2,0},{3,1},{4,6},{5,7},{6,4},{7,5},{8,10},{9,11},{10,... | collective-permute-start | bytes 313352 | tf_op jit(solution)/shard_map/ppermute | solution.py:457
  68.9 12.1 %collective-permute-done.7.refs_4_.refs_1_ = bf16[408,128]{1,0:T(8,128)(2,1)S(1)} collective-permute-done((bf16[408,128]{1,0:T(8,128)(2,1)S(1)}, bf16[408,128]{1,0:T(8,128)(2,1)S(1)}, u32[]{:S(2)}, u32[]{:S(2)}) %collective-permute-start.7) | collective-permute-done | bytes 104480 | tf_op jit(solution)/shard_map/ppermute | solution.py:457
  81.6 0.5 collective-permute-start.18
  82.1 2.7 %collective-permute-start.11 = (bf16[408,128]{1,0:T(8,128)(2,1)S(1)}, bf16[408,128]{1,0:T(8,128)(2,1)S(1)}, u32[]{:S(2)}, u32[]{:S(2)}) collective-permute-start(bf16[408,128]{1,0:T(8,128)(2,1)S(1)} %get-tuple-element.84), channel_id=1, source_target_pairs={{0,5},{1,4},{2,7},{3,6},{4,1},{5,0},{6,3},{7,2},{8,13},{9,12},{10,... | collective-permute-start | bytes 313352 | tf_op jit(solution)/shard_map/ppermute | solution.py:457
  84.7 0.4 collective-permute-start.9
  85.2 1.5 %collective-permute-start.10 = (bf16[408,128]{1,0:T(8,128)(2,1)S(1)}, bf16[408,128]{1,0:T(8,128)(2,1)S(1)}, u32[]{:S(2)}, u32[]{:S(2)}) collective-permute-start(bf16[408,128]{1,0:T(8,128)(2,1)S(1)} %get-tuple-element.83), channel_id=1, source_target_pairs={{0,3},{1,2},{2,1},{3,0},{4,7},{5,6},{6,5},{7,4},{8,11},{9,10},{10,... | collective-permute-start | bytes 313352 | tf_op jit(solution)/shard_map/ppermute | solution.py:457
  86.7 0.8 collective-permute-done.11.refs_8_.refs_5_
  87.6 1.9 %collective-permute-start.12 = (bf16[408,128]{1,0:T(8,128)(2,1)S(1)}, bf16[408,128]{1,0:T(8,128)(2,1)S(1)}, u32[]{:S(2)}, u32[]{:S(2)}) collective-permute-start(bf16[408,128]{1,0:T(8,128)(2,1)S(1)} %get-tuple-element.85), channel_id=1, source_target_pairs={{0,6},{1,7},{2,4},{3,5},{4,2},{5,3},{6,0},{7,1},{8,14},{9,15},{10,... | collective-permute-start | bytes 313352 | tf_op jit(solution)/shard_map/ppermute | solution.py:457
  89.5 2.2 %collective-permute-start.13 = (bf16[408,128]{1,0:T(8,128)(2,1)S(1)}, bf16[408,128]{1,0:T(8,128)(2,1)S(1)}, u32[]{:S(2)}, u32[]{:S(2)}) collective-permute-start(bf16[408,128]{1,0:T(8,128)(2,1)S(1)} %get-tuple-element.86), channel_id=1, source_target_pairs={{0,7},{1,6},{2,5},{3,4},{4,3},{5,2},{6,1},{7,0},{8,15},{9,14},{10,... | collective-permute-start | bytes 313352 | tf_op jit(solution)/shard_map/ppermute | solution.py:457
  91.8 1.1 collective-permute-start.20
  92.9 1.3 %collective-permute-start.19 = (bf16[64,1024]{1,0:T(8,128)(2,1)S(1)}, bf16[64,1024]{1,0:T(8,128)(2,1)S(1)}, u32[]{:S(2)}, u32[]{:S(2)}) collective-permute-start(bf16[64,1024]{1,0:T(8,128)(2,1)S(1)} %get-tuple-element.98.refs_13_), channel_id=1, source_target_pairs={{0,4},{4,0},{1,5},{5,1},{2,6},{6,2},{3,7},{7,3},{8,12},{12,8},{9,1... | collective-permute-start | bytes 393224 | tf_op jit(solution)/shard_map/ppermute | solution.py:22
  94.3 2.0 %collective-permute-done.12.refs_6_ = bf16[408,128]{1,0:T(8,128)(2,1)S(1)} collective-permute-done((bf16[408,128]{1,0:T(8,128)(2,1)S(1)}, bf16[408,128]{1,0:T(8,128)(2,1)S(1)}, u32[]{:S(2)}, u32[]{:S(2)}) %collective-permute-start.12) | collective-permute-done | bytes 104480 | tf_op jit(solution)/shard_map/ppermute | solution.py:457
  96.3 1.4 %collective-permute-done.13.refs_7_ = bf16[408,128]{1,0:T(8,128)(2,1)S(1)} collective-permute-done((bf16[408,128]{1,0:T(8,128)(2,1)S(1)}, bf16[408,128]{1,0:T(8,128)(2,1)S(1)}, u32[]{:S(2)}, u32[]{:S(2)}) %collective-permute-start.13) | collective-permute-done | bytes 104480 | tf_op jit(solution)/shard_map/ppermute | solution.py:457
  97.7 1.4 %shard_map.135 = bf16[136,1024]{1,0:T(8,128)(2,1)S(1)} custom-call(s32[1]{0:T(128)} %bitcast.me_ref, bf16[408,128]{1,0:T(8,128)(2,1)S(1)} %get-tuple-element.79.refs_0_, bf16[408,128]{1,0:T(8,128)(2,1)S(1)} %collective-permute-done.7.refs_4_.refs_1_, bf16[408,128]{1,0:T(8,128)(2,1)S(1)} %collective-permute-done.8.refs_5_.refs_2_, ...), custom_call_target="tpu_custom_call" | custom-call | flops 1500000000 | bytes 1024 | tf_op jit(solution)/shard_map/pallas_call | solution.py:200
  99.0 12.3 %collective-permute-done.20.got_b = bf16[64,1024]{1,0:T(8,128)(2,1)S(1)} collective-permute-done((bf16[64,1024]{1,0:T(8,128)(2,1)S(1)}, bf16[64,1024]{1,0:T(8,128)(2,1)S(1)}, u32[]{:S(2)}, u32[]{:S(2)}) %collective-permute-start.20) | collective-permute-done | bytes 131104 | tf_op jit(solution)/shard_map/ppermute | solution.py:22
  111.3 3.1 %collective-permute-done.19.got_a = bf16[64,1024]{1,0:T(8,128)(2,1)S(1)} collective-permute-done((bf16[64,1024]{1,0:T(8,128)(2,1)S(1)}, bf16[64,1024]{1,0:T(8,128)(2,1)S(1)}, u32[]{:S(2)}, u32[]{:S(2)}) %collective-permute-start.19) | collective-permute-done | bytes 131104 | tf_op jit(solution)/shard_map/ppermute | solution.py:22
  114.4 0.8 shard_map.136
  115.3 4.0 %collective-permute-start.21 = (bf16[136,1024]{1,0:T(8,128)(2,1)S(1)}, bf16[136,1024]{1,0:T(8,128)(2,1)S(1)}, u32[]{:S(2)}, u32[]{:S(2)}) collective-permute-start(bf16[136,1024]{1,0:T(8,128)(2,1)S(1)} %shard_map.135), channel_id=1, source_target_pairs={{8,0},{16,8},{24,16},{9,1},{17,9},{25,17},{10,2},{18,10},{26,18},{... | collective-permute-start | bytes 835592 | tf_op jit(solution)/shard_map/ppermute | solution.py:28
  119.2 1.0 shard_map.138
  120.2 4.3 %collective-permute-done.21.rows_ref = bf16[136,1024]{1,0:T(8,128)(2,1)S(1)} collective-permute-done((bf16[136,1024]{1,0:T(8,128)(2,1)S(1)}, bf16[136,1024]{1,0:T(8,128)(2,1)S(1)}, u32[]{:S(2)}, u32[]{:S(2)}) %collective-permute-start.21) | collective-permute-done | bytes 278560 | tf_op jit(solution)/shard_map/ppermute | solution.py:28
  124.6 1.0 shard_map.137
  (36 shorter events, 1.2 us)
Async XLA Ops:
  0.6 15.8 %collective-permute-start.2 = (bf16[136,1024]{1,0:T(8,128)(2,1)}, bf16[136,1024]{1,0:T(8,128)(2,1)S(1)}, u32[]{:S(2)}, u32[]{:S(2)}) collective-permute-start(bf16[136,1024]{1,0:T(8,128)(2,1)} %bitcast.14), channel_id=1, source_target_pairs={{0,4},{4,0},{1,5},{5,1},{2,6},{6,2},{3,7},{7,3},{8,12},{12,8},{9,1... | collective-permute-start | bytes 835592 | tf_op jit(solution)/shard_map/ppermute | solution.py:22
  3.8 14.9 %collective-permute-start.1 = (bf16[136,1024]{1,0:T(8,128)(2,1)}, bf16[136,1024]{1,0:T(8,128)(2,1)S(1)}, u32[]{:S(2)}, u32[]{:S(2)}) collective-permute-start(bf16[136,1024]{1,0:T(8,128)(2,1)} %bitcast.15), channel_id=1, source_target_pairs={{0,2},{2,0},{1,3},{3,1},{4,6},{6,4},{5,7},{7,5},{8,10},{10,8},{9,1... | collective-permute-start | bytes 835592 | tf_op jit(solution)/shard_map/ppermute | solution.py:22
  5.1 24.4 %collective-permute-start = (bf16[136,1024]{1,0:T(8,128)(2,1)}, bf16[136,1024]{1,0:T(8,128)(2,1)S(1)}, u32[]{:S(2)}, u32[]{:S(2)}) collective-permute-start(bf16[136,1024]{1,0:T(8,128)(2,1)} %bitcast.16), channel_id=1, source_target_pairs={{0,1},{1,0},{2,3},{3,2},{4,5},{5,4},{6,7},{7,6},{8,9},{9,8},{10,11... | collective-permute-start | bytes 835592 | tf_op jit(solution)/shard_map/ppermute | solution.py:22
  16.4 6.9 %collective-permute-start.4 = (bf16[136,1024]{1,0:T(8,128)(2,1)S(1)}, bf16[136,1024]{1,0:T(8,128)(2,1)S(1)}, u32[]{:S(2)}, u32[]{:S(2)}) collective-permute-start(bf16[136,1024]{1,0:T(8,128)(2,1)S(1)} %collective-permute-done.2.refs_3_), channel_id=1, source_target_pairs={{0,1},{1,0},{2,3},{3,2},{4,5},{5,4},{6,7},{7,6},{8,9},{9,8},{10,11... | collective-permute-start | bytes 835592 | tf_op jit(solution)/shard_map/ppermute | solution.py:22
  18.8 10.8 %collective-permute-start.3 = (bf16[136,1024]{1,0:T(8,128)(2,1)S(1)}, bf16[136,1024]{1,0:T(8,128)(2,1)S(1)}, u32[]{:S(2)}, u32[]{:S(2)}) collective-permute-start(bf16[136,1024]{1,0:T(8,128)(2,1)S(1)} %collective-permute-done.1.refs_2_), channel_id=1, source_target_pairs={{0,1},{1,0},{2,3},{3,2},{4,5},{5,4},{6,7},{7,6},{8,9},{9,8},{10,11... | collective-permute-start | bytes 835592 | tf_op jit(solution)/shard_map/ppermute | solution.py:22
  19.7 11.4 %collective-permute-start.5 = (bf16[136,1024]{1,0:T(8,128)(2,1)S(1)}, bf16[136,1024]{1,0:T(8,128)(2,1)S(1)}, u32[]{:S(2)}, u32[]{:S(2)}) collective-permute-start(bf16[136,1024]{1,0:T(8,128)(2,1)S(1)} %collective-permute-done.2.refs_3_), channel_id=1, source_target_pairs={{0,2},{2,0},{1,3},{3,1},{4,6},{6,4},{5,7},{7,5},{8,10},{10,8},{9,1... | collective-permute-start | bytes 835592 | tf_op jit(solution)/shard_map/ppermute | solution.py:22
  23.3 9.0 %collective-permute-start.6 = (bf16[136,1024]{1,0:T(8,128)(2,1)S(1)}, bf16[136,1024]{1,0:T(8,128)(2,1)S(1)}, u32[]{:S(2)}, u32[]{:S(2)}) collective-permute-start(bf16[136,1024]{1,0:T(8,128)(2,1)S(1)} %collective-permute-done.4.refs_5_), channel_id=1, source_target_pairs={{0,2},{2,0},{1,3},{3,1},{4,6},{6,4},{5,7},{7,5},{8,10},{10,8},{9,1... | collective-permute-start | bytes 835592 | tf_op jit(solution)/shard_map/ppermute | solution.py:22
  25.4 1.2 copy-start.1
  26.6 1.2 copy-start.3
  27.9 1.2 copy-start.5
  29.1 1.0 copy-start.7
  32.3 16.8 %copy-start = (bf16[1,512,2048]{2,1,0:T(8,128)(2,1)S(1)}, bf16[1,512,2048]{2,1,0:T(8,128)(2,1)}, u32[]{:S(2)}) copy-start(bf16[1,512,2048]{2,1,0:T(8,128)(2,1)} %param.14) | copy-start | bytes 6291460
  32.3 16.8 %copy-start.8 = (bf16[1,136,1024]{2,1,0:T(8,128)(2,1)S(1)}, bf16[1,136,1024]{2,1,0:T(8,128)(2,1)}, u32[]{:S(2)}) copy-start(bf16[1,136,1024]{2,1,0:T(8,128)(2,1)} %param.10) | copy-start | bytes 835588
  60.0 21.4 %collective-permute-start.14 = (bf16[136,1024]{1,0:T(8,128)(2,1)S(1)}, bf16[136,1024]{1,0:T(8,128)(2,1)S(1)}, u32[]{:S(2)}, u32[]{:S(2)}) collective-permute-start(bf16[136,1024]{1,0:T(8,128)(2,1)S(1)} %get-tuple-element.87), channel_id=1, source_target_pairs={{0,7},{1,6},{2,5},{3,4},{4,3},{5,2},{6,1},{7,0},{8,15},{9,14},{10,... | collective-permute-start | bytes 835592 | tf_op jit(solution)/shard_map/ppermute | solution.py:457
  60.9 20.4 %collective-permute-start.15 = (bf16[256,1024]{1,0:T(8,128)(2,1)S(1)}, bf16[256,1024]{1,0:T(8,128)(2,1)S(1)}, u32[]{:S(2)}, u32[]{:S(2)}) collective-permute-start(bf16[256,1024]{1,0:T(8,128)(2,1)S(1)} %get-tuple-element.92), channel_id=1, source_target_pairs={{0,1},{1,0},{2,3},{3,2},{4,5},{5,4},{6,7},{7,6},{8,9},{9,8},{10,11... | collective-permute-start | bytes 1572872 | tf_op jit(solution)/shard_map/ppermute | solution.py:22
  61.4 19.9 %collective-permute-start.16 = (bf16[256,1024]{1,0:T(8,128)(2,1)S(1)}, bf16[256,1024]{1,0:T(8,128)(2,1)S(1)}, u32[]{:S(2)}, u32[]{:S(2)}) collective-permute-start(bf16[256,1024]{1,0:T(8,128)(2,1)S(1)} %get-tuple-element.93), channel_id=1, source_target_pairs={{0,2},{2,0},{1,3},{3,1},{4,6},{6,4},{5,7},{7,5},{8,10},{10,8},{9,1... | collective-permute-start | bytes 1572872 | tf_op jit(solution)/shard_map/ppermute | solution.py:22
  66.5 14.5 %collective-permute-start.7 = (bf16[408,128]{1,0:T(8,128)(2,1)S(1)}, bf16[408,128]{1,0:T(8,128)(2,1)S(1)}, u32[]{:S(2)}, u32[]{:S(2)}) collective-permute-start(bf16[408,128]{1,0:T(8,128)(2,1)S(1)} %get-tuple-element.80), channel_id=1, source_target_pairs={{0,1},{1,0},{2,3},{3,2},{4,5},{5,4},{6,7},{7,6},{8,9},{9,8},{10,11... | collective-permute-start | bytes 313352 | tf_op jit(solution)/shard_map/ppermute | solution.py:457
  67.4 13.9 %collective-permute-start.8 = (bf16[408,128]{1,0:T(8,128)(2,1)S(1)}, bf16[408,128]{1,0:T(8,128)(2,1)S(1)}, u32[]{:S(2)}, u32[]{:S(2)}) collective-permute-start(bf16[408,128]{1,0:T(8,128)(2,1)S(1)} %get-tuple-element.81), channel_id=1, source_target_pairs={{0,2},{1,3},{2,0},{3,1},{4,6},{5,7},{6,4},{7,5},{8,10},{9,11},{10,... | collective-permute-start | bytes 313352 | tf_op jit(solution)/shard_map/ppermute | solution.py:457
  81.5 8.0 %collective-permute-start.17 = (bf16[128,1024]{1,0:T(8,128)(2,1)S(1)}, bf16[128,1024]{1,0:T(8,128)(2,1)S(1)}, u32[]{:S(2)}, u32[]{:S(2)}) collective-permute-start(bf16[128,1024]{1,0:T(8,128)(2,1)S(1)} %get-tuple-element.96), channel_id=1, source_target_pairs={{0,2},{2,0},{1,3},{3,1},{4,6},{6,4},{5,7},{7,5},{8,10},{10,8},{9,1... | collective-permute-start | bytes 786440 | tf_op jit(solution)/shard_map/ppermute | solution.py:22
  81.6 10.1 %collective-permute-start.18 = (bf16[128,1024]{1,0:T(8,128)(2,1)S(1)}, bf16[128,1024]{1,0:T(8,128)(2,1)S(1)}, u32[]{:S(2)}, u32[]{:S(2)}) collective-permute-start(bf16[128,1024]{1,0:T(8,128)(2,1)S(1)} %get-tuple-element.97), channel_id=1, source_target_pairs={{0,1},{1,0},{2,3},{3,2},{4,5},{5,4},{6,7},{7,6},{8,9},{9,8},{10,11... | collective-permute-start | bytes 786440 | tf_op jit(solution)/shard_map/ppermute | solution.py:22
  82.1 5.5 %collective-permute-start.11 = (bf16[408,128]{1,0:T(8,128)(2,1)S(1)}, bf16[408,128]{1,0:T(8,128)(2,1)S(1)}, u32[]{:S(2)}, u32[]{:S(2)}) collective-permute-start(bf16[408,128]{1,0:T(8,128)(2,1)S(1)} %get-tuple-element.84), channel_id=1, source_target_pairs={{0,5},{1,4},{2,7},{3,6},{4,1},{5,0},{6,3},{7,2},{8,13},{9,12},{10,... | collective-permute-start | bytes 313352 | tf_op jit(solution)/shard_map/ppermute | solution.py:457
  84.7 8.2 %collective-permute-start.9 = (bf16[408,128]{1,0:T(8,128)(2,1)S(1)}, bf16[408,128]{1,0:T(8,128)(2,1)S(1)}, u32[]{:S(2)}, u32[]{:S(2)}) collective-permute-start(bf16[408,128]{1,0:T(8,128)(2,1)S(1)} %get-tuple-element.82), channel_id=1, source_target_pairs={{0,4},{1,5},{2,6},{3,7},{4,0},{5,1},{6,2},{7,3},{8,12},{9,13},{10,... | collective-permute-start | bytes 313352 | tf_op jit(solution)/shard_map/ppermute | solution.py:457
  85.2 9.1 %collective-permute-start.10 = (bf16[408,128]{1,0:T(8,128)(2,1)S(1)}, bf16[408,128]{1,0:T(8,128)(2,1)S(1)}, u32[]{:S(2)}, u32[]{:S(2)}) collective-permute-start(bf16[408,128]{1,0:T(8,128)(2,1)S(1)} %get-tuple-element.83), channel_id=1, source_target_pairs={{0,3},{1,2},{2,1},{3,0},{4,7},{5,6},{6,5},{7,4},{8,11},{9,10},{10,... | collective-permute-start | bytes 313352 | tf_op jit(solution)/shard_map/ppermute | solution.py:457
  87.6 8.7 %collective-permute-start.12 = (bf16[408,128]{1,0:T(8,128)(2,1)S(1)}, bf16[408,128]{1,0:T(8,128)(2,1)S(1)}, u32[]{:S(2)}, u32[]{:S(2)}) collective-permute-start(bf16[408,128]{1,0:T(8,128)(2,1)S(1)} %get-tuple-element.85), channel_id=1, source_target_pairs={{0,6},{1,7},{2,4},{3,5},{4,2},{5,3},{6,0},{7,1},{8,14},{9,15},{10,... | collective-permute-start | bytes 313352 | tf_op jit(solution)/shard_map/ppermute | solution.py:457
  89.5 8.2 %copy-start.2 = (bf16[1,1024,512]{2,1,0:T(8,128)(2,1)S(1)}, bf16[1,1024,512]{2,1,0:T(8,128)(2,1)}, u32[]{:S(2)}) copy-start(bf16[1,1024,512]{2,1,0:T(8,128)(2,1)} %param.11) | copy-start | bytes 3145732
  89.5 8.2 %copy-start.4 = (bf16[1,1024,512]{2,1,0:T(8,128)(2,1)S(1)}, bf16[1,1024,512]{2,1,0:T(8,128)(2,1)}, u32[]{:S(2)}) copy-start(bf16[1,1024,512]{2,1,0:T(8,128)(2,1)} %param.12) | copy-start | bytes 3145732
  89.5 8.2 %copy-start.6 = (bf16[1,1024,512]{2,1,0:T(8,128)(2,1)S(1)}, bf16[1,1024,512]{2,1,0:T(8,128)(2,1)}, u32[]{:S(2)}) copy-start(bf16[1,1024,512]{2,1,0:T(8,128)(2,1)} %param.13) | copy-start | bytes 3145732
  89.5 8.2 %collective-permute-start.13 = (bf16[408,128]{1,0:T(8,128)(2,1)S(1)}, bf16[408,128]{1,0:T(8,128)(2,1)S(1)}, u32[]{:S(2)}, u32[]{:S(2)}) collective-permute-start(bf16[408,128]{1,0:T(8,128)(2,1)S(1)} %get-tuple-element.86), channel_id=1, source_target_pairs={{0,7},{1,6},{2,5},{3,4},{4,3},{5,2},{6,1},{7,0},{8,15},{9,14},{10,... | collective-permute-start | bytes 313352 | tf_op jit(solution)/shard_map/ppermute | solution.py:457
  91.8 19.5 %collective-permute-start.20 = (bf16[64,1024]{1,0:T(8,128)(2,1)S(1)}, bf16[64,1024]{1,0:T(8,128)(2,1)S(1)}, u32[]{:S(2)}, u32[]{:S(2)}) collective-permute-start(bf16[64,1024]{1,0:T(8,128)(2,1)S(1)} %get-tuple-element.101), channel_id=1, source_target_pairs={{0,4},{4,0},{1,5},{5,1},{2,6},{6,2},{3,7},{7,3},{8,12},{12,8},{9,1... | collective-permute-start | bytes 393224 | tf_op jit(solution)/shard_map/ppermute | solution.py:22
  92.9 21.5 %collective-permute-start.19 = (bf16[64,1024]{1,0:T(8,128)(2,1)S(1)}, bf16[64,1024]{1,0:T(8,128)(2,1)S(1)}, u32[]{:S(2)}, u32[]{:S(2)}) collective-permute-start(bf16[64,1024]{1,0:T(8,128)(2,1)S(1)} %get-tuple-element.98.refs_13_), channel_id=1, source_target_pairs={{0,4},{4,0},{1,5},{5,1},{2,6},{6,2},{3,7},{7,3},{8,12},{12,8},{9,1... | collective-permute-start | bytes 393224 | tf_op jit(solution)/shard_map/ppermute | solution.py:22
  115.3 9.3 %copy-start.9 = (s32[1,136]{1,0:T(1,128)S(1)}, s32[1,136]{1,0:T(1,128)}, u32[]{:S(2)}) copy-start(s32[1,136]{1,0:T(1,128)} %order_ref.1) | copy-start | bytes 1636
  115.3 9.3 %collective-permute-start.21 = (bf16[136,1024]{1,0:T(8,128)(2,1)S(1)}, bf16[136,1024]{1,0:T(8,128)(2,1)S(1)}, u32[]{:S(2)}, u32[]{:S(2)}) collective-permute-start(bf16[136,1024]{1,0:T(8,128)(2,1)S(1)} %shard_map.135), channel_id=1, source_target_pairs={{8,0},{16,8},{24,16},{9,1},{17,9},{25,17},{10,2},{18,10},{26,18},{... | collective-permute-start | bytes 835592 | tf_op jit(solution)/shard_map/ppermute | solution.py:28

commit v10 on v9

--- a/solution.py
+++ b/solution.py
@@ -272,10 +272,20 @@
     out_ref[:, 2 * HEAD_DIM :] = low(jnp.where(odd, swap(v), v)[:, :HEAD_DIM])
 
 
+def joined(refs, width):
+    pieces, blocks = [], []
+    for ref in refs:
+        pieces.append(ref[...])
+        if sum(piece.shape[1] for piece in pieces) == width:
+            blocks.append(jnp.concatenate(pieces, axis=1) if len(pieces) > 1 else pieces[0])
+            pieces = []
+    return blocks
+
+
 def project_kernel(*refs):
     blocks, (weight_ref, normed_ref, unit_ref, scale_ref, value_ref) = refs[:-5], refs[-5:]
-    for m, block in enumerate(blocks):
-        made = project(block[...], weight_ref[...])
+    for m, block in enumerate(joined(blocks, normed_ref.shape[2])):
+        made = project(block, weight_ref[...])
         for ref, part in zip((normed_ref, unit_ref, scale_ref, value_ref), made):
             ref[m] = part.astype(ref.dtype)
 
@@ -289,18 +299,19 @@
 
 
 def attend_kernel(
-    me_ref, unit_ref, value_ref, near_ref, last_ref, weight_ref, row_ids, column_ids, *out_refs
+    me_ref, unit_ref, value_ref, weight_ref, row_ids, column_ids, *refs
 ):
+    pieces, out_refs = refs[:-8], refs[-8:]
     normed_ref, late_unit, late_scale, prob_ref, qk_ref, v_ref, out_t_ref = out_refs[:7]
     early, rows = unit_ref.shape[:2]
     units = [unit_ref[m] for m in range(early)]
     values = [value_ref[m] for m in range(early)]
-    for m, ref in enumerate((near_ref, last_ref)):
-        normed, unit, scale, value = project(ref[...], weight_ref[...])
+    for m, block in enumerate(joined(pieces, normed_ref.shape[2])):
+        normed, unit, scale, value = project(block, weight_ref[...])
         normed_ref[m], late_unit[m], late_scale[m] = normed, unit, scale
         units.append(unit)
         values.append(value)
-    parts = len(units)
+    parts = early + normed_ref.shape[0]
     tokens = parts * rows
     qk = jnp.concatenate(units, axis=0).astype(jnp.bfloat16)
     value = jnp.concatenate(values, axis=0).astype(jnp.bfloat16)
@@ -424,12 +435,12 @@
 
 
 def input_kernel(me_ref, *refs):
-    slabs, (wq_ref, wk_ref, wv_ref, act_ref, up_ref, _, out_ref) = refs[:HEADS], refs[HEADS:-1]
+    slabs, (wq_ref, wk_ref, wv_ref, *acts, up_ref, _, out_ref) = refs[:HEADS], refs[HEADS:-1]
     held_ref = refs[-1]
-    rows = act_ref.shape[0]
+    rows = up_ref.shape[0]
     for m, slab in enumerate(slabs):
         held_ref[me_ref[0] ^ DISTANCES[m]] = slab[: PACKED + rows, :]
-    unit, row_scale = normalize(act_ref[...])
+    unit, row_scale = normalize(joined(acts, up_ref.shape[1])[0])
     queries, keys, values = [], [], []
     for pair in range(HEADS // 2):
         even, odd = [wide(held_ref[2 * pair + i]) for i in range(2)]
@@ -466,12 +477,16 @@
 
 
 def spread(block):
-    side, near, far = [partner(block, "seq", bit) for bit in range(3)]
-    side_far = partner(far, "seq", 0)
-    near_far = partner(far, "seq", 1)
-    side_near = partner(near, "seq", 0)
-    last = partner(side_far, "seq", 1)
-    return block, side, near, far, side_near, side_far, near_far, last
+    middle = block.shape[1] // 2
+    pieces = [block[:, :middle], block[:, middle:]]
+    far = [hop(piece, 4) for piece in pieces]
+    near, side = hop(block, 2), hop(block, 1)
+    side_far = [hop(piece, 1) for piece in far]
+    near_far = [hop(piece, 2) for piece in far]
+    side_near = hop(near, 1)
+    last = [hop(side_far[0], 2), hop(near_far[1], 1)]
+    early = [block, side, near, *far, side_near, *side_far]
+    return early, near_far, last
 
 
 DISTANCES = (0, 1, 2, 4, 3, 5, 6, 7)
@@ -503,7 +518,7 @@
     def out(*dims, dtype=jnp.bfloat16):
         return jax.ShapeDtypeStruct(dims, dtype)
 
-    blocks = spread(field)
+    first_blocks, near_far, mirrored = spread(field)
     order = me[0] ^ jnp.array(DISTANCES, jnp.int32)
     ids = jnp.take(block_ids.reshape(parts, rows), order, axis=0).reshape(tokens)
     (weight,) = call(
@@ -517,7 +532,7 @@
     normed, unit, unit_scale, projected = call(
         project_kernel,
         2,
-        [("v", block) for block in blocks[:EARLY]] + [("v", weight)],
+        [("v", block) for block in first_blocks] + [("v", weight)],
         [
             out(EARLY, rows, width),
             out(EARLY, rows, pair, dtype=f32),
@@ -529,8 +544,9 @@
     made = call(
         attend_kernel,
         5,
-        [("s", me), ("v", unit), ("v", projected), *[("v", block) for block in blocks[EARLY:]]]
-        + [("v", weight), ("v", ids[None, :]), ("v", ids[:, None])],
+        [("s", me), ("v", unit), ("v", projected), ("v", weight)]
+        + [("v", ids[None, :]), ("v", ids[:, None])]
+        + [("v", block) for block in (*near_far, *mirrored)],
         [
             out(late, rows, width),
             out(late, rows, pair, dtype=f32),
@@ -587,18 +603,18 @@
     (grad_input,) = call(
         input_kernel,
         1.5,
-        [("s", me)] + [("v", x) for x in (*slabs, wq, wk, wv, blocks[-1], scaled)] + [("a", leaving[0])],
+        [("s", me)] + [("v", x) for x in (*slabs, wq, wk, wv, *mirrored, scaled)] + [("a", leaving[0])],
         [out(rows, width)],
         [pltpu.VMEM((HEADS, PACKED + rows, 128), jnp.bfloat16)],
     )
+    grad_input, rest[0] = lax.optimization_barrier((grad_input, rest[0]))
+    moved = to_previous(grad_input)
     (grad_out,) = call(
         last_sum_kernel,
         1,
         [("v", x) for x in (keep_a, keep_b, *rest)],
         [out(1, keep_a.shape[0], 2 * width, dtype=f32)],
     )
-    grad_input, grad_out = lax.optimization_barrier((grad_input, grad_out))
-    moved = to_previous(grad_input)
     grad_q, grad_k, grad_v = call(
         turn_kernel,
         1,

time: 126 us -> 124 us (0.984)
  the two profiles are of different devices: /device:TPU:1 before, /device:TPU:5 now
where the time goes in v10:
time: 124 us; the launch traced here: 123 us
  starting transfers between devices  41.2 us (33%)
  waiting for transfers between devices  37.4 us (30%)
  blocking collectives  19.5 us (16%)
  Pallas kernels  16.8 us (14%)
  local copies, waits for them, and re-layouts  6.33 us (5%)
    ppermute x19, waiting for transfers between devices, hop(): return lax.ppermute(block, 'seq', route)  23.6 us
    ppermute x19, starting transfers between devices, hop(): return lax.ppermute(block, 'seq', route)  20.6 us
    all_to_all x2, blocking collectives, switch(): return lax.all_to_all(slabs, 'seq', split_axis=0, concat_axis=0, tiled=True)  19.5 us
    pallas_call x11, Pallas kernels, call(): pl.pallas_call(kernel, out_shape=tuple(outs), in_specs=[pl.BlockSpec(memo...  16.8 us
    ppermute x1, starting transfers between devices, shifted(): return lax.ppermute(block, axis, route)  14.1 us
    ppermute x6, waiting for transfers between devices, partner(): return lax.ppermute(block, axis, route)  13.8 us
    ppermute x6, starting transfers between devices, partner(): return lax.ppermute(block, axis, route)  6.46 us
    unnamed x20, local copies, waits for them, and re-layouts  3.7 us
  transfers between devices with their start and end apart: 26, of which 14 were waited for; matrix products, arithmetic and copies ran while one was open for 3% of the time, Pallas kernels for 8%

profile of v10, /device:TPU:5, one launch (start us, length us, event | category | flops | bytes accessed | tf_op | source)
XLA Modules:
  0.0 122.7 jit_solution(2593667697641260926)
XLA Ops:
  0.6 1.4 %collective-permute-start.1 = (bf16[136,1024]{1,0:T(8,128)(2,1)}, bf16[136,1024]{1,0:T(8,128)(2,1)S(1)}, u32[]{:S(2)}, u32[]{:S(2)}) collective-permute-start(bf16[136,1024]{1,0:T(8,128)(2,1)} %bitcast.7), channel_id=1, source_target_pairs={{0,2},{1,3},{2,0},{3,1},{4,6},{5,7},{6,4},{7,5},{8,10},{9,11},{10,... | collective-permute-start | bytes 835592 | tf_op jit(solution)/shard_map/ppermute | solution.py:468
  2.0 1.2 collective-permute-start
  3.2 1.0 fusion
  4.2 2.4 %collective-permute-start.3 = (bf16[136,512]{1,0:T(8,128)(2,1)S(1)}, bf16[136,512]{1,0:T(8,128)(2,1)S(1)}, u32[]{:S(2)}, u32[]{:S(2)}) collective-permute-start(bf16[136,512]{1,0:T(8,128)(2,1)S(1)} %get-tuple-element.109), channel_id=1, source_target_pairs={{0,4},{1,5},{2,6},{3,7},{4,0},{5,1},{6,2},{7,3},{8,12},{9,13},{10,... | collective-permute-start | bytes 417800 | tf_op jit(solution)/shard_map/ppermute | solution.py:468
  6.7 0.8 reshape.64
  7.4 0.7 compare_and_fusion
  8.1 0.6 gather_fusion
  8.7 2.5 %collective-permute-done.1.refs_2_ = bf16[136,1024]{1,0:T(8,128)(2,1)S(1)} collective-permute-done((bf16[136,1024]{1,0:T(8,128)(2,1)}, bf16[136,1024]{1,0:T(8,128)(2,1)S(1)}, u32[]{:S(2)}, u32[]{:S(2)}) %collective-permute-start.1) | collective-permute-done | bytes 278560 | tf_op jit(solution)/shard_map/ppermute | solution.py:468
  11.2 3.1 %collective-permute-start.4 = (bf16[136,1024]{1,0:T(8,128)(2,1)S(1)}, bf16[136,1024]{1,0:T(8,128)(2,1)S(1)}, u32[]{:S(2)}, u32[]{:S(2)}) collective-permute-start(bf16[136,1024]{1,0:T(8,128)(2,1)S(1)} %collective-permute-done.1.refs_2_), channel_id=1, source_target_pairs={{0,1},{1,0},{2,3},{3,2},{4,5},{5,4},{6,7},{7,6},{8,9},{9,8},{10,11... | collective-permute-start | bytes 835592 | tf_op jit(solution)/shard_map/ppermute | solution.py:468
  14.9 4.2 %collective-permute-done.2.refs_3_ = bf16[136,512]{1,0:T(8,128)(2,1)S(1)} collective-permute-done((bf16[136,512]{1,0:T(8,128)(2,1)S(1)}, bf16[136,512]{1,0:T(8,128)(2,1)S(1)}, u32[]{:S(2)}, u32[]{:S(2)}) %collective-permute-start.2) | collective-permute-done | bytes 139296 | tf_op jit(solution)/shard_map/ppermute | solution.py:468
  19.3 1.2 copy-done.2
  20.6 1.2 copy-done.4
  21.8 1.2 copy-done.6
  23.0 0.5 shard_map.128.refs_8_.weight_ref
  23.6 1.3 %collective-permute-start.10 = (bf16[136,512]{1,0:T(8,128)(2,1)S(1)}, bf16[136,512]{1,0:T(8,128)(2,1)S(1)}, u32[]{:S(2)}, u32[]{:S(2)}) collective-permute-start(bf16[136,512]{1,0:T(8,128)(2,1)S(1)} %collective-permute-done.8.refs_1_), channel_id=1, source_target_pairs={{0,1},{1,0},{2,3},{3,2},{4,5},{5,4},{6,7},{7,6},{8,9},{9,8},{10,11... | collective-permute-start | bytes 417800 | tf_op jit(solution)/shard_map/ppermute | solution.py:468
  24.9 0.7 collective-permute-done.5.refs_6_
  25.6 0.7 collective-permute-start.9
  26.3 1.0 shard_map.129
  27.3 0.4 collective-permute-done.7.refs_0_
  27.8 1.1 collective-permute-done.10.refs_3_.refs_12_
  28.9 2.3 %collective-permute-done.9.refs_2_.refs_11_ = bf16[136,512]{1,0:T(8,128)(2,1)S(1)} collective-permute-done((bf16[136,512]{1,0:T(8,128)(2,1)S(1)}, bf16[136,512]{1,0:T(8,128)(2,1)S(1)}, u32[]{:S(2)}, u32[]{:S(2)}) %collective-permute-start.9) | collective-permute-done | bytes 139296 | tf_op jit(solution)/shard_map/ppermute | solution.py:468
  31.3 3.7 %shard_map.130 = (bf16[2,136,1024]{2,1,0:T(8,128)(2,1)S(1)}, f32[2,136,128]{2,1,0:T(8,128)S(1)}, f32[2,136,128]{2,1,0:T(8,128)S(1)}, bf16[1088,1088]{1,0:T(8,128...) custom-call(s32[1]{0:T(128)} %bitcast.me_ref, ...), custom_call_target="tpu_custom_call" | custom-call | flops 5000000000 | bytes 1024 | tf_op jit(solution)/shard_map/pallas_call | solution.py:200
  35.0 10.6 %all_to_all.10.slab_ref = bf16[8,80,128]{2,1,0:T(8,128)(2,1)S(1)} all-to-all(bf16[8,80,128]{2,1,0:T(8,128)(2,1)S(1)} %get-tuple-element.58), channel_id=1, replica_groups=mesh['section'=4,'seq'=8] {'seq'}, dimensions={0} | all-to-all | bytes 327680 | tf_op jit(solution)/shard_map/all_to_all | solution.py:476
  45.6 2.0 %shard_map.131 = (bf16[136,1024]{1,0:T(8,128)(2,1)S(1)}, bf16[8,80,128]{2,1,0:T(8,128)(2,1)S(1)}, bf16[256,1024]{1,0:T(8,128)(2,1)S(1)}, bf16[128,1024]{1,0:T(8,...) custom-call(s32[1]{0:T(128)} %bitcast.me_ref, ...), custom_call_target="tpu_custom_call" | custom-call | flops 3000000000 | bytes 1024 | tf_op jit(solution)/shard_map/pallas_call | solution.py:200
  47.6 8.8 %all_to_all.11.slab_ref = bf16[8,80,128]{2,1,0:T(8,128)(2,1)S(1)} all-to-all(bf16[8,80,128]{2,1,0:T(8,128)(2,1)S(1)} %get-tuple-element.59), channel_id=1, replica_groups=mesh['section'=4,'seq'=8] {'seq'}, dimensions={0} | all-to-all | bytes 327680 | tf_op jit(solution)/shard_map/all_to_all | solution.py:476
  56.5 0.9 collective-permute-start.18
  57.4 0.5 collective-permute-start.19
  58.0 5.0 %shard_map.132 = (bf16[408,128]{1,0:T(8,128)(2,1)S(1)}, bf16[408,128]{1,0:T(8,128)(2,1)S(1)}, bf16[408,128]{1,0:T(8,128)(2,1)S(1)}, bf16[408,128]{1,0:T(8,128)(2...) custom-call(s32[1]{0:T(128)} %bitcast.me_ref, ...), custom_call_target="tpu_custom_call" | custom-call | flops 6000000000 | bytes 1024 | tf_op jit(solution)/shard_map/pallas_call | solution.py:200
  63.0 0.9 collective-permute-start.11
  63.9 1.5 %collective-permute-start.12 = (bf16[408,128]{1,0:T(8,128)(2,1)S(1)}, bf16[408,128]{1,0:T(8,128)(2,1)S(1)}, u32[]{:S(2)}, u32[]{:S(2)}) collective-permute-start(bf16[408,128]{1,0:T(8,128)(2,1)S(1)} %get-tuple-element.81), channel_id=1, source_target_pairs={{0,2},{1,3},{2,0},{3,1},{4,6},{5,7},{6,4},{7,5},{8,10},{9,11},{10,... | collective-permute-start | bytes 313352 | tf_op jit(solution)/shard_map/ppermute | solution.py:468
  65.4 4.6 %collective-permute-done.11.refs_4_.refs_1_ = bf16[408,128]{1,0:T(8,128)(2,1)S(1)} collective-permute-done((bf16[408,128]{1,0:T(8,128)(2,1)S(1)}, bf16[408,128]{1,0:T(8,128)(2,1)S(1)}, u32[]{:S(2)}, u32[]{:S(2)}) %collective-permute-start.11) | collective-permute-done | bytes 104480 | tf_op jit(solution)/shard_map/ppermute | solution.py:468
  70.0 0.8 collective-permute-done.12.refs_5_.refs_2_
  70.9 4.4 %collective-permute-start.21 = (bf16[128,1024]{1,0:T(8,128)(2,1)S(1)}, bf16[128,1024]{1,0:T(8,128)(2,1)S(1)}, u32[]{:S(2)}, u32[]{:S(2)}) collective-permute-start(bf16[128,1024]{1,0:T(8,128)(2,1)S(1)} %get-tuple-element.96), channel_id=1, source_target_pairs={{0,2},{2,0},{1,3},{3,1},{4,6},{6,4},{5,7},{7,5},{8,10},{10,8},{9,1... | collective-permute-start | bytes 786440 | tf_op jit(solution)/shard_map/ppermute | solution.py:22
  75.3 0.5 collective-permute-start.22
  76.0 2.8 %collective-permute-start.13 = (bf16[408,128]{1,0:T(8,128)(2,1)S(1)}, bf16[408,128]{1,0:T(8,128)(2,1)S(1)}, u32[]{:S(2)}, u32[]{:S(2)}) collective-permute-start(bf16[408,128]{1,0:T(8,128)(2,1)S(1)} %get-tuple-element.82), channel_id=1, source_target_pairs={{0,4},{1,5},{2,6},{3,7},{4,0},{5,1},{6,2},{7,3},{8,12},{9,13},{10,... | collective-permute-start | bytes 313352 | tf_op jit(solution)/shard_map/ppermute | solution.py:468
  79.2 2.8 %collective-permute-done.15.refs_8_.refs_5_ = bf16[408,128]{1,0:T(8,128)(2,1)S(1)} collective-permute-done((bf16[408,128]{1,0:T(8,128)(2,1)S(1)}, bf16[408,128]{1,0:T(8,128)(2,1)S(1)}, u32[]{:S(2)}, u32[]{:S(2)}) %collective-permute-start.15) | collective-permute-done | bytes 104480 | tf_op jit(solution)/shard_map/ppermute | solution.py:468
  82.0 1.4 %collective-permute-start.16 = (bf16[408,128]{1,0:T(8,128)(2,1)S(1)}, bf16[408,128]{1,0:T(8,128)(2,1)S(1)}, u32[]{:S(2)}, u32[]{:S(2)}) collective-permute-start(bf16[408,128]{1,0:T(8,128)(2,1)S(1)} %get-tuple-element.85), channel_id=1, source_target_pairs={{0,6},{1,7},{2,4},{3,5},{4,2},{5,3},{6,0},{7,1},{8,14},{9,15},{10,... | collective-permute-start | bytes 313352 | tf_op jit(solution)/shard_map/ppermute | solution.py:468
  83.3 1.1 collective-permute-done.21.refs_6_
  84.5 1.9 %collective-permute-start.17 = (bf16[408,128]{1,0:T(8,128)(2,1)S(1)}, bf16[408,128]{1,0:T(8,128)(2,1)S(1)}, u32[]{:S(2)}, u32[]{:S(2)}) collective-permute-start(bf16[408,128]{1,0:T(8,128)(2,1)S(1)} %get-tuple-element.86), channel_id=1, source_target_pairs={{0,7},{1,6},{2,5},{3,4},{4,3},{5,2},{6,1},{7,0},{8,15},{9,14},{10,... | collective-permute-start | bytes 313352 | tf_op jit(solution)/shard_map/ppermute | solution.py:468
  86.6 0.9 collective-permute-start.23
  87.9 3.7 %collective-permute-done.17.refs_7_ = bf16[408,128]{1,0:T(8,128)(2,1)S(1)} collective-permute-done((bf16[408,128]{1,0:T(8,128)(2,1)S(1)}, bf16[408,128]{1,0:T(8,128)(2,1)S(1)}, u32[]{:S(2)}, u32[]{:S(2)}) %collective-permute-start.17) | collective-permute-done | bytes 104480 | tf_op jit(solution)/shard_map/ppermute | solution.py:468
  91.6 1.4 %shard_map.135 = bf16[136,1024]{1,0:T(8,128)(2,1)S(1)} custom-call(s32[1]{0:T(128)} %bitcast.me_ref, bf16[408,128]{1,0:T(8,128)(2,1)S(1)} %get-tuple-element.79.refs_0_, bf16[408,128]{1,0:T(8,128)(2,1)S(1)} %collective-permute-done.11.refs_4_.refs_1_, bf16[408,128]{1,0:T(8,128)(2,1)S(1)} %collective-permute-done.12.refs_5_.refs_2_, ...), custom_call_target="tpu_custom_call" | custom-call | flops 1500000000 | bytes 1024 | tf_op jit(solution)/shard_map/pallas_call | solution.py:200
  93.0 4.7 %collective-permute-done.23.got_a = bf16[64,1024]{1,0:T(8,128)(2,1)S(1)} collective-permute-done((bf16[64,1024]{1,0:T(8,128)(2,1)S(1)}, bf16[64,1024]{1,0:T(8,128)(2,1)S(1)}, u32[]{:S(2)}, u32[]{:S(2)}) %collective-permute-start.23) | collective-permute-done | bytes 131104 | tf_op jit(solution)/shard_map/ppermute | solution.py:22
  97.6 14.1 %collective-permute-start.24 = (bf16[136,1024]{1,0:T(8,128)(2,1)S(1)}, bf16[136,1024]{1,0:T(8,128)(2,1)S(1)}, u32[]{:S(2)}, u32[]{:S(2)}) collective-permute-start(bf16[136,1024]{1,0:T(8,128)(2,1)S(1)} %shard_map.135), channel_id=1, source_target_pairs={{8,0},{16,8},{24,16},{9,1},{17,9},{25,17},{10,2},{18,10},{26,18},{... | collective-permute-start | bytes 835592 | tf_op jit(solution)/shard_map/ppermute | solution.py:28
  111.8 1.0 shard_map.137
  112.8 8.0 %collective-permute-done.25.got_b = bf16[64,1024]{1,0:T(8,128)(2,1)S(1)} collective-permute-done((bf16[64,1024]{1,0:T(8,128)(2,1)S(1)}, bf16[64,1024]{1,0:T(8,128)(2,1)S(1)}, u32[]{:S(2)}, u32[]{:S(2)}) %collective-permute-start.25) | collective-permute-done | bytes 131104 | tf_op jit(solution)/shard_map/ppermute | solution.py:22
  120.8 0.8 shard_map.138
  121.7 1.0 shard_map.136
  (45 shorter events, 2.5 us)
Async XLA Ops:
  0.6 10.5 %collective-permute-start.1 = (bf16[136,1024]{1,0:T(8,128)(2,1)}, bf16[136,1024]{1,0:T(8,128)(2,1)S(1)}, u32[]{:S(2)}, u32[]{:S(2)}) collective-permute-start(bf16[136,1024]{1,0:T(8,128)(2,1)} %bitcast.7), channel_id=1, source_target_pairs={{0,2},{1,3},{2,0},{3,1},{4,6},{5,7},{6,4},{7,5},{8,10},{9,11},{10,... | collective-permute-start | bytes 835592 | tf_op jit(solution)/shard_map/ppermute | solution.py:468
  2.0 24.3 %collective-permute-start = (bf16[136,1024]{1,0:T(8,128)(2,1)}, bf16[136,1024]{1,0:T(8,128)(2,1)S(1)}, u32[]{:S(2)}, u32[]{:S(2)}) collective-permute-start(bf16[136,1024]{1,0:T(8,128)(2,1)} %bitcast.8), channel_id=1, source_target_pairs={{0,1},{1,0},{2,3},{3,2},{4,5},{5,4},{6,7},{7,6},{8,9},{9,8},{10,11... | collective-permute-start | bytes 835592 | tf_op jit(solution)/shard_map/ppermute | solution.py:468
  4.2 10.4 %collective-permute-start.3 = (bf16[136,512]{1,0:T(8,128)(2,1)S(1)}, bf16[136,512]{1,0:T(8,128)(2,1)S(1)}, u32[]{:S(2)}, u32[]{:S(2)}) collective-permute-start(bf16[136,512]{1,0:T(8,128)(2,1)S(1)} %get-tuple-element.109), channel_id=1, source_target_pairs={{0,4},{1,5},{2,6},{3,7},{4,0},{5,1},{6,2},{7,3},{8,12},{9,13},{10,... | collective-permute-start | bytes 417800 | tf_op jit(solution)/shard_map/ppermute | solution.py:468
  6.6 12.5 %collective-permute-start.2 = (bf16[136,512]{1,0:T(8,128)(2,1)S(1)}, bf16[136,512]{1,0:T(8,128)(2,1)S(1)}, u32[]{:S(2)}, u32[]{:S(2)}) collective-permute-start(bf16[136,512]{1,0:T(8,128)(2,1)S(1)} %get-tuple-element.110), channel_id=1, source_target_pairs={{0,4},{1,5},{2,6},{3,7},{4,0},{5,1},{6,2},{7,3},{8,12},{9,13},{10,... | collective-permute-start | bytes 417800 | tf_op jit(solution)/shard_map/ppermute | solution.py:468
  11.2 15.1 %collective-permute-start.4 = (bf16[136,1024]{1,0:T(8,128)(2,1)S(1)}, bf16[136,1024]{1,0:T(8,128)(2,1)S(1)}, u32[]{:S(2)}, u32[]{:S(2)}) collective-permute-start(bf16[136,1024]{1,0:T(8,128)(2,1)S(1)} %collective-permute-done.1.refs_2_), channel_id=1, source_target_pairs={{0,1},{1,0},{2,3},{3,2},{4,5},{5,4},{6,7},{7,6},{8,9},{9,8},{10,11... | collective-permute-start | bytes 835592 | tf_op jit(solution)/shard_map/ppermute | solution.py:468
  14.6 8.9 %collective-permute-start.8 = (bf16[136,512]{1,0:T(8,128)(2,1)S(1)}, bf16[136,512]{1,0:T(8,128)(2,1)S(1)}, u32[]{:S(2)}, u32[]{:S(2)}) collective-permute-start(bf16[136,512]{1,0:T(8,128)(2,1)S(1)} %collective-permute-done.3.refs_4_), channel_id=1, source_target_pairs={{0,2},{1,3},{2,0},{3,1},{4,6},{5,7},{6,4},{7,5},{8,10},{9,11},{10,... | collective-permute-start | bytes 417800 | tf_op jit(solution)/shard_map/ppermute | solution.py:468
  14.7 8.9 %collective-permute-start.6 = (bf16[136,512]{1,0:T(8,128)(2,1)S(1)}, bf16[136,512]{1,0:T(8,128)(2,1)S(1)}, u32[]{:S(2)}, u32[]{:S(2)}) collective-permute-start(bf16[136,512]{1,0:T(8,128)(2,1)S(1)} %collective-permute-done.3.refs_4_), channel_id=1, source_target_pairs={{0,1},{1,0},{2,3},{3,2},{4,5},{5,4},{6,7},{7,6},{8,9},{9,8},{10,11... | collective-permute-start | bytes 417800 | tf_op jit(solution)/shard_map/ppermute | solution.py:468
  19.1 6.5 %collective-permute-start.5 = (bf16[136,512]{1,0:T(8,128)(2,1)S(1)}, bf16[136,512]{1,0:T(8,128)(2,1)S(1)}, u32[]{:S(2)}, u32[]{:S(2)}) collective-permute-start(bf16[136,512]{1,0:T(8,128)(2,1)S(1)} %collective-permute-done.2.refs_3_), channel_id=1, source_target_pairs={{0,1},{1,0},{2,3},{3,2},{4,5},{5,4},{6,7},{7,6},{8,9},{9,8},{10,11... | collective-permute-start | bytes 417800 | tf_op jit(solution)/shard_map/ppermute | solution.py:468
  19.3 1.2 copy-start.2
  20.6 1.2 copy-start.4
  21.8 1.2 copy-start.6
  23.0 3.3 %copy-start = (bf16[1,136,1024]{2,1,0:T(8,128)(2,1)S(1)}, bf16[1,136,1024]{2,1,0:T(8,128)(2,1)}, u32[]{:S(2)}) copy-start(bf16[1,136,1024]{2,1,0:T(8,128)(2,1)} %param.9) | copy-start | bytes 835588
  23.5 4.3 %collective-permute-start.7 = (bf16[136,512]{1,0:T(8,128)(2,1)S(1)}, bf16[136,512]{1,0:T(8,128)(2,1)S(1)}, u32[]{:S(2)}, u32[]{:S(2)}) collective-permute-start(bf16[136,512]{1,0:T(8,128)(2,1)S(1)} %collective-permute-done.2.refs_3_), channel_id=1, source_target_pairs={{0,2},{1,3},{2,0},{3,1},{4,6},{5,7},{6,4},{7,5},{8,10},{9,11},{10,... | collective-permute-start | bytes 417800 | tf_op jit(solution)/shard_map/ppermute | solution.py:468
  23.6 5.3 %collective-permute-start.10 = (bf16[136,512]{1,0:T(8,128)(2,1)S(1)}, bf16[136,512]{1,0:T(8,128)(2,1)S(1)}, u32[]{:S(2)}, u32[]{:S(2)}) collective-permute-start(bf16[136,512]{1,0:T(8,128)(2,1)S(1)} %collective-permute-done.8.refs_1_), channel_id=1, source_target_pairs={{0,1},{1,0},{2,3},{3,2},{4,5},{5,4},{6,7},{7,6},{8,9},{9,8},{10,11... | collective-permute-start | bytes 417800 | tf_op jit(solution)/shard_map/ppermute | solution.py:468
  25.6 5.6 %collective-permute-start.9 = (bf16[136,512]{1,0:T(8,128)(2,1)S(1)}, bf16[136,512]{1,0:T(8,128)(2,1)S(1)}, u32[]{:S(2)}, u32[]{:S(2)}) collective-permute-start(bf16[136,512]{1,0:T(8,128)(2,1)S(1)} %collective-permute-done.5.refs_6_), channel_id=1, source_target_pairs={{0,2},{1,3},{2,0},{3,1},{4,6},{5,7},{6,4},{7,5},{8,10},{9,11},{10,... | collective-permute-start | bytes 417800 | tf_op jit(solution)/shard_map/ppermute | solution.py:468
  31.2 14.4 %copy-start.1 = (bf16[1,512,2048]{2,1,0:T(8,128)(2,1)S(1)}, bf16[1,512,2048]{2,1,0:T(8,128)(2,1)}, u32[]{:S(2)}) copy-start(bf16[1,512,2048]{2,1,0:T(8,128)(2,1)} %param.14) | copy-start | bytes 6291460
  31.2 14.4 %copy-start.8 = (bf16[1,136,1024]{2,1,0:T(8,128)(2,1)S(1)}, bf16[1,136,1024]{2,1,0:T(8,128)(2,1)}, u32[]{:S(2)}) copy-start(bf16[1,136,1024]{2,1,0:T(8,128)(2,1)} %param.10) | copy-start | bytes 835588
  56.5 14.3 %collective-permute-start.18 = (bf16[136,1024]{1,0:T(8,128)(2,1)S(1)}, bf16[136,1024]{1,0:T(8,128)(2,1)S(1)}, u32[]{:S(2)}, u32[]{:S(2)}) collective-permute-start(bf16[136,1024]{1,0:T(8,128)(2,1)S(1)} %get-tuple-element.87), channel_id=1, source_target_pairs={{0,7},{1,6},{2,5},{3,4},{4,3},{5,2},{6,1},{7,0},{8,15},{9,14},{10,... | collective-permute-start | bytes 835592 | tf_op jit(solution)/shard_map/ppermute | solution.py:468
  57.4 13.4 %collective-permute-start.19 = (bf16[256,1024]{1,0:T(8,128)(2,1)S(1)}, bf16[256,1024]{1,0:T(8,128)(2,1)S(1)}, u32[]{:S(2)}, u32[]{:S(2)}) collective-permute-start(bf16[256,1024]{1,0:T(8,128)(2,1)S(1)} %get-tuple-element.92), channel_id=1, source_target_pairs={{0,1},{1,0},{2,3},{3,2},{4,5},{5,4},{6,7},{7,6},{8,9},{9,8},{10,11... | collective-permute-start | bytes 1572872 | tf_op jit(solution)/shard_map/ppermute | solution.py:22
  57.9 12.9 %collective-permute-start.20 = (bf16[256,1024]{1,0:T(8,128)(2,1)S(1)}, bf16[256,1024]{1,0:T(8,128)(2,1)S(1)}, u32[]{:S(2)}, u32[]{:S(2)}) collective-permute-start(bf16[256,1024]{1,0:T(8,128)(2,1)S(1)} %get-tuple-element.93), channel_id=1, source_target_pairs={{0,2},{2,0},{1,3},{3,1},{4,6},{6,4},{5,7},{7,5},{8,10},{10,8},{9,1... | collective-permute-start | bytes 1572872 | tf_op jit(solution)/shard_map/ppermute | solution.py:22
  63.0 7.0 %collective-permute-start.11 = (bf16[408,128]{1,0:T(8,128)(2,1)S(1)}, bf16[408,128]{1,0:T(8,128)(2,1)S(1)}, u32[]{:S(2)}, u32[]{:S(2)}) collective-permute-start(bf16[408,128]{1,0:T(8,128)(2,1)S(1)} %get-tuple-element.80), channel_id=1, source_target_pairs={{0,1},{1,0},{2,3},{3,2},{4,5},{5,4},{6,7},{7,6},{8,9},{9,8},{10,11... | collective-permute-start | bytes 313352 | tf_op jit(solution)/shard_map/ppermute | solution.py:468
  63.9 6.9 %collective-permute-start.12 = (bf16[408,128]{1,0:T(8,128)(2,1)S(1)}, bf16[408,128]{1,0:T(8,128)(2,1)S(1)}, u32[]{:S(2)}, u32[]{:S(2)}) collective-permute-start(bf16[408,128]{1,0:T(8,128)(2,1)S(1)} %get-tuple-element.81), channel_id=1, source_target_pairs={{0,2},{1,3},{2,0},{3,1},{4,6},{5,7},{6,4},{7,5},{8,10},{9,11},{10,... | collective-permute-start | bytes 313352 | tf_op jit(solution)/shard_map/ppermute | solution.py:468
  70.9 13.6 %collective-permute-start.21 = (bf16[128,1024]{1,0:T(8,128)(2,1)S(1)}, bf16[128,1024]{1,0:T(8,128)(2,1)S(1)}, u32[]{:S(2)}, u32[]{:S(2)}) collective-permute-start(bf16[128,1024]{1,0:T(8,128)(2,1)S(1)} %get-tuple-element.96), channel_id=1, source_target_pairs={{0,2},{2,0},{1,3},{3,1},{4,6},{6,4},{5,7},{7,5},{8,10},{10,8},{9,1... | collective-permute-start | bytes 786440 | tf_op jit(solution)/shard_map/ppermute | solution.py:22
  75.3 11.1 %collective-permute-start.22 = (bf16[128,1024]{1,0:T(8,128)(2,1)S(1)}, bf16[128,1024]{1,0:T(8,128)(2,1)S(1)}, u32[]{:S(2)}, u32[]{:S(2)}) collective-permute-start(bf16[128,1024]{1,0:T(8,128)(2,1)S(1)} %get-tuple-element.97), channel_id=1, source_target_pairs={{0,1},{1,0},{2,3},{3,2},{4,5},{5,4},{6,7},{7,6},{8,9},{9,8},{10,11... | collective-permute-start | bytes 786440 | tf_op jit(solution)/shard_map/ppermute | solution.py:22
  75.8 6.1 %collective-permute-start.15 = (bf16[408,128]{1,0:T(8,128)(2,1)S(1)}, bf16[408,128]{1,0:T(8,128)(2,1)S(1)}, u32[]{:S(2)}, u32[]{:S(2)}) collective-permute-start(bf16[408,128]{1,0:T(8,128)(2,1)S(1)} %get-tuple-element.84), channel_id=1, source_target_pairs={{0,5},{1,4},{2,7},{3,6},{4,1},{5,0},{6,3},{7,2},{8,13},{9,12},{10,... | collective-permute-start | bytes 313352 | tf_op jit(solution)/shard_map/ppermute | solution.py:468
  76.0 11.5 %collective-permute-start.13 = (bf16[408,128]{1,0:T(8,128)(2,1)S(1)}, bf16[408,128]{1,0:T(8,128)(2,1)S(1)}, u32[]{:S(2)}, u32[]{:S(2)}) collective-permute-start(bf16[408,128]{1,0:T(8,128)(2,1)S(1)} %get-tuple-element.82), channel_id=1, source_target_pairs={{0,4},{1,5},{2,6},{3,7},{4,0},{5,1},{6,2},{7,3},{8,12},{9,13},{10,... | collective-permute-start | bytes 313352 | tf_op jit(solution)/shard_map/ppermute | solution.py:468
  78.9 8.6 %collective-permute-start.14 = (bf16[408,128]{1,0:T(8,128)(2,1)S(1)}, bf16[408,128]{1,0:T(8,128)(2,1)S(1)}, u32[]{:S(2)}, u32[]{:S(2)}) collective-permute-start(bf16[408,128]{1,0:T(8,128)(2,1)S(1)} %get-tuple-element.83), channel_id=1, source_target_pairs={{0,3},{1,2},{2,1},{3,0},{4,7},{5,6},{6,5},{7,4},{8,11},{9,10},{10,... | collective-permute-start | bytes 313352 | tf_op jit(solution)/shard_map/ppermute | solution.py:468
  82.0 5.9 %collective-permute-start.16 = (bf16[408,128]{1,0:T(8,128)(2,1)S(1)}, bf16[408,128]{1,0:T(8,128)(2,1)S(1)}, u32[]{:S(2)}, u32[]{:S(2)}) collective-permute-start(bf16[408,128]{1,0:T(8,128)(2,1)S(1)} %get-tuple-element.85), channel_id=1, source_target_pairs={{0,6},{1,7},{2,4},{3,5},{4,2},{5,3},{6,0},{7,1},{8,14},{9,15},{10,... | collective-permute-start | bytes 313352 | tf_op jit(solution)/shard_map/ppermute | solution.py:468
  84.5 7.1 %copy-start.3 = (bf16[1,1024,512]{2,1,0:T(8,128)(2,1)S(1)}, bf16[1,1024,512]{2,1,0:T(8,128)(2,1)}, u32[]{:S(2)}) copy-start(bf16[1,1024,512]{2,1,0:T(8,128)(2,1)} %param.11) | copy-start | bytes 3145732
  84.5 7.1 %copy-start.5 = (bf16[1,1024,512]{2,1,0:T(8,128)(2,1)S(1)}, bf16[1,1024,512]{2,1,0:T(8,128)(2,1)}, u32[]{:S(2)}) copy-start(bf16[1,1024,512]{2,1,0:T(8,128)(2,1)} %param.12) | copy-start | bytes 3145732
  84.5 7.1 %copy-start.7 = (bf16[1,1024,512]{2,1,0:T(8,128)(2,1)S(1)}, bf16[1,1024,512]{2,1,0:T(8,128)(2,1)}, u32[]{:S(2)}) copy-start(bf16[1,1024,512]{2,1,0:T(8,128)(2,1)} %param.13) | copy-start | bytes 3145732
  84.5 7.1 %collective-permute-start.17 = (bf16[408,128]{1,0:T(8,128)(2,1)S(1)}, bf16[408,128]{1,0:T(8,128)(2,1)S(1)}, u32[]{:S(2)}, u32[]{:S(2)}) collective-permute-start(bf16[408,128]{1,0:T(8,128)(2,1)S(1)} %get-tuple-element.86), channel_id=1, source_target_pairs={{0,7},{1,6},{2,5},{3,4},{4,3},{5,2},{6,1},{7,0},{8,15},{9,14},{10,... | collective-permute-start | bytes 313352 | tf_op jit(solution)/shard_map/ppermute | solution.py:468
  86.6 11.0 %collective-permute-start.23 = (bf16[64,1024]{1,0:T(8,128)(2,1)S(1)}, bf16[64,1024]{1,0:T(8,128)(2,1)S(1)}, u32[]{:S(2)}, u32[]{:S(2)}) collective-permute-start(bf16[64,1024]{1,0:T(8,128)(2,1)S(1)} %get-tuple-element.98.refs_14_), channel_id=1, source_target_pairs={{0,4},{4,0},{1,5},{5,1},{2,6},{6,2},{3,7},{7,3},{8,12},{12,8},{9,1... | collective-permute-start | bytes 393224 | tf_op jit(solution)/shard_map/ppermute | solution.py:22
  97.6 24.0 %collective-permute-start.24 = (bf16[136,1024]{1,0:T(8,128)(2,1)S(1)}, bf16[136,1024]{1,0:T(8,128)(2,1)S(1)}, u32[]{:S(2)}, u32[]{:S(2)}) collective-permute-start(bf16[136,1024]{1,0:T(8,128)(2,1)S(1)} %shard_map.135), channel_id=1, source_target_pairs={{8,0},{16,8},{24,16},{9,1},{17,9},{25,17},{10,2},{18,10},{26,18},{... | collective-permute-start | bytes 835592 | tf_op jit(solution)/shard_map/ppermute | solution.py:28
  111.8 9.1 %collective-permute-start.25 = (bf16[64,1024]{1,0:T(8,128)(2,1)S(1)}, bf16[64,1024]{1,0:T(8,128)(2,1)S(1)}, u32[]{:S(2)}, u32[]{:S(2)}) collective-permute-start(bf16[64,1024]{1,0:T(8,128)(2,1)S(1)} %get-tuple-element.106), channel_id=1, source_target_pairs={{0,4},{4,0},{1,5},{5,1},{2,6},{6,2},{3,7},{7,3},{8,12},{12,8},{9,1... | collective-permute-start | bytes 393224 | tf_op jit(solution)/shard_map/ppermute | solution.py:22
  112.8 8.8 %copy-start.9 = (s32[1,136]{1,0:T(1,128)S(1)}, s32[1,136]{1,0:T(1,128)}, u32[]{:S(2)}) copy-start(s32[1,136]{1,0:T(1,128)} %order_ref.1) | copy-start | bytes 1636

commit v11 on v10

--- a/solution.py
+++ b/solution.py
@@ -403,7 +403,7 @@
 
 
 def turn_kernel(me_ref, *refs):
-    slabs, out_refs, held_ref = refs[:HEADS], refs[HEADS:-1], refs[-1]
+    slabs, out_refs, held_ref = refs[:HEADS], refs[HEADS + 2 : -1], refs[-1]
     start = slabs[0].shape[0] - 3 * HEAD_DIM
     for m, slab in enumerate(slabs):
         held_ref[me_ref[0] ^ DISTANCES[m]] = slab[start:, :]
@@ -476,17 +476,18 @@
     return lax.all_to_all(slabs, "seq", split_axis=0, concat_axis=0, tiled=True)
 
 
-def spread(block):
+def spread(block, weight):
     middle = block.shape[1] // 2
     pieces = [block[:, :middle], block[:, middle:]]
     far = [hop(piece, 4) for piece in pieces]
     near, side = hop(block, 2), hop(block, 1)
+    near, weight = lax.optimization_barrier((near, weight))
     side_far = [hop(piece, 1) for piece in far]
     near_far = [hop(piece, 2) for piece in far]
     side_near = hop(near, 1)
     last = [hop(side_far[0], 2), hop(near_far[1], 1)]
     early = [block, side, near, *far, side_near, *side_far]
-    return early, near_far, last
+    return early, near_far, last, weight
 
 
 DISTANCES = (0, 1, 2, 4, 3, 5, 6, 7)
@@ -518,7 +519,6 @@
     def out(*dims, dtype=jnp.bfloat16):
         return jax.ShapeDtypeStruct(dims, dtype)
 
-    first_blocks, near_far, mirrored = spread(field)
     order = me[0] ^ jnp.array(DISTANCES, jnp.int32)
     ids = jnp.take(block_ids.reshape(parts, rows), order, axis=0).reshape(tokens)
     (weight,) = call(
@@ -528,6 +528,7 @@
         [out(width, 3 * HEAD_DIM)],
         [pltpu.VMEM((width, 2 * HEAD_DIM), jnp.bfloat16)] * 3 + [pltpu.SemaphoreType.DMA((3,))],
     )
+    first_blocks, near_far, mirrored, weight = spread(field, weight)
     pair = 2 * HEAD_DIM
     normed, unit, unit_scale, projected = call(
         project_kernel,
@@ -607,18 +608,17 @@
         [out(rows, width)],
         [pltpu.VMEM((HEADS, PACKED + rows, 128), jnp.bfloat16)],
     )
-    grad_input, rest[0] = lax.optimization_barrier((grad_input, rest[0]))
     moved = to_previous(grad_input)
     (grad_out,) = call(
         last_sum_kernel,
-        1,
+        2,
         [("v", x) for x in (keep_a, keep_b, *rest)],
         [out(1, keep_a.shape[0], 2 * width, dtype=f32)],
     )
     grad_q, grad_k, grad_v = call(
         turn_kernel,
-        1,
-        [("s", me)] + [("v", x) for x in slabs],
+        3,
+        [("s", me)] + [("v", x) for x in slabs] + [("a", x) for x in rest],
         [out(1, width // parts, inner, dtype=f32)] * 3,
         [pltpu.VMEM((HEADS, 3 * HEAD_DIM, 128), jnp.bfloat16)],
     )

time: 124 us -> 119 us (0.960)
  the two profiles are of different devices: /device:TPU:5 before, /device:TPU:1 now
where the time goes in v11:
time: 119 us
  starting transfers between devices  46.3 us (39%)
  waiting for transfers between devices  29.2 us (25%)
  blocking collectives  19.3 us (16%)
  Pallas kernels  16.7 us (14%)
  local copies, waits for them, and re-layouts  5.64 us (5%)
    ppermute x19, waiting for transfers between devices, hop(): return lax.ppermute(block, 'seq', route)  23.8 us
    ppermute x19, starting transfers between devices, hop(): return lax.ppermute(block, 'seq', route)  21.3 us
    ppermute x1, starting transfers between devices, shifted(): return lax.ppermute(block, axis, route)  20.8 us
    all_to_all x2, blocking collectives, switch(): return lax.all_to_all(slabs, 'seq', split_axis=0, concat_axis=0, tiled=True)  19.3 us
    pallas_call x11, Pallas kernels, call(): pl.pallas_call(kernel, out_shape=tuple(outs), in_specs=[pl.BlockSpec(memo...  16.7 us
    ppermute x6, starting transfers between devices, partner(): return lax.ppermute(block, axis, route)  4.12 us
    unnamed x22, local copies, waits for them, and re-layouts  3.7 us
    ppermute x1, waiting for transfers between devices, shifted(): return lax.ppermute(block, axis, route)  3.46 us
  transfers between devices with their start and end apart: 26, of which 13 were waited for; matrix products, arithmetic and copies ran while one was open for 2% of the time, Pallas kernels for 8%

profile of v11, /device:TPU:1, one launch (start us, length us, event | category | flops | bytes accessed | tf_op | source)
XLA Modules:
  0.0 118.7 jit_solution(3399415667772544398)
XLA Ops:
  0.6 2.2 %collective-permute-start.1 = (bf16[136,1024]{1,0:T(8,128)(2,1)}, bf16[136,1024]{1,0:T(8,128)(2,1)S(1)}, u32[]{:S(2)}, u32[]{:S(2)}) collective-permute-start(bf16[136,1024]{1,0:T(8,128)(2,1)} %bitcast.7), channel_id=1, source_target_pairs={{0,2},{1,3},{2,0},{3,1},{4,6},{5,7},{6,4},{7,5},{8,10},{9,11},{10,... | collective-permute-start | bytes 835592 | tf_op jit(solution)/shard_map/ppermute | solution.py:468
  2.8 1.2 %collective-permute-start = (bf16[136,1024]{1,0:T(8,128)(2,1)}, bf16[136,1024]{1,0:T(8,128)(2,1)S(1)}, u32[]{:S(2)}, u32[]{:S(2)}) collective-permute-start(bf16[136,1024]{1,0:T(8,128)(2,1)} %bitcast.8), channel_id=1, source_target_pairs={{0,1},{1,0},{2,3},{3,2},{4,5},{5,4},{6,7},{7,6},{8,9},{9,8},{10,11... | collective-permute-start | bytes 835592 | tf_op jit(solution)/shard_map/ppermute | solution.py:468
  4.0 1.0 fusion
  5.0 2.4 %collective-permute-start.3 = (bf16[136,512]{1,0:T(8,128)(2,1)S(1)}, bf16[136,512]{1,0:T(8,128)(2,1)S(1)}, u32[]{:S(2)}, u32[]{:S(2)}) collective-permute-start(bf16[136,512]{1,0:T(8,128)(2,1)S(1)} %get-tuple-element.109), channel_id=1, source_target_pairs={{0,4},{1,5},{2,6},{3,7},{4,0},{5,1},{6,2},{7,3},{8,12},{9,13},{10,... | collective-permute-start | bytes 417800 | tf_op jit(solution)/shard_map/ppermute | solution.py:468
  7.5 0.7 compare_and_fusion
  8.2 1.2 %copy-done.2 = bf16[1,1024,512]{2,1,0:T(8,128)(2,1)S(1)} copy-done((bf16[1,1024,512]{2,1,0:T(8,128)(2,1)S(1)}, bf16[1,1024,512]{2,1,0:T(8,128)(2,1)}, u32[]{:S(2)}) %copy-start.2) | copy-done | bytes 1048600
  9.4 1.2 %copy-done.4 = bf16[1,1024,512]{2,1,0:T(8,128)(2,1)S(1)} copy-done((bf16[1,1024,512]{2,1,0:T(8,128)(2,1)S(1)}, bf16[1,1024,512]{2,1,0:T(8,128)(2,1)}, u32[]{:S(2)}) %copy-start.4) | copy-done | bytes 1048600
  10.6 1.2 %copy-done.6 = bf16[1,1024,512]{2,1,0:T(8,128)(2,1)S(1)} copy-done((bf16[1,1024,512]{2,1,0:T(8,128)(2,1)S(1)}, bf16[1,1024,512]{2,1,0:T(8,128)(2,1)}, u32[]{:S(2)}) %copy-start.6) | copy-done | bytes 1048600
  11.8 0.5 shard_map.128.refs_8_.weight_ref
  12.3 2.7 %collective-permute-start.4 = (bf16[136,1024]{1,0:T(8,128)(2,1)S(1)}, bf16[136,1024]{1,0:T(8,128)(2,1)S(1)}, u32[]{:S(2)}, u32[]{:S(2)}) collective-permute-start(bf16[136,1024]{1,0:T(8,128)(2,1)S(1)} %collective-permute-done.1.refs_2_), channel_id=1, source_target_pairs={{0,1},{1,0},{2,3},{3,2},{4,5},{5,4},{6,7},{7,6},{8,9},{9,8},{10,11... | collective-permute-start | bytes 835592 | tf_op jit(solution)/shard_map/ppermute | solution.py:468
  15.2 0.6 gather_fusion
  15.9 4.1 %collective-permute-done.2.refs_3_ = bf16[136,512]{1,0:T(8,128)(2,1)S(1)} collective-permute-done((bf16[136,512]{1,0:T(8,128)(2,1)S(1)}, bf16[136,512]{1,0:T(8,128)(2,1)S(1)}, u32[]{:S(2)}, u32[]{:S(2)}) %collective-permute-start.2) | collective-permute-done | bytes 139296 | tf_op jit(solution)/shard_map/ppermute | solution.py:468
  20.5 1.8 %collective-permute-done.8.refs_1_ = bf16[136,512]{1,0:T(8,128)(2,1)S(1)} collective-permute-done((bf16[136,512]{1,0:T(8,128)(2,1)S(1)}, bf16[136,512]{1,0:T(8,128)(2,1)S(1)}, u32[]{:S(2)}, u32[]{:S(2)}) %collective-permute-start.8) | collective-permute-done | bytes 139296 | tf_op jit(solution)/shard_map/ppermute | solution.py:468
  22.3 1.1 collective-permute-done.6.refs_7_
  23.5 1.2 collective-permute-start.10
  24.6 1.8 %collective-permute-done.5.refs_6_ = bf16[136,512]{1,0:T(8,128)(2,1)S(1)} collective-permute-done((bf16[136,512]{1,0:T(8,128)(2,1)S(1)}, bf16[136,512]{1,0:T(8,128)(2,1)S(1)}, u32[]{:S(2)}, u32[]{:S(2)}) %collective-permute-start.5) | collective-permute-done | bytes 139296 | tf_op jit(solution)/shard_map/ppermute | solution.py:468
  26.5 1.0 shard_map.129
  27.5 2.0 %collective-permute-done.10.refs_3_.refs_12_ = bf16[136,512]{1,0:T(8,128)(2,1)S(1)} collective-permute-done((bf16[136,512]{1,0:T(8,128)(2,1)S(1)}, bf16[136,512]{1,0:T(8,128)(2,1)S(1)}, u32[]{:S(2)}, u32[]{:S(2)}) %collective-permute-start.10) | collective-permute-done | bytes 139296 | tf_op jit(solution)/shard_map/ppermute | solution.py:468
  29.4 1.2 %collective-permute-done.9.refs_2_.refs_11_ = bf16[136,512]{1,0:T(8,128)(2,1)S(1)} collective-permute-done((bf16[136,512]{1,0:T(8,128)(2,1)S(1)}, bf16[136,512]{1,0:T(8,128)(2,1)S(1)}, u32[]{:S(2)}, u32[]{:S(2)}) %collective-permute-start.9) | collective-permute-done | bytes 139296 | tf_op jit(solution)/shard_map/ppermute | solution.py:468
  30.7 3.7 %shard_map.130 = (bf16[2,136,1024]{2,1,0:T(8,128)(2,1)S(1)}, f32[2,136,128]{2,1,0:T(8,128)S(1)}, f32[2,136,128]{2,1,0:T(8,128)S(1)}, bf16[1088,1088]{1,0:T(8,128...) custom-call(s32[1]{0:T(128)} %bitcast.me_ref, ...), custom_call_target="tpu_custom_call" | custom-call | flops 5000000000 | bytes 1024 | tf_op jit(solution)/shard_map/pallas_call | solution.py:200
  34.4 10.4 %all_to_all.10.slab_ref = bf16[8,80,128]{2,1,0:T(8,128)(2,1)S(1)} all-to-all(bf16[8,80,128]{2,1,0:T(8,128)(2,1)S(1)} %get-tuple-element.60), channel_id=1, replica_groups=mesh['section'=4,'seq'=8] {'seq'}, dimensions={0} | all-to-all | bytes 327680 | tf_op jit(solution)/shard_map/all_to_all | solution.py:476
  44.9 2.0 %shard_map.131 = (bf16[136,1024]{1,0:T(8,128)(2,1)S(1)}, bf16[8,80,128]{2,1,0:T(8,128)(2,1)S(1)}, bf16[256,1024]{1,0:T(8,128)(2,1)S(1)}, bf16[128,1024]{1,0:T(8,...) custom-call(s32[1]{0:T(128)} %bitcast.me_ref, ...), custom_call_target="tpu_custom_call" | custom-call | flops 3000000000 | bytes 1024 | tf_op jit(solution)/shard_map/pallas_call | solution.py:200
  46.8 8.8 %all_to_all.11.slab_ref = bf16[8,80,128]{2,1,0:T(8,128)(2,1)S(1)} all-to-all(bf16[8,80,128]{2,1,0:T(8,128)(2,1)S(1)} %get-tuple-element.61), channel_id=1, replica_groups=mesh['section'=4,'seq'=8] {'seq'}, dimensions={0} | all-to-all | bytes 327680 | tf_op jit(solution)/shard_map/all_to_all | solution.py:476
  55.6 0.9 collective-permute-start.18
  56.6 0.5 collective-permute-start.19
  57.2 5.0 %shard_map.132 = (bf16[408,128]{1,0:T(8,128)(2,1)S(1)}, bf16[408,128]{1,0:T(8,128)(2,1)S(1)}, bf16[408,128]{1,0:T(8,128)(2,1)S(1)}, bf16[408,128]{1,0:T(8,128)(2...) custom-call(s32[1]{0:T(128)} %bitcast.me_ref, ...), custom_call_target="tpu_custom_call" | custom-call | flops 6000000000 | bytes 1024 | tf_op jit(solution)/shard_map/pallas_call | solution.py:200
  62.2 0.9 collective-permute-start.11
  63.1 1.5 %collective-permute-start.12 = (bf16[408,128]{1,0:T(8,128)(2,1)S(1)}, bf16[408,128]{1,0:T(8,128)(2,1)S(1)}, u32[]{:S(2)}, u32[]{:S(2)}) collective-permute-start(bf16[408,128]{1,0:T(8,128)(2,1)S(1)} %get-tuple-element.83), channel_id=1, source_target_pairs={{0,2},{1,3},{2,0},{3,1},{4,6},{5,7},{6,4},{7,5},{8,10},{9,11},{10,... | collective-permute-start | bytes 313352 | tf_op jit(solution)/shard_map/ppermute | solution.py:468
  64.6 4.9 %collective-permute-done.11.refs_4_.refs_1_ = bf16[408,128]{1,0:T(8,128)(2,1)S(1)} collective-permute-done((bf16[408,128]{1,0:T(8,128)(2,1)S(1)}, bf16[408,128]{1,0:T(8,128)(2,1)S(1)}, u32[]{:S(2)}, u32[]{:S(2)}) %collective-permute-start.11) | collective-permute-done | bytes 104480 | tf_op jit(solution)/shard_map/ppermute | solution.py:468
  69.4 0.7 collective-permute-done.12.refs_5_.refs_2_
  70.3 1.0 collective-permute-start.22
  71.3 2.1 %collective-permute-start.15 = (bf16[408,128]{1,0:T(8,128)(2,1)S(1)}, bf16[408,128]{1,0:T(8,128)(2,1)S(1)}, u32[]{:S(2)}, u32[]{:S(2)}) collective-permute-start(bf16[408,128]{1,0:T(8,128)(2,1)S(1)} %get-tuple-element.86), channel_id=1, source_target_pairs={{0,5},{1,4},{2,7},{3,6},{4,1},{5,0},{6,3},{7,2},{8,13},{9,12},{10,... | collective-permute-start | bytes 313352 | tf_op jit(solution)/shard_map/ppermute | solution.py:468
  73.5 0.5 collective-permute-start.13
  74.0 2.0 %collective-permute-start.14 = (bf16[408,128]{1,0:T(8,128)(2,1)S(1)}, bf16[408,128]{1,0:T(8,128)(2,1)S(1)}, u32[]{:S(2)}, u32[]{:S(2)}) collective-permute-start(bf16[408,128]{1,0:T(8,128)(2,1)S(1)} %get-tuple-element.85), channel_id=1, source_target_pairs={{0,3},{1,2},{2,1},{3,0},{4,7},{5,6},{6,5},{7,4},{8,11},{9,10},{10,... | collective-permute-start | bytes 313352 | tf_op jit(solution)/shard_map/ppermute | solution.py:468
  76.0 2.8 %collective-permute-done.15.refs_8_.refs_5_ = bf16[408,128]{1,0:T(8,128)(2,1)S(1)} collective-permute-done((bf16[408,128]{1,0:T(8,128)(2,1)S(1)}, bf16[408,128]{1,0:T(8,128)(2,1)S(1)}, u32[]{:S(2)}, u32[]{:S(2)}) %collective-permute-start.15) | collective-permute-done | bytes 104480 | tf_op jit(solution)/shard_map/ppermute | solution.py:468
  78.8 2.1 %collective-permute-start.16 = (bf16[408,128]{1,0:T(8,128)(2,1)S(1)}, bf16[408,128]{1,0:T(8,128)(2,1)S(1)}, u32[]{:S(2)}, u32[]{:S(2)}) collective-permute-start(bf16[408,128]{1,0:T(8,128)(2,1)S(1)} %get-tuple-element.87), channel_id=1, source_target_pairs={{0,6},{1,7},{2,4},{3,5},{4,2},{5,3},{6,0},{7,1},{8,14},{9,15},{10,... | collective-permute-start | bytes 313352 | tf_op jit(solution)/shard_map/ppermute | solution.py:468
  80.9 1.9 %collective-permute-done.21.refs_6_ = bf16[128,1024]{1,0:T(8,128)(2,1)S(1)} collective-permute-done((bf16[128,1024]{1,0:T(8,128)(2,1)S(1)}, bf16[128,1024]{1,0:T(8,128)(2,1)S(1)}, u32[]{:S(2)}, u32[]{:S(2)}) %collective-permute-start.21) | collective-permute-done | bytes 262176 | tf_op jit(solution)/shard_map/ppermute | solution.py:22
  82.9 1.1 collective-permute-start.17
  84.1 0.7 collective-permute-start.25
  84.8 1.7 %collective-permute-start.24 = (bf16[64,1024]{1,0:T(8,128)(2,1)S(1)}, bf16[64,1024]{1,0:T(8,128)(2,1)S(1)}, u32[]{:S(2)}, u32[]{:S(2)}) collective-permute-start(bf16[64,1024]{1,0:T(8,128)(2,1)S(1)} %get-tuple-element.100.refs_14_), channel_id=1, source_target_pairs={{0,4},{4,0},{1,5},{5,1},{2,6},{6,2},{3,7},{7,3},{8,12},{12,8},{9,1... | collective-permute-start | bytes 393224 | tf_op jit(solution)/shard_map/ppermute | solution.py:22
  86.6 1.5 %collective-permute-done.16.refs_6_ = bf16[408,128]{1,0:T(8,128)(2,1)S(1)} collective-permute-done((bf16[408,128]{1,0:T(8,128)(2,1)S(1)}, bf16[408,128]{1,0:T(8,128)(2,1)S(1)}, u32[]{:S(2)}, u32[]{:S(2)}) %collective-permute-start.16) | collective-permute-done | bytes 104480 | tf_op jit(solution)/shard_map/ppermute | solution.py:468
  88.1 2.1 %collective-permute-done.17.refs_7_ = bf16[408,128]{1,0:T(8,128)(2,1)S(1)} collective-permute-done((bf16[408,128]{1,0:T(8,128)(2,1)S(1)}, bf16[408,128]{1,0:T(8,128)(2,1)S(1)}, u32[]{:S(2)}, u32[]{:S(2)}) %collective-permute-start.17) | collective-permute-done | bytes 104480 | tf_op jit(solution)/shard_map/ppermute | solution.py:468
  90.1 1.4 %shard_map.135 = bf16[136,1024]{1,0:T(8,128)(2,1)S(1)} custom-call(s32[1]{0:T(128)} %bitcast.me_ref, bf16[408,128]{1,0:T(8,128)(2,1)S(1)} %get-tuple-element.81.refs_0_, bf16[408,128]{1,0:T(8,128)(2,1)S(1)} %collective-permute-done.11.refs_4_.refs_1_, bf16[408,128]{1,0:T(8,128)(2,1)S(1)} %collective-permute-done.12.refs_5_.refs_2_, ...), custom_call_target="tpu_custom_call" | custom-call | flops 1500000000 | bytes 1024 | tf_op jit(solution)/shard_map/pallas_call | solution.py:200
  91.5 20.8 %collective-permute-start.23 = (bf16[136,1024]{1,0:T(8,128)(2,1)S(1)}, bf16[136,1024]{1,0:T(8,128)(2,1)S(1)}, u32[]{:S(2)}, u32[]{:S(2)}) collective-permute-start(bf16[136,1024]{1,0:T(8,128)(2,1)S(1)} %shard_map.135), channel_id=1, source_target_pairs={{8,0},{16,8},{24,16},{9,1},{17,9},{25,17},{10,2},{18,10},{26,18},{... | collective-permute-start | bytes 835592 | tf_op jit(solution)/shard_map/ppermute | solution.py:28
  112.4 0.8 shard_map.138
  113.2 1.0 shard_map.137
  114.3 3.5 %collective-permute-done.23.rows_ref = bf16[136,1024]{1,0:T(8,128)(2,1)S(1)} collective-permute-done((bf16[136,1024]{1,0:T(8,128)(2,1)S(1)}, bf16[136,1024]{1,0:T(8,128)(2,1)S(1)}, u32[]{:S(2)}, u32[]{:S(2)}) %collective-permute-start.23) | collective-permute-done | bytes 278560 | tf_op jit(solution)/shard_map/ppermute | solution.py:28
  117.7 1.0 shard_map.136
  (47 shorter events, 1.4 us)
Async XLA Ops:
  0.6 11.7 %collective-permute-start.1 = (bf16[136,1024]{1,0:T(8,128)(2,1)}, bf16[136,1024]{1,0:T(8,128)(2,1)S(1)}, u32[]{:S(2)}, u32[]{:S(2)}) collective-permute-start(bf16[136,1024]{1,0:T(8,128)(2,1)} %bitcast.7), channel_id=1, source_target_pairs={{0,2},{1,3},{2,0},{3,1},{4,6},{5,7},{6,4},{7,5},{8,10},{9,11},{10,... | collective-permute-start | bytes 835592 | tf_op jit(solution)/shard_map/ppermute | solution.py:468
  2.8 23.6 %collective-permute-start = (bf16[136,1024]{1,0:T(8,128)(2,1)}, bf16[136,1024]{1,0:T(8,128)(2,1)S(1)}, u32[]{:S(2)}, u32[]{:S(2)}) collective-permute-start(bf16[136,1024]{1,0:T(8,128)(2,1)} %bitcast.8), channel_id=1, source_target_pairs={{0,1},{1,0},{2,3},{3,2},{4,5},{5,4},{6,7},{7,6},{8,9},{9,8},{10,11... | collective-permute-start | bytes 835592 | tf_op jit(solution)/shard_map/ppermute | solution.py:468
  5.0 10.7 %collective-permute-start.3 = (bf16[136,512]{1,0:T(8,128)(2,1)S(1)}, bf16[136,512]{1,0:T(8,128)(2,1)S(1)}, u32[]{:S(2)}, u32[]{:S(2)}) collective-permute-start(bf16[136,512]{1,0:T(8,128)(2,1)S(1)} %get-tuple-element.109), channel_id=1, source_target_pairs={{0,4},{1,5},{2,6},{3,7},{4,0},{5,1},{6,2},{7,3},{8,12},{9,13},{10,... | collective-permute-start | bytes 417800 | tf_op jit(solution)/shard_map/ppermute | solution.py:468
  7.4 12.5 %collective-permute-start.2 = (bf16[136,512]{1,0:T(8,128)(2,1)S(1)}, bf16[136,512]{1,0:T(8,128)(2,1)S(1)}, u32[]{:S(2)}, u32[]{:S(2)}) collective-permute-start(bf16[136,512]{1,0:T(8,128)(2,1)S(1)} %get-tuple-element.110), channel_id=1, source_target_pairs={{0,4},{1,5},{2,6},{3,7},{4,0},{5,1},{6,2},{7,3},{8,12},{9,13},{10,... | collective-permute-start | bytes 417800 | tf_op jit(solution)/shard_map/ppermute | solution.py:468
  8.2 1.2 %copy-start.2 = (bf16[1,1024,512]{2,1,0:T(8,128)(2,1)S(1)}, bf16[1,1024,512]{2,1,0:T(8,128)(2,1)}, u32[]{:S(2)}) copy-start(bf16[1,1024,512]{2,1,0:T(8,128)(2,1)} %param.11) | copy-start | bytes 3145732
  9.4 1.2 %copy-start.4 = (bf16[1,1024,512]{2,1,0:T(8,128)(2,1)S(1)}, bf16[1,1024,512]{2,1,0:T(8,128)(2,1)}, u32[]{:S(2)}) copy-start(bf16[1,1024,512]{2,1,0:T(8,128)(2,1)} %param.12) | copy-start | bytes 3145732
  10.6 1.2 %copy-start.6 = (bf16[1,1024,512]{2,1,0:T(8,128)(2,1)S(1)}, bf16[1,1024,512]{2,1,0:T(8,128)(2,1)}, u32[]{:S(2)}) copy-start(bf16[1,1024,512]{2,1,0:T(8,128)(2,1)} %param.13) | copy-start | bytes 3145732
  11.8 3.2 %copy-start.10 = (s32[1088]{0:T(1024)S(1)}, s32[1088]{0:T(1024)}, u32[]{:S(2)}) copy-start(s32[1088]{0:T(1024)} %param.15) | copy-start | bytes 13060
  11.8 14.6 %copy-start = (bf16[1,136,1024]{2,1,0:T(8,128)(2,1)S(1)}, bf16[1,136,1024]{2,1,0:T(8,128)(2,1)}, u32[]{:S(2)}) copy-start(bf16[1,136,1024]{2,1,0:T(8,128)(2,1)} %param.9) | copy-start | bytes 835588
  12.3 14.1 %collective-permute-start.4 = (bf16[136,1024]{1,0:T(8,128)(2,1)S(1)}, bf16[136,1024]{1,0:T(8,128)(2,1)S(1)}, u32[]{:S(2)}, u32[]{:S(2)}) collective-permute-start(bf16[136,1024]{1,0:T(8,128)(2,1)S(1)} %collective-permute-done.1.refs_2_), channel_id=1, source_target_pairs={{0,1},{1,0},{2,3},{3,2},{4,5},{5,4},{6,7},{7,6},{8,9},{9,8},{10,11... | collective-permute-start | bytes 835592 | tf_op jit(solution)/shard_map/ppermute | solution.py:468
  15.7 6.6 %collective-permute-start.8 = (bf16[136,512]{1,0:T(8,128)(2,1)S(1)}, bf16[136,512]{1,0:T(8,128)(2,1)S(1)}, u32[]{:S(2)}, u32[]{:S(2)}) collective-permute-start(bf16[136,512]{1,0:T(8,128)(2,1)S(1)} %collective-permute-done.3.refs_4_), channel_id=1, source_target_pairs={{0,2},{1,3},{2,0},{3,1},{4,6},{5,7},{6,4},{7,5},{8,10},{9,11},{10,... | collective-permute-start | bytes 417800 | tf_op jit(solution)/shard_map/ppermute | solution.py:468
  15.8 7.7 %collective-permute-start.6 = (bf16[136,512]{1,0:T(8,128)(2,1)S(1)}, bf16[136,512]{1,0:T(8,128)(2,1)S(1)}, u32[]{:S(2)}, u32[]{:S(2)}) collective-permute-start(bf16[136,512]{1,0:T(8,128)(2,1)S(1)} %collective-permute-done.3.refs_4_), channel_id=1, source_target_pairs={{0,1},{1,0},{2,3},{3,2},{4,5},{5,4},{6,7},{7,6},{8,9},{9,8},{10,11... | collective-permute-start | bytes 417800 | tf_op jit(solution)/shard_map/ppermute | solution.py:468
  20.0 6.5 %collective-permute-start.5 = (bf16[136,512]{1,0:T(8,128)(2,1)S(1)}, bf16[136,512]{1,0:T(8,128)(2,1)S(1)}, u32[]{:S(2)}, u32[]{:S(2)}) collective-permute-start(bf16[136,512]{1,0:T(8,128)(2,1)S(1)} %collective-permute-done.2.refs_3_), channel_id=1, source_target_pairs={{0,1},{1,0},{2,3},{3,2},{4,5},{5,4},{6,7},{7,6},{8,9},{9,8},{10,11... | collective-permute-start | bytes 417800 | tf_op jit(solution)/shard_map/ppermute | solution.py:468
  22.3 5.1 %collective-permute-start.7 = (bf16[136,512]{1,0:T(8,128)(2,1)S(1)}, bf16[136,512]{1,0:T(8,128)(2,1)S(1)}, u32[]{:S(2)}, u32[]{:S(2)}) collective-permute-start(bf16[136,512]{1,0:T(8,128)(2,1)S(1)} %collective-permute-done.2.refs_3_), channel_id=1, source_target_pairs={{0,2},{1,3},{2,0},{3,1},{4,6},{5,7},{6,4},{7,5},{8,10},{9,11},{10,... | collective-permute-start | bytes 417800 | tf_op jit(solution)/shard_map/ppermute | solution.py:468
  23.5 6.0 %collective-permute-start.10 = (bf16[136,512]{1,0:T(8,128)(2,1)S(1)}, bf16[136,512]{1,0:T(8,128)(2,1)S(1)}, u32[]{:S(2)}, u32[]{:S(2)}) collective-permute-start(bf16[136,512]{1,0:T(8,128)(2,1)S(1)} %collective-permute-done.8.refs_1_), channel_id=1, source_target_pairs={{0,1},{1,0},{2,3},{3,2},{4,5},{5,4},{6,7},{7,6},{8,9},{9,8},{10,11... | collective-permute-start | bytes 417800 | tf_op jit(solution)/shard_map/ppermute | solution.py:468
  26.4 4.2 %collective-permute-start.9 = (bf16[136,512]{1,0:T(8,128)(2,1)S(1)}, bf16[136,512]{1,0:T(8,128)(2,1)S(1)}, u32[]{:S(2)}, u32[]{:S(2)}) collective-permute-start(bf16[136,512]{1,0:T(8,128)(2,1)S(1)} %collective-permute-done.5.refs_6_), channel_id=1, source_target_pairs={{0,2},{1,3},{2,0},{3,1},{4,6},{5,7},{6,4},{7,5},{8,10},{9,11},{10,... | collective-permute-start | bytes 417800 | tf_op jit(solution)/shard_map/ppermute | solution.py:468
  30.6 14.2 %copy-start.1 = (bf16[1,512,2048]{2,1,0:T(8,128)(2,1)S(1)}, bf16[1,512,2048]{2,1,0:T(8,128)(2,1)}, u32[]{:S(2)}) copy-start(bf16[1,512,2048]{2,1,0:T(8,128)(2,1)} %param.14) | copy-start | bytes 6291460
  30.7 14.2 %copy-start.8 = (bf16[1,136,1024]{2,1,0:T(8,128)(2,1)S(1)}, bf16[1,136,1024]{2,1,0:T(8,128)(2,1)}, u32[]{:S(2)}) copy-start(bf16[1,136,1024]{2,1,0:T(8,128)(2,1)} %param.10) | copy-start | bytes 835588
  55.6 14.5 %collective-permute-start.18 = (bf16[136,1024]{1,0:T(8,128)(2,1)S(1)}, bf16[136,1024]{1,0:T(8,128)(2,1)S(1)}, u32[]{:S(2)}, u32[]{:S(2)}) collective-permute-start(bf16[136,1024]{1,0:T(8,128)(2,1)S(1)} %get-tuple-element.89), channel_id=1, source_target_pairs={{0,7},{1,6},{2,5},{3,4},{4,3},{5,2},{6,1},{7,0},{8,15},{9,14},{10,... | collective-permute-start | bytes 835592 | tf_op jit(solution)/shard_map/ppermute | solution.py:468
  56.6 13.5 %collective-permute-start.19 = (bf16[256,1024]{1,0:T(8,128)(2,1)S(1)}, bf16[256,1024]{1,0:T(8,128)(2,1)S(1)}, u32[]{:S(2)}, u32[]{:S(2)}) collective-permute-start(bf16[256,1024]{1,0:T(8,128)(2,1)S(1)} %get-tuple-element.94), channel_id=1, source_target_pairs={{0,1},{1,0},{2,3},{3,2},{4,5},{5,4},{6,7},{7,6},{8,9},{9,8},{10,11... | collective-permute-start | bytes 1572872 | tf_op jit(solution)/shard_map/ppermute | solution.py:22
  57.1 13.0 %collective-permute-start.20 = (bf16[256,1024]{1,0:T(8,128)(2,1)S(1)}, bf16[256,1024]{1,0:T(8,128)(2,1)S(1)}, u32[]{:S(2)}, u32[]{:S(2)}) collective-permute-start(bf16[256,1024]{1,0:T(8,128)(2,1)S(1)} %get-tuple-element.95), channel_id=1, source_target_pairs={{0,2},{2,0},{1,3},{3,1},{4,6},{6,4},{5,7},{7,5},{8,10},{10,8},{9,1... | collective-permute-start | bytes 1572872 | tf_op jit(solution)/shard_map/ppermute | solution.py:22
  62.2 7.3 %collective-permute-start.11 = (bf16[408,128]{1,0:T(8,128)(2,1)S(1)}, bf16[408,128]{1,0:T(8,128)(2,1)S(1)}, u32[]{:S(2)}, u32[]{:S(2)}) collective-permute-start(bf16[408,128]{1,0:T(8,128)(2,1)S(1)} %get-tuple-element.82), channel_id=1, source_target_pairs={{0,1},{1,0},{2,3},{3,2},{4,5},{5,4},{6,7},{7,6},{8,9},{9,8},{10,11... | collective-permute-start | bytes 313352 | tf_op jit(solution)/shard_map/ppermute | solution.py:468
  63.1 7.0 %collective-permute-start.12 = (bf16[408,128]{1,0:T(8,128)(2,1)S(1)}, bf16[408,128]{1,0:T(8,128)(2,1)S(1)}, u32[]{:S(2)}, u32[]{:S(2)}) collective-permute-start(bf16[408,128]{1,0:T(8,128)(2,1)S(1)} %get-tuple-element.83), channel_id=1, source_target_pairs={{0,2},{1,3},{2,0},{3,1},{4,6},{5,7},{6,4},{7,5},{8,10},{9,11},{10,... | collective-permute-start | bytes 313352 | tf_op jit(solution)/shard_map/ppermute | solution.py:468
  70.3 12.6 %collective-permute-start.21 = (bf16[128,1024]{1,0:T(8,128)(2,1)S(1)}, bf16[128,1024]{1,0:T(8,128)(2,1)S(1)}, u32[]{:S(2)}, u32[]{:S(2)}) collective-permute-start(bf16[128,1024]{1,0:T(8,128)(2,1)S(1)} %get-tuple-element.98), channel_id=1, source_target_pairs={{0,2},{2,0},{1,3},{3,1},{4,6},{6,4},{5,7},{7,5},{8,10},{10,8},{9,1... | collective-permute-start | bytes 786440 | tf_op jit(solution)/shard_map/ppermute | solution.py:22
  70.3 13.6 %collective-permute-start.22 = (bf16[128,1024]{1,0:T(8,128)(2,1)S(1)}, bf16[128,1024]{1,0:T(8,128)(2,1)S(1)}, u32[]{:S(2)}, u32[]{:S(2)}) collective-permute-start(bf16[128,1024]{1,0:T(8,128)(2,1)S(1)} %get-tuple-element.99), channel_id=1, source_target_pairs={{0,1},{1,0},{2,3},{3,2},{4,5},{5,4},{6,7},{7,6},{8,9},{9,8},{10,11... | collective-permute-start | bytes 786440 | tf_op jit(solution)/shard_map/ppermute | solution.py:22
  71.3 7.4 %collective-permute-start.15 = (bf16[408,128]{1,0:T(8,128)(2,1)S(1)}, bf16[408,128]{1,0:T(8,128)(2,1)S(1)}, u32[]{:S(2)}, u32[]{:S(2)}) collective-permute-start(bf16[408,128]{1,0:T(8,128)(2,1)S(1)} %get-tuple-element.86), channel_id=1, source_target_pairs={{0,5},{1,4},{2,7},{3,6},{4,1},{5,0},{6,3},{7,2},{8,13},{9,12},{10,... | collective-permute-start | bytes 313352 | tf_op jit(solution)/shard_map/ppermute | solution.py:468
  73.5 11.4 %collective-permute-start.13 = (bf16[408,128]{1,0:T(8,128)(2,1)S(1)}, bf16[408,128]{1,0:T(8,128)(2,1)S(1)}, u32[]{:S(2)}, u32[]{:S(2)}) collective-permute-start(bf16[408,128]{1,0:T(8,128)(2,1)S(1)} %get-tuple-element.84), channel_id=1, source_target_pairs={{0,4},{1,5},{2,6},{3,7},{4,0},{5,1},{6,2},{7,3},{8,12},{9,13},{10,... | collective-permute-start | bytes 313352 | tf_op jit(solution)/shard_map/ppermute | solution.py:468
  74.0 12.6 %collective-permute-start.14 = (bf16[408,128]{1,0:T(8,128)(2,1)S(1)}, bf16[408,128]{1,0:T(8,128)(2,1)S(1)}, u32[]{:S(2)}, u32[]{:S(2)}) collective-permute-start(bf16[408,128]{1,0:T(8,128)(2,1)S(1)} %get-tuple-element.85), channel_id=1, source_target_pairs={{0,3},{1,2},{2,1},{3,0},{4,7},{5,6},{6,5},{7,4},{8,11},{9,10},{10,... | collective-permute-start | bytes 313352 | tf_op jit(solution)/shard_map/ppermute | solution.py:468
  78.8 9.3 %collective-permute-start.16 = (bf16[408,128]{1,0:T(8,128)(2,1)S(1)}, bf16[408,128]{1,0:T(8,128)(2,1)S(1)}, u32[]{:S(2)}, u32[]{:S(2)}) collective-permute-start(bf16[408,128]{1,0:T(8,128)(2,1)S(1)} %get-tuple-element.87), channel_id=1, source_target_pairs={{0,6},{1,7},{2,4},{3,5},{4,2},{5,3},{6,0},{7,1},{8,14},{9,15},{10,... | collective-permute-start | bytes 313352 | tf_op jit(solution)/shard_map/ppermute | solution.py:468
  82.8 7.3 %copy-start.3 = (bf16[1,1024,512]{2,1,0:T(8,128)(2,1)S(1)}, bf16[1,1024,512]{2,1,0:T(8,128)(2,1)}, u32[]{:S(2)}) copy-start(bf16[1,1024,512]{2,1,0:T(8,128)(2,1)} %param.11) | copy-start | bytes 3145732
  82.9 7.3 %copy-start.5 = (bf16[1,1024,512]{2,1,0:T(8,128)(2,1)S(1)}, bf16[1,1024,512]{2,1,0:T(8,128)(2,1)}, u32[]{:S(2)}) copy-start(bf16[1,1024,512]{2,1,0:T(8,128)(2,1)} %param.12) | copy-start | bytes 3145732
  82.9 7.3 %copy-start.7 = (bf16[1,1024,512]{2,1,0:T(8,128)(2,1)S(1)}, bf16[1,1024,512]{2,1,0:T(8,128)(2,1)}, u32[]{:S(2)}) copy-start(bf16[1,1024,512]{2,1,0:T(8,128)(2,1)} %param.13) | copy-start | bytes 3145732
  82.9 7.3 %collective-permute-start.17 = (bf16[408,128]{1,0:T(8,128)(2,1)S(1)}, bf16[408,128]{1,0:T(8,128)(2,1)S(1)}, u32[]{:S(2)}, u32[]{:S(2)}) collective-permute-start(bf16[408,128]{1,0:T(8,128)(2,1)S(1)} %get-tuple-element.88), channel_id=1, source_target_pairs={{0,7},{1,6},{2,5},{3,4},{4,3},{5,2},{6,1},{7,0},{8,15},{9,14},{10,... | collective-permute-start | bytes 313352 | tf_op jit(solution)/shard_map/ppermute | solution.py:468
  84.1 28.2 %collective-permute-start.25 = (bf16[64,1024]{1,0:T(8,128)(2,1)S(1)}, bf16[64,1024]{1,0:T(8,128)(2,1)S(1)}, u32[]{:S(2)}, u32[]{:S(2)}) collective-permute-start(bf16[64,1024]{1,0:T(8,128)(2,1)S(1)} %get-tuple-element.101), channel_id=1, source_target_pairs={{0,4},{4,0},{1,5},{5,1},{2,6},{6,2},{3,7},{7,3},{8,12},{12,8},{9,1... | collective-permute-start | bytes 393224 | tf_op jit(solution)/shard_map/ppermute | solution.py:22
  84.8 27.5 %collective-permute-start.24 = (bf16[64,1024]{1,0:T(8,128)(2,1)S(1)}, bf16[64,1024]{1,0:T(8,128)(2,1)S(1)}, u32[]{:S(2)}, u32[]{:S(2)}) collective-permute-start(bf16[64,1024]{1,0:T(8,128)(2,1)S(1)} %get-tuple-element.100.refs_14_), channel_id=1, source_target_pairs={{0,4},{4,0},{1,5},{5,1},{2,6},{6,2},{3,7},{7,3},{8,12},{12,8},{9,1... | collective-permute-start | bytes 393224 | tf_op jit(solution)/shard_map/ppermute | solution.py:22
  91.5 26.2 %collective-permute-start.23 = (bf16[136,1024]{1,0:T(8,128)(2,1)S(1)}, bf16[136,1024]{1,0:T(8,128)(2,1)S(1)}, u32[]{:S(2)}, u32[]{:S(2)}) collective-permute-start(bf16[136,1024]{1,0:T(8,128)(2,1)S(1)} %shard_map.135), channel_id=1, source_target_pairs={{8,0},{16,8},{24,16},{9,1},{17,9},{25,17},{10,2},{18,10},{26,18},{... | collective-permute-start | bytes 835592 | tf_op jit(solution)/shard_map/ppermute | solution.py:28
  113.2 4.5 %copy-start.9 = (s32[1,136]{1,0:T(1,128)S(1)}, s32[1,136]{1,0:T(1,128)}, u32[]{:S(2)}) copy-start(s32[1,136]{1,0:T(1,128)} %order_ref.1) | copy-start | bytes 1636

commit v12 on v11

--- a/solution.py
+++ b/solution.py
@@ -357,7 +357,7 @@
 
 
 def backward_kernel(me_ref, slab_ref, prob_ref, qk_ref, v_ref, out_t_ref, *refs):
-    early, late, out_refs = refs[:3], refs[3:6], refs[6:-4]
+    early, late, out_refs = refs[:3], refs[3:6], refs[7:-4]
     gk_ref, gv_ref, gq_ref, held_ref = refs[-4:]
     first, rows = early[0].shape[:2]
     slabs = [wide(slab_ref[me_ref[0] ^ distance]) for distance in DISTANCES]
@@ -568,8 +568,8 @@
         + [out(len(group) * HEAD_DIM, width) for order in ORDERS for group in order],
     )
     grad_slabs = switch(grad_slabs)
-    grad_slabs, terms, scaled = lax.optimization_barrier((grad_slabs, terms, scaled))
     scaled = hop(scaled, parts - 1)
+    grad_slabs, terms = lax.optimization_barrier((grad_slabs, terms))
     first, second, third, keep = zip(terms[:4], terms[4:])
     got = [partner(part, "seq", bit) for bit, part in enumerate(first)]
     grads = call(
@@ -577,7 +577,8 @@
         6,
         [("s", me)]
         + [("v", x) for x in (grad_slabs, probs, qk, value, out_t)]
-        + [("v", x) for x in (normed, unit, unit_scale, *late_parts)],
+        + [("v", x) for x in (normed, unit, unit_scale, *late_parts)]
+        + [("a", scaled)],
         [out(PACKED + rows + 3 * HEAD_DIM, 128)] * parts,
         [
             pltpu.VMEM((tokens, HEAD_DIM), f32),
@@ -590,7 +591,7 @@
     leaving = call(
         second_sum_kernel,
         1,
-        [("v", x) for x in (*second, *got)] + [("a", x) for x in (*slabs[1:3], scaled)],
+        [("v", x) for x in (*second, *got)] + [("a", x) for x in (slabs[3], slabs[6])],
         [out(*second[0].shape)] * 2,
     )
     more = [partner(part, "seq", 1 - bit) for bit, part in enumerate(leaving)]

time: 119 us -> 135 us (1.13)
  the two profiles are of different devices: /device:TPU:1 before, /device:TPU:9 now
where the time goes in v12:
time: 135 us; the launch traced here: 134 us
  starting transfers between devices  55.4 us (41%)
  waiting for transfers between devices  28 us (21%)
  local copies, waits for them, and re-layouts  22.2 us (16%)
  Pallas kernels  16.9 us (13%)
  blocking collectives  9.81 us (7%)
    ppermute x19, starting transfers between devices, hop(): return lax.ppermute(block, 'seq', route)  23.4 us
    ppermute x19, waiting for transfers between devices, hop(): return lax.ppermute(block, 'seq', route)  22 us
    ppermute x1, starting transfers between devices, shifted(): return lax.ppermute(block, axis, route)  20.4 us
    unnamed x74, local copies, waits for them, and re-layouts  20.2 us
    pallas_call x11, Pallas kernels, call(): pl.pallas_call(kernel, out_shape=tuple(outs), in_specs=[pl.BlockSpec(memo...  16.9 us
    all_to_all x1, blocking collectives, switch(): return lax.all_to_all(slabs, 'seq', split_axis=0, concat_axis=0, tiled=True)  9.81 us
    ppermute x6, starting transfers between devices, partner(): return lax.ppermute(block, axis, route)  6.49 us
    all_to_all x1, starting transfers between devices, switch(): return lax.all_to_all(slabs, 'seq', split_axis=0, concat_axis=0, tiled=True)  5.16 us
  transfers between devices with their start and end apart: 27, of which 10 were waited for; matrix products, arithmetic and copies ran while one was open for 2% of the time, Pallas kernels for 7%

profile of v12, /device:TPU:9, one launch (start us, length us, event | category | flops | bytes accessed | tf_op | source)
XLA Modules:
  0.0 134.0 jit_solution(5588868943966128104)
XLA Ops:
  0.7 1.4 %collective-permute-start = (bf16[136,1024]{1,0:T(8,128)(2,1)}, bf16[136,1024]{1,0:T(8,128)(2,1)S(1)}, u32[]{:S(2)}, u32[]{:S(2)}) collective-permute-start(bf16[136,1024]{1,0:T(8,128)(2,1)} %bitcast.8), channel_id=1, source_target_pairs={{0,1},{1,0},{2,3},{3,2},{4,5},{5,4},{6,7},{7,6},{8,9},{9,8},{10,11... | collective-permute-start | bytes 835592 | tf_op jit(solution)/shard_map/ppermute | solution.py:468
  2.1 1.0 fusion
  3.1 2.4 %collective-permute-start.3 = (bf16[136,512]{1,0:T(8,128)(2,1)S(1)}, bf16[136,512]{1,0:T(8,128)(2,1)S(1)}, u32[]{:S(2)}, u32[]{:S(2)}) collective-permute-start(bf16[136,512]{1,0:T(8,128)(2,1)S(1)} %get-tuple-element.107), channel_id=1, source_target_pairs={{0,4},{1,5},{2,6},{3,7},{4,0},{5,1},{6,2},{7,3},{8,12},{9,13},{10,... | collective-permute-start | bytes 417800 | tf_op jit(solution)/shard_map/ppermute | solution.py:468
  6.2 1.2 copy-done.2
  7.4 1.2 copy-done.4
  8.6 1.2 copy-done.6
  10.4 1.5 %collective-permute-start.4 = (bf16[136,1024]{1,0:T(8,128)(2,1)S(1)}, bf16[136,1024]{1,0:T(8,128)(2,1)S(1)}, u32[]{:S(2)}, u32[]{:S(2)}) collective-permute-start(bf16[136,1024]{1,0:T(8,128)(2,1)S(1)} %collective-permute-done.1.refs_2_), channel_id=1, source_target_pairs={{0,1},{1,0},{2,3},{3,2},{4,5},{5,4},{6,7},{7,6},{8,9},{9,8},{10,11... | collective-permute-start | bytes 835592 | tf_op jit(solution)/shard_map/ppermute | solution.py:468
  12.5 2.6 %collective-permute-start.8 = (bf16[136,512]{1,0:T(8,128)(2,1)S(1)}, bf16[136,512]{1,0:T(8,128)(2,1)S(1)}, u32[]{:S(2)}, u32[]{:S(2)}) collective-permute-start(bf16[136,512]{1,0:T(8,128)(2,1)S(1)} %collective-permute-done.3.refs_4_), channel_id=1, source_target_pairs={{0,2},{1,3},{2,0},{3,1},{4,6},{5,7},{6,4},{7,5},{8,10},{9,11},{10,... | collective-permute-start | bytes 417800 | tf_op jit(solution)/shard_map/ppermute | solution.py:468
  15.1 1.2 collective-permute-done.2.refs_3_
  17.1 2.4 %collective-permute-done.8.refs_1_ = bf16[136,512]{1,0:T(8,128)(2,1)S(1)} collective-permute-done((bf16[136,512]{1,0:T(8,128)(2,1)S(1)}, bf16[136,512]{1,0:T(8,128)(2,1)S(1)}, u32[]{:S(2)}, u32[]{:S(2)}) %collective-permute-start.8) | collective-permute-done | bytes 139296 | tf_op jit(solution)/shard_map/ppermute | solution.py:468
  19.5 2.2 %collective-permute-start.7 = (bf16[136,512]{1,0:T(8,128)(2,1)S(1)}, bf16[136,512]{1,0:T(8,128)(2,1)S(1)}, u32[]{:S(2)}, u32[]{:S(2)}) collective-permute-start(bf16[136,512]{1,0:T(8,128)(2,1)S(1)} %collective-permute-done.2.refs_3_), channel_id=1, source_target_pairs={{0,2},{1,3},{2,0},{3,1},{4,6},{5,7},{6,4},{7,5},{8,10},{9,11},{10,... | collective-permute-start | bytes 417800 | tf_op jit(solution)/shard_map/ppermute | solution.py:468
  21.8 4.0 %collective-permute-start.9 = (bf16[136,512]{1,0:T(8,128)(2,1)S(1)}, bf16[136,512]{1,0:T(8,128)(2,1)S(1)}, u32[]{:S(2)}, u32[]{:S(2)}) collective-permute-start(bf16[136,512]{1,0:T(8,128)(2,1)S(1)} %collective-permute-done.5.refs_6_), channel_id=1, source_target_pairs={{0,2},{1,3},{2,0},{3,1},{4,6},{5,7},{6,4},{7,5},{8,10},{9,11},{10,... | collective-permute-start | bytes 417800 | tf_op jit(solution)/shard_map/ppermute | solution.py:468
  25.8 1.0 shard_map.129
  26.8 1.2 copy-done.10
  28.8 3.7 %shard_map.130 = (bf16[2,136,1024]{2,1,0:T(8,128)(2,1)S(1)}, f32[2,136,128]{2,1,0:T(8,128)S(1)}, f32[2,136,128]{2,1,0:T(8,128)S(1)}, bf16[1088,1088]{1,0:T(8,128...) custom-call(s32[1]{0:T(128)} %bitcast.me_ref, ...), custom_call_target="tpu_custom_call" | custom-call | flops 5000000000 | bytes 1024 | tf_op jit(solution)/shard_map/pallas_call | solution.py:200
  32.5 1.4 %copy-done.16 = bf16[1088,1088]{1,0:T(8,128)(2,1)} copy-done((bf16[1088,1088]{1,0:T(8,128)(2,1)}, bf16[1088,1088]{1,0:T(8,128)(2,1)S(1)}, u32[]{:S(2)}) %copy-start.16) | copy-done | bytes 2367512
  35.3 9.8 %all_to_all.10.slab_ref = bf16[8,80,128]{2,1,0:T(8,128)(2,1)S(1)} all-to-all(bf16[8,80,128]{2,1,0:T(8,128)(2,1)S(1)} %get-tuple-element.59), channel_id=1, replica_groups=mesh['section'=4,'seq'=8] {'seq'}, dimensions={0} | all-to-all | bytes 327680 | tf_op jit(solution)/shard_map/all_to_all | solution.py:476
  45.1 2.2 %shard_map.131 = (bf16[136,1024]{1,0:T(8,128)(2,1)S(1)}, bf16[8,80,128]{2,1,0:T(8,128)(2,1)}, bf16[256,1024]{1,0:T(8,128)(2,1)S(1)}, bf16[128,1024]{1,0:T(8,128)...) custom-call(s32[1]{0:T(128)} %bitcast.me_ref, ...), custom_call_target="tpu_custom_call" | custom-call | flops 3000000000 | bytes 1024 | tf_op jit(solution)/shard_map/pallas_call | solution.py:200
  49.3 5.2 %all-to-all-start.1 = ((bf16[8,80,128]{2,1,0:T(8,128)(2,1)}), bf16[8,80,128]{2,1,0:T(8,128)(2,1)S(1)}, u32[]{:S(2)}, u32[]{:S(2)}) async-start(bf16[8,80,128]{2,1,0:T(8,128)(2,1)} %get-tuple-element.60), calls=%async_computation.1 | async-start | bytes 327680 | tf_op jit(solution)/shard_map/all_to_all | solution.py:476
  54.4 2.1 %collective-permute-start.11 = (bf16[136,1024]{1,0:T(8,128)(2,1)S(1)}, bf16[136,1024]{1,0:T(8,128)(2,1)S(1)}, u32[]{:S(2)}, u32[]{:S(2)}) collective-permute-start(bf16[136,1024]{1,0:T(8,128)(2,1)S(1)} %get-tuple-element.79), channel_id=1, source_target_pairs={{0,7},{1,6},{2,5},{3,4},{4,3},{5,2},{6,1},{7,0},{8,15},{9,14},{10,... | collective-permute-start | bytes 835592 | tf_op jit(solution)/shard_map/ppermute | solution.py:468
  56.5 2.5 %all-to-all-done.1.slab_ref = bf16[8,80,128]{2,1,0:T(8,128)(2,1)S(1)} async-done(((bf16[8,80,128]{2,1,0:T(8,128)(2,1)}), bf16[8,80,128]{2,1,0:T(8,128)(2,1)S(1)}, u32[]{:S(2)}, u32[]{:S(2)}) %all-to-all-start.1) | async-done | bytes 163872 | tf_op jit(solution)/shard_map/all_to_all | solution.py:476
  59.0 1.2 collective-permute-start.19
  60.9 5.7 %collective-permute-done.11.refs_6_.refs_13_ = bf16[136,1024]{1,0:T(8,128)(2,1)S(1)} collective-permute-done((bf16[136,1024]{1,0:T(8,128)(2,1)S(1)}, bf16[136,1024]{1,0:T(8,128)(2,1)S(1)}, u32[]{:S(2)}, u32[]{:S(2)}) %collective-permute-start.11) | collective-permute-done | bytes 278560 | tf_op jit(solution)/shard_map/ppermute | solution.py:468
  66.6 1.4 %copy-done.11 = bf16[6,136,1024]{2,1,0:T(8,128)(2,1)S(1)} copy-done((bf16[6,136,1024]{2,1,0:T(8,128)(2,1)S(1)}, bf16[6,136,1024]{2,1,0:T(8,128)(2,1)}, u32[]{:S(2)}) %copy-start.11) | copy-done | bytes 1671192
  68.0 1.0 copy-done.15
  69.0 1.7 %copy-done.17 = bf16[1088,1088]{1,0:T(8,128)(2,1)S(1)} copy-done((bf16[1088,1088]{1,0:T(8,128)(2,1)S(1)}, bf16[1088,1088]{1,0:T(8,128)(2,1)}, u32[]{:S(2)}) %copy-start.17) | copy-done | bytes 2367512
  70.7 1.1 copy-done.25
  71.8 1.0 copy-done.27
  72.8 1.0 copy-done.29
  73.7 1.0 copy-done.31
  74.7 0.9 copy-done.33
  75.6 0.9 copy-done.35
  76.5 5.0 %shard_map.132 = (bf16[408,128]{1,0:T(8,128)(2,1)S(1)}, bf16[408,128]{1,0:T(8,128)(2,1)S(1)}, bf16[408,128]{1,0:T(8,128)(2,1)S(1)}, bf16[408,128]{1,0:T(8,128)(2...) custom-call(s32[1]{0:T(128)} %bitcast.me_ref, ...), custom_call_target="tpu_custom_call" | custom-call | flops 6000000000 | bytes 1024 | tf_op jit(solution)/shard_map/pallas_call | solution.py:200
  82.3 3.8 %collective-permute-done.14.refs_4_.refs_3_ = bf16[408,128]{1,0:T(8,128)(2,1)S(1)} collective-permute-done((bf16[408,128]{1,0:T(8,128)(2,1)S(1)}, bf16[408,128]{1,0:T(8,128)(2,1)S(1)}, u32[]{:S(2)}, u32[]{:S(2)}) %collective-permute-start.14) | collective-permute-done | bytes 104480 | tf_op jit(solution)/shard_map/ppermute | solution.py:468
  86.1 1.6 %collective-permute-done.17.refs_5_.refs_6_ = bf16[408,128]{1,0:T(8,128)(2,1)S(1)} collective-permute-done((bf16[408,128]{1,0:T(8,128)(2,1)S(1)}, bf16[408,128]{1,0:T(8,128)(2,1)S(1)}, u32[]{:S(2)}, u32[]{:S(2)}) %collective-permute-start.17) | collective-permute-done | bytes 104480 | tf_op jit(solution)/shard_map/ppermute | solution.py:468
  87.8 1.2 collective-permute-start.21
  89.0 1.0 collective-permute-start.22
  90.0 1.0 collective-permute-start.16
  91.6 1.0 collective-permute-start.13
  92.6 4.5 %collective-permute-done.16.refs_8_.refs_5_ = bf16[408,128]{1,0:T(8,128)(2,1)S(1)} collective-permute-done((bf16[408,128]{1,0:T(8,128)(2,1)S(1)}, bf16[408,128]{1,0:T(8,128)(2,1)S(1)}, u32[]{:S(2)}, u32[]{:S(2)}) %collective-permute-start.16) | collective-permute-done | bytes 104480 | tf_op jit(solution)/shard_map/ppermute | solution.py:468
  97.1 3.2 %collective-permute-start.15 = (bf16[408,128]{1,0:T(8,128)(2,1)S(1)}, bf16[408,128]{1,0:T(8,128)(2,1)S(1)}, u32[]{:S(2)}, u32[]{:S(2)}) collective-permute-start(bf16[408,128]{1,0:T(8,128)(2,1)S(1)} %get-tuple-element.84), channel_id=1, source_target_pairs={{0,3},{1,2},{2,1},{3,0},{4,7},{5,6},{6,5},{7,4},{8,11},{9,10},{10,... | collective-permute-start | bytes 313352 | tf_op jit(solution)/shard_map/ppermute | solution.py:468
  100.7 2.1 %collective-permute-start.25 = (bf16[64,1024]{1,0:T(8,128)(2,1)S(1)}, bf16[64,1024]{1,0:T(8,128)(2,1)S(1)}, u32[]{:S(2)}, u32[]{:S(2)}) collective-permute-start(bf16[64,1024]{1,0:T(8,128)(2,1)S(1)} %get-tuple-element.99), channel_id=1, source_target_pairs={{0,4},{4,0},{1,5},{5,1},{2,6},{6,2},{3,7},{7,3},{8,12},{12,8},{9,1... | collective-permute-start | bytes 393224 | tf_op jit(solution)/shard_map/ppermute | solution.py:22
  103.2 2.7 %collective-permute-done.18.refs_7_ = bf16[408,128]{1,0:T(8,128)(2,1)S(1)} collective-permute-done((bf16[408,128]{1,0:T(8,128)(2,1)S(1)}, bf16[408,128]{1,0:T(8,128)(2,1)S(1)}, u32[]{:S(2)}, u32[]{:S(2)}) %collective-permute-start.18) | collective-permute-done | bytes 104480 | tf_op jit(solution)/shard_map/ppermute | solution.py:468
  105.9 1.4 %shard_map.135 = bf16[136,1024]{1,0:T(8,128)(2,1)S(1)} custom-call(s32[1]{0:T(128)} %bitcast.me_ref, bf16[408,128]{1,0:T(8,128)(2,1)S(1)} %get-tuple-element.80.refs_0_, bf16[408,128]{1,0:T(8,128)(2,1)S(1)} %collective-permute-done.12.refs_1_, bf16[408,128]{1,0:T(8,128)(2,1)S(1)} %collective-permute-done.13.refs_2_, ...), custom_call_target="tpu_custom_call" | custom-call | flops 1500000000 | bytes 1024 | tf_op jit(solution)/shard_map/pallas_call | solution.py:200
  107.3 20.4 %collective-permute-start.23 = (bf16[136,1024]{1,0:T(8,128)(2,1)S(1)}, bf16[136,1024]{1,0:T(8,128)(2,1)S(1)}, u32[]{:S(2)}, u32[]{:S(2)}) collective-permute-start(bf16[136,1024]{1,0:T(8,128)(2,1)S(1)} %shard_map.135), channel_id=1, source_target_pairs={{8,0},{16,8},{24,16},{9,1},{17,9},{25,17},{10,2},{18,10},{26,18},{... | collective-permute-start | bytes 835592 | tf_op jit(solution)/shard_map/ppermute | solution.py:28
  128.5 1.0 shard_map.137
  129.6 3.5 %collective-permute-done.23.rows_ref = bf16[136,1024]{1,0:T(8,128)(2,1)S(1)} collective-permute-done((bf16[136,1024]{1,0:T(8,128)(2,1)S(1)}, bf16[136,1024]{1,0:T(8,128)(2,1)S(1)}, u32[]{:S(2)}, u32[]{:S(2)}) %collective-permute-start.23) | collective-permute-done | bytes 278560 | tf_op jit(solution)/shard_map/ppermute | solution.py:28
  133.0 1.0 shard_map.136
  (100 shorter events, 10.7 us)
Async XLA Ops:
  0.6 9.7 %collective-permute-start.1 = (bf16[136,1024]{1,0:T(8,128)(2,1)}, bf16[136,1024]{1,0:T(8,128)(2,1)S(1)}, u32[]{:S(2)}, u32[]{:S(2)}) collective-permute-start(bf16[136,1024]{1,0:T(8,128)(2,1)} %bitcast.7), channel_id=1, source_target_pairs={{0,2},{1,3},{2,0},{3,1},{4,6},{5,7},{6,4},{7,5},{8,10},{9,11},{10,... | collective-permute-start | bytes 835592 | tf_op jit(solution)/shard_map/ppermute | solution.py:468
  0.7 25.1 %collective-permute-start = (bf16[136,1024]{1,0:T(8,128)(2,1)}, bf16[136,1024]{1,0:T(8,128)(2,1)S(1)}, u32[]{:S(2)}, u32[]{:S(2)}) collective-permute-start(bf16[136,1024]{1,0:T(8,128)(2,1)} %bitcast.8), channel_id=1, source_target_pairs={{0,1},{1,0},{2,3},{3,2},{4,5},{5,4},{6,7},{7,6},{8,9},{9,8},{10,11... | collective-permute-start | bytes 835592 | tf_op jit(solution)/shard_map/ppermute | solution.py:468
  3.1 9.5 %collective-permute-start.3 = (bf16[136,512]{1,0:T(8,128)(2,1)S(1)}, bf16[136,512]{1,0:T(8,128)(2,1)S(1)}, u32[]{:S(2)}, u32[]{:S(2)}) collective-permute-start(bf16[136,512]{1,0:T(8,128)(2,1)S(1)} %get-tuple-element.107), channel_id=1, source_target_pairs={{0,4},{1,5},{2,6},{3,7},{4,0},{5,1},{6,2},{7,3},{8,12},{9,13},{10,... | collective-permute-start | bytes 417800 | tf_op jit(solution)/shard_map/ppermute | solution.py:468
  5.5 10.9 %collective-permute-start.2 = (bf16[136,512]{1,0:T(8,128)(2,1)S(1)}, bf16[136,512]{1,0:T(8,128)(2,1)S(1)}, u32[]{:S(2)}, u32[]{:S(2)}) collective-permute-start(bf16[136,512]{1,0:T(8,128)(2,1)S(1)} %get-tuple-element.108), channel_id=1, source_target_pairs={{0,4},{1,5},{2,6},{3,7},{4,0},{5,1},{6,2},{7,3},{8,12},{9,13},{10,... | collective-permute-start | bytes 417800 | tf_op jit(solution)/shard_map/ppermute | solution.py:468
  6.2 1.2 copy-start.2
  9.9 2.0 %copy-start.36 = (s32[1088]{0:T(1024)S(1)}, s32[1088]{0:T(1024)}, u32[]{:S(2)}) copy-start(s32[1088]{0:T(1024)} %param.15) | copy-start | bytes 13060
  9.9 15.9 %copy-start = (bf16[1,136,1024]{2,1,0:T(8,128)(2,1)S(1)}, bf16[1,136,1024]{2,1,0:T(8,128)(2,1)}, u32[]{:S(2)}) copy-start(bf16[1,136,1024]{2,1,0:T(8,128)(2,1)} %param.9) | copy-start | bytes 835588
  10.4 15.4 %collective-permute-start.4 = (bf16[136,1024]{1,0:T(8,128)(2,1)S(1)}, bf16[136,1024]{1,0:T(8,128)(2,1)S(1)}, u32[]{:S(2)}, u32[]{:S(2)}) collective-permute-start(bf16[136,1024]{1,0:T(8,128)(2,1)S(1)} %collective-permute-done.1.refs_2_), channel_id=1, source_target_pairs={{0,1},{1,0},{2,3},{3,2},{4,5},{5,4},{6,7},{7,6},{8,9},{9,8},{10,11... | collective-permute-start | bytes 835592 | tf_op jit(solution)/shard_map/ppermute | solution.py:468
  12.5 6.9 %collective-permute-start.8 = (bf16[136,512]{1,0:T(8,128)(2,1)S(1)}, bf16[136,512]{1,0:T(8,128)(2,1)S(1)}, u32[]{:S(2)}, u32[]{:S(2)}) collective-permute-start(bf16[136,512]{1,0:T(8,128)(2,1)S(1)} %collective-permute-done.3.refs_4_), channel_id=1, source_target_pairs={{0,2},{1,3},{2,0},{3,1},{4,6},{5,7},{6,4},{7,5},{8,10},{9,11},{10,... | collective-permute-start | bytes 417800 | tf_op jit(solution)/shard_map/ppermute | solution.py:468
  15.1 6.5 %collective-permute-start.6 = (bf16[136,512]{1,0:T(8,128)(2,1)S(1)}, bf16[136,512]{1,0:T(8,128)(2,1)S(1)}, u32[]{:S(2)}, u32[]{:S(2)}) collective-permute-start(bf16[136,512]{1,0:T(8,128)(2,1)S(1)} %collective-permute-done.3.refs_4_), channel_id=1, source_target_pairs={{0,1},{1,0},{2,3},{3,2},{4,5},{5,4},{6,7},{7,6},{8,9},{9,8},{10,11... | collective-permute-start | bytes 417800 | tf_op jit(solution)/shard_map/ppermute | solution.py:468
  16.3 5.5 %collective-permute-start.5 = (bf16[136,512]{1,0:T(8,128)(2,1)S(1)}, bf16[136,512]{1,0:T(8,128)(2,1)S(1)}, u32[]{:S(2)}, u32[]{:S(2)}) collective-permute-start(bf16[136,512]{1,0:T(8,128)(2,1)S(1)} %collective-permute-done.2.refs_3_), channel_id=1, source_target_pairs={{0,1},{1,0},{2,3},{3,2},{4,5},{5,4},{6,7},{7,6},{8,9},{9,8},{10,11... | collective-permute-start | bytes 417800 | tf_op jit(solution)/shard_map/ppermute | solution.py:468
  19.5 9.2 %collective-permute-start.7 = (bf16[136,512]{1,0:T(8,128)(2,1)S(1)}, bf16[136,512]{1,0:T(8,128)(2,1)S(1)}, u32[]{:S(2)}, u32[]{:S(2)}) collective-permute-start(bf16[136,512]{1,0:T(8,128)(2,1)S(1)} %collective-permute-done.2.refs_3_), channel_id=1, source_target_pairs={{0,2},{1,3},{2,0},{3,1},{4,6},{5,7},{6,4},{7,5},{8,10},{9,11},{10,... | collective-permute-start | bytes 417800 | tf_op jit(solution)/shard_map/ppermute | solution.py:468
  21.7 7.0 %collective-permute-start.10 = (bf16[136,512]{1,0:T(8,128)(2,1)S(1)}, bf16[136,512]{1,0:T(8,128)(2,1)S(1)}, u32[]{:S(2)}, u32[]{:S(2)}) collective-permute-start(bf16[136,512]{1,0:T(8,128)(2,1)S(1)} %collective-permute-done.8.refs_1_), channel_id=1, source_target_pairs={{0,1},{1,0},{2,3},{3,2},{4,5},{5,4},{6,7},{7,6},{8,9},{9,8},{10,11... | collective-permute-start | bytes 417800 | tf_op jit(solution)/shard_map/ppermute | solution.py:468
  21.8 6.9 %collective-permute-start.9 = (bf16[136,512]{1,0:T(8,128)(2,1)S(1)}, bf16[136,512]{1,0:T(8,128)(2,1)S(1)}, u32[]{:S(2)}, u32[]{:S(2)}) collective-permute-start(bf16[136,512]{1,0:T(8,128)(2,1)S(1)} %collective-permute-done.5.refs_6_), channel_id=1, source_target_pairs={{0,2},{1,3},{2,0},{3,1},{4,6},{5,7},{6,4},{7,5},{8,10},{9,11},{10,... | collective-permute-start | bytes 417800 | tf_op jit(solution)/shard_map/ppermute | solution.py:468
  28.7 3.8 %copy-start.12 = (f32[6,136,128]{2,1,0:T(8,128)}, f32[6,136,128]{2,1,0:T(8,128)S(1)}, u32[]{:S(2)}) copy-start(f32[6,136,128]{2,1,0:T(8,128)S(1)} %get-tuple-element.57.unit_ref.refs_1_) | copy-start | bytes 1253380
  28.7 16.4 %copy-start.1 = (bf16[1,512,2048]{2,1,0:T(8,128)(2,1)S(1)}, bf16[1,512,2048]{2,1,0:T(8,128)(2,1)}, u32[]{:S(2)}) copy-start(bf16[1,512,2048]{2,1,0:T(8,128)(2,1)} %param.14) | copy-start | bytes 6291460
  28.7 16.3 %copy-start.8 = (bf16[1,136,1024]{2,1,0:T(8,128)(2,1)S(1)}, bf16[1,136,1024]{2,1,0:T(8,128)(2,1)}, u32[]{:S(2)}) copy-start(bf16[1,136,1024]{2,1,0:T(8,128)(2,1)} %param.10) | copy-start | bytes 835588
  32.5 1.4 %copy-start.16 = (bf16[1088,1088]{1,0:T(8,128)(2,1)}, bf16[1088,1088]{1,0:T(8,128)(2,1)S(1)}, u32[]{:S(2)}) copy-start(bf16[1088,1088]{1,0:T(8,128)(2,1)S(1)} %get-tuple-element.70.prob_ref) | copy-start | bytes 7102468
  35.3 12.0 %copy-start.24 = (bf16[2,136,1024]{2,1,0:T(8,128)(2,1)}, bf16[2,136,1024]{2,1,0:T(8,128)(2,1)S(1)}, u32[]{:S(2)}) copy-start(bf16[2,136,1024]{2,1,0:T(8,128)(2,1)S(1)} %get-tuple-element.76.refs_3_) | copy-start | bytes 1671172
  35.3 12.0 %copy-start.26 = (f32[64,1088]{1,0:T(8,128)}, f32[64,1088]{1,0:T(8,128)S(1)}, u32[]{:S(2)}) copy-start(f32[64,1088]{1,0:T(8,128)S(1)} %get-tuple-element.73.out_t_ref) | copy-start | bytes 835588
  35.3 12.0 %copy-start.28 = (bf16[1088,128]{1,0:T(8,128)(2,1)}, bf16[1088,128]{1,0:T(8,128)(2,1)S(1)}, u32[]{:S(2)}) copy-start(bf16[1088,128]{1,0:T(8,128)(2,1)S(1)} %get-tuple-element.71.qk_ref) | copy-start | bytes 835588
  35.3 12.0 %copy-start.30 = (bf16[1088,64]{1,0:T(8,128)(2,1)}, bf16[1088,64]{1,0:T(8,128)(2,1)S(1)}, u32[]{:S(2)}) copy-start(bf16[1088,64]{1,0:T(8,128)(2,1)S(1)} %get-tuple-element.72.v_ref) | copy-start | bytes 417796
  45.1 21.5 %copy-start.13 = (f32[6,136,128]{2,1,0:T(8,128)S(1)}, f32[6,136,128]{2,1,0:T(8,128)}, u32[]{:S(2)}) copy-start(f32[6,136,128]{2,1,0:T(8,128)} %copy-done.12) | copy-start | bytes 1253380
  49.3 9.7 %all-to-all-start.1 = ((bf16[8,80,128]{2,1,0:T(8,128)(2,1)}), bf16[8,80,128]{2,1,0:T(8,128)(2,1)S(1)}, u32[]{:S(2)}, u32[]{:S(2)}) async-start(bf16[8,80,128]{2,1,0:T(8,128)(2,1)} %get-tuple-element.60), calls=%async_computation.1 | async-start | bytes 327680 | tf_op jit(solution)/shard_map/all_to_all | solution.py:476
  54.4 12.1 %collective-permute-start.11 = (bf16[136,1024]{1,0:T(8,128)(2,1)S(1)}, bf16[136,1024]{1,0:T(8,128)(2,1)S(1)}, u32[]{:S(2)}, u32[]{:S(2)}) collective-permute-start(bf16[136,1024]{1,0:T(8,128)(2,1)S(1)} %get-tuple-element.79), channel_id=1, source_target_pairs={{0,7},{1,6},{2,5},{3,4},{4,3},{5,2},{6,1},{7,0},{8,15},{9,14},{10,... | collective-permute-start | bytes 835592 | tf_op jit(solution)/shard_map/ppermute | solution.py:468
  59.0 28.7 %collective-permute-start.19 = (bf16[256,1024]{1,0:T(8,128)(2,1)S(1)}, bf16[256,1024]{1,0:T(8,128)(2,1)S(1)}, u32[]{:S(2)}, u32[]{:S(2)}) collective-permute-start(bf16[256,1024]{1,0:T(8,128)(2,1)S(1)} %get-tuple-element.92), channel_id=1, source_target_pairs={{0,1},{1,0},{2,3},{3,2},{4,5},{5,4},{6,7},{7,6},{8,9},{9,8},{10,11... | collective-permute-start | bytes 1572872 | tf_op jit(solution)/shard_map/ppermute | solution.py:22
  60.2 27.5 %collective-permute-start.20 = (bf16[256,1024]{1,0:T(8,128)(2,1)S(1)}, bf16[256,1024]{1,0:T(8,128)(2,1)S(1)}, u32[]{:S(2)}, u32[]{:S(2)}) collective-permute-start(bf16[256,1024]{1,0:T(8,128)(2,1)S(1)} %get-tuple-element.93), channel_id=1, source_target_pairs={{0,2},{2,0},{1,3},{3,1},{4,6},{6,4},{5,7},{7,5},{8,10},{10,8},{9,1... | collective-permute-start | bytes 1572872 | tf_op jit(solution)/shard_map/ppermute | solution.py:22
  66.6 1.4 %copy-start.11 = (bf16[6,136,1024]{2,1,0:T(8,128)(2,1)S(1)}, bf16[6,136,1024]{2,1,0:T(8,128)(2,1)}, u32[]{:S(2)}) copy-start(bf16[6,136,1024]{2,1,0:T(8,128)(2,1)} %copy-done.10) | copy-start | bytes 5013508
  69.0 1.7 %copy-start.17 = (bf16[1088,1088]{1,0:T(8,128)(2,1)S(1)}, bf16[1088,1088]{1,0:T(8,128)(2,1)}, u32[]{:S(2)}) copy-start(bf16[1088,1088]{1,0:T(8,128)(2,1)} %copy-done.16) | copy-start | bytes 7102468
  81.5 19.0 %copy-start.19 = (bf16[64,1024]{1,0:T(8,128)(2,1)S(1)}, bf16[64,1024]{1,0:T(8,128)(2,1)}, u32[]{:S(2)}) copy-start(bf16[64,1024]{1,0:T(8,128)(2,1)} %copy-done.18) | copy-start | bytes 393220
  81.5 19.0 %copy-start.21 = (bf16[64,1024]{1,0:T(8,128)(2,1)S(1)}, bf16[64,1024]{1,0:T(8,128)(2,1)}, u32[]{:S(2)}) copy-start(bf16[64,1024]{1,0:T(8,128)(2,1)} %copy-done.20) | copy-start | bytes 393220
  81.5 19.0 %copy-start.23 = (bf16[64,1024]{1,0:T(8,128)(2,1)S(1)}, bf16[64,1024]{1,0:T(8,128)(2,1)}, u32[]{:S(2)}) copy-start(bf16[64,1024]{1,0:T(8,128)(2,1)} %copy-done.22) | copy-start | bytes 393220
  81.5 4.6 %collective-permute-start.14 = (bf16[408,128]{1,0:T(8,128)(2,1)S(1)}, bf16[408,128]{1,0:T(8,128)(2,1)S(1)}, u32[]{:S(2)}, u32[]{:S(2)}) collective-permute-start(bf16[408,128]{1,0:T(8,128)(2,1)S(1)} %get-tuple-element.83), channel_id=1, source_target_pairs={{0,4},{1,5},{2,6},{3,7},{4,0},{5,1},{6,2},{7,3},{8,12},{9,13},{10,... | collective-permute-start | bytes 313352 | tf_op jit(solution)/shard_map/ppermute | solution.py:468
  81.6 6.1 %collective-permute-start.17 = (bf16[408,128]{1,0:T(8,128)(2,1)S(1)}, bf16[408,128]{1,0:T(8,128)(2,1)S(1)}, u32[]{:S(2)}, u32[]{:S(2)}) collective-permute-start(bf16[408,128]{1,0:T(8,128)(2,1)S(1)} %get-tuple-element.86), channel_id=1, source_target_pairs={{0,6},{1,7},{2,4},{3,5},{4,2},{5,3},{6,0},{7,1},{8,14},{9,15},{10,... | collective-permute-start | bytes 313352 | tf_op jit(solution)/shard_map/ppermute | solution.py:468
  87.8 12.5 %collective-permute-start.21 = (bf16[128,1024]{1,0:T(8,128)(2,1)S(1)}, bf16[128,1024]{1,0:T(8,128)(2,1)S(1)}, u32[]{:S(2)}, u32[]{:S(2)}) collective-permute-start(bf16[128,1024]{1,0:T(8,128)(2,1)S(1)} %get-tuple-element.96), channel_id=1, source_target_pairs={{0,2},{2,0},{1,3},{3,1},{4,6},{6,4},{5,7},{7,5},{8,10},{10,8},{9,1... | collective-permute-start | bytes 786440 | tf_op jit(solution)/shard_map/ppermute | solution.py:22
  89.0 11.5 %collective-permute-start.22 = (bf16[128,1024]{1,0:T(8,128)(2,1)S(1)}, bf16[128,1024]{1,0:T(8,128)(2,1)S(1)}, u32[]{:S(2)}, u32[]{:S(2)}) collective-permute-start(bf16[128,1024]{1,0:T(8,128)(2,1)S(1)} %get-tuple-element.97), channel_id=1, source_target_pairs={{0,1},{1,0},{2,3},{3,2},{4,5},{5,4},{6,7},{7,6},{8,9},{9,8},{10,11... | collective-permute-start | bytes 786440 | tf_op jit(solution)/shard_map/ppermute | solution.py:22
  90.0 7.1 %collective-permute-start.16 = (bf16[408,128]{1,0:T(8,128)(2,1)S(1)}, bf16[408,128]{1,0:T(8,128)(2,1)S(1)}, u32[]{:S(2)}, u32[]{:S(2)}) collective-permute-start(bf16[408,128]{1,0:T(8,128)(2,1)S(1)} %get-tuple-element.85), channel_id=1, source_target_pairs={{0,5},{1,4},{2,7},{3,6},{4,1},{5,0},{6,3},{7,2},{8,13},{9,12},{10,... | collective-permute-start | bytes 313352 | tf_op jit(solution)/shard_map/ppermute | solution.py:468
  91.0 11.7 %collective-permute-start.12 = (bf16[408,128]{1,0:T(8,128)(2,1)S(1)}, bf16[408,128]{1,0:T(8,128)(2,1)S(1)}, u32[]{:S(2)}, u32[]{:S(2)}) collective-permute-start(bf16[408,128]{1,0:T(8,128)(2,1)S(1)} %get-tuple-element.81), channel_id=1, source_target_pairs={{0,1},{1,0},{2,3},{3,2},{4,5},{5,4},{6,7},{7,6},{8,9},{9,8},{10,11... | collective-permute-start | bytes 313352 | tf_op jit(solution)/shard_map/ppermute | solution.py:468
  91.6 11.5 %collective-permute-start.13 = (bf16[408,128]{1,0:T(8,128)(2,1)S(1)}, bf16[408,128]{1,0:T(8,128)(2,1)S(1)}, u32[]{:S(2)}, u32[]{:S(2)}) collective-permute-start(bf16[408,128]{1,0:T(8,128)(2,1)S(1)} %get-tuple-element.82), channel_id=1, source_target_pairs={{0,2},{1,3},{2,0},{3,1},{4,6},{5,7},{6,4},{7,5},{8,10},{9,11},{10,... | collective-permute-start | bytes 313352 | tf_op jit(solution)/shard_map/ppermute | solution.py:468
  97.1 6.0 %collective-permute-start.15 = (bf16[408,128]{1,0:T(8,128)(2,1)S(1)}, bf16[408,128]{1,0:T(8,128)(2,1)S(1)}, u32[]{:S(2)}, u32[]{:S(2)}) collective-permute-start(bf16[408,128]{1,0:T(8,128)(2,1)S(1)} %get-tuple-element.84), channel_id=1, source_target_pairs={{0,3},{1,2},{2,1},{3,0},{4,7},{5,6},{6,5},{7,4},{8,11},{9,10},{10,... | collective-permute-start | bytes 313352 | tf_op jit(solution)/shard_map/ppermute | solution.py:468
  100.3 5.6 %copy-start.3 = (bf16[1,1024,512]{2,1,0:T(8,128)(2,1)S(1)}, bf16[1,1024,512]{2,1,0:T(8,128)(2,1)}, u32[]{:S(2)}) copy-start(bf16[1,1024,512]{2,1,0:T(8,128)(2,1)} %param.11) | copy-start | bytes 3145732
  100.3 5.6 %copy-start.5 = (bf16[1,1024,512]{2,1,0:T(8,128)(2,1)S(1)}, bf16[1,1024,512]{2,1,0:T(8,128)(2,1)}, u32[]{:S(2)}) copy-start(bf16[1,1024,512]{2,1,0:T(8,128)(2,1)} %param.12) | copy-start | bytes 3145732
  100.3 5.6 %copy-start.7 = (bf16[1,1024,512]{2,1,0:T(8,128)(2,1)S(1)}, bf16[1,1024,512]{2,1,0:T(8,128)(2,1)}, u32[]{:S(2)}) copy-start(bf16[1,1024,512]{2,1,0:T(8,128)(2,1)} %param.13) | copy-start | bytes 3145732
  100.3 5.5 %collective-permute-start.18 = (bf16[408,128]{1,0:T(8,128)(2,1)S(1)}, bf16[408,128]{1,0:T(8,128)(2,1)S(1)}, u32[]{:S(2)}, u32[]{:S(2)}) collective-permute-start(bf16[408,128]{1,0:T(8,128)(2,1)S(1)} %get-tuple-element.87), channel_id=1, source_target_pairs={{0,7},{1,6},{2,5},{3,4},{4,3},{5,2},{6,1},{7,0},{8,15},{9,14},{10,... | collective-permute-start | bytes 313352 | tf_op jit(solution)/shard_map/ppermute | solution.py:468
  100.7 26.9 %collective-permute-start.25 = (bf16[64,1024]{1,0:T(8,128)(2,1)S(1)}, bf16[64,1024]{1,0:T(8,128)(2,1)S(1)}, u32[]{:S(2)}, u32[]{:S(2)}) collective-permute-start(bf16[64,1024]{1,0:T(8,128)(2,1)S(1)} %get-tuple-element.99), channel_id=1, source_target_pairs={{0,4},{4,0},{1,5},{5,1},{2,6},{6,2},{3,7},{7,3},{8,12},{12,8},{9,1... | collective-permute-start | bytes 393224 | tf_op jit(solution)/shard_map/ppermute | solution.py:22
  102.8 24.9 %collective-permute-start.24 = (bf16[64,1024]{1,0:T(8,128)(2,1)S(1)}, bf16[64,1024]{1,0:T(8,128)(2,1)S(1)}, u32[]{:S(2)}, u32[]{:S(2)}) collective-permute-start(bf16[64,1024]{1,0:T(8,128)(2,1)S(1)} %get-tuple-element.98.refs_14_), channel_id=1, source_target_pairs={{0,4},{4,0},{1,5},{5,1},{2,6},{6,2},{3,7},{7,3},{8,12},{12,8},{9,1... | collective-permute-start | bytes 393224 | tf_op jit(solution)/shard_map/ppermute | solution.py:22
  107.3 25.7 %collective-permute-start.23 = (bf16[136,1024]{1,0:T(8,128)(2,1)S(1)}, bf16[136,1024]{1,0:T(8,128)(2,1)S(1)}, u32[]{:S(2)}, u32[]{:S(2)}) collective-permute-start(bf16[136,1024]{1,0:T(8,128)(2,1)S(1)} %shard_map.135), channel_id=1, source_target_pairs={{8,0},{16,8},{24,16},{9,1},{17,9},{25,17},{10,2},{18,10},{26,18},{... | collective-permute-start | bytes 835592 | tf_op jit(solution)/shard_map/ppermute | solution.py:28
  128.5 4.5 %copy-start.9 = (s32[1,136]{1,0:T(1,128)S(1)}, s32[1,136]{1,0:T(1,128)}, u32[]{:S(2)}) copy-start(s32[1,136]{1,0:T(1,128)} %order_ref.1) | copy-start | bytes 1636
  (16 other events, 14.4 us)

commit v13 on v11

--- a/solution.py
+++ b/solution.py
@@ -590,14 +590,14 @@
     leaving = call(
         second_sum_kernel,
         1,
-        [("v", x) for x in (*second, *got)] + [("a", x) for x in (*slabs[1:3], scaled)],
+        [("v", x) for x in (*second, *got)] + [("a", slabs[i]) for i in (3, 6, 7)],
         [out(*second[0].shape)] * 2,
     )
     more = [partner(part, "seq", 1 - bit) for bit, part in enumerate(leaving)]
     *leaving, keep_a, keep_b = call(
         third_sum_kernel,
         2,
-        [("v", x) for x in (*third, *keep, *got, *more)] + [("a", slabs[5])],
+        [("v", x) for x in (*third, *keep, *got, *more)] + [("a", slabs[2])],
         [out(*third[0].shape)] * 2 + [out(*keep[0].shape, dtype=f32)] * 2,
     )
     rest = [partner(part, "seq", 2) for part in leaving]

time: 119 us -> 119 us (level)
  the two profiles are of different devices: /device:TPU:1 before, /device:TPU:3 now
where the time goes in v13:
time: 119 us
  starting transfers between devices  39.2 us (33%)
  waiting for transfers between devices  37.3 us (31%)
  blocking collectives  18.2 us (15%)
  Pallas kernels  16.7 us (14%)
  local copies, waits for them, and re-layouts  5.65 us (5%)
    ppermute x19, waiting for transfers between devices, hop(): return lax.ppermute(block, 'seq', route)  33.9 us
    ppermute x1, starting transfers between devices, shifted(): return lax.ppermute(block, axis, route)  18.6 us
    all_to_all x2, blocking collectives, switch(): return lax.all_to_all(slabs, 'seq', split_axis=0, concat_axis=0, tiled=True)  18.2 us
    pallas_call x11, Pallas kernels, call(): pl.pallas_call(kernel, out_shape=tuple(outs), in_specs=[pl.BlockSpec(memo...  16.7 us
    ppermute x19, starting transfers between devices, hop(): return lax.ppermute(block, 'seq', route)  15.5 us
    ppermute x6, starting transfers between devices, partner(): return lax.ppermute(block, axis, route)  5.06 us
    unnamed x22, local copies, waits for them, and re-layouts  3.71 us
    ppermute x1, waiting for transfers between devices, shifted(): return lax.ppermute(block, axis, route)  3.46 us
  transfers between devices with their start and end apart: 26, of which 12 were waited for; matrix products, arithmetic and copies ran while one was open for 2% of the time, Pallas kernels for 8%

profile of v13, /device:TPU:3, one launch (start us, length us, event | category | flops | bytes accessed | tf_op | source)
XLA Modules:
  0.0 118.7 jit_solution(11589474661626068761)
XLA Ops:
  0.6 1.4 %collective-permute-start.1 = (bf16[136,1024]{1,0:T(8,128)(2,1)}, bf16[136,1024]{1,0:T(8,128)(2,1)S(1)}, u32[]{:S(2)}, u32[]{:S(2)}) collective-permute-start(bf16[136,1024]{1,0:T(8,128)(2,1)} %bitcast.7), channel_id=1, source_target_pairs={{0,2},{1,3},{2,0},{3,1},{4,6},{5,7},{6,4},{7,5},{8,10},{9,11},{10,... | collective-permute-start | bytes 835592 | tf_op jit(solution)/shard_map/ppermute | solution.py:468
  2.0 0.3 collective-permute-start
  2.2 1.0 fusion
  3.2 2.4 %collective-permute-start.3 = (bf16[136,512]{1,0:T(8,128)(2,1)S(1)}, bf16[136,512]{1,0:T(8,128)(2,1)S(1)}, u32[]{:S(2)}, u32[]{:S(2)}) collective-permute-start(bf16[136,512]{1,0:T(8,128)(2,1)S(1)} %get-tuple-element.109), channel_id=1, source_target_pairs={{0,4},{1,5},{2,6},{3,7},{4,0},{5,1},{6,2},{7,3},{8,12},{9,13},{10,... | collective-permute-start | bytes 417800 | tf_op jit(solution)/shard_map/ppermute | solution.py:468
  5.7 0.7 compare_and_fusion
  6.4 1.2 %copy-done.2 = bf16[1,1024,512]{2,1,0:T(8,128)(2,1)S(1)} copy-done((bf16[1,1024,512]{2,1,0:T(8,128)(2,1)S(1)}, bf16[1,1024,512]{2,1,0:T(8,128)(2,1)}, u32[]{:S(2)}) %copy-start.2) | copy-done | bytes 1048600
  7.6 1.2 %copy-done.4 = bf16[1,1024,512]{2,1,0:T(8,128)(2,1)S(1)} copy-done((bf16[1,1024,512]{2,1,0:T(8,128)(2,1)S(1)}, bf16[1,1024,512]{2,1,0:T(8,128)(2,1)}, u32[]{:S(2)}) %copy-start.4) | copy-done | bytes 1048600
  8.8 1.2 %copy-done.6 = bf16[1,1024,512]{2,1,0:T(8,128)(2,1)S(1)} copy-done((bf16[1,1024,512]{2,1,0:T(8,128)(2,1)S(1)}, bf16[1,1024,512]{2,1,0:T(8,128)(2,1)}, u32[]{:S(2)}) %copy-start.6) | copy-done | bytes 1048600
  10.0 0.5 shard_map.128.refs_8_.weight_ref
  10.5 2.5 %collective-permute-done.1.refs_2_ = bf16[136,1024]{1,0:T(8,128)(2,1)S(1)} collective-permute-done((bf16[136,1024]{1,0:T(8,128)(2,1)}, bf16[136,1024]{1,0:T(8,128)(2,1)S(1)}, u32[]{:S(2)}, u32[]{:S(2)}) %collective-permute-start.1) | collective-permute-done | bytes 278560 | tf_op jit(solution)/shard_map/ppermute | solution.py:468
  13.1 0.6 gather_fusion
  13.8 1.5 %collective-permute-start.6 = (bf16[136,512]{1,0:T(8,128)(2,1)S(1)}, bf16[136,512]{1,0:T(8,128)(2,1)S(1)}, u32[]{:S(2)}, u32[]{:S(2)}) collective-permute-start(bf16[136,512]{1,0:T(8,128)(2,1)S(1)} %collective-permute-done.3.refs_4_), channel_id=1, source_target_pairs={{0,1},{1,0},{2,3},{3,2},{4,5},{5,4},{6,7},{7,6},{8,9},{9,8},{10,11... | collective-permute-start | bytes 417800 | tf_op jit(solution)/shard_map/ppermute | solution.py:468
  15.3 2.8 %collective-permute-done.2.refs_3_ = bf16[136,512]{1,0:T(8,128)(2,1)S(1)} collective-permute-done((bf16[136,512]{1,0:T(8,128)(2,1)S(1)}, bf16[136,512]{1,0:T(8,128)(2,1)S(1)}, u32[]{:S(2)}, u32[]{:S(2)}) %collective-permute-start.2) | collective-permute-done | bytes 139296 | tf_op jit(solution)/shard_map/ppermute | solution.py:468
  18.1 1.3 %collective-permute-start.5 = (bf16[136,512]{1,0:T(8,128)(2,1)S(1)}, bf16[136,512]{1,0:T(8,128)(2,1)S(1)}, u32[]{:S(2)}, u32[]{:S(2)}) collective-permute-start(bf16[136,512]{1,0:T(8,128)(2,1)S(1)} %collective-permute-done.2.refs_3_), channel_id=1, source_target_pairs={{0,1},{1,0},{2,3},{3,2},{4,5},{5,4},{6,7},{7,6},{8,9},{9,8},{10,11... | collective-permute-start | bytes 417800 | tf_op jit(solution)/shard_map/ppermute | solution.py:468
  19.5 0.1 select_n.31.row_ids
  19.5 0.2 select_n.33.column_ids
  19.9 2.8 %collective-permute-done.6.refs_7_ = bf16[136,512]{1,0:T(8,128)(2,1)S(1)} collective-permute-done((bf16[136,512]{1,0:T(8,128)(2,1)S(1)}, bf16[136,512]{1,0:T(8,128)(2,1)S(1)}, u32[]{:S(2)}, u32[]{:S(2)}) %collective-permute-start.6) | collective-permute-done | bytes 139296 | tf_op jit(solution)/shard_map/ppermute | solution.py:468
  22.6 0.3 collective-permute-start.10
  22.9 2.7 %collective-permute-done.5.refs_6_ = bf16[136,512]{1,0:T(8,128)(2,1)S(1)} collective-permute-done((bf16[136,512]{1,0:T(8,128)(2,1)S(1)}, bf16[136,512]{1,0:T(8,128)(2,1)S(1)}, u32[]{:S(2)}, u32[]{:S(2)}) %collective-permute-start.5) | collective-permute-done | bytes 139296 | tf_op jit(solution)/shard_map/ppermute | solution.py:468
  25.6 1.0 shard_map.129
  26.6 2.0 %collective-permute-done.10.refs_3_.refs_12_ = bf16[136,512]{1,0:T(8,128)(2,1)S(1)} collective-permute-done((bf16[136,512]{1,0:T(8,128)(2,1)S(1)}, bf16[136,512]{1,0:T(8,128)(2,1)S(1)}, u32[]{:S(2)}, u32[]{:S(2)}) %collective-permute-start.10) | collective-permute-done | bytes 139296 | tf_op jit(solution)/shard_map/ppermute | solution.py:468
  28.6 0.9 collective-permute-done.9.refs_2_.refs_11_
  29.5 3.7 %shard_map.130 = (bf16[2,136,1024]{2,1,0:T(8,128)(2,1)S(1)}, f32[2,136,128]{2,1,0:T(8,128)S(1)}, f32[2,136,128]{2,1,0:T(8,128)S(1)}, bf16[1088,1088]{1,0:T(8,128...) custom-call(s32[1]{0:T(128)} %bitcast.me_ref, ...), custom_call_target="tpu_custom_call" | custom-call | flops 5000000000 | bytes 1024 | tf_op jit(solution)/shard_map/pallas_call | solution.py:200
  33.3 9.4 %all_to_all.10.slab_ref = bf16[8,80,128]{2,1,0:T(8,128)(2,1)S(1)} all-to-all(bf16[8,80,128]{2,1,0:T(8,128)(2,1)S(1)} %get-tuple-element.60), channel_id=1, replica_groups=mesh['section'=4,'seq'=8] {'seq'}, dimensions={0} | all-to-all | bytes 327680 | tf_op jit(solution)/shard_map/all_to_all | solution.py:476
  42.7 2.0 %shard_map.131 = (bf16[136,1024]{1,0:T(8,128)(2,1)S(1)}, bf16[8,80,128]{2,1,0:T(8,128)(2,1)S(1)}, bf16[256,1024]{1,0:T(8,128)(2,1)S(1)}, bf16[128,1024]{1,0:T(8,...) custom-call(s32[1]{0:T(128)} %bitcast.me_ref, ...), custom_call_target="tpu_custom_call" | custom-call | flops 3000000000 | bytes 1024 | tf_op jit(solution)/shard_map/pallas_call | solution.py:200
  44.6 8.8 %all_to_all.11.slab_ref = bf16[8,80,128]{2,1,0:T(8,128)(2,1)S(1)} all-to-all(bf16[8,80,128]{2,1,0:T(8,128)(2,1)S(1)} %get-tuple-element.61), channel_id=1, replica_groups=mesh['section'=4,'seq'=8] {'seq'}, dimensions={0} | all-to-all | bytes 327680 | tf_op jit(solution)/shard_map/all_to_all | solution.py:476
  53.5 1.6 %collective-permute-start.19 = (bf16[256,1024]{1,0:T(8,128)(2,1)S(1)}, bf16[256,1024]{1,0:T(8,128)(2,1)S(1)}, u32[]{:S(2)}, u32[]{:S(2)}) collective-permute-start(bf16[256,1024]{1,0:T(8,128)(2,1)S(1)} %get-tuple-element.94), channel_id=1, source_target_pairs={{0,1},{1,0},{2,3},{3,2},{4,5},{5,4},{6,7},{7,6},{8,9},{9,8},{10,11... | collective-permute-start | bytes 1572872 | tf_op jit(solution)/shard_map/ppermute | solution.py:22
  55.1 5.0 %shard_map.132 = (bf16[408,128]{1,0:T(8,128)(2,1)S(1)}, bf16[408,128]{1,0:T(8,128)(2,1)S(1)}, bf16[408,128]{1,0:T(8,128)(2,1)S(1)}, bf16[408,128]{1,0:T(8,128)(2...) custom-call(s32[1]{0:T(128)} %bitcast.me_ref, ...), custom_call_target="tpu_custom_call" | custom-call | flops 6000000000 | bytes 1024 | tf_op jit(solution)/shard_map/pallas_call | solution.py:200
  60.1 0.6 collective-permute-start.13
  60.7 3.0 %collective-permute-start.16 = (bf16[408,128]{1,0:T(8,128)(2,1)S(1)}, bf16[408,128]{1,0:T(8,128)(2,1)S(1)}, u32[]{:S(2)}, u32[]{:S(2)}) collective-permute-start(bf16[408,128]{1,0:T(8,128)(2,1)S(1)} %get-tuple-element.87), channel_id=1, source_target_pairs={{0,6},{1,7},{2,4},{3,5},{4,2},{5,3},{6,0},{7,1},{8,14},{9,15},{10,... | collective-permute-start | bytes 313352 | tf_op jit(solution)/shard_map/ppermute | solution.py:468
  63.7 0.9 collective-permute-start.17
  64.7 2.4 %collective-permute-done.16.refs_5_.refs_6_ = bf16[408,128]{1,0:T(8,128)(2,1)S(1)} collective-permute-done((bf16[408,128]{1,0:T(8,128)(2,1)S(1)}, bf16[408,128]{1,0:T(8,128)(2,1)S(1)}, u32[]{:S(2)}, u32[]{:S(2)}) %collective-permute-start.16) | collective-permute-done | bytes 104480 | tf_op jit(solution)/shard_map/ppermute | solution.py:468
  67.1 4.0 %collective-permute-done.17.refs_6_.refs_7_ = bf16[408,128]{1,0:T(8,128)(2,1)S(1)} collective-permute-done((bf16[408,128]{1,0:T(8,128)(2,1)S(1)}, bf16[408,128]{1,0:T(8,128)(2,1)S(1)}, u32[]{:S(2)}, u32[]{:S(2)}) %collective-permute-start.17) | collective-permute-done | bytes 104480 | tf_op jit(solution)/shard_map/ppermute | solution.py:468
  71.1 0.1 shard_map.133
  71.3 0.7 collective-permute-start.22
  72.0 0.8 collective-permute-start.12
  72.8 1.4 %collective-permute-start.18 = (bf16[136,1024]{1,0:T(8,128)(2,1)S(1)}, bf16[136,1024]{1,0:T(8,128)(2,1)S(1)}, u32[]{:S(2)}, u32[]{:S(2)}) collective-permute-start(bf16[136,1024]{1,0:T(8,128)(2,1)S(1)} %get-tuple-element.89), channel_id=1, source_target_pairs={{0,7},{1,6},{2,5},{3,4},{4,3},{5,2},{6,1},{7,0},{8,15},{9,14},{10,... | collective-permute-start | bytes 835592 | tf_op jit(solution)/shard_map/ppermute | solution.py:468
  74.2 1.5 %collective-permute-start.11 = (bf16[408,128]{1,0:T(8,128)(2,1)S(1)}, bf16[408,128]{1,0:T(8,128)(2,1)S(1)}, u32[]{:S(2)}, u32[]{:S(2)}) collective-permute-start(bf16[408,128]{1,0:T(8,128)(2,1)S(1)} %get-tuple-element.82), channel_id=1, source_target_pairs={{0,1},{1,0},{2,3},{3,2},{4,5},{5,4},{6,7},{7,6},{8,9},{9,8},{10,11... | collective-permute-start | bytes 313352 | tf_op jit(solution)/shard_map/ppermute | solution.py:468
  75.6 8.5 %collective-permute-done.12.refs_8_.refs_2_ = bf16[408,128]{1,0:T(8,128)(2,1)S(1)} collective-permute-done((bf16[408,128]{1,0:T(8,128)(2,1)S(1)}, bf16[408,128]{1,0:T(8,128)(2,1)S(1)}, u32[]{:S(2)}, u32[]{:S(2)}) %collective-permute-start.12) | collective-permute-done | bytes 104480 | tf_op jit(solution)/shard_map/ppermute | solution.py:468
  84.2 0.2 shard_map.134
  84.4 2.6 %collective-permute-start.25 = (bf16[64,1024]{1,0:T(8,128)(2,1)S(1)}, bf16[64,1024]{1,0:T(8,128)(2,1)S(1)}, u32[]{:S(2)}, u32[]{:S(2)}) collective-permute-start(bf16[64,1024]{1,0:T(8,128)(2,1)S(1)} %get-tuple-element.101), channel_id=1, source_target_pairs={{0,4},{4,0},{1,5},{5,1},{2,6},{6,2},{3,7},{7,3},{8,12},{12,8},{9,1... | collective-permute-start | bytes 393224 | tf_op jit(solution)/shard_map/ppermute | solution.py:22
  87.1 5.2 %collective-permute-done.14.refs_4_ = bf16[408,128]{1,0:T(8,128)(2,1)S(1)} collective-permute-done((bf16[408,128]{1,0:T(8,128)(2,1)S(1)}, bf16[408,128]{1,0:T(8,128)(2,1)S(1)}, u32[]{:S(2)}, u32[]{:S(2)}) %collective-permute-start.14) | collective-permute-done | bytes 104480 | tf_op jit(solution)/shard_map/ppermute | solution.py:468
  92.4 1.4 %shard_map.135 = bf16[136,1024]{1,0:T(8,128)(2,1)S(1)} custom-call(s32[1]{0:T(128)} %bitcast.me_ref, bf16[408,128]{1,0:T(8,128)(2,1)S(1)} %get-tuple-element.81.refs_0_, bf16[408,128]{1,0:T(8,128)(2,1)S(1)} %collective-permute-done.11.refs_1_, bf16[408,128]{1,0:T(8,128)(2,1)S(1)} %collective-permute-done.12.refs_8_.refs_2_, ...), custom_call_target="tpu_custom_call" | custom-call | flops 1500000000 | bytes 1024 | tf_op jit(solution)/shard_map/pallas_call | solution.py:200
  93.7 18.6 %collective-permute-start.23 = (bf16[136,1024]{1,0:T(8,128)(2,1)S(1)}, bf16[136,1024]{1,0:T(8,128)(2,1)S(1)}, u32[]{:S(2)}, u32[]{:S(2)}) collective-permute-start(bf16[136,1024]{1,0:T(8,128)(2,1)S(1)} %shard_map.135), channel_id=1, source_target_pairs={{8,0},{16,8},{24,16},{9,1},{17,9},{25,17},{10,2},{18,10},{26,18},{... | collective-permute-start | bytes 835592 | tf_op jit(solution)/shard_map/ppermute | solution.py:28
  112.4 0.8 shard_map.138
  113.2 1.0 shard_map.137
  114.2 3.5 %collective-permute-done.23.rows_ref = bf16[136,1024]{1,0:T(8,128)(2,1)S(1)} collective-permute-done((bf16[136,1024]{1,0:T(8,128)(2,1)S(1)}, bf16[136,1024]{1,0:T(8,128)(2,1)S(1)}, u32[]{:S(2)}, u32[]{:S(2)}) %collective-permute-start.23) | collective-permute-done | bytes 278560 | tf_op jit(solution)/shard_map/ppermute | solution.py:28
  117.7 1.0 shard_map.136
  (47 shorter events, 0.8 us)
Async XLA Ops:
  0.6 12.4 %collective-permute-start.1 = (bf16[136,1024]{1,0:T(8,128)(2,1)}, bf16[136,1024]{1,0:T(8,128)(2,1)S(1)}, u32[]{:S(2)}, u32[]{:S(2)}) collective-permute-start(bf16[136,1024]{1,0:T(8,128)(2,1)} %bitcast.7), channel_id=1, source_target_pairs={{0,2},{1,3},{2,0},{3,1},{4,6},{5,7},{6,4},{7,5},{8,10},{9,11},{10,... | collective-permute-start | bytes 835592 | tf_op jit(solution)/shard_map/ppermute | solution.py:468
  2.0 23.6 %collective-permute-start = (bf16[136,1024]{1,0:T(8,128)(2,1)}, bf16[136,1024]{1,0:T(8,128)(2,1)S(1)}, u32[]{:S(2)}, u32[]{:S(2)}) collective-permute-start(bf16[136,1024]{1,0:T(8,128)(2,1)} %bitcast.8), channel_id=1, source_target_pairs={{0,1},{1,0},{2,3},{3,2},{4,5},{5,4},{6,7},{7,6},{8,9},{9,8},{10,11... | collective-permute-start | bytes 835592 | tf_op jit(solution)/shard_map/ppermute | solution.py:468
  3.2 10.4 %collective-permute-start.3 = (bf16[136,512]{1,0:T(8,128)(2,1)S(1)}, bf16[136,512]{1,0:T(8,128)(2,1)S(1)}, u32[]{:S(2)}, u32[]{:S(2)}) collective-permute-start(bf16[136,512]{1,0:T(8,128)(2,1)S(1)} %get-tuple-element.109), channel_id=1, source_target_pairs={{0,4},{1,5},{2,6},{3,7},{4,0},{5,1},{6,2},{7,3},{8,12},{9,13},{10,... | collective-permute-start | bytes 417800 | tf_op jit(solution)/shard_map/ppermute | solution.py:468
  5.6 12.5 %collective-permute-start.2 = (bf16[136,512]{1,0:T(8,128)(2,1)S(1)}, bf16[136,512]{1,0:T(8,128)(2,1)S(1)}, u32[]{:S(2)}, u32[]{:S(2)}) collective-permute-start(bf16[136,512]{1,0:T(8,128)(2,1)S(1)} %get-tuple-element.110), channel_id=1, source_target_pairs={{0,4},{1,5},{2,6},{3,7},{4,0},{5,1},{6,2},{7,3},{8,12},{9,13},{10,... | collective-permute-start | bytes 417800 | tf_op jit(solution)/shard_map/ppermute | solution.py:468
  6.4 1.2 %copy-start.2 = (bf16[1,1024,512]{2,1,0:T(8,128)(2,1)S(1)}, bf16[1,1024,512]{2,1,0:T(8,128)(2,1)}, u32[]{:S(2)}) copy-start(bf16[1,1024,512]{2,1,0:T(8,128)(2,1)} %param.11) | copy-start | bytes 3145732
  7.6 1.2 %copy-start.4 = (bf16[1,1024,512]{2,1,0:T(8,128)(2,1)S(1)}, bf16[1,1024,512]{2,1,0:T(8,128)(2,1)}, u32[]{:S(2)}) copy-start(bf16[1,1024,512]{2,1,0:T(8,128)(2,1)} %param.12) | copy-start | bytes 3145732
  8.8 1.2 %copy-start.6 = (bf16[1,1024,512]{2,1,0:T(8,128)(2,1)S(1)}, bf16[1,1024,512]{2,1,0:T(8,128)(2,1)}, u32[]{:S(2)}) copy-start(bf16[1,1024,512]{2,1,0:T(8,128)(2,1)} %param.13) | copy-start | bytes 3145732
  10.0 3.0 %copy-start.10 = (s32[1088]{0:T(1024)S(1)}, s32[1088]{0:T(1024)}, u32[]{:S(2)}) copy-start(s32[1088]{0:T(1024)} %param.15) | copy-start | bytes 13060
  10.0 15.6 %copy-start = (bf16[1,136,1024]{2,1,0:T(8,128)(2,1)S(1)}, bf16[1,136,1024]{2,1,0:T(8,128)(2,1)}, u32[]{:S(2)}) copy-start(bf16[1,136,1024]{2,1,0:T(8,128)(2,1)} %param.9) | copy-start | bytes 835588
  13.0 12.6 %collective-permute-start.4 = (bf16[136,1024]{1,0:T(8,128)(2,1)S(1)}, bf16[136,1024]{1,0:T(8,128)(2,1)S(1)}, u32[]{:S(2)}, u32[]{:S(2)}) collective-permute-start(bf16[136,1024]{1,0:T(8,128)(2,1)S(1)} %collective-permute-done.1.refs_2_), channel_id=1, source_target_pairs={{0,1},{1,0},{2,3},{3,2},{4,5},{5,4},{6,7},{7,6},{8,9},{9,8},{10,11... | collective-permute-start | bytes 835592 | tf_op jit(solution)/shard_map/ppermute | solution.py:468
  13.7 6.1 %collective-permute-start.8 = (bf16[136,512]{1,0:T(8,128)(2,1)S(1)}, bf16[136,512]{1,0:T(8,128)(2,1)S(1)}, u32[]{:S(2)}, u32[]{:S(2)}) collective-permute-start(bf16[136,512]{1,0:T(8,128)(2,1)S(1)} %collective-permute-done.3.refs_4_), channel_id=1, source_target_pairs={{0,2},{1,3},{2,0},{3,1},{4,6},{5,7},{6,4},{7,5},{8,10},{9,11},{10,... | collective-permute-start | bytes 417800 | tf_op jit(solution)/shard_map/ppermute | solution.py:468
  13.8 8.8 %collective-permute-start.6 = (bf16[136,512]{1,0:T(8,128)(2,1)S(1)}, bf16[136,512]{1,0:T(8,128)(2,1)S(1)}, u32[]{:S(2)}, u32[]{:S(2)}) collective-permute-start(bf16[136,512]{1,0:T(8,128)(2,1)S(1)} %collective-permute-done.3.refs_4_), channel_id=1, source_target_pairs={{0,1},{1,0},{2,3},{3,2},{4,5},{5,4},{6,7},{7,6},{8,9},{9,8},{10,11... | collective-permute-start | bytes 417800 | tf_op jit(solution)/shard_map/ppermute | solution.py:468
  18.1 7.5 %collective-permute-start.5 = (bf16[136,512]{1,0:T(8,128)(2,1)S(1)}, bf16[136,512]{1,0:T(8,128)(2,1)S(1)}, u32[]{:S(2)}, u32[]{:S(2)}) collective-permute-start(bf16[136,512]{1,0:T(8,128)(2,1)S(1)} %collective-permute-done.2.refs_3_), channel_id=1, source_target_pairs={{0,1},{1,0},{2,3},{3,2},{4,5},{5,4},{6,7},{7,6},{8,9},{9,8},{10,11... | collective-permute-start | bytes 417800 | tf_op jit(solution)/shard_map/ppermute | solution.py:468
  19.8 6.8 %collective-permute-start.7 = (bf16[136,512]{1,0:T(8,128)(2,1)S(1)}, bf16[136,512]{1,0:T(8,128)(2,1)S(1)}, u32[]{:S(2)}, u32[]{:S(2)}) collective-permute-start(bf16[136,512]{1,0:T(8,128)(2,1)S(1)} %collective-permute-done.2.refs_3_), channel_id=1, source_target_pairs={{0,2},{1,3},{2,0},{3,1},{4,6},{5,7},{6,4},{7,5},{8,10},{9,11},{10,... | collective-permute-start | bytes 417800 | tf_op jit(solution)/shard_map/ppermute | solution.py:468
  22.6 6.0 %collective-permute-start.10 = (bf16[136,512]{1,0:T(8,128)(2,1)S(1)}, bf16[136,512]{1,0:T(8,128)(2,1)S(1)}, u32[]{:S(2)}, u32[]{:S(2)}) collective-permute-start(bf16[136,512]{1,0:T(8,128)(2,1)S(1)} %collective-permute-done.8.refs_1_), channel_id=1, source_target_pairs={{0,1},{1,0},{2,3},{3,2},{4,5},{5,4},{6,7},{7,6},{8,9},{9,8},{10,11... | collective-permute-start | bytes 417800 | tf_op jit(solution)/shard_map/ppermute | solution.py:468
  25.6 3.9 %collective-permute-start.9 = (bf16[136,512]{1,0:T(8,128)(2,1)S(1)}, bf16[136,512]{1,0:T(8,128)(2,1)S(1)}, u32[]{:S(2)}, u32[]{:S(2)}) collective-permute-start(bf16[136,512]{1,0:T(8,128)(2,1)S(1)} %collective-permute-done.5.refs_6_), channel_id=1, source_target_pairs={{0,2},{1,3},{2,0},{3,1},{4,6},{5,7},{6,4},{7,5},{8,10},{9,11},{10,... | collective-permute-start | bytes 417800 | tf_op jit(solution)/shard_map/ppermute | solution.py:468
  29.5 13.2 %copy-start.1 = (bf16[1,512,2048]{2,1,0:T(8,128)(2,1)S(1)}, bf16[1,512,2048]{2,1,0:T(8,128)(2,1)}, u32[]{:S(2)}) copy-start(bf16[1,512,2048]{2,1,0:T(8,128)(2,1)} %param.14) | copy-start | bytes 6291460
  29.5 13.2 %copy-start.8 = (bf16[1,136,1024]{2,1,0:T(8,128)(2,1)S(1)}, bf16[1,136,1024]{2,1,0:T(8,128)(2,1)}, u32[]{:S(2)}) copy-start(bf16[1,136,1024]{2,1,0:T(8,128)(2,1)} %param.10) | copy-start | bytes 835588
  53.5 17.6 %collective-permute-start.19 = (bf16[256,1024]{1,0:T(8,128)(2,1)S(1)}, bf16[256,1024]{1,0:T(8,128)(2,1)S(1)}, u32[]{:S(2)}, u32[]{:S(2)}) collective-permute-start(bf16[256,1024]{1,0:T(8,128)(2,1)S(1)} %get-tuple-element.94), channel_id=1, source_target_pairs={{0,1},{1,0},{2,3},{3,2},{4,5},{5,4},{6,7},{7,6},{8,9},{9,8},{10,11... | collective-permute-start | bytes 1572872 | tf_op jit(solution)/shard_map/ppermute | solution.py:22
  55.1 16.0 %collective-permute-start.20 = (bf16[256,1024]{1,0:T(8,128)(2,1)S(1)}, bf16[256,1024]{1,0:T(8,128)(2,1)S(1)}, u32[]{:S(2)}, u32[]{:S(2)}) collective-permute-start(bf16[256,1024]{1,0:T(8,128)(2,1)S(1)} %get-tuple-element.95), channel_id=1, source_target_pairs={{0,2},{2,0},{1,3},{3,1},{4,6},{6,4},{5,7},{7,5},{8,10},{10,8},{9,1... | collective-permute-start | bytes 1572872 | tf_op jit(solution)/shard_map/ppermute | solution.py:22
  60.1 4.6 %collective-permute-start.13 = (bf16[408,128]{1,0:T(8,128)(2,1)S(1)}, bf16[408,128]{1,0:T(8,128)(2,1)S(1)}, u32[]{:S(2)}, u32[]{:S(2)}) collective-permute-start(bf16[408,128]{1,0:T(8,128)(2,1)S(1)} %get-tuple-element.84), channel_id=1, source_target_pairs={{0,4},{1,5},{2,6},{3,7},{4,0},{5,1},{6,2},{7,3},{8,12},{9,13},{10,... | collective-permute-start | bytes 313352 | tf_op jit(solution)/shard_map/ppermute | solution.py:468
  60.7 6.4 %collective-permute-start.16 = (bf16[408,128]{1,0:T(8,128)(2,1)S(1)}, bf16[408,128]{1,0:T(8,128)(2,1)S(1)}, u32[]{:S(2)}, u32[]{:S(2)}) collective-permute-start(bf16[408,128]{1,0:T(8,128)(2,1)S(1)} %get-tuple-element.87), channel_id=1, source_target_pairs={{0,6},{1,7},{2,4},{3,5},{4,2},{5,3},{6,0},{7,1},{8,14},{9,15},{10,... | collective-permute-start | bytes 313352 | tf_op jit(solution)/shard_map/ppermute | solution.py:468
  63.7 7.4 %collective-permute-start.17 = (bf16[408,128]{1,0:T(8,128)(2,1)S(1)}, bf16[408,128]{1,0:T(8,128)(2,1)S(1)}, u32[]{:S(2)}, u32[]{:S(2)}) collective-permute-start(bf16[408,128]{1,0:T(8,128)(2,1)S(1)} %get-tuple-element.88), channel_id=1, source_target_pairs={{0,7},{1,6},{2,5},{3,4},{4,3},{5,2},{6,1},{7,0},{8,15},{9,14},{10,... | collective-permute-start | bytes 313352 | tf_op jit(solution)/shard_map/ppermute | solution.py:468
  71.2 12.9 %collective-permute-start.21 = (bf16[128,1024]{1,0:T(8,128)(2,1)S(1)}, bf16[128,1024]{1,0:T(8,128)(2,1)S(1)}, u32[]{:S(2)}, u32[]{:S(2)}) collective-permute-start(bf16[128,1024]{1,0:T(8,128)(2,1)S(1)} %get-tuple-element.98), channel_id=1, source_target_pairs={{0,2},{2,0},{1,3},{3,1},{4,6},{6,4},{5,7},{7,5},{8,10},{10,8},{9,1... | collective-permute-start | bytes 786440 | tf_op jit(solution)/shard_map/ppermute | solution.py:22
  71.3 12.9 %collective-permute-start.22 = (bf16[128,1024]{1,0:T(8,128)(2,1)S(1)}, bf16[128,1024]{1,0:T(8,128)(2,1)S(1)}, u32[]{:S(2)}, u32[]{:S(2)}) collective-permute-start(bf16[128,1024]{1,0:T(8,128)(2,1)S(1)} %get-tuple-element.99), channel_id=1, source_target_pairs={{0,1},{1,0},{2,3},{3,2},{4,5},{5,4},{6,7},{7,6},{8,9},{9,8},{10,11... | collective-permute-start | bytes 786440 | tf_op jit(solution)/shard_map/ppermute | solution.py:22
  72.0 12.1 %collective-permute-start.12 = (bf16[408,128]{1,0:T(8,128)(2,1)S(1)}, bf16[408,128]{1,0:T(8,128)(2,1)S(1)}, u32[]{:S(2)}, u32[]{:S(2)}) collective-permute-start(bf16[408,128]{1,0:T(8,128)(2,1)S(1)} %get-tuple-element.83), channel_id=1, source_target_pairs={{0,2},{1,3},{2,0},{3,1},{4,6},{5,7},{6,4},{7,5},{8,10},{9,11},{10,... | collective-permute-start | bytes 313352 | tf_op jit(solution)/shard_map/ppermute | solution.py:468
  72.8 19.6 %collective-permute-start.18 = (bf16[136,1024]{1,0:T(8,128)(2,1)S(1)}, bf16[136,1024]{1,0:T(8,128)(2,1)S(1)}, u32[]{:S(2)}, u32[]{:S(2)}) collective-permute-start(bf16[136,1024]{1,0:T(8,128)(2,1)S(1)} %get-tuple-element.89), channel_id=1, source_target_pairs={{0,7},{1,6},{2,5},{3,4},{4,3},{5,2},{6,1},{7,0},{8,15},{9,14},{10,... | collective-permute-start | bytes 835592 | tf_op jit(solution)/shard_map/ppermute | solution.py:468
  74.2 12.9 %collective-permute-start.11 = (bf16[408,128]{1,0:T(8,128)(2,1)S(1)}, bf16[408,128]{1,0:T(8,128)(2,1)S(1)}, u32[]{:S(2)}, u32[]{:S(2)}) collective-permute-start(bf16[408,128]{1,0:T(8,128)(2,1)S(1)} %get-tuple-element.82), channel_id=1, source_target_pairs={{0,1},{1,0},{2,3},{3,2},{4,5},{5,4},{6,7},{7,6},{8,9},{9,8},{10,11... | collective-permute-start | bytes 313352 | tf_op jit(solution)/shard_map/ppermute | solution.py:468
  84.1 8.2 %collective-permute-start.14 = (bf16[408,128]{1,0:T(8,128)(2,1)S(1)}, bf16[408,128]{1,0:T(8,128)(2,1)S(1)}, u32[]{:S(2)}, u32[]{:S(2)}) collective-permute-start(bf16[408,128]{1,0:T(8,128)(2,1)S(1)} %get-tuple-element.85), channel_id=1, source_target_pairs={{0,3},{1,2},{2,1},{3,0},{4,7},{5,6},{6,5},{7,4},{8,11},{9,10},{10,... | collective-permute-start | bytes 313352 | tf_op jit(solution)/shard_map/ppermute | solution.py:468
  84.1 8.2 %copy-start.3 = (bf16[1,1024,512]{2,1,0:T(8,128)(2,1)S(1)}, bf16[1,1024,512]{2,1,0:T(8,128)(2,1)}, u32[]{:S(2)}) copy-start(bf16[1,1024,512]{2,1,0:T(8,128)(2,1)} %param.11) | copy-start | bytes 3145732
  84.1 8.2 %copy-start.5 = (bf16[1,1024,512]{2,1,0:T(8,128)(2,1)S(1)}, bf16[1,1024,512]{2,1,0:T(8,128)(2,1)}, u32[]{:S(2)}) copy-start(bf16[1,1024,512]{2,1,0:T(8,128)(2,1)} %param.12) | copy-start | bytes 3145732
  84.1 8.2 %copy-start.7 = (bf16[1,1024,512]{2,1,0:T(8,128)(2,1)S(1)}, bf16[1,1024,512]{2,1,0:T(8,128)(2,1)}, u32[]{:S(2)}) copy-start(bf16[1,1024,512]{2,1,0:T(8,128)(2,1)} %param.13) | copy-start | bytes 3145732
  84.1 8.2 %collective-permute-start.15 = (bf16[408,128]{1,0:T(8,128)(2,1)S(1)}, bf16[408,128]{1,0:T(8,128)(2,1)S(1)}, u32[]{:S(2)}, u32[]{:S(2)}) collective-permute-start(bf16[408,128]{1,0:T(8,128)(2,1)S(1)} %get-tuple-element.86), channel_id=1, source_target_pairs={{0,5},{1,4},{2,7},{3,6},{4,1},{5,0},{6,3},{7,2},{8,13},{9,12},{10,... | collective-permute-start | bytes 313352 | tf_op jit(solution)/shard_map/ppermute | solution.py:468
  84.4 27.9 %collective-permute-start.25 = (bf16[64,1024]{1,0:T(8,128)(2,1)S(1)}, bf16[64,1024]{1,0:T(8,128)(2,1)S(1)}, u32[]{:S(2)}, u32[]{:S(2)}) collective-permute-start(bf16[64,1024]{1,0:T(8,128)(2,1)S(1)} %get-tuple-element.101), channel_id=1, source_target_pairs={{0,4},{4,0},{1,5},{5,1},{2,6},{6,2},{3,7},{7,3},{8,12},{12,8},{9,1... | collective-permute-start | bytes 393224 | tf_op jit(solution)/shard_map/ppermute | solution.py:22
  87.0 25.3 %collective-permute-start.24 = (bf16[64,1024]{1,0:T(8,128)(2,1)S(1)}, bf16[64,1024]{1,0:T(8,128)(2,1)S(1)}, u32[]{:S(2)}, u32[]{:S(2)}) collective-permute-start(bf16[64,1024]{1,0:T(8,128)(2,1)S(1)} %get-tuple-element.100.refs_14_), channel_id=1, source_target_pairs={{0,4},{4,0},{1,5},{5,1},{2,6},{6,2},{3,7},{7,3},{8,12},{12,8},{9,1... | collective-permute-start | bytes 393224 | tf_op jit(solution)/shard_map/ppermute | solution.py:22
  93.7 23.9 %collective-permute-start.23 = (bf16[136,1024]{1,0:T(8,128)(2,1)S(1)}, bf16[136,1024]{1,0:T(8,128)(2,1)S(1)}, u32[]{:S(2)}, u32[]{:S(2)}) collective-permute-start(bf16[136,1024]{1,0:T(8,128)(2,1)S(1)} %shard_map.135), channel_id=1, source_target_pairs={{8,0},{16,8},{24,16},{9,1},{17,9},{25,17},{10,2},{18,10},{26,18},{... | collective-permute-start | bytes 835592 | tf_op jit(solution)/shard_map/ppermute | solution.py:28
  113.2 4.5 %copy-start.9 = (s32[1,136]{1,0:T(1,128)S(1)}, s32[1,136]{1,0:T(1,128)}, u32[]{:S(2)}) copy-start(s32[1,136]{1,0:T(1,128)} %order_ref.1) | copy-start | bytes 1636

commit v14 on v13

--- a/solution.py
+++ b/solution.py
@@ -597,7 +597,7 @@
     *leaving, keep_a, keep_b = call(
         third_sum_kernel,
         2,
-        [("v", x) for x in (*third, *keep, *got, *more)] + [("a", slabs[2])],
+        [("v", x) for x in (*third, *keep, *got, *more)] + [("a", slabs[5])],
         [out(*third[0].shape)] * 2 + [out(*keep[0].shape, dtype=f32)] * 2,
     )
     rest = [partner(part, "seq", 2) for part in leaving]

time: 119 us -> 120 us (level)
  the two profiles are of different devices: /device:TPU:3 before, /device:TPU:1 now
where the time goes in v14:
time: 120 us; the launch traced here: 119 us
  starting transfers between devices  45.3 us (38%)
  waiting for transfers between devices  30.9 us (26%)
  blocking collectives  19.3 us (16%)
  Pallas kernels  16.7 us (14%)
  local copies, waits for them, and re-layouts  5.65 us (5%)
    ppermute x19, waiting for transfers between devices, hop(): return lax.ppermute(block, 'seq', route)  27.5 us
    ppermute x19, starting transfers between devices, hop(): return lax.ppermute(block, 'seq', route)  20.2 us
    ppermute x1, starting transfers between devices, shifted(): return lax.ppermute(block, axis, route)  20.2 us
    all_to_all x2, blocking collectives, switch(): return lax.all_to_all(slabs, 'seq', split_axis=0, concat_axis=0, tiled=True)  19.3 us
    pallas_call x11, Pallas kernels, call(): pl.pallas_call(kernel, out_shape=tuple(outs), in_specs=[pl.BlockSpec(memo...  16.7 us
    ppermute x6, starting transfers between devices, partner(): return lax.ppermute(block, axis, route)  4.9 us
    unnamed x22, local copies, waits for them, and re-layouts  3.71 us
    ppermute x1, waiting for transfers between devices, shifted(): return lax.ppermute(block, axis, route)  3.46 us
  transfers between devices with their start and end apart: 26, of which 11 were waited for; matrix products, arithmetic and copies ran while one was open for 2% of the time, Pallas kernels for 8%

profile of v14, /device:TPU:1, one launch (start us, length us, event | category | flops | bytes accessed | tf_op | source)
XLA Modules:
  0.0 119.4 jit_solution(12671653126819778067)
XLA Ops:
  0.6 2.2 %collective-permute-start.1 = (bf16[136,1024]{1,0:T(8,128)(2,1)}, bf16[136,1024]{1,0:T(8,128)(2,1)S(1)}, u32[]{:S(2)}, u32[]{:S(2)}) collective-permute-start(bf16[136,1024]{1,0:T(8,128)(2,1)} %bitcast.7), channel_id=1, source_target_pairs={{0,2},{1,3},{2,0},{3,1},{4,6},{5,7},{6,4},{7,5},{8,10},{9,11},{10,... | collective-permute-start | bytes 835592 | tf_op jit(solution)/shard_map/ppermute | solution.py:468
  2.8 1.2 %collective-permute-start = (bf16[136,1024]{1,0:T(8,128)(2,1)}, bf16[136,1024]{1,0:T(8,128)(2,1)S(1)}, u32[]{:S(2)}, u32[]{:S(2)}) collective-permute-start(bf16[136,1024]{1,0:T(8,128)(2,1)} %bitcast.8), channel_id=1, source_target_pairs={{0,1},{1,0},{2,3},{3,2},{4,5},{5,4},{6,7},{7,6},{8,9},{9,8},{10,11... | collective-permute-start | bytes 835592 | tf_op jit(solution)/shard_map/ppermute | solution.py:468
  4.0 1.0 fusion
  5.0 2.4 %collective-permute-start.3 = (bf16[136,512]{1,0:T(8,128)(2,1)S(1)}, bf16[136,512]{1,0:T(8,128)(2,1)S(1)}, u32[]{:S(2)}, u32[]{:S(2)}) collective-permute-start(bf16[136,512]{1,0:T(8,128)(2,1)S(1)} %get-tuple-element.109), channel_id=1, source_target_pairs={{0,4},{1,5},{2,6},{3,7},{4,0},{5,1},{6,2},{7,3},{8,12},{9,13},{10,... | collective-permute-start | bytes 417800 | tf_op jit(solution)/shard_map/ppermute | solution.py:468
  7.5 0.7 compare_and_fusion
  8.2 1.2 %copy-done.2 = bf16[1,1024,512]{2,1,0:T(8,128)(2,1)S(1)} copy-done((bf16[1,1024,512]{2,1,0:T(8,128)(2,1)S(1)}, bf16[1,1024,512]{2,1,0:T(8,128)(2,1)}, u32[]{:S(2)}) %copy-start.2) | copy-done | bytes 1048600
  9.4 1.2 %copy-done.4 = bf16[1,1024,512]{2,1,0:T(8,128)(2,1)S(1)} copy-done((bf16[1,1024,512]{2,1,0:T(8,128)(2,1)S(1)}, bf16[1,1024,512]{2,1,0:T(8,128)(2,1)}, u32[]{:S(2)}) %copy-start.4) | copy-done | bytes 1048600
  10.6 1.2 %copy-done.6 = bf16[1,1024,512]{2,1,0:T(8,128)(2,1)S(1)} copy-done((bf16[1,1024,512]{2,1,0:T(8,128)(2,1)S(1)}, bf16[1,1024,512]{2,1,0:T(8,128)(2,1)}, u32[]{:S(2)}) %copy-start.6) | copy-done | bytes 1048600
  11.8 0.5 shard_map.128.refs_8_.weight_ref
  12.3 2.7 %collective-permute-start.4 = (bf16[136,1024]{1,0:T(8,128)(2,1)S(1)}, bf16[136,1024]{1,0:T(8,128)(2,1)S(1)}, u32[]{:S(2)}, u32[]{:S(2)}) collective-permute-start(bf16[136,1024]{1,0:T(8,128)(2,1)S(1)} %collective-permute-done.1.refs_2_), channel_id=1, source_target_pairs={{0,1},{1,0},{2,3},{3,2},{4,5},{5,4},{6,7},{7,6},{8,9},{9,8},{10,11... | collective-permute-start | bytes 835592 | tf_op jit(solution)/shard_map/ppermute | solution.py:468
  15.2 0.6 gather_fusion
  15.9 4.1 %collective-permute-done.2.refs_3_ = bf16[136,512]{1,0:T(8,128)(2,1)S(1)} collective-permute-done((bf16[136,512]{1,0:T(8,128)(2,1)S(1)}, bf16[136,512]{1,0:T(8,128)(2,1)S(1)}, u32[]{:S(2)}, u32[]{:S(2)}) %collective-permute-start.2) | collective-permute-done | bytes 139296 | tf_op jit(solution)/shard_map/ppermute | solution.py:468
  20.0 0.2 collective-permute-start.5
  20.3 0.2 select_n.33.column_ids
  20.5 1.8 %collective-permute-done.8.refs_1_ = bf16[136,512]{1,0:T(8,128)(2,1)S(1)} collective-permute-done((bf16[136,512]{1,0:T(8,128)(2,1)S(1)}, bf16[136,512]{1,0:T(8,128)(2,1)S(1)}, u32[]{:S(2)}, u32[]{:S(2)}) %collective-permute-start.8) | collective-permute-done | bytes 139296 | tf_op jit(solution)/shard_map/ppermute | solution.py:468
  22.3 1.1 collective-permute-done.6.refs_7_
  23.5 1.2 collective-permute-start.10
  24.6 1.8 %collective-permute-done.5.refs_6_ = bf16[136,512]{1,0:T(8,128)(2,1)S(1)} collective-permute-done((bf16[136,512]{1,0:T(8,128)(2,1)S(1)}, bf16[136,512]{1,0:T(8,128)(2,1)S(1)}, u32[]{:S(2)}, u32[]{:S(2)}) %collective-permute-start.5) | collective-permute-done | bytes 139296 | tf_op jit(solution)/shard_map/ppermute | solution.py:468
  26.5 1.0 shard_map.129
  27.5 2.0 %collective-permute-done.10.refs_3_.refs_12_ = bf16[136,512]{1,0:T(8,128)(2,1)S(1)} collective-permute-done((bf16[136,512]{1,0:T(8,128)(2,1)S(1)}, bf16[136,512]{1,0:T(8,128)(2,1)S(1)}, u32[]{:S(2)}, u32[]{:S(2)}) %collective-permute-start.10) | collective-permute-done | bytes 139296 | tf_op jit(solution)/shard_map/ppermute | solution.py:468
  29.4 1.2 %collective-permute-done.9.refs_2_.refs_11_ = bf16[136,512]{1,0:T(8,128)(2,1)S(1)} collective-permute-done((bf16[136,512]{1,0:T(8,128)(2,1)S(1)}, bf16[136,512]{1,0:T(8,128)(2,1)S(1)}, u32[]{:S(2)}, u32[]{:S(2)}) %collective-permute-start.9) | collective-permute-done | bytes 139296 | tf_op jit(solution)/shard_map/ppermute | solution.py:468
  30.7 3.7 %shard_map.130 = (bf16[2,136,1024]{2,1,0:T(8,128)(2,1)S(1)}, f32[2,136,128]{2,1,0:T(8,128)S(1)}, f32[2,136,128]{2,1,0:T(8,128)S(1)}, bf16[1088,1088]{1,0:T(8,128...) custom-call(s32[1]{0:T(128)} %bitcast.me_ref, ...), custom_call_target="tpu_custom_call" | custom-call | flops 5000000000 | bytes 1024 | tf_op jit(solution)/shard_map/pallas_call | solution.py:200
  34.4 10.4 %all_to_all.10.slab_ref = bf16[8,80,128]{2,1,0:T(8,128)(2,1)S(1)} all-to-all(bf16[8,80,128]{2,1,0:T(8,128)(2,1)S(1)} %get-tuple-element.60), channel_id=1, replica_groups=mesh['section'=4,'seq'=8] {'seq'}, dimensions={0} | all-to-all | bytes 327680 | tf_op jit(solution)/shard_map/all_to_all | solution.py:476
  44.9 2.0 %shard_map.131 = (bf16[136,1024]{1,0:T(8,128)(2,1)S(1)}, bf16[8,80,128]{2,1,0:T(8,128)(2,1)S(1)}, bf16[256,1024]{1,0:T(8,128)(2,1)S(1)}, bf16[128,1024]{1,0:T(8,...) custom-call(s32[1]{0:T(128)} %bitcast.me_ref, ...), custom_call_target="tpu_custom_call" | custom-call | flops 3000000000 | bytes 1024 | tf_op jit(solution)/shard_map/pallas_call | solution.py:200
  46.8 8.8 %all_to_all.11.slab_ref = bf16[8,80,128]{2,1,0:T(8,128)(2,1)S(1)} all-to-all(bf16[8,80,128]{2,1,0:T(8,128)(2,1)S(1)} %get-tuple-element.61), channel_id=1, replica_groups=mesh['section'=4,'seq'=8] {'seq'}, dimensions={0} | all-to-all | bytes 327680 | tf_op jit(solution)/shard_map/all_to_all | solution.py:476
  55.7 0.8 collective-permute-start.20
  56.4 5.0 %shard_map.132 = (bf16[408,128]{1,0:T(8,128)(2,1)S(1)}, bf16[408,128]{1,0:T(8,128)(2,1)S(1)}, bf16[408,128]{1,0:T(8,128)(2,1)S(1)}, bf16[408,128]{1,0:T(8,128)(2...) custom-call(s32[1]{0:T(128)} %bitcast.me_ref, ...), custom_call_target="tpu_custom_call" | custom-call | flops 6000000000 | bytes 1024 | tf_op jit(solution)/shard_map/pallas_call | solution.py:200
  61.4 0.8 collective-permute-start.13
  62.2 2.1 %collective-permute-start.16 = (bf16[408,128]{1,0:T(8,128)(2,1)S(1)}, bf16[408,128]{1,0:T(8,128)(2,1)S(1)}, u32[]{:S(2)}, u32[]{:S(2)}) collective-permute-start(bf16[408,128]{1,0:T(8,128)(2,1)S(1)} %get-tuple-element.87), channel_id=1, source_target_pairs={{0,6},{1,7},{2,4},{3,5},{4,2},{5,3},{6,0},{7,1},{8,14},{9,15},{10,... | collective-permute-start | bytes 313352 | tf_op jit(solution)/shard_map/ppermute | solution.py:468
  64.3 1.5 %collective-permute-start.17 = (bf16[408,128]{1,0:T(8,128)(2,1)S(1)}, bf16[408,128]{1,0:T(8,128)(2,1)S(1)}, u32[]{:S(2)}, u32[]{:S(2)}) collective-permute-start(bf16[408,128]{1,0:T(8,128)(2,1)S(1)} %get-tuple-element.88), channel_id=1, source_target_pairs={{0,7},{1,6},{2,5},{3,4},{4,3},{5,2},{6,1},{7,0},{8,15},{9,14},{10,... | collective-permute-start | bytes 313352 | tf_op jit(solution)/shard_map/ppermute | solution.py:468
  65.7 2.5 %collective-permute-done.13.refs_4_.refs_3_ = bf16[408,128]{1,0:T(8,128)(2,1)S(1)} collective-permute-done((bf16[408,128]{1,0:T(8,128)(2,1)S(1)}, bf16[408,128]{1,0:T(8,128)(2,1)S(1)}, u32[]{:S(2)}, u32[]{:S(2)}) %collective-permute-start.13) | collective-permute-done | bytes 104480 | tf_op jit(solution)/shard_map/ppermute | solution.py:468
  68.2 3.4 %collective-permute-done.17.refs_6_.refs_7_ = bf16[408,128]{1,0:T(8,128)(2,1)S(1)} collective-permute-done((bf16[408,128]{1,0:T(8,128)(2,1)S(1)}, bf16[408,128]{1,0:T(8,128)(2,1)S(1)}, u32[]{:S(2)}, u32[]{:S(2)}) %collective-permute-start.17) | collective-permute-done | bytes 104480 | tf_op jit(solution)/shard_map/ppermute | solution.py:468
  71.7 0.8 collective-permute-start.21
  72.6 0.9 collective-permute-start.22
  73.4 1.6 %collective-permute-start.15 = (bf16[408,128]{1,0:T(8,128)(2,1)S(1)}, bf16[408,128]{1,0:T(8,128)(2,1)S(1)}, u32[]{:S(2)}, u32[]{:S(2)}) collective-permute-start(bf16[408,128]{1,0:T(8,128)(2,1)S(1)} %get-tuple-element.86), channel_id=1, source_target_pairs={{0,5},{1,4},{2,7},{3,6},{4,1},{5,0},{6,3},{7,2},{8,13},{9,12},{10,... | collective-permute-start | bytes 313352 | tf_op jit(solution)/shard_map/ppermute | solution.py:468
  75.0 2.8 %collective-permute-start.18 = (bf16[136,1024]{1,0:T(8,128)(2,1)S(1)}, bf16[136,1024]{1,0:T(8,128)(2,1)S(1)}, u32[]{:S(2)}, u32[]{:S(2)}) collective-permute-start(bf16[136,1024]{1,0:T(8,128)(2,1)S(1)} %get-tuple-element.89), channel_id=1, source_target_pairs={{0,7},{1,6},{2,5},{3,4},{4,3},{5,2},{6,1},{7,0},{8,15},{9,14},{10,... | collective-permute-start | bytes 835592 | tf_op jit(solution)/shard_map/ppermute | solution.py:468
  77.8 8.9 %collective-permute-done.15.refs_8_.refs_5_ = bf16[408,128]{1,0:T(8,128)(2,1)S(1)} collective-permute-done((bf16[408,128]{1,0:T(8,128)(2,1)S(1)}, bf16[408,128]{1,0:T(8,128)(2,1)S(1)}, u32[]{:S(2)}, u32[]{:S(2)}) %collective-permute-start.15) | collective-permute-done | bytes 104480 | tf_op jit(solution)/shard_map/ppermute | solution.py:468
  86.7 1.4 %collective-permute-start.14 = (bf16[408,128]{1,0:T(8,128)(2,1)S(1)}, bf16[408,128]{1,0:T(8,128)(2,1)S(1)}, u32[]{:S(2)}, u32[]{:S(2)}) collective-permute-start(bf16[408,128]{1,0:T(8,128)(2,1)S(1)} %get-tuple-element.85), channel_id=1, source_target_pairs={{0,3},{1,2},{2,1},{3,0},{4,7},{5,6},{6,5},{7,4},{8,11},{9,10},{10,... | collective-permute-start | bytes 313352 | tf_op jit(solution)/shard_map/ppermute | solution.py:468
  88.1 0.2 shard_map.134
  88.3 0.3 collective-permute-start.25
  88.6 2.2 %collective-permute-start.24 = (bf16[64,1024]{1,0:T(8,128)(2,1)S(1)}, bf16[64,1024]{1,0:T(8,128)(2,1)S(1)}, u32[]{:S(2)}, u32[]{:S(2)}) collective-permute-start(bf16[64,1024]{1,0:T(8,128)(2,1)S(1)} %get-tuple-element.100.refs_14_), channel_id=1, source_target_pairs={{0,4},{4,0},{1,5},{5,1},{2,6},{6,2},{3,7},{7,3},{8,12},{12,8},{9,1... | collective-permute-start | bytes 393224 | tf_op jit(solution)/shard_map/ppermute | solution.py:22
  90.8 0.7 collective-permute-done.12.refs_2_
  91.5 1.4 %shard_map.135 = bf16[136,1024]{1,0:T(8,128)(2,1)S(1)} custom-call(s32[1]{0:T(128)} %bitcast.me_ref, bf16[408,128]{1,0:T(8,128)(2,1)S(1)} %get-tuple-element.81.refs_0_, bf16[408,128]{1,0:T(8,128)(2,1)S(1)} %collective-permute-done.11.refs_1_, bf16[408,128]{1,0:T(8,128)(2,1)S(1)} %collective-permute-done.12.refs_2_, ...), custom_call_target="tpu_custom_call" | custom-call | flops 1500000000 | bytes 1024 | tf_op jit(solution)/shard_map/pallas_call | solution.py:200
  92.8 20.2 %collective-permute-start.23 = (bf16[136,1024]{1,0:T(8,128)(2,1)S(1)}, bf16[136,1024]{1,0:T(8,128)(2,1)S(1)}, u32[]{:S(2)}, u32[]{:S(2)}) collective-permute-start(bf16[136,1024]{1,0:T(8,128)(2,1)S(1)} %shard_map.135), channel_id=1, source_target_pairs={{8,0},{16,8},{24,16},{9,1},{17,9},{25,17},{10,2},{18,10},{26,18},{... | collective-permute-start | bytes 835592 | tf_op jit(solution)/shard_map/ppermute | solution.py:28
  113.1 0.8 shard_map.138
  113.9 1.0 shard_map.137
  114.9 3.5 %collective-permute-done.23.rows_ref = bf16[136,1024]{1,0:T(8,128)(2,1)S(1)} collective-permute-done((bf16[136,1024]{1,0:T(8,128)(2,1)S(1)}, bf16[136,1024]{1,0:T(8,128)(2,1)S(1)}, u32[]{:S(2)}, u32[]{:S(2)}) %collective-permute-start.23) | collective-permute-done | bytes 278560 | tf_op jit(solution)/shard_map/ppermute | solution.py:28
  118.4 1.0 shard_map.136
  (47 shorter events, 0.7 us)
Async XLA Ops:
  0.6 11.7 %collective-permute-start.1 = (bf16[136,1024]{1,0:T(8,128)(2,1)}, bf16[136,1024]{1,0:T(8,128)(2,1)S(1)}, u32[]{:S(2)}, u32[]{:S(2)}) collective-permute-start(bf16[136,1024]{1,0:T(8,128)(2,1)} %bitcast.7), channel_id=1, source_target_pairs={{0,2},{1,3},{2,0},{3,1},{4,6},{5,7},{6,4},{7,5},{8,10},{9,11},{10,... | collective-permute-start | bytes 835592 | tf_op jit(solution)/shard_map/ppermute | solution.py:468
  2.8 23.6 %collective-permute-start = (bf16[136,1024]{1,0:T(8,128)(2,1)}, bf16[136,1024]{1,0:T(8,128)(2,1)S(1)}, u32[]{:S(2)}, u32[]{:S(2)}) collective-permute-start(bf16[136,1024]{1,0:T(8,128)(2,1)} %bitcast.8), channel_id=1, source_target_pairs={{0,1},{1,0},{2,3},{3,2},{4,5},{5,4},{6,7},{7,6},{8,9},{9,8},{10,11... | collective-permute-start | bytes 835592 | tf_op jit(solution)/shard_map/ppermute | solution.py:468
  5.0 10.7 %collective-permute-start.3 = (bf16[136,512]{1,0:T(8,128)(2,1)S(1)}, bf16[136,512]{1,0:T(8,128)(2,1)S(1)}, u32[]{:S(2)}, u32[]{:S(2)}) collective-permute-start(bf16[136,512]{1,0:T(8,128)(2,1)S(1)} %get-tuple-element.109), channel_id=1, source_target_pairs={{0,4},{1,5},{2,6},{3,7},{4,0},{5,1},{6,2},{7,3},{8,12},{9,13},{10,... | collective-permute-start | bytes 417800 | tf_op jit(solution)/shard_map/ppermute | solution.py:468
  7.4 12.5 %collective-permute-start.2 = (bf16[136,512]{1,0:T(8,128)(2,1)S(1)}, bf16[136,512]{1,0:T(8,128)(2,1)S(1)}, u32[]{:S(2)}, u32[]{:S(2)}) collective-permute-start(bf16[136,512]{1,0:T(8,128)(2,1)S(1)} %get-tuple-element.110), channel_id=1, source_target_pairs={{0,4},{1,5},{2,6},{3,7},{4,0},{5,1},{6,2},{7,3},{8,12},{9,13},{10,... | collective-permute-start | bytes 417800 | tf_op jit(solution)/shard_map/ppermute | solution.py:468
  8.2 1.2 %copy-start.2 = (bf16[1,1024,512]{2,1,0:T(8,128)(2,1)S(1)}, bf16[1,1024,512]{2,1,0:T(8,128)(2,1)}, u32[]{:S(2)}) copy-start(bf16[1,1024,512]{2,1,0:T(8,128)(2,1)} %param.11) | copy-start | bytes 3145732
  9.4 1.2 %copy-start.4 = (bf16[1,1024,512]{2,1,0:T(8,128)(2,1)S(1)}, bf16[1,1024,512]{2,1,0:T(8,128)(2,1)}, u32[]{:S(2)}) copy-start(bf16[1,1024,512]{2,1,0:T(8,128)(2,1)} %param.12) | copy-start | bytes 3145732
  10.6 1.2 %copy-start.6 = (bf16[1,1024,512]{2,1,0:T(8,128)(2,1)S(1)}, bf16[1,1024,512]{2,1,0:T(8,128)(2,1)}, u32[]{:S(2)}) copy-start(bf16[1,1024,512]{2,1,0:T(8,128)(2,1)} %param.13) | copy-start | bytes 3145732
  11.8 3.2 %copy-start.10 = (s32[1088]{0:T(1024)S(1)}, s32[1088]{0:T(1024)}, u32[]{:S(2)}) copy-start(s32[1088]{0:T(1024)} %param.15) | copy-start | bytes 13060
  11.8 14.6 %copy-start = (bf16[1,136,1024]{2,1,0:T(8,128)(2,1)S(1)}, bf16[1,136,1024]{2,1,0:T(8,128)(2,1)}, u32[]{:S(2)}) copy-start(bf16[1,136,1024]{2,1,0:T(8,128)(2,1)} %param.9) | copy-start | bytes 835588
  12.3 14.1 %collective-permute-start.4 = (bf16[136,1024]{1,0:T(8,128)(2,1)S(1)}, bf16[136,1024]{1,0:T(8,128)(2,1)S(1)}, u32[]{:S(2)}, u32[]{:S(2)}) collective-permute-start(bf16[136,1024]{1,0:T(8,128)(2,1)S(1)} %collective-permute-done.1.refs_2_), channel_id=1, source_target_pairs={{0,1},{1,0},{2,3},{3,2},{4,5},{5,4},{6,7},{7,6},{8,9},{9,8},{10,11... | collective-permute-start | bytes 835592 | tf_op jit(solution)/shard_map/ppermute | solution.py:468
  15.7 6.6 %collective-permute-start.8 = (bf16[136,512]{1,0:T(8,128)(2,1)S(1)}, bf16[136,512]{1,0:T(8,128)(2,1)S(1)}, u32[]{:S(2)}, u32[]{:S(2)}) collective-permute-start(bf16[136,512]{1,0:T(8,128)(2,1)S(1)} %collective-permute-done.3.refs_4_), channel_id=1, source_target_pairs={{0,2},{1,3},{2,0},{3,1},{4,6},{5,7},{6,4},{7,5},{8,10},{9,11},{10,... | collective-permute-start | bytes 417800 | tf_op jit(solution)/shard_map/ppermute | solution.py:468
  15.8 7.7 %collective-permute-start.6 = (bf16[136,512]{1,0:T(8,128)(2,1)S(1)}, bf16[136,512]{1,0:T(8,128)(2,1)S(1)}, u32[]{:S(2)}, u32[]{:S(2)}) collective-permute-start(bf16[136,512]{1,0:T(8,128)(2,1)S(1)} %collective-permute-done.3.refs_4_), channel_id=1, source_target_pairs={{0,1},{1,0},{2,3},{3,2},{4,5},{5,4},{6,7},{7,6},{8,9},{9,8},{10,11... | collective-permute-start | bytes 417800 | tf_op jit(solution)/shard_map/ppermute | solution.py:468
  20.0 6.5 %collective-permute-start.5 = (bf16[136,512]{1,0:T(8,128)(2,1)S(1)}, bf16[136,512]{1,0:T(8,128)(2,1)S(1)}, u32[]{:S(2)}, u32[]{:S(2)}) collective-permute-start(bf16[136,512]{1,0:T(8,128)(2,1)S(1)} %collective-permute-done.2.refs_3_), channel_id=1, source_target_pairs={{0,1},{1,0},{2,3},{3,2},{4,5},{5,4},{6,7},{7,6},{8,9},{9,8},{10,11... | collective-permute-start | bytes 417800 | tf_op jit(solution)/shard_map/ppermute | solution.py:468
  22.3 5.1 %collective-permute-start.7 = (bf16[136,512]{1,0:T(8,128)(2,1)S(1)}, bf16[136,512]{1,0:T(8,128)(2,1)S(1)}, u32[]{:S(2)}, u32[]{:S(2)}) collective-permute-start(bf16[136,512]{1,0:T(8,128)(2,1)S(1)} %collective-permute-done.2.refs_3_), channel_id=1, source_target_pairs={{0,2},{1,3},{2,0},{3,1},{4,6},{5,7},{6,4},{7,5},{8,10},{9,11},{10,... | collective-permute-start | bytes 417800 | tf_op jit(solution)/shard_map/ppermute | solution.py:468
  23.5 6.0 %collective-permute-start.10 = (bf16[136,512]{1,0:T(8,128)(2,1)S(1)}, bf16[136,512]{1,0:T(8,128)(2,1)S(1)}, u32[]{:S(2)}, u32[]{:S(2)}) collective-permute-start(bf16[136,512]{1,0:T(8,128)(2,1)S(1)} %collective-permute-done.8.refs_1_), channel_id=1, source_target_pairs={{0,1},{1,0},{2,3},{3,2},{4,5},{5,4},{6,7},{7,6},{8,9},{9,8},{10,11... | collective-permute-start | bytes 417800 | tf_op jit(solution)/shard_map/ppermute | solution.py:468
  26.4 4.2 %collective-permute-start.9 = (bf16[136,512]{1,0:T(8,128)(2,1)S(1)}, bf16[136,512]{1,0:T(8,128)(2,1)S(1)}, u32[]{:S(2)}, u32[]{:S(2)}) collective-permute-start(bf16[136,512]{1,0:T(8,128)(2,1)S(1)} %collective-permute-done.5.refs_6_), channel_id=1, source_target_pairs={{0,2},{1,3},{2,0},{3,1},{4,6},{5,7},{6,4},{7,5},{8,10},{9,11},{10,... | collective-permute-start | bytes 417800 | tf_op jit(solution)/shard_map/ppermute | solution.py:468
  30.6 14.2 %copy-start.1 = (bf16[1,512,2048]{2,1,0:T(8,128)(2,1)S(1)}, bf16[1,512,2048]{2,1,0:T(8,128)(2,1)}, u32[]{:S(2)}) copy-start(bf16[1,512,2048]{2,1,0:T(8,128)(2,1)} %param.14) | copy-start | bytes 6291460
  30.7 14.2 %copy-start.8 = (bf16[1,136,1024]{2,1,0:T(8,128)(2,1)S(1)}, bf16[1,136,1024]{2,1,0:T(8,128)(2,1)}, u32[]{:S(2)}) copy-start(bf16[1,136,1024]{2,1,0:T(8,128)(2,1)} %param.10) | copy-start | bytes 835588
  55.6 16.0 %collective-permute-start.19 = (bf16[256,1024]{1,0:T(8,128)(2,1)S(1)}, bf16[256,1024]{1,0:T(8,128)(2,1)S(1)}, u32[]{:S(2)}, u32[]{:S(2)}) collective-permute-start(bf16[256,1024]{1,0:T(8,128)(2,1)S(1)} %get-tuple-element.94), channel_id=1, source_target_pairs={{0,1},{1,0},{2,3},{3,2},{4,5},{5,4},{6,7},{7,6},{8,9},{9,8},{10,11... | collective-permute-start | bytes 1572872 | tf_op jit(solution)/shard_map/ppermute | solution.py:22
  55.7 16.0 %collective-permute-start.20 = (bf16[256,1024]{1,0:T(8,128)(2,1)S(1)}, bf16[256,1024]{1,0:T(8,128)(2,1)S(1)}, u32[]{:S(2)}, u32[]{:S(2)}) collective-permute-start(bf16[256,1024]{1,0:T(8,128)(2,1)S(1)} %get-tuple-element.95), channel_id=1, source_target_pairs={{0,2},{2,0},{1,3},{3,1},{4,6},{6,4},{5,7},{7,5},{8,10},{10,8},{9,1... | collective-permute-start | bytes 1572872 | tf_op jit(solution)/shard_map/ppermute | solution.py:22
  61.4 6.8 %collective-permute-start.13 = (bf16[408,128]{1,0:T(8,128)(2,1)S(1)}, bf16[408,128]{1,0:T(8,128)(2,1)S(1)}, u32[]{:S(2)}, u32[]{:S(2)}) collective-permute-start(bf16[408,128]{1,0:T(8,128)(2,1)S(1)} %get-tuple-element.84), channel_id=1, source_target_pairs={{0,4},{1,5},{2,6},{3,7},{4,0},{5,1},{6,2},{7,3},{8,12},{9,13},{10,... | collective-permute-start | bytes 313352 | tf_op jit(solution)/shard_map/ppermute | solution.py:468
  62.2 6.1 %collective-permute-start.16 = (bf16[408,128]{1,0:T(8,128)(2,1)S(1)}, bf16[408,128]{1,0:T(8,128)(2,1)S(1)}, u32[]{:S(2)}, u32[]{:S(2)}) collective-permute-start(bf16[408,128]{1,0:T(8,128)(2,1)S(1)} %get-tuple-element.87), channel_id=1, source_target_pairs={{0,6},{1,7},{2,4},{3,5},{4,2},{5,3},{6,0},{7,1},{8,14},{9,15},{10,... | collective-permute-start | bytes 313352 | tf_op jit(solution)/shard_map/ppermute | solution.py:468
  64.3 7.3 %collective-permute-start.17 = (bf16[408,128]{1,0:T(8,128)(2,1)S(1)}, bf16[408,128]{1,0:T(8,128)(2,1)S(1)}, u32[]{:S(2)}, u32[]{:S(2)}) collective-permute-start(bf16[408,128]{1,0:T(8,128)(2,1)S(1)} %get-tuple-element.88), channel_id=1, source_target_pairs={{0,7},{1,6},{2,5},{3,4},{4,3},{5,2},{6,1},{7,0},{8,15},{9,14},{10,... | collective-permute-start | bytes 313352 | tf_op jit(solution)/shard_map/ppermute | solution.py:468
  71.7 15.0 %collective-permute-start.21 = (bf16[128,1024]{1,0:T(8,128)(2,1)S(1)}, bf16[128,1024]{1,0:T(8,128)(2,1)S(1)}, u32[]{:S(2)}, u32[]{:S(2)}) collective-permute-start(bf16[128,1024]{1,0:T(8,128)(2,1)S(1)} %get-tuple-element.98), channel_id=1, source_target_pairs={{0,2},{2,0},{1,3},{3,1},{4,6},{6,4},{5,7},{7,5},{8,10},{10,8},{9,1... | collective-permute-start | bytes 786440 | tf_op jit(solution)/shard_map/ppermute | solution.py:22
  72.6 15.6 %collective-permute-start.22 = (bf16[128,1024]{1,0:T(8,128)(2,1)S(1)}, bf16[128,1024]{1,0:T(8,128)(2,1)S(1)}, u32[]{:S(2)}, u32[]{:S(2)}) collective-permute-start(bf16[128,1024]{1,0:T(8,128)(2,1)S(1)} %get-tuple-element.99), channel_id=1, source_target_pairs={{0,1},{1,0},{2,3},{3,2},{4,5},{5,4},{6,7},{7,6},{8,9},{9,8},{10,11... | collective-permute-start | bytes 786440 | tf_op jit(solution)/shard_map/ppermute | solution.py:22
  73.4 13.3 %collective-permute-start.15 = (bf16[408,128]{1,0:T(8,128)(2,1)S(1)}, bf16[408,128]{1,0:T(8,128)(2,1)S(1)}, u32[]{:S(2)}, u32[]{:S(2)}) collective-permute-start(bf16[408,128]{1,0:T(8,128)(2,1)S(1)} %get-tuple-element.86), channel_id=1, source_target_pairs={{0,5},{1,4},{2,7},{3,6},{4,1},{5,0},{6,3},{7,2},{8,13},{9,12},{10,... | collective-permute-start | bytes 313352 | tf_op jit(solution)/shard_map/ppermute | solution.py:468
  75.0 16.4 %collective-permute-start.18 = (bf16[136,1024]{1,0:T(8,128)(2,1)S(1)}, bf16[136,1024]{1,0:T(8,128)(2,1)S(1)}, u32[]{:S(2)}, u32[]{:S(2)}) collective-permute-start(bf16[136,1024]{1,0:T(8,128)(2,1)S(1)} %get-tuple-element.89), channel_id=1, source_target_pairs={{0,7},{1,6},{2,5},{3,4},{4,3},{5,2},{6,1},{7,0},{8,15},{9,14},{10,... | collective-permute-start | bytes 835592 | tf_op jit(solution)/shard_map/ppermute | solution.py:468
  77.8 10.8 %collective-permute-start.11 = (bf16[408,128]{1,0:T(8,128)(2,1)S(1)}, bf16[408,128]{1,0:T(8,128)(2,1)S(1)}, u32[]{:S(2)}, u32[]{:S(2)}) collective-permute-start(bf16[408,128]{1,0:T(8,128)(2,1)S(1)} %get-tuple-element.82), channel_id=1, source_target_pairs={{0,1},{1,0},{2,3},{3,2},{4,5},{5,4},{6,7},{7,6},{8,9},{9,8},{10,11... | collective-permute-start | bytes 313352 | tf_op jit(solution)/shard_map/ppermute | solution.py:468
  86.7 4.7 %collective-permute-start.12 = (bf16[408,128]{1,0:T(8,128)(2,1)S(1)}, bf16[408,128]{1,0:T(8,128)(2,1)S(1)}, u32[]{:S(2)}, u32[]{:S(2)}) collective-permute-start(bf16[408,128]{1,0:T(8,128)(2,1)S(1)} %get-tuple-element.83), channel_id=1, source_target_pairs={{0,2},{1,3},{2,0},{3,1},{4,6},{5,7},{6,4},{7,5},{8,10},{9,11},{10,... | collective-permute-start | bytes 313352 | tf_op jit(solution)/shard_map/ppermute | solution.py:468
  86.7 4.7 %copy-start.3 = (bf16[1,1024,512]{2,1,0:T(8,128)(2,1)S(1)}, bf16[1,1024,512]{2,1,0:T(8,128)(2,1)}, u32[]{:S(2)}) copy-start(bf16[1,1024,512]{2,1,0:T(8,128)(2,1)} %param.11) | copy-start | bytes 3145732
  86.7 4.7 %copy-start.5 = (bf16[1,1024,512]{2,1,0:T(8,128)(2,1)S(1)}, bf16[1,1024,512]{2,1,0:T(8,128)(2,1)}, u32[]{:S(2)}) copy-start(bf16[1,1024,512]{2,1,0:T(8,128)(2,1)} %param.12) | copy-start | bytes 3145732
  86.7 4.7 %copy-start.7 = (bf16[1,1024,512]{2,1,0:T(8,128)(2,1)S(1)}, bf16[1,1024,512]{2,1,0:T(8,128)(2,1)}, u32[]{:S(2)}) copy-start(bf16[1,1024,512]{2,1,0:T(8,128)(2,1)} %param.13) | copy-start | bytes 3145732
  86.7 4.7 %collective-permute-start.14 = (bf16[408,128]{1,0:T(8,128)(2,1)S(1)}, bf16[408,128]{1,0:T(8,128)(2,1)S(1)}, u32[]{:S(2)}, u32[]{:S(2)}) collective-permute-start(bf16[408,128]{1,0:T(8,128)(2,1)S(1)} %get-tuple-element.85), channel_id=1, source_target_pairs={{0,3},{1,2},{2,1},{3,0},{4,7},{5,6},{6,5},{7,4},{8,11},{9,10},{10,... | collective-permute-start | bytes 313352 | tf_op jit(solution)/shard_map/ppermute | solution.py:468
  88.3 24.7 %collective-permute-start.25 = (bf16[64,1024]{1,0:T(8,128)(2,1)S(1)}, bf16[64,1024]{1,0:T(8,128)(2,1)S(1)}, u32[]{:S(2)}, u32[]{:S(2)}) collective-permute-start(bf16[64,1024]{1,0:T(8,128)(2,1)S(1)} %get-tuple-element.101), channel_id=1, source_target_pairs={{0,4},{4,0},{1,5},{5,1},{2,6},{6,2},{3,7},{7,3},{8,12},{12,8},{9,1... | collective-permute-start | bytes 393224 | tf_op jit(solution)/shard_map/ppermute | solution.py:22
  88.6 24.5 %collective-permute-start.24 = (bf16[64,1024]{1,0:T(8,128)(2,1)S(1)}, bf16[64,1024]{1,0:T(8,128)(2,1)S(1)}, u32[]{:S(2)}, u32[]{:S(2)}) collective-permute-start(bf16[64,1024]{1,0:T(8,128)(2,1)S(1)} %get-tuple-element.100.refs_14_), channel_id=1, source_target_pairs={{0,4},{4,0},{1,5},{5,1},{2,6},{6,2},{3,7},{7,3},{8,12},{12,8},{9,1... | collective-permute-start | bytes 393224 | tf_op jit(solution)/shard_map/ppermute | solution.py:22
  92.8 25.5 %collective-permute-start.23 = (bf16[136,1024]{1,0:T(8,128)(2,1)S(1)}, bf16[136,1024]{1,0:T(8,128)(2,1)S(1)}, u32[]{:S(2)}, u32[]{:S(2)}) collective-permute-start(bf16[136,1024]{1,0:T(8,128)(2,1)S(1)} %shard_map.135), channel_id=1, source_target_pairs={{8,0},{16,8},{24,16},{9,1},{17,9},{25,17},{10,2},{18,10},{26,18},{... | collective-permute-start | bytes 835592 | tf_op jit(solution)/shard_map/ppermute | solution.py:28
  113.9 4.5 %copy-start.9 = (s32[1,136]{1,0:T(1,128)S(1)}, s32[1,136]{1,0:T(1,128)}, u32[]{:S(2)}) copy-start(s32[1,136]{1,0:T(1,128)} %order_ref.1) | copy-start | bytes 1636

commit v15 on v13

--- a/solution.py
+++ b/solution.py
@@ -357,7 +357,7 @@
 
 
 def backward_kernel(me_ref, slab_ref, prob_ref, qk_ref, v_ref, out_t_ref, *refs):
-    early, late, out_refs = refs[:3], refs[3:6], refs[6:-4]
+    early, late, up_ref, out_refs = refs[:3], refs[3:6], refs[6], refs[7:-4]
     gk_ref, gv_ref, gq_ref, held_ref = refs[-4:]
     first, rows = early[0].shape[:2]
     slabs = [wide(slab_ref[me_ref[0] ^ distance]) for distance in DISTANCES]
@@ -395,18 +395,22 @@
         qk_sum = qk_sum + dot(back, normed, ((0,), (0,)))
         v_sum = v_sum + dot(grad_v.astype(jnp.bfloat16), normed, ((0,), (0,)))
     step = qk_sum.shape[1] // HEADS
+    middle = PACKED + rows + 2 * HEAD_DIM
     for g in range(HEADS):
         own = slice(g * step, (g + 1) * step)
         held_ref[g] = low(jnp.concatenate([qk_sum[:, own], v_sum[:, own]], axis=0))
     for m, out_ref in enumerate(out_refs):
-        out_ref[PACKED + rows :, :] = held_ref[me_ref[0] ^ DISTANCES[m]]
+        out_ref[PACKED + rows : middle + HEAD_DIM, :] = held_ref[me_ref[0] ^ DISTANCES[m]]
+    for i in range(up_ref.shape[1] // 128):
+        start = middle + HEAD_DIM + i * rows
+        out_refs[-1][start : start + rows, :] = up_ref[:, i * 128 : (i + 1) * 128]
 
 
 def turn_kernel(me_ref, *refs):
     slabs, out_refs, held_ref = refs[:HEADS], refs[HEADS + 2 : -1], refs[-1]
     start = slabs[0].shape[0] - 3 * HEAD_DIM
     for m, slab in enumerate(slabs):
-        held_ref[me_ref[0] ^ DISTANCES[m]] = slab[start:, :]
+        held_ref[me_ref[0] ^ DISTANCES[m]] = slab[start : start + 3 * HEAD_DIM, :]
     for i, out_ref in enumerate(out_refs):
         own = slice(i * HEAD_DIM, (i + 1) * HEAD_DIM)
         heads = [wide(held_ref[h, own, :]) for h in range(HEADS)]
@@ -435,12 +439,15 @@
 
 
 def input_kernel(me_ref, *refs):
-    slabs, (wq_ref, wk_ref, wv_ref, *acts, up_ref, _, out_ref) = refs[:HEADS], refs[HEADS:-1]
+    slabs, (wq_ref, wk_ref, wv_ref, *acts, _, out_ref) = refs[:HEADS], refs[HEADS:-1]
     held_ref = refs[-1]
-    rows = up_ref.shape[0]
+    rows, width = out_ref.shape
+    start = slabs[0].shape[0]
+    starts = range(start, start + rows * width // 128, rows)
+    scaled = jnp.concatenate([wide(slabs[-1][i : i + rows, :]) for i in starts], axis=1)
     for m, slab in enumerate(slabs):
         held_ref[me_ref[0] ^ DISTANCES[m]] = slab[: PACKED + rows, :]
-    unit, row_scale = normalize(joined(acts, up_ref.shape[1])[0])
+    unit, row_scale = normalize(joined(acts, width)[0])
     queries, keys, values = [], [], []
     for pair in range(HEADS // 2):
         even, odd = [wide(held_ref[2 * pair + i]) for i in range(2)]
@@ -453,7 +460,7 @@
         left = jnp.concatenate(parts, axis=1).astype(jnp.bfloat16)
         total = total + dot(left, ref[...], ((1,), (1,)))
     total = total - unit * jnp.mean(total * unit, axis=-1, keepdims=True)
-    out_ref[...] = (wide(up_ref[...]) + row_scale * total).astype(jnp.bfloat16)
+    out_ref[...] = (scaled + row_scale * total).astype(jnp.bfloat16)
 
 
 def reorder_kernel(order_ref, rows_ref, out_ref):
@@ -568,8 +575,7 @@
         + [out(len(group) * HEAD_DIM, width) for order in ORDERS for group in order],
     )
     grad_slabs = switch(grad_slabs)
-    grad_slabs, terms, scaled = lax.optimization_barrier((grad_slabs, terms, scaled))
-    scaled = hop(scaled, parts - 1)
+    grad_slabs, terms = lax.optimization_barrier((grad_slabs, terms))
     first, second, third, keep = zip(terms[:4], terms[4:])
     got = [partner(part, "seq", bit) for bit, part in enumerate(first)]
     grads = call(
@@ -577,8 +583,9 @@
         6,
         [("s", me)]
         + [("v", x) for x in (grad_slabs, probs, qk, value, out_t)]
-        + [("v", x) for x in (normed, unit, unit_scale, *late_parts)],
-        [out(PACKED + rows + 3 * HEAD_DIM, 128)] * parts,
+        + [("v", x) for x in (normed, unit, unit_scale, *late_parts, scaled)],
+        [out(PACKED + rows + 3 * HEAD_DIM, 128)] * (parts - 1)
+        + [out(PACKED + rows + 3 * HEAD_DIM + rows * width // 128, 128)],
         [
             pltpu.VMEM((tokens, HEAD_DIM), f32),
             pltpu.VMEM((tokens, HEAD_DIM), f32),
@@ -604,7 +611,7 @@
     (grad_input,) = call(
         input_kernel,
         1.5,
-        [("s", me)] + [("v", x) for x in (*slabs, wq, wk, wv, *mirrored, scaled)] + [("a", leaving[0])],
+        [("s", me)] + [("v", x) for x in (*slabs, wq, wk, wv, *mirrored)] + [("a", leaving[0])],
         [out(rows, width)],
         [pltpu.VMEM((HEADS, PACKED + rows, 128), jnp.bfloat16)],
     )

time: 119 us -> 117 us (0.983)
  the two profiles are of different devices: /device:TPU:3 before, /device:TPU:27 now
where the time goes in v15:
time: 117 us
  starting transfers between devices  42.8 us (37%)
  waiting for transfers between devices  32.9 us (28%)
  blocking collectives  17.2 us (15%)
  Pallas kernels  16.7 us (14%)
  local copies, waits for them, and re-layouts  5.64 us (5%)
    ppermute x18, waiting for transfers between devices, hop(): return lax.ppermute(block, 'seq', route)  29.5 us
    all_to_all x2, blocking collectives, switch(): return lax.all_to_all(slabs, 'seq', split_axis=0, concat_axis=0, tiled=True)  17.2 us
    pallas_call x11, Pallas kernels, call(): pl.pallas_call(kernel, out_shape=tuple(outs), in_specs=[pl.BlockSpec(memo...  16.7 us
    ppermute x18, starting transfers between devices, hop(): return lax.ppermute(block, 'seq', route)  15.3 us
    ppermute x6, starting transfers between devices, partner(): return lax.ppermute(block, axis, route)  13.9 us
    ppermute x1, starting transfers between devices, shifted(): return lax.ppermute(block, axis, route)  13.7 us
    unnamed x22, local copies, waits for them, and re-layouts  3.7 us
    ppermute x1, waiting for transfers between devices, shifted(): return lax.ppermute(block, axis, route)  3.46 us
  transfers between devices with their start and end apart: 25, of which 11 were waited for; matrix products, arithmetic and copies ran while one was open for 2% of the time, Pallas kernels for 8%

profile of v15, /device:TPU:27, one launch (start us, length us, event | category | flops | bytes accessed | tf_op | source)
XLA Modules:
  0.0 116.9 jit_solution(1740620322124928454)
XLA Ops:
  0.6 0.2 collective-permute-start.1
  0.9 0.3 collective-permute-start
  1.1 1.0 fusion
  2.2 2.4 %collective-permute-start.2 = (bf16[136,512]{1,0:T(8,128)(2,1)S(1)}, bf16[136,512]{1,0:T(8,128)(2,1)S(1)}, u32[]{:S(2)}, u32[]{:S(2)}) collective-permute-start(bf16[136,512]{1,0:T(8,128)(2,1)S(1)} %get-tuple-element.108), channel_id=1, source_target_pairs={{0,4},{1,5},{2,6},{3,7},{4,0},{5,1},{6,2},{7,3},{8,12},{9,13},{10,... | collective-permute-start | bytes 417800 | tf_op jit(solution)/shard_map/ppermute | solution.py:475
  4.6 0.7 compare_and_fusion
  5.2 1.2 %copy-done.2 = bf16[1,1024,512]{2,1,0:T(8,128)(2,1)S(1)} copy-done((bf16[1,1024,512]{2,1,0:T(8,128)(2,1)S(1)}, bf16[1,1024,512]{2,1,0:T(8,128)(2,1)}, u32[]{:S(2)}) %copy-start.2) | copy-done | bytes 1048600
  6.4 1.2 %copy-done.4 = bf16[1,1024,512]{2,1,0:T(8,128)(2,1)S(1)} copy-done((bf16[1,1024,512]{2,1,0:T(8,128)(2,1)S(1)}, bf16[1,1024,512]{2,1,0:T(8,128)(2,1)}, u32[]{:S(2)}) %copy-start.4) | copy-done | bytes 1048600
  7.7 1.2 %copy-done.6 = bf16[1,1024,512]{2,1,0:T(8,128)(2,1)S(1)} copy-done((bf16[1,1024,512]{2,1,0:T(8,128)(2,1)S(1)}, bf16[1,1024,512]{2,1,0:T(8,128)(2,1)}, u32[]{:S(2)}) %copy-start.6) | copy-done | bytes 1048600
  8.9 0.5 shard_map.128.refs_8_.weight_ref
  9.4 2.7 %collective-permute-done.1.refs_2_ = bf16[136,1024]{1,0:T(8,128)(2,1)S(1)} collective-permute-done((bf16[136,1024]{1,0:T(8,128)(2,1)}, bf16[136,1024]{1,0:T(8,128)(2,1)S(1)}, u32[]{:S(2)}, u32[]{:S(2)}) %collective-permute-start.1) | collective-permute-done | bytes 278560 | tf_op jit(solution)/shard_map/ppermute | solution.py:475
  12.2 0.6 gather_fusion
  12.8 1.5 %collective-permute-start.6 = (bf16[136,512]{1,0:T(8,128)(2,1)S(1)}, bf16[136,512]{1,0:T(8,128)(2,1)S(1)}, u32[]{:S(2)}, u32[]{:S(2)}) collective-permute-start(bf16[136,512]{1,0:T(8,128)(2,1)S(1)} %collective-permute-done.3.refs_4_), channel_id=1, source_target_pairs={{0,1},{1,0},{2,3},{3,2},{4,5},{5,4},{6,7},{7,6},{8,9},{9,8},{10,11... | collective-permute-start | bytes 417800 | tf_op jit(solution)/shard_map/ppermute | solution.py:475
  14.3 1.7 %collective-permute-done.2.refs_3_ = bf16[136,512]{1,0:T(8,128)(2,1)S(1)} collective-permute-done((bf16[136,512]{1,0:T(8,128)(2,1)S(1)}, bf16[136,512]{1,0:T(8,128)(2,1)S(1)}, u32[]{:S(2)}, u32[]{:S(2)}) %collective-permute-start.2) | collective-permute-done | bytes 139296 | tf_op jit(solution)/shard_map/ppermute | solution.py:475
  16.1 1.3 %collective-permute-start.5 = (bf16[136,512]{1,0:T(8,128)(2,1)S(1)}, bf16[136,512]{1,0:T(8,128)(2,1)S(1)}, u32[]{:S(2)}, u32[]{:S(2)}) collective-permute-start(bf16[136,512]{1,0:T(8,128)(2,1)S(1)} %collective-permute-done.2.refs_3_), channel_id=1, source_target_pairs={{0,1},{1,0},{2,3},{3,2},{4,5},{5,4},{6,7},{7,6},{8,9},{9,8},{10,11... | collective-permute-start | bytes 417800 | tf_op jit(solution)/shard_map/ppermute | solution.py:475
  17.6 0.2 select_n.33.column_ids
  17.8 1.4 %collective-permute-done.8.refs_1_ = bf16[136,512]{1,0:T(8,128)(2,1)S(1)} collective-permute-done((bf16[136,512]{1,0:T(8,128)(2,1)S(1)}, bf16[136,512]{1,0:T(8,128)(2,1)S(1)}, u32[]{:S(2)}, u32[]{:S(2)}) %collective-permute-start.8) | collective-permute-done | bytes 139296 | tf_op jit(solution)/shard_map/ppermute | solution.py:475
  19.2 2.5 %collective-permute-done.6.refs_7_ = bf16[136,512]{1,0:T(8,128)(2,1)S(1)} collective-permute-done((bf16[136,512]{1,0:T(8,128)(2,1)S(1)}, bf16[136,512]{1,0:T(8,128)(2,1)S(1)}, u32[]{:S(2)}, u32[]{:S(2)}) %collective-permute-start.6) | collective-permute-done | bytes 139296 | tf_op jit(solution)/shard_map/ppermute | solution.py:475
  21.6 0.3 collective-permute-start.10
  21.9 2.7 %collective-permute-done.5.refs_6_ = bf16[136,512]{1,0:T(8,128)(2,1)S(1)} collective-permute-done((bf16[136,512]{1,0:T(8,128)(2,1)S(1)}, bf16[136,512]{1,0:T(8,128)(2,1)S(1)}, u32[]{:S(2)}, u32[]{:S(2)}) %collective-permute-start.5) | collective-permute-done | bytes 139296 | tf_op jit(solution)/shard_map/ppermute | solution.py:475
  24.6 1.0 shard_map.129
  25.6 2.0 %collective-permute-done.10.refs_3_.refs_12_ = bf16[136,512]{1,0:T(8,128)(2,1)S(1)} collective-permute-done((bf16[136,512]{1,0:T(8,128)(2,1)S(1)}, bf16[136,512]{1,0:T(8,128)(2,1)S(1)}, u32[]{:S(2)}, u32[]{:S(2)}) %collective-permute-start.10) | collective-permute-done | bytes 139296 | tf_op jit(solution)/shard_map/ppermute | solution.py:475
  27.6 0.9 collective-permute-done.9.refs_2_.refs_11_
  28.5 3.7 %shard_map.130 = (bf16[2,136,1024]{2,1,0:T(8,128)(2,1)S(1)}, f32[2,136,128]{2,1,0:T(8,128)S(1)}, f32[2,136,128]{2,1,0:T(8,128)S(1)}, bf16[1088,1088]{1,0:T(8,128...) custom-call(s32[1]{0:T(128)} %bitcast.me_ref, ...), custom_call_target="tpu_custom_call" | custom-call | flops 5000000000 | bytes 1024 | tf_op jit(solution)/shard_map/pallas_call | solution.py:200
  32.3 8.4 %all_to_all.10.slab_ref = bf16[8,80,128]{2,1,0:T(8,128)(2,1)S(1)} all-to-all(bf16[8,80,128]{2,1,0:T(8,128)(2,1)S(1)} %get-tuple-element.59), channel_id=1, replica_groups=mesh['section'=4,'seq'=8] {'seq'}, dimensions={0} | all-to-all | bytes 327680 | tf_op jit(solution)/shard_map/all_to_all | solution.py:483
  40.7 2.0 %shard_map.131 = (bf16[136,1024]{1,0:T(8,128)(2,1)S(1)}, bf16[8,80,128]{2,1,0:T(8,128)(2,1)S(1)}, bf16[256,1024]{1,0:T(8,128)(2,1)S(1)}, bf16[128,1024]{1,0:T(8,...) custom-call(s32[1]{0:T(128)} %bitcast.me_ref, ...), custom_call_target="tpu_custom_call" | custom-call | flops 3000000000 | bytes 1024 | tf_op jit(solution)/shard_map/pallas_call | solution.py:200
  42.7 8.8 %all_to_all.11.slab_ref = bf16[8,80,128]{2,1,0:T(8,128)(2,1)S(1)} all-to-all(bf16[8,80,128]{2,1,0:T(8,128)(2,1)S(1)} %get-tuple-element.60), channel_id=1, replica_groups=mesh['section'=4,'seq'=8] {'seq'}, dimensions={0} | all-to-all | bytes 327680 | tf_op jit(solution)/shard_map/all_to_all | solution.py:483
  51.5 0.5 collective-permute-start.18
  52.0 1.0 collective-permute-start.19
  53.0 5.0 %shard_map.132 = (bf16[408,128]{1,0:T(8,128)(2,1)S(1)}, bf16[408,128]{1,0:T(8,128)(2,1)S(1)}, bf16[408,128]{1,0:T(8,128)(2,1)S(1)}, bf16[408,128]{1,0:T(8,128)(2...) custom-call(s32[1]{0:T(128)} %bitcast.me_ref, ...), custom_call_target="tpu_custom_call" | custom-call | flops 6000000000 | bytes 1024 | tf_op jit(solution)/shard_map/pallas_call | solution.py:200
  58.0 2.6 %collective-permute-start.17 = (bf16[1496,128]{1,0:T(8,128)(2,1)S(1)}, bf16[1496,128]{1,0:T(8,128)(2,1)S(1)}, u32[]{:S(2)}, u32[]{:S(2)}) collective-permute-start(bf16[1496,128]{1,0:T(8,128)(2,1)S(1)} %get-tuple-element.87), channel_id=1, source_target_pairs={{0,7},{1,6},{2,5},{3,4},{4,3},{5,2},{6,1},{7,0},{8,15},{9,14},{10,... | collective-permute-start | bytes 1148936 | tf_op jit(solution)/shard_map/ppermute | solution.py:475
  60.6 1.9 %collective-permute-start.16 = (bf16[408,128]{1,0:T(8,128)(2,1)S(1)}, bf16[408,128]{1,0:T(8,128)(2,1)S(1)}, u32[]{:S(2)}, u32[]{:S(2)}) collective-permute-start(bf16[408,128]{1,0:T(8,128)(2,1)S(1)} %get-tuple-element.86), channel_id=1, source_target_pairs={{0,6},{1,7},{2,4},{3,5},{4,2},{5,3},{6,0},{7,1},{8,14},{9,15},{10,... | collective-permute-start | bytes 313352 | tf_op jit(solution)/shard_map/ppermute | solution.py:475
  62.5 11.2 %collective-permute-done.13.refs_4_.refs_3_ = bf16[408,128]{1,0:T(8,128)(2,1)S(1)} collective-permute-done((bf16[408,128]{1,0:T(8,128)(2,1)S(1)}, bf16[408,128]{1,0:T(8,128)(2,1)S(1)}, u32[]{:S(2)}, u32[]{:S(2)}) %collective-permute-start.13) | collective-permute-done | bytes 104480 | tf_op jit(solution)/shard_map/ppermute | solution.py:475
  73.9 9.2 %collective-permute-start.20 = (bf16[128,1024]{1,0:T(8,128)(2,1)S(1)}, bf16[128,1024]{1,0:T(8,128)(2,1)S(1)}, u32[]{:S(2)}, u32[]{:S(2)}) collective-permute-start(bf16[128,1024]{1,0:T(8,128)(2,1)S(1)} %get-tuple-element.96), channel_id=1, source_target_pairs={{0,2},{2,0},{1,3},{3,1},{4,6},{6,4},{5,7},{7,5},{8,10},{10,8},{9,1... | collective-permute-start | bytes 786440 | tf_op jit(solution)/shard_map/ppermute | solution.py:22
  83.1 0.7 collective-permute-start.21
  83.9 0.7 collective-permute-start.11
  84.6 1.8 %collective-permute-start.14 = (bf16[408,128]{1,0:T(8,128)(2,1)S(1)}, bf16[408,128]{1,0:T(8,128)(2,1)S(1)}, u32[]{:S(2)}, u32[]{:S(2)}) collective-permute-start(bf16[408,128]{1,0:T(8,128)(2,1)S(1)} %get-tuple-element.84), channel_id=1, source_target_pairs={{0,3},{1,2},{2,1},{3,0},{4,7},{5,6},{6,5},{7,4},{8,11},{9,10},{10,... | collective-permute-start | bytes 313352 | tf_op jit(solution)/shard_map/ppermute | solution.py:475
  86.5 2.6 %collective-permute-done.12.refs_8_.refs_2_ = bf16[408,128]{1,0:T(8,128)(2,1)S(1)} collective-permute-done((bf16[408,128]{1,0:T(8,128)(2,1)S(1)}, bf16[408,128]{1,0:T(8,128)(2,1)S(1)}, u32[]{:S(2)}, u32[]{:S(2)}) %collective-permute-start.12) | collective-permute-done | bytes 104480 | tf_op jit(solution)/shard_map/ppermute | solution.py:475
  89.1 2.1 %collective-permute-start.15 = (bf16[408,128]{1,0:T(8,128)(2,1)S(1)}, bf16[408,128]{1,0:T(8,128)(2,1)S(1)}, u32[]{:S(2)}, u32[]{:S(2)}) collective-permute-start(bf16[408,128]{1,0:T(8,128)(2,1)S(1)} %get-tuple-element.85), channel_id=1, source_target_pairs={{0,5},{1,4},{2,7},{3,6},{4,1},{5,0},{6,3},{7,2},{8,13},{9,12},{10,... | collective-permute-start | bytes 313352 | tf_op jit(solution)/shard_map/ppermute | solution.py:475
  91.2 0.2 shard_map.134
  91.4 0.8 collective-permute-start.24
  92.2 1.6 %collective-permute-start.23 = (bf16[64,1024]{1,0:T(8,128)(2,1)S(1)}, bf16[64,1024]{1,0:T(8,128)(2,1)S(1)}, u32[]{:S(2)}, u32[]{:S(2)}) collective-permute-start(bf16[64,1024]{1,0:T(8,128)(2,1)S(1)} %get-tuple-element.98.refs_13_), channel_id=1, source_target_pairs={{0,4},{4,0},{1,5},{5,1},{2,6},{6,2},{3,7},{7,3},{8,12},{12,8},{9,1... | collective-permute-start | bytes 393224 | tf_op jit(solution)/shard_map/ppermute | solution.py:22
  93.8 1.7 %collective-permute-done.15.refs_5_ = bf16[408,128]{1,0:T(8,128)(2,1)S(1)} collective-permute-done((bf16[408,128]{1,0:T(8,128)(2,1)S(1)}, bf16[408,128]{1,0:T(8,128)(2,1)S(1)}, u32[]{:S(2)}, u32[]{:S(2)}) %collective-permute-start.15) | collective-permute-done | bytes 104480 | tf_op jit(solution)/shard_map/ppermute | solution.py:475
  95.5 1.4 %shard_map.135 = bf16[136,1024]{1,0:T(8,128)(2,1)S(1)} custom-call(s32[1]{0:T(128)} %bitcast.me_ref, bf16[408,128]{1,0:T(8,128)(2,1)S(1)} %get-tuple-element.80.refs_0_, bf16[408,128]{1,0:T(8,128)(2,1)S(1)} %collective-permute-done.11.refs_1_, bf16[408,128]{1,0:T(8,128)(2,1)S(1)} %collective-permute-done.12.refs_8_.refs_2_, ...), custom_call_target="tpu_custom_call" | custom-call | flops 1500000000 | bytes 1024 | tf_op jit(solution)/shard_map/pallas_call | solution.py:200
  96.9 13.7 %collective-permute-start.22 = (bf16[136,1024]{1,0:T(8,128)(2,1)S(1)}, bf16[136,1024]{1,0:T(8,128)(2,1)S(1)}, u32[]{:S(2)}, u32[]{:S(2)}) collective-permute-start(bf16[136,1024]{1,0:T(8,128)(2,1)S(1)} %shard_map.135), channel_id=1, source_target_pairs={{8,0},{16,8},{24,16},{9,1},{17,9},{25,17},{10,2},{18,10},{26,18},{... | collective-permute-start | bytes 835592 | tf_op jit(solution)/shard_map/ppermute | solution.py:28
  110.6 0.8 shard_map.138
  111.5 1.0 shard_map.137
  112.5 3.5 %collective-permute-done.22.rows_ref = bf16[136,1024]{1,0:T(8,128)(2,1)S(1)} collective-permute-done((bf16[136,1024]{1,0:T(8,128)(2,1)S(1)}, bf16[136,1024]{1,0:T(8,128)(2,1)S(1)}, u32[]{:S(2)}, u32[]{:S(2)}) %collective-permute-start.22) | collective-permute-done | bytes 278560 | tf_op jit(solution)/shard_map/ppermute | solution.py:28
  115.9 1.0 shard_map.136
  (45 shorter events, 0.7 us)
Async XLA Ops:
  0.6 11.4 %collective-permute-start.1 = (bf16[136,1024]{1,0:T(8,128)(2,1)}, bf16[136,1024]{1,0:T(8,128)(2,1)S(1)}, u32[]{:S(2)}, u32[]{:S(2)}) collective-permute-start(bf16[136,1024]{1,0:T(8,128)(2,1)} %bitcast.7), channel_id=1, source_target_pairs={{0,2},{1,3},{2,0},{3,1},{4,6},{5,7},{6,4},{7,5},{8,10},{9,11},{10,... | collective-permute-start | bytes 835592 | tf_op jit(solution)/shard_map/ppermute | solution.py:475
  0.9 23.8 %collective-permute-start = (bf16[136,1024]{1,0:T(8,128)(2,1)}, bf16[136,1024]{1,0:T(8,128)(2,1)S(1)}, u32[]{:S(2)}, u32[]{:S(2)}) collective-permute-start(bf16[136,1024]{1,0:T(8,128)(2,1)} %bitcast.8), channel_id=1, source_target_pairs={{0,1},{1,0},{2,3},{3,2},{4,5},{5,4},{6,7},{7,6},{8,9},{9,8},{10,11... | collective-permute-start | bytes 835592 | tf_op jit(solution)/shard_map/ppermute | solution.py:475
  2.1 10.6 %collective-permute-start.3 = (bf16[136,512]{1,0:T(8,128)(2,1)S(1)}, bf16[136,512]{1,0:T(8,128)(2,1)S(1)}, u32[]{:S(2)}, u32[]{:S(2)}) collective-permute-start(bf16[136,512]{1,0:T(8,128)(2,1)S(1)} %get-tuple-element.107), channel_id=1, source_target_pairs={{0,4},{1,5},{2,6},{3,7},{4,0},{5,1},{6,2},{7,3},{8,12},{9,13},{10,... | collective-permute-start | bytes 417800 | tf_op jit(solution)/shard_map/ppermute | solution.py:475
  2.2 13.9 %collective-permute-start.2 = (bf16[136,512]{1,0:T(8,128)(2,1)S(1)}, bf16[136,512]{1,0:T(8,128)(2,1)S(1)}, u32[]{:S(2)}, u32[]{:S(2)}) collective-permute-start(bf16[136,512]{1,0:T(8,128)(2,1)S(1)} %get-tuple-element.108), channel_id=1, source_target_pairs={{0,4},{1,5},{2,6},{3,7},{4,0},{5,1},{6,2},{7,3},{8,12},{9,13},{10,... | collective-permute-start | bytes 417800 | tf_op jit(solution)/shard_map/ppermute | solution.py:475
  5.2 1.2 %copy-start.2 = (bf16[1,1024,512]{2,1,0:T(8,128)(2,1)S(1)}, bf16[1,1024,512]{2,1,0:T(8,128)(2,1)}, u32[]{:S(2)}) copy-start(bf16[1,1024,512]{2,1,0:T(8,128)(2,1)} %param.11) | copy-start | bytes 3145732
  6.4 1.2 %copy-start.4 = (bf16[1,1024,512]{2,1,0:T(8,128)(2,1)S(1)}, bf16[1,1024,512]{2,1,0:T(8,128)(2,1)}, u32[]{:S(2)}) copy-start(bf16[1,1024,512]{2,1,0:T(8,128)(2,1)} %param.12) | copy-start | bytes 3145732
  7.7 1.2 %copy-start.6 = (bf16[1,1024,512]{2,1,0:T(8,128)(2,1)S(1)}, bf16[1,1024,512]{2,1,0:T(8,128)(2,1)}, u32[]{:S(2)}) copy-start(bf16[1,1024,512]{2,1,0:T(8,128)(2,1)} %param.13) | copy-start | bytes 3145732
  8.9 3.2 %copy-start.10 = (s32[1088]{0:T(1024)S(1)}, s32[1088]{0:T(1024)}, u32[]{:S(2)}) copy-start(s32[1088]{0:T(1024)} %param.15) | copy-start | bytes 13060
  8.9 15.7 %copy-start = (bf16[1,136,1024]{2,1,0:T(8,128)(2,1)S(1)}, bf16[1,136,1024]{2,1,0:T(8,128)(2,1)}, u32[]{:S(2)}) copy-start(bf16[1,136,1024]{2,1,0:T(8,128)(2,1)} %param.9) | copy-start | bytes 835588
  12.0 12.6 %collective-permute-start.4 = (bf16[136,1024]{1,0:T(8,128)(2,1)S(1)}, bf16[136,1024]{1,0:T(8,128)(2,1)S(1)}, u32[]{:S(2)}, u32[]{:S(2)}) collective-permute-start(bf16[136,1024]{1,0:T(8,128)(2,1)S(1)} %collective-permute-done.1.refs_2_), channel_id=1, source_target_pairs={{0,1},{1,0},{2,3},{3,2},{4,5},{5,4},{6,7},{7,6},{8,9},{9,8},{10,11... | collective-permute-start | bytes 835592 | tf_op jit(solution)/shard_map/ppermute | solution.py:475
  12.7 6.4 %collective-permute-start.8 = (bf16[136,512]{1,0:T(8,128)(2,1)S(1)}, bf16[136,512]{1,0:T(8,128)(2,1)S(1)}, u32[]{:S(2)}, u32[]{:S(2)}) collective-permute-start(bf16[136,512]{1,0:T(8,128)(2,1)S(1)} %collective-permute-done.3.refs_4_), channel_id=1, source_target_pairs={{0,2},{1,3},{2,0},{3,1},{4,6},{5,7},{6,4},{7,5},{8,10},{9,11},{10,... | collective-permute-start | bytes 417800 | tf_op jit(solution)/shard_map/ppermute | solution.py:475
  12.8 8.8 %collective-permute-start.6 = (bf16[136,512]{1,0:T(8,128)(2,1)S(1)}, bf16[136,512]{1,0:T(8,128)(2,1)S(1)}, u32[]{:S(2)}, u32[]{:S(2)}) collective-permute-start(bf16[136,512]{1,0:T(8,128)(2,1)S(1)} %collective-permute-done.3.refs_4_), channel_id=1, source_target_pairs={{0,1},{1,0},{2,3},{3,2},{4,5},{5,4},{6,7},{7,6},{8,9},{9,8},{10,11... | collective-permute-start | bytes 417800 | tf_op jit(solution)/shard_map/ppermute | solution.py:475
  16.1 8.6 %collective-permute-start.5 = (bf16[136,512]{1,0:T(8,128)(2,1)S(1)}, bf16[136,512]{1,0:T(8,128)(2,1)S(1)}, u32[]{:S(2)}, u32[]{:S(2)}) collective-permute-start(bf16[136,512]{1,0:T(8,128)(2,1)S(1)} %collective-permute-done.2.refs_3_), channel_id=1, source_target_pairs={{0,1},{1,0},{2,3},{3,2},{4,5},{5,4},{6,7},{7,6},{8,9},{9,8},{10,11... | collective-permute-start | bytes 417800 | tf_op jit(solution)/shard_map/ppermute | solution.py:475
  19.2 6.5 %collective-permute-start.7 = (bf16[136,512]{1,0:T(8,128)(2,1)S(1)}, bf16[136,512]{1,0:T(8,128)(2,1)S(1)}, u32[]{:S(2)}, u32[]{:S(2)}) collective-permute-start(bf16[136,512]{1,0:T(8,128)(2,1)S(1)} %collective-permute-done.2.refs_3_), channel_id=1, source_target_pairs={{0,2},{1,3},{2,0},{3,1},{4,6},{5,7},{6,4},{7,5},{8,10},{9,11},{10,... | collective-permute-start | bytes 417800 | tf_op jit(solution)/shard_map/ppermute | solution.py:475
  21.6 6.0 %collective-permute-start.10 = (bf16[136,512]{1,0:T(8,128)(2,1)S(1)}, bf16[136,512]{1,0:T(8,128)(2,1)S(1)}, u32[]{:S(2)}, u32[]{:S(2)}) collective-permute-start(bf16[136,512]{1,0:T(8,128)(2,1)S(1)} %collective-permute-done.8.refs_1_), channel_id=1, source_target_pairs={{0,1},{1,0},{2,3},{3,2},{4,5},{5,4},{6,7},{7,6},{8,9},{9,8},{10,11... | collective-permute-start | bytes 417800 | tf_op jit(solution)/shard_map/ppermute | solution.py:475
  24.6 3.9 %collective-permute-start.9 = (bf16[136,512]{1,0:T(8,128)(2,1)S(1)}, bf16[136,512]{1,0:T(8,128)(2,1)S(1)}, u32[]{:S(2)}, u32[]{:S(2)}) collective-permute-start(bf16[136,512]{1,0:T(8,128)(2,1)S(1)} %collective-permute-done.5.refs_6_), channel_id=1, source_target_pairs={{0,2},{1,3},{2,0},{3,1},{4,6},{5,7},{6,4},{7,5},{8,10},{9,11},{10,... | collective-permute-start | bytes 417800 | tf_op jit(solution)/shard_map/ppermute | solution.py:475
  28.5 12.2 %copy-start.1 = (bf16[1,512,2048]{2,1,0:T(8,128)(2,1)S(1)}, bf16[1,512,2048]{2,1,0:T(8,128)(2,1)}, u32[]{:S(2)}) copy-start(bf16[1,512,2048]{2,1,0:T(8,128)(2,1)} %param.14) | copy-start | bytes 6291460
  28.5 12.2 %copy-start.8 = (bf16[1,136,1024]{2,1,0:T(8,128)(2,1)S(1)}, bf16[1,136,1024]{2,1,0:T(8,128)(2,1)}, u32[]{:S(2)}) copy-start(bf16[1,136,1024]{2,1,0:T(8,128)(2,1)} %param.10) | copy-start | bytes 835588
  51.5 22.2 %collective-permute-start.18 = (bf16[256,1024]{1,0:T(8,128)(2,1)S(1)}, bf16[256,1024]{1,0:T(8,128)(2,1)S(1)}, u32[]{:S(2)}, u32[]{:S(2)}) collective-permute-start(bf16[256,1024]{1,0:T(8,128)(2,1)S(1)} %get-tuple-element.92), channel_id=1, source_target_pairs={{0,1},{1,0},{2,3},{3,2},{4,5},{5,4},{6,7},{7,6},{8,9},{9,8},{10,11... | collective-permute-start | bytes 1572872 | tf_op jit(solution)/shard_map/ppermute | solution.py:22
  52.0 21.7 %collective-permute-start.19 = (bf16[256,1024]{1,0:T(8,128)(2,1)S(1)}, bf16[256,1024]{1,0:T(8,128)(2,1)S(1)}, u32[]{:S(2)}, u32[]{:S(2)}) collective-permute-start(bf16[256,1024]{1,0:T(8,128)(2,1)S(1)} %get-tuple-element.93), channel_id=1, source_target_pairs={{0,2},{2,0},{1,3},{3,1},{4,6},{6,4},{5,7},{7,5},{8,10},{10,8},{9,1... | collective-permute-start | bytes 1572872 | tf_op jit(solution)/shard_map/ppermute | solution.py:22
  58.0 15.7 %collective-permute-start.17 = (bf16[1496,128]{1,0:T(8,128)(2,1)S(1)}, bf16[1496,128]{1,0:T(8,128)(2,1)S(1)}, u32[]{:S(2)}, u32[]{:S(2)}) collective-permute-start(bf16[1496,128]{1,0:T(8,128)(2,1)S(1)} %get-tuple-element.87), channel_id=1, source_target_pairs={{0,7},{1,6},{2,5},{3,4},{4,3},{5,2},{6,1},{7,0},{8,15},{9,14},{10,... | collective-permute-start | bytes 1148936 | tf_op jit(solution)/shard_map/ppermute | solution.py:475
  60.6 13.1 %collective-permute-start.13 = (bf16[408,128]{1,0:T(8,128)(2,1)S(1)}, bf16[408,128]{1,0:T(8,128)(2,1)S(1)}, u32[]{:S(2)}, u32[]{:S(2)}) collective-permute-start(bf16[408,128]{1,0:T(8,128)(2,1)S(1)} %get-tuple-element.83), channel_id=1, source_target_pairs={{0,4},{1,5},{2,6},{3,7},{4,0},{5,1},{6,2},{7,3},{8,12},{9,13},{10,... | collective-permute-start | bytes 313352 | tf_op jit(solution)/shard_map/ppermute | solution.py:475
  60.6 13.1 %collective-permute-start.16 = (bf16[408,128]{1,0:T(8,128)(2,1)S(1)}, bf16[408,128]{1,0:T(8,128)(2,1)S(1)}, u32[]{:S(2)}, u32[]{:S(2)}) collective-permute-start(bf16[408,128]{1,0:T(8,128)(2,1)S(1)} %get-tuple-element.86), channel_id=1, source_target_pairs={{0,6},{1,7},{2,4},{3,5},{4,2},{5,3},{6,0},{7,1},{8,14},{9,15},{10,... | collective-permute-start | bytes 313352 | tf_op jit(solution)/shard_map/ppermute | solution.py:475
  73.9 17.3 %collective-permute-start.20 = (bf16[128,1024]{1,0:T(8,128)(2,1)S(1)}, bf16[128,1024]{1,0:T(8,128)(2,1)S(1)}, u32[]{:S(2)}, u32[]{:S(2)}) collective-permute-start(bf16[128,1024]{1,0:T(8,128)(2,1)S(1)} %get-tuple-element.96), channel_id=1, source_target_pairs={{0,2},{2,0},{1,3},{3,1},{4,6},{6,4},{5,7},{7,5},{8,10},{10,8},{9,1... | collective-permute-start | bytes 786440 | tf_op jit(solution)/shard_map/ppermute | solution.py:22
  83.1 8.1 %collective-permute-start.21 = (bf16[128,1024]{1,0:T(8,128)(2,1)S(1)}, bf16[128,1024]{1,0:T(8,128)(2,1)S(1)}, u32[]{:S(2)}, u32[]{:S(2)}) collective-permute-start(bf16[128,1024]{1,0:T(8,128)(2,1)S(1)} %get-tuple-element.97), channel_id=1, source_target_pairs={{0,1},{1,0},{2,3},{3,2},{4,5},{5,4},{6,7},{7,6},{8,9},{9,8},{10,11... | collective-permute-start | bytes 786440 | tf_op jit(solution)/shard_map/ppermute | solution.py:22
  83.8 5.3 %collective-permute-start.12 = (bf16[408,128]{1,0:T(8,128)(2,1)S(1)}, bf16[408,128]{1,0:T(8,128)(2,1)S(1)}, u32[]{:S(2)}, u32[]{:S(2)}) collective-permute-start(bf16[408,128]{1,0:T(8,128)(2,1)S(1)} %get-tuple-element.82), channel_id=1, source_target_pairs={{0,2},{1,3},{2,0},{3,1},{4,6},{5,7},{6,4},{7,5},{8,10},{9,11},{10,... | collective-permute-start | bytes 313352 | tf_op jit(solution)/shard_map/ppermute | solution.py:475
  83.9 9.9 %collective-permute-start.11 = (bf16[408,128]{1,0:T(8,128)(2,1)S(1)}, bf16[408,128]{1,0:T(8,128)(2,1)S(1)}, u32[]{:S(2)}, u32[]{:S(2)}) collective-permute-start(bf16[408,128]{1,0:T(8,128)(2,1)S(1)} %get-tuple-element.81), channel_id=1, source_target_pairs={{0,1},{1,0},{2,3},{3,2},{4,5},{5,4},{6,7},{7,6},{8,9},{9,8},{10,11... | collective-permute-start | bytes 313352 | tf_op jit(solution)/shard_map/ppermute | solution.py:475
  84.6 9.2 %collective-permute-start.14 = (bf16[408,128]{1,0:T(8,128)(2,1)S(1)}, bf16[408,128]{1,0:T(8,128)(2,1)S(1)}, u32[]{:S(2)}, u32[]{:S(2)}) collective-permute-start(bf16[408,128]{1,0:T(8,128)(2,1)S(1)} %get-tuple-element.84), channel_id=1, source_target_pairs={{0,3},{1,2},{2,1},{3,0},{4,7},{5,6},{6,5},{7,4},{8,11},{9,10},{10,... | collective-permute-start | bytes 313352 | tf_op jit(solution)/shard_map/ppermute | solution.py:475
  89.1 6.4 %copy-start.3 = (bf16[1,1024,512]{2,1,0:T(8,128)(2,1)S(1)}, bf16[1,1024,512]{2,1,0:T(8,128)(2,1)}, u32[]{:S(2)}) copy-start(bf16[1,1024,512]{2,1,0:T(8,128)(2,1)} %param.11) | copy-start | bytes 3145732
  89.1 6.4 %copy-start.5 = (bf16[1,1024,512]{2,1,0:T(8,128)(2,1)S(1)}, bf16[1,1024,512]{2,1,0:T(8,128)(2,1)}, u32[]{:S(2)}) copy-start(bf16[1,1024,512]{2,1,0:T(8,128)(2,1)} %param.12) | copy-start | bytes 3145732
  89.1 6.4 %copy-start.7 = (bf16[1,1024,512]{2,1,0:T(8,128)(2,1)S(1)}, bf16[1,1024,512]{2,1,0:T(8,128)(2,1)}, u32[]{:S(2)}) copy-start(bf16[1,1024,512]{2,1,0:T(8,128)(2,1)} %param.13) | copy-start | bytes 3145732
  89.1 6.4 %collective-permute-start.15 = (bf16[408,128]{1,0:T(8,128)(2,1)S(1)}, bf16[408,128]{1,0:T(8,128)(2,1)S(1)}, u32[]{:S(2)}, u32[]{:S(2)}) collective-permute-start(bf16[408,128]{1,0:T(8,128)(2,1)S(1)} %get-tuple-element.85), channel_id=1, source_target_pairs={{0,5},{1,4},{2,7},{3,6},{4,1},{5,0},{6,3},{7,2},{8,13},{9,12},{10,... | collective-permute-start | bytes 313352 | tf_op jit(solution)/shard_map/ppermute | solution.py:475
  91.4 19.2 %collective-permute-start.24 = (bf16[64,1024]{1,0:T(8,128)(2,1)S(1)}, bf16[64,1024]{1,0:T(8,128)(2,1)S(1)}, u32[]{:S(2)}, u32[]{:S(2)}) collective-permute-start(bf16[64,1024]{1,0:T(8,128)(2,1)S(1)} %get-tuple-element.99), channel_id=1, source_target_pairs={{0,4},{4,0},{1,5},{5,1},{2,6},{6,2},{3,7},{7,3},{8,12},{12,8},{9,1... | collective-permute-start | bytes 393224 | tf_op jit(solution)/shard_map/ppermute | solution.py:22
  92.2 18.4 %collective-permute-start.23 = (bf16[64,1024]{1,0:T(8,128)(2,1)S(1)}, bf16[64,1024]{1,0:T(8,128)(2,1)S(1)}, u32[]{:S(2)}, u32[]{:S(2)}) collective-permute-start(bf16[64,1024]{1,0:T(8,128)(2,1)S(1)} %get-tuple-element.98.refs_13_), channel_id=1, source_target_pairs={{0,4},{4,0},{1,5},{5,1},{2,6},{6,2},{3,7},{7,3},{8,12},{12,8},{9,1... | collective-permute-start | bytes 393224 | tf_op jit(solution)/shard_map/ppermute | solution.py:22
  96.9 19.0 %collective-permute-start.22 = (bf16[136,1024]{1,0:T(8,128)(2,1)S(1)}, bf16[136,1024]{1,0:T(8,128)(2,1)S(1)}, u32[]{:S(2)}, u32[]{:S(2)}) collective-permute-start(bf16[136,1024]{1,0:T(8,128)(2,1)S(1)} %shard_map.135), channel_id=1, source_target_pairs={{8,0},{16,8},{24,16},{9,1},{17,9},{25,17},{10,2},{18,10},{26,18},{... | collective-permute-start | bytes 835592 | tf_op jit(solution)/shard_map/ppermute | solution.py:28
  111.5 4.5 %copy-start.9 = (s32[1,136]{1,0:T(1,128)S(1)}, s32[1,136]{1,0:T(1,128)}, u32[]{:S(2)}) copy-start(s32[1,136]{1,0:T(1,128)} %order_ref.1) | copy-start | bytes 1636
